TPU v7x, 256 devices: a whole 4x4x8 slice. The times are simulated.
256 devices in a mesh: seq: 32 (over x, z), own: 8 (over y, core).
Axes of the slice: x: 4, y: 4, z: 8, core: 2. Of those that a mesh axis runs over, the one named last changes fastest.
Arguments:
- queries: bfloat16 [8192, 8192], P('seq', 'own'), may hold values from -75 to 75
- key_rows: bfloat16 [8192, 1024], P('seq', 'own'), may hold values from -6 to 6
- value_rows: bfloat16 [8192, 1024], P('seq', 'own'), may hold values from -6 to 6
- out_grad: bfloat16 [8192, 8192], P('seq', 'own'), may hold values from -6 to 6
- inputs: bfloat16 [8192, 8192], P('seq', 'own'), may hold values from -6 to 6
- key_weight: bfloat16 [8192, 1024], P('own', 'seq'), may hold values from -0.0625 to 0.0625
- value_weight: bfloat16 [8192, 1024], P('own', 'seq'), may hold values from -0.0625 to 0.0625
- far_blocks: int32 [64, 4], P('seq'), may hold values from 0 to 60, as said below
- far_count: int32 [64], P('seq'), may hold values from 0 to 4, as said below
Outputs:
- query_grad: bfloat16 [8192, 8192], P('seq', 'own')
- input_grad: bfloat16 [8192, 8192], P('seq', 'own')
- key_weight_grad: float32 [8192, 1024], P('own', 'seq')
- value_weight_grad: float32 [8192, 1024], P('own', 'seq')
Inputs may be any that keep to these rules, and one draw needn't show every extreme that they name: `far_blocks`: the first far_count[i] entries of row i are distinct blocks below i - 2; the other entries are 0. far_count[i] is at most min(4, i - 2) and at least 1 where that bound is positive.
All inputs are finite; a program needn't handle non-finite values.
Results may differ from a plain program's by a relative error of at most 0.0095.
Values may be sent and summed in bfloat16 or wider, within the bound.
No kernel may reach another device: no remote copies, remote signals or barrier semaphores. Data moves between devices by JAX's collectives and lax.ppermute only.
A program may use at most 128 MiB of HBM per device.

v0:
```python
import math

import jax
import jax.numpy as jnp
from jax import lax
from jax.sharding import PartitionSpec as P

DH = 128
GQ = 8
BLK = 128
WIN = 3
FARS = 4


def shifted(value, axis, steps):
    count = lax.axis_size(axis)
    leading, last = (max(0, -steps), min(count, count - steps))
    return lax.ppermute(value, axis, [(source, source + steps) for source in range(leading, last)])


def attend_block(query_block, grad_block, key_block, value_block, allowed):
    count_rows = query_block.shape[0]
    inv_root = 1.0 / math.sqrt(DH)
    q_heads = (
        query_block.reshape(count_rows, GQ, DH).transpose(1, 0, 2).reshape(GQ * count_rows, DH)
    )
    g_heads = grad_block.reshape(count_rows, GQ, DH).transpose(1, 0, 2).reshape(GQ * count_rows, DH)
    scores = (
        lax.dot_general(
            q_heads, key_block, (((1,), (1,)), ((), ())), preferred_element_type=jnp.float32
        )
        * inv_root
    )
    wide_mask = jnp.tile(allowed, (GQ, 1))
    scores = jnp.where(wide_mask, scores, jnp.float32(-1e30))
    row_max = jnp.max(scores, axis=1, keepdims=True)
    exp_scores = jnp.exp(scores - row_max)
    soft_p = exp_scores / jnp.sum(exp_scores, axis=1, keepdims=True)
    soft_b = soft_p.astype(jnp.bfloat16)
    output = jnp.dot(soft_b, value_block, preferred_element_type=jnp.float32)
    deltas = jnp.sum(g_heads.astype(jnp.float32) * output, axis=1, keepdims=True)
    grad_p = lax.dot_general(
        g_heads, value_block, (((1,), (1,)), ((), ())), preferred_element_type=jnp.float32
    )
    grad_sb = (soft_p * (grad_p - deltas) * inv_root).astype(jnp.bfloat16)
    grad_q = jnp.dot(grad_sb, key_block, preferred_element_type=jnp.float32).astype(jnp.bfloat16)
    grad_q = grad_q.reshape(GQ, count_rows, DH).transpose(1, 0, 2).reshape(count_rows, GQ * DH)
    grad_k = lax.dot_general(
        grad_sb, q_heads, (((0,), (0,)), ((), ())), preferred_element_type=jnp.float32
    )
    grad_v = lax.dot_general(
        soft_b, g_heads, (((0,), (0,)), ((), ())), preferred_element_type=jnp.float32
    )
    return (grad_q, grad_k, grad_v)


def block_mask(block_index, live_count):
    query_pos = block_index * BLK + jnp.arange(BLK, dtype=jnp.int32)[:, None]
    key_pos = (block_index - WIN + 1) * BLK + jnp.arange(WIN * BLK, dtype=jnp.int32)[None, :]
    window_ok = (key_pos <= query_pos) & (key_pos >= 0)
    far_slots = (jnp.arange(FARS * BLK, dtype=jnp.int32) // BLK)[None, :]
    far_ok = jnp.broadcast_to(far_slots < live_count, (BLK, FARS * BLK))
    return jnp.concatenate([window_ok, far_ok], axis=1)


def add_into(buffer, addend, offset):
    current = lax.dynamic_slice_in_dim(buffer, offset, addend.shape[0], 0)
    return lax.dynamic_update_slice_in_dim(buffer, current + addend, offset, 0)


def local(
    queries, key_rows, value_rows, out_grad, inputs, key_weight, value_weight, far_blocks, far_count
):
    tok_rows = queries.shape[0]
    block_count = tok_rows // BLK
    halo_rows = (WIN - 1) * BLK
    head_width = key_rows.shape[1]
    seq_index = lax.axis_index("seq")
    key_proj, value_proj = (
        lax.all_gather(key_weight, "seq", axis=1, tiled=True),
        lax.all_gather(value_weight, "seq", axis=1, tiled=True),
    )
    keys_whole, values_whole = (
        lax.all_gather(key_rows, "seq", axis=0, tiled=True),
        lax.all_gather(value_rows, "seq", axis=0, tiled=True),
    )
    total_rows = keys_whole.shape[0]
    keys_before, values_before = shifted((key_rows, value_rows), "seq", 1)
    keys_extended = jnp.concatenate([keys_before, key_rows])
    values_extended = jnp.concatenate([values_before, value_rows])
    first_block = seq_index * block_count

    def visit(block_index, loop_state):
        query_acc, key_local, value_local, key_spread, value_spread = loop_state
        query_block = lax.dynamic_slice_in_dim(queries, block_index * BLK, BLK, 0)
        grad_block = lax.dynamic_slice_in_dim(out_grad, block_index * BLK, BLK, 0)
        listed = lax.dynamic_index_in_dim(far_blocks, block_index, 0, keepdims=False)
        live_count = lax.dynamic_index_in_dim(far_count, block_index, 0, keepdims=False)
        key_parts = [lax.dynamic_slice_in_dim(keys_extended, block_index * BLK, WIN * BLK, 0)]
        value_parts = [lax.dynamic_slice_in_dim(values_extended, block_index * BLK, WIN * BLK, 0)]
        for slot_index in range(FARS):
            key_parts.append(lax.dynamic_slice_in_dim(keys_whole, listed[slot_index] * BLK, BLK, 0))
            value_parts.append(
                lax.dynamic_slice_in_dim(values_whole, listed[slot_index] * BLK, BLK, 0)
            )
        allowed = block_mask(first_block + block_index, live_count)
        grad_q, grad_k, grad_v = attend_block(
            query_block,
            grad_block,
            jnp.concatenate(key_parts),
            jnp.concatenate(value_parts),
            allowed,
        )
        query_acc = lax.dynamic_update_slice_in_dim(query_acc, grad_q, block_index * BLK, 0)
        key_local = add_into(key_local, grad_k[: WIN * BLK], block_index * BLK)
        value_local = add_into(value_local, grad_v[: WIN * BLK], block_index * BLK)
        for slot_index in range(FARS):
            far_start = halo_rows + listed[slot_index] * BLK
            lower = (WIN + slot_index) * BLK
            key_spread = add_into(key_spread, grad_k[lower : lower + BLK], far_start)
            value_spread = add_into(value_spread, grad_v[lower : lower + BLK], far_start)
        return (query_acc, key_local, value_local, key_spread, value_spread)

    local_zero = jnp.zeros((halo_rows + tok_rows, head_width), jnp.float32)
    spread_zero = jnp.zeros((halo_rows + total_rows, head_width), jnp.float32)
    query_zero = jnp.zeros((tok_rows, queries.shape[1]), jnp.bfloat16)
    query_grad, key_local, value_local, key_spread, value_spread = lax.fori_loop(
        0, block_count, visit, (query_zero, local_zero, local_zero, spread_zero, spread_zero)
    )
    key_back, value_back = shifted((key_local[:halo_rows], value_local[:halo_rows]), "seq", -1)
    zero_tail = jnp.zeros((tok_rows - halo_rows, head_width), jnp.float32)
    key_own = key_local[halo_rows:] + jnp.concatenate([zero_tail, key_back])
    value_own = value_local[halo_rows:] + jnp.concatenate([zero_tail, value_back])
    key_far, value_far = (
        lax.psum_scatter(key_spread[halo_rows:], "seq", scatter_dimension=0, tiled=True),
        lax.psum_scatter(value_spread[halo_rows:], "seq", scatter_dimension=0, tiled=True),
    )
    key_grad = (key_far + key_own).astype(jnp.bfloat16)
    value_grad = (value_far + value_own).astype(jnp.bfloat16)
    key_all, value_all = (
        lax.all_gather(key_grad, "own", axis=1, tiled=True),
        lax.all_gather(value_grad, "own", axis=1, tiled=True),
    )
    contract_cols = (((1,), (1,)), ((), ()))
    input_grad = lax.dot_general(
        key_all, key_proj, contract_cols, preferred_element_type=jnp.float32
    ) + lax.dot_general(value_all, value_proj, contract_cols, preferred_element_type=jnp.float32)
    contract_rows = (((0,), (0,)), ((), ()))
    key_term = lax.dot_general(inputs, key_all, contract_rows, preferred_element_type=jnp.float32)
    value_term = lax.dot_general(
        inputs, value_all, contract_rows, preferred_element_type=jnp.float32
    )
    key_weight_grad, value_weight_grad = (
        lax.psum_scatter(key_term, "seq", scatter_dimension=1, tiled=True),
        lax.psum_scatter(value_term, "seq", scatter_dimension=1, tiled=True),
    )
    return (query_grad, input_grad.astype(jnp.bfloat16), key_weight_grad, value_weight_grad)


def solution(mesh):
    return jax.shard_map(
        local,
        mesh=mesh,
        in_specs=(
            P("seq", "own"),
            P("seq", "own"),
            P("seq", "own"),
            P("seq", "own"),
            P("seq", "own"),
            P("own", "seq"),
            P("own", "seq"),
            P("seq", None),
            P("seq"),
        ),
        out_specs=(P("seq", "own"), P("seq", "own"), P("own", "seq"), P("own", "seq")),
        check_vma=False,
    )
```

profile of v0, /device:TPU:1, one launch (start us, length us, event | category | flops | bytes accessed | tf_op | source)
XLA Modules:
  0.0 1301.6 jit_solution(8954734506460564920)
XLA Ops:
  8.7 4.4 collective-permute-start
  13.1 3.5 collective-permute-start.1
  19.8 68.6 %all-gather.5.cloned.1.call-done = bf16[8192,128]{1,0:T(8,128)(2,1)} async-done(((bf16[256,128]{1,0:T(8,128)(2,1)}), bf16[8192,128]{1,0:T(8,128)(2,1)}) %all-gather.5.cloned.1.call-update) | async-done | bytes 2097168 | tf_op jit(solution)/shard_map/all_gather | solution.py:84
  88.4 77.7 %all-gather.7.cloned.1.call-done = bf16[8192,128]{1,0:T(8,128)(2,1)} async-done(((bf16[256,128]{1,0:T(8,128)(2,1)}), bf16[8192,128]{1,0:T(8,128)(2,1)}) %all-gather.7.cloned.1.call-update) | async-done | bytes 2097168 | tf_op jit(solution)/shard_map/all_gather | solution.py:85
  170.6 2.2 broadcast_in_dim.67.clone
  172.8 72.7 %while.26 = (s32[]{:T(128)}, bf16[256,1024]{1,0:T(8,128)(2,1)}, f32[512,128]{1,0:T(8,128)}, f32[512,128]{1,0:T(8,128)}, f32[8448,128]{1,0:T(8,128)}, /*index=5*/...) while((s32[]{:T(128)}, bf16[256,1024]{1,0:T(8,128)(2,1)}, ...), condition=%wide.region_4.5_spmd, body=%wide.region_0.4_spmd.sunk | while | flops 1423100672 | bytes 61846076 | solution.py:127
  191.7 3.2 multiply_convert_fusion.2
  228.0 3.2 multiply_convert_fusion.2
  245.5 4.5 slice.226
  250.0 4.4 slice.229
  257.9 4.4 collective-permute-done.2
  262.3 205.3 %reduce-scatter.5.cloned.1.call-done = f32[256,128]{1,0:T(8,128)} async-done(((f32[8192,128]{1,0:T(8,128)}), f32[256,128]{1,0:T(8,128)}) %reduce-scatter.5.cloned.1.call-update) | async-done | bytes 131088 | tf_op jit(solution)/shard_map/reduce_scatter | solution.py:135
  468.6 18.8 %all_gather.20 = bf16[256,1024]{1,0:T(8,128)(2,1)S(1)} all-gather(bf16[256,128]{1,0:T(8,128)(2,1)S(1)} %add_convert_fusion.1), channel_id=1, replica_groups=mesh['seq'=32,'own'=8] {'own'}, dimensions={1}, use_global_device_ids=true | all-gather | bytes 589824 | tf_op jit(solution)/shard_map/all_gather | solution.py:141
  487.4 2.8 convolution_bitcast_fusion.1
  492.4 6.3 collective-permute-done.3
  498.8 192.6 %reduce-scatter.7.cloned.1.call-done = f32[256,128]{1,0:T(8,128)} async-done(((f32[8192,128]{1,0:T(8,128)}), f32[256,128]{1,0:T(8,128)}) %reduce-scatter.7.cloned.1.call-update) | async-done | bytes 131088 | tf_op jit(solution)/shard_map/reduce_scatter | solution.py:136
  692.4 18.9 %all_gather.22 = bf16[256,1024]{1,0:T(8,128)(2,1)S(1)} all-gather(bf16[256,128]{1,0:T(8,128)(2,1)S(1)} %add_convert_fusion), channel_id=1, replica_groups=mesh['seq'=32,'own'=8] {'own'}, dimensions={1}, use_global_device_ids=true | all-gather | bytes 589824 | tf_op jit(solution)/shard_map/all_gather | solution.py:142
  711.3 2.7 convolution_bitcast_fusion
  714.0 57.2 %all-gather.11.cloned.1.call-done = bf16[1024,1024]{0,1:T(8,128)(2,1)} async-done(((bf16[1024,32]{0,1:T(8,128)(2,1)}), bf16[1024,1024]{0,1:T(8,128)(2,1)}) %all-gather.11.cloned.1.call-update) | async-done | bytes 2097168 | tf_op jit(solution)/shard_map/all_gather | solution.py:81
  771.2 2.3 fusion.27
  773.5 75.3 %all-gather.9.cloned.1.call-done = bf16[1024,1024]{0,1:T(8,128)(2,1)} async-done(((bf16[1024,32]{0,1:T(8,128)(2,1)}), bf16[1024,1024]{0,1:T(8,128)(2,1)}) %all-gather.9.cloned.1.call-update) | async-done | bytes 2097168 | tf_op jit(solution)/shard_map/all_gather | solution.py:80
  848.8 3.1 fusion.23
  851.9 218.7 %reduce-scatter.9.cloned.1.call-done = f32[1024,32]{0,1:T(8,128)} async-done(((f32[1024,1024]{0,1:T(8,128)}), f32[1024,32]{0,1:T(8,128)}) %reduce-scatter.9.cloned.1.call-update) | async-done | bytes 131088 | tf_op jit(solution)/shard_map/reduce_scatter | solution.py:154
  1070.5 224.2 %reduce-scatter.11.cloned.1.call-done = f32[1024,32]{0,1:T(8,128)} async-done(((f32[1024,1024]{0,1:T(8,128)}), f32[1024,32]{0,1:T(8,128)}) %reduce-scatter.11.cloned.1.call-update) | async-done | bytes 131088 | tf_op jit(solution)/shard_map/reduce_scatter | solution.py:155
  (148 shorter events, 77.8 us)
Async XLA Ops:
  7.2 480.2 %copy-start = (bf16[256,1024]{1,0:T(8,128)(2,1)S(1)}, bf16[256,1024]{1,0:T(8,128)(2,1)}, u32[]{:S(2)}) copy-start(bf16[256,1024]{1,0:T(8,128)(2,1)} %param.15) | copy-start | bytes 1572868
  7.2 81.2 %all-gather.5.cloned.1.call-start = ((), (), s32[]{:S(2)}) async-start(), calls=%async_computation.4 | async-start | bytes 2162688 | tf_op jit(solution)/shard_map/all_gather | solution.py:84
  7.9 158.3 %all-gather.7.cloned.1.call-start = ((), (), s32[]{:S(2)}) async-start(), calls=%async_computation.5 | async-start | bytes 2162688 | tf_op jit(solution)/shard_map/all_gather | solution.py:85
  8.7 458.9 %reduce-scatter.5.cloned.1.call-start = ((), (), s32[]{:S(2)}) async-start(), calls=%async_computation.6 | async-start | bytes 4325376 | tf_op jit(solution)/shard_map/reduce_scatter | solution.py:135
  8.7 7.9 collective-permute-start
  13.1 5.2 collective-permute-start.1
  168.5 4.3 copy-start.8
  168.5 4.3 copy-start.9
  185.0 3.0 copy-start.2
  188.0 1.8 copy-start.1
  188.6 1.4 copy-start.4
  191.6 3.2 copy-start.3
  191.6 3.9 copy-start.6
  221.3 3.0 copy-start.2
  224.4 1.8 copy-start.1
  228.0 3.2 copy-start.3
  228.0 3.9 copy-start.6
  250.0 441.4 %reduce-scatter.7.cloned.1.call-start = ((), (), s32[]{:S(2)}) async-start(), calls=%async_computation.8 | async-start | bytes 4325376 | tf_op jit(solution)/shard_map/reduce_scatter | solution.py:136
  254.4 516.7 %all-gather.11.cloned.1.call-start = ((), (), s32[]{:S(2)}) async-start(), calls=%async_computation.9 | async-start | bytes 2162688 | tf_op jit(solution)/shard_map/all_gather | solution.py:81
  255.0 593.8 %all-gather.9.cloned.1.call-start = ((), (), s32[]{:S(2)}) async-start(), calls=%async_computation.7 | async-start | bytes 2162688 | tf_op jit(solution)/shard_map/all_gather | solution.py:80
  255.6 814.9 %reduce-scatter.9.cloned.1.call-start = ((), (), s32[]{:S(2)}) async-start(), calls=%async_computation.10 | async-start | bytes 4325376 | tf_op jit(solution)/shard_map/reduce_scatter | solution.py:154
  256.6 5.7 collective-permute-start.2
  490.2 804.5 %reduce-scatter.11.cloned.1.call-start = ((), (), s32[]{:S(2)}) async-start(), calls=%async_computation.11 | async-start | bytes 4325376 | tf_op jit(solution)/shard_map/reduce_scatter | solution.py:155
  491.1 7.6 collective-permute-start.3
  (5 other events, 5.4 us)
Sparse Core Ops, SparseCore 0:
  10.6 77.7 all-gather.4
  91.0 75.1 all-gather.6
  250.1 217.4 reduce-scatter.4
  471.9 219.5 reduce-scatter.6
  693.8 77.2 all-gather.10
  773.6 75.1 all-gather.8
  853.3 217.2 reduce-scatter.8
  1075.5 219.1 reduce-scatter.10
where the time goes:
time: 1310 us; the launch traced here: 1300 us
  waiting for transfers between devices  1130 us (86%)
  local copies, waits for them, and re-layouts  40.9 us (3%)
  blocking collectives  37.7 us (3%)
  other arithmetic  33.1 us (3%)
  matrix products  25.9 us (2%)
  between operations  14.2 us (1%)
    reduce_scatter x1, waiting for transfers between devices, local(): lax.psum_scatter(value_term, 'seq', scatter_dimension=1, tiled=True)  224 us
    reduce_scatter x1, waiting for transfers between devices, local(): lax.psum_scatter(key_term, 'seq', scatter_dimension=1, tiled=True)  219 us
    reduce_scatter x1, waiting for transfers between devices, local(): lax.psum_scatter(key_spread[halo_rows:], 'seq', scatter_dimension=0, tile...  205 us
    reduce_scatter x1, waiting for transfers between devices, local(): lax.psum_scatter(value_spread[halo_rows:], 'seq', scatter_dimension=0, ti...  193 us
    all_gather x1, waiting for transfers between devices, local(): lax.all_gather(value_rows, 'seq', axis=0, tiled=True)  77.7 us
    all_gather x1, waiting for transfers between devices, local(): lax.all_gather(key_weight, 'seq', axis=1, tiled=True)  75.3 us
    all_gather x1, waiting for transfers between devices, local(): lax.all_gather(key_rows, 'seq', axis=0, tiled=True)  68.6 us
    all_gather x1, waiting for transfers between devices, local(): lax.all_gather(value_weight, 'seq', axis=1, tiled=True)  57.2 us
  transfers between devices with their start and end apart: 12, of which 11 were waited for; matrix products, arithmetic and copies ran while one was open for 2% of the time, Pallas kernels for 0%

commit v1 on v0

v1 whole, which is shorter than its diff:
```python
import functools
import math

import jax
import jax.numpy as jnp
from jax import lax
from jax.experimental import pallas as pl
from jax.experimental.pallas import tpu as pltpu
from jax.sharding import PartitionSpec as P

DH = 128
GQ = 8
BLK = 128
WIN = 3
FARS = 4
NX = 4
NZ = 8
NB = 2
PLANE = NB * NZ
SLOTS = NB * FARS
X_GROUPS = [[x * NZ + z for x in range(NX)] for z in range(NZ)]
Z_GROUPS = [[x * NZ + z for z in range(NZ)] for x in range(NX)]
SCALE = 1.0 / math.sqrt(DH)
EXP2_SCALE = SCALE * math.log2(math.e)
NEG = -1e30

SMEM = pl.BlockSpec(memory_space=pltpu.SMEM)
VMEM = pl.BlockSpec(memory_space=pltpu.VMEM)
NT = (((1,), (1,)), ((), ()))
F32 = jnp.float32
BF16 = jnp.bfloat16


def params(mib):
    return pltpu.CompilerParams(vmem_limit_bytes=mib << 20)


def shifted(value, axis, steps):
    count = lax.axis_size(axis)
    leading, last = (max(0, -steps), min(count, count - steps))
    return lax.ppermute(value, axis, [(source, source + steps) for source in range(leading, last)])


def pick_kernel(lists_ref, plane_ref, out_ref):
    def body(i, carry):
        row = pl.multiple_of(lax.rem(lists_ref[i], PLANE) * BLK, BLK)
        out_ref[i] = plane_ref[pl.ds(row, BLK), :]
        return carry

    lax.fori_loop(0, NX * SLOTS, body, 0)


def pick(lists, plane):
    return pl.pallas_call(
        pick_kernel,
        out_shape=jax.ShapeDtypeStruct((NX * SLOTS, BLK, 2 * DH), BF16),
        in_specs=[SMEM, VMEM],
        out_specs=VMEM,
        compiler_params=params(16),
        name="pick_far",
    )(lists, plane)


def attend_kernel(
    at_ref, far_ref, count_ref, q_ref, g_ref, prev_ref, own_ref, far_kv_ref,
    qg_ref, win_ref, farg_ref, k_ref, v_ref, kt_ref, acc_ref, tri_ref,
):
    win_ref[...] = jnp.zeros_like(win_ref)
    key_at = lax.broadcasted_iota(jnp.int32, (BLK, 2 * BLK), 0)
    query_at = lax.broadcasted_iota(jnp.int32, (BLK, 2 * BLK), 1) % BLK
    tri_ref[...] = jnp.where(key_at <= query_at, 0.0, NEG)

    def block(b, carry):
        index = at_ref[0] * NB + b
        for w in range(WIN):
            local = b + w
            lower = pl.multiple_of(lax.rem(local, NB) * BLK, BLK)
            before = prev_ref[pl.ds(lower, BLK), :]
            mine = own_ref[pl.ds(lower, BLK), :]
            both = jnp.where(local < NB, before, mine)
            k_ref[w * BLK : (w + 1) * BLK, :] = both[:, :DH]
            v_ref[w * BLK : (w + 1) * BLK, :] = both[:, DH:]
        for j in range(FARS):
            slot = b * FARS + j
            owner = lax.div(far_ref[slot], PLANE)
            both = far_kv_ref[owner * SLOTS + slot]
            k_ref[(WIN + j) * BLK : (WIN + j + 1) * BLK, :] = both[:, :DH]
            v_ref[(WIN + j) * BLK : (WIN + j + 1) * BLK, :] = both[:, DH:]
        kt_ref[...] = k_ref[...].astype(F32).T.astype(BF16)
        acc_ref[...] = jnp.zeros_like(acc_ref)
        biases = [
            jnp.where(index >= 2, 0.0, NEG).astype(F32),
            jnp.where(index >= 1, 0.0, NEG).astype(F32),
            None,
        ] + [jnp.where(j < count_ref[b], 0.0, NEG).astype(F32) for j in range(FARS)]
        rows = pl.ds(pl.multiple_of(b * BLK, BLK), BLK)
        for pair in range(GQ // 2):
            lo = pair * 2 * DH
            q2 = jnp.concatenate([q_ref[rows, lo : lo + DH], q_ref[rows, lo + DH : lo + 2 * DH]])
            g2 = jnp.concatenate([g_ref[rows, lo : lo + DH], g_ref[rows, lo + DH : lo + 2 * DH]])
            scores = lax.dot_general(k_ref[...], q2, NT, preferred_element_type=F32)
            parts = []
            for c in range(WIN + FARS):
                part = scores[c * BLK : (c + 1) * BLK, :]
                bias = tri_ref[...] if biases[c] is None else biases[c]
                parts.append(part + bias)
            scores = jnp.concatenate(parts)
            top = jnp.max(scores, axis=0, keepdims=True)
            expo = jnp.exp2((scores - top) * EXP2_SCALE)
            inv = 1.0 / jnp.sum(expo, axis=0, keepdims=True)
            soft = expo * inv
            grad_p = lax.dot_general(v_ref[...], g2, NT, preferred_element_type=F32)
            delta = jnp.sum(soft * grad_p, axis=0, keepdims=True)
            soft_b = soft.astype(BF16)
            grad_s = (soft * (grad_p - delta)).astype(BF16)
            acc_ref[:, :DH] += jnp.dot(grad_s, q2, preferred_element_type=F32)
            acc_ref[:, DH:] += jnp.dot(soft_b, g2, preferred_element_type=F32)
            grad_q = jnp.dot(kt_ref[...], grad_s, preferred_element_type=F32).T * SCALE
            qg_ref[rows, lo : lo + DH] = grad_q[:BLK].astype(BF16)
            qg_ref[rows, lo + DH : lo + 2 * DH] = grad_q[BLK:].astype(BF16)
        acc_ref[:, :DH] = acc_ref[:, :DH] * SCALE
        window = pl.ds(pl.multiple_of(b * BLK, BLK), WIN * BLK)
        win_ref[window, :] += acc_ref[: WIN * BLK, :]
        for j in range(FARS):
            farg_ref[b * FARS + j] = acc_ref[(WIN + j) * BLK : (WIN + j + 1) * BLK, :].astype(BF16)
        return carry

    lax.fori_loop(0, NB, block, 0)


def attend(at, far, count, queries, out_grad, prev, own, far_kv):
    keys = (WIN + FARS) * BLK
    return pl.pallas_call(
        attend_kernel,
        out_shape=(
            jax.ShapeDtypeStruct((NB * BLK, GQ * DH), BF16),
            jax.ShapeDtypeStruct((2 * NB * BLK, 2 * DH), F32),
            jax.ShapeDtypeStruct((SLOTS, BLK, 2 * DH), BF16),
        ),
        in_specs=[SMEM, SMEM, SMEM] + [VMEM] * 5,
        out_specs=(VMEM, VMEM, VMEM),
        scratch_shapes=[
            pltpu.VMEM((keys, DH), BF16),
            pltpu.VMEM((keys, DH), BF16),
            pltpu.VMEM((DH, keys), BF16),
            pltpu.VMEM((keys, 2 * DH), F32),
            pltpu.VMEM((BLK, 2 * BLK), F32),
        ],
        compiler_params=params(40),
        cost_estimate=pl.CostEstimate(flops=2_400_000_000 * 4, bytes_accessed=6 << 20, transcendentals=2_000_000),
        name="attend",
    )(at, far, count, queries, out_grad, prev, own, far_kv)


def spread_kernel(x_ref, lists_ref, far_ref, out_ref, acc_ref):
    acc_ref[...] = jnp.zeros_like(acc_ref)

    def body(i, carry):
        listed = lists_ref[i]

        @pl.when(lax.div(listed, PLANE) == x_ref[0])
        def _():
            at = lax.rem(listed, PLANE)
            acc_ref[at] += far_ref[i].astype(F32)

        return carry

    lax.fori_loop(0, NX * SLOTS, body, 0)
    out_ref[...] = acc_ref[...].astype(BF16)


def spread(x_at, lists, far_all):
    return pl.pallas_call(
        spread_kernel,
        out_shape=jax.ShapeDtypeStruct((PLANE, BLK, 2 * DH), BF16),
        in_specs=[SMEM, SMEM, VMEM],
        out_specs=VMEM,
        scratch_shapes=[pltpu.VMEM((PLANE, BLK, 2 * DH), F32)],
        compiler_params=params(16),
        name="spread_far",
    )(x_at, lists, far_all)


def local(
    queries, key_rows, value_rows, out_grad, inputs, key_weight, value_weight, far_blocks, far_count
):
    tokens = queries.shape[0]
    seq_index = lax.axis_index("seq").astype(jnp.int32)
    x_index = lax.div(seq_index, NZ)
    at = seq_index.reshape(1)
    own_kv = jnp.concatenate([key_rows, value_rows], axis=1)

    lists = lax.all_gather(far_blocks, "seq", axis=0, axis_index_groups=X_GROUPS, tiled=True)
    lists = lists.reshape(NX * SLOTS)
    prev_kv = shifted(own_kv, "seq", 1)
    plane = lax.all_gather(own_kv, "seq", axis=0, axis_index_groups=Z_GROUPS, tiled=True)
    chosen = pick(lists, plane)
    far_kv = lax.all_to_all(chosen, "seq", 0, 0, axis_index_groups=X_GROUPS, tiled=True)

    key_weight, value_weight, inputs, far_kv = lax.optimization_barrier(
        (key_weight, value_weight, inputs, far_kv)
    )
    key_proj = lax.all_gather(key_weight.T, "seq", axis=0, tiled=True)
    value_proj = lax.all_gather(value_weight.T, "seq", axis=0, tiled=True)
    inputs_x = lax.all_gather(inputs, "seq", axis=0, axis_index_groups=X_GROUPS, tiled=True)

    query_grad, window, far_grad = attend(
        at, far_blocks.reshape(SLOTS), far_count, queries, out_grad, prev_kv, own_kv, far_kv
    )
    back = shifted(window[:tokens].astype(BF16), "seq", -1)
    far_all = lax.all_gather(far_grad, "seq", axis=0, axis_index_groups=X_GROUPS, tiled=True)
    dense = spread(x_index.reshape(1), lists, far_all)
    dense = dense.reshape(NZ, tokens, 2 * DH)
    terms = lax.all_to_all(dense, "seq", 0, 0, axis_index_groups=Z_GROUPS, tiled=True)
    kv_grad = jnp.sum(terms.astype(F32), axis=0) + back.astype(F32) + window[tokens:]
    kv_grad = kv_grad.astype(BF16)

    heads = lax.all_gather(kv_grad, "own", axis=0)
    key_all = heads[:, :, :DH].transpose(1, 0, 2).reshape(tokens, -1)
    value_all = heads[:, :, DH:].transpose(1, 0, 2).reshape(tokens, -1)
    input_grad = jnp.dot(key_all, key_proj, preferred_element_type=F32) + jnp.dot(
        value_all, value_proj, preferred_element_type=F32
    )

    quarter = lax.all_to_all(heads, "seq", 0, 0, axis_index_groups=X_GROUPS, tiled=True)
    quarter = quarter.reshape(NX, 2, tokens, 2, DH).transpose(1, 3, 4, 0, 2)
    quarter = quarter.reshape(4 * DH, NX * tokens)
    weight_t = jnp.dot(quarter, inputs_x, preferred_element_type=F32).astype(BF16)
    width = weight_t.shape[1]
    weight_t = weight_t.reshape(2, 2, 4, 32, width).transpose(0, 2, 1, 3, 4).reshape(NZ, 64, width)
    pieces = lax.all_to_all(weight_t, "seq", 0, 0, axis_index_groups=Z_GROUPS, tiled=True)
    weight_grad = jnp.sum(pieces.astype(F32), axis=0)
    return (
        query_grad,
        input_grad.astype(BF16),
        weight_grad[:32].T,
        weight_grad[32:].T,
    )


def solution(mesh):
    return jax.shard_map(
        local,
        mesh=mesh,
        in_specs=(
            P("seq", "own"),
            P("seq", "own"),
            P("seq", "own"),
            P("seq", "own"),
            P("seq", "own"),
            P("own", "seq"),
            P("own", "seq"),
            P("seq", None),
            P("seq"),
        ),
        out_specs=(P("seq", "own"), P("seq", "own"), P("own", "seq"), P("own", "seq")),
        check_vma=False,
    )
```

time: 1310 us -> 397 us (0.30)
  waiting for transfers between devices: 1130 us -> 293 us
  other arithmetic: 33.1 us -> 1.02 us
  local copies, waits for them, and re-layouts: 40.9 us -> 10.8 us
  matrix products: 25.9 us -> 8.27 us
  Pallas kernels: 0 us -> 14.7 us
    reduce_scatter x4 -> x0, waiting for transfers between devices: 841 us -> none  [the longest x1 224 us: local(): lax.psum_scatter(value_term, 'seq', scatter_dimension=1, tiled=True)]
    all_to_all x0 -> x3, waiting for transfers between devices: none -> 49.3 us  [the longest x1 27.8 us: local(): lax.all_to_all(dense, 'seq', 0, 0, axis_index_groups=Z_GROUPS, tiled=True)]
    all_gather x4 -> x6, waiting for transfers between devices: 279 us -> 242 us  [the longest x1 75.3 us: local(): value_proj = lax.all_gather(value_weight.T, 'seq', axis=0, tiled=True)]
    all_gather x2 -> x1, blocking collectives: 37.7 us -> 8.78 us  [local(): lax.all_gather(far_blocks, 'seq', axis=0, axis_index_groups=X_GROUPS, til...]
    dynamic_update_slice x16 -> x0, other arithmetic: 24.4 us -> none  [add_into(): return lax.dynamic_update_slice_in_dim(buffer, current + addend, offset, 0)]
    all_to_all x0 -> x1, blocking collectives: none -> 20.4 us  [local(): lax.all_to_all(heads, 'seq', 0, 0, axis_index_groups=X_GROUPS, tiled=True)]
    dot_general x16 -> x3, matrix products: 25.9 us -> 8.27 us  [the longest x1 3.11 us: local(): jnp.dot(value_all, value_proj, preferred_element_type=F32)]
    all_to_all x0 -> x3, starting transfers between devices: none -> 17.5 us  [the longest x1 6.73 us: local(): lax.all_to_all(weight_t, 'seq', 0, 0, axis_index_groups=Z_GROUPS, tiled=T...]
  transfers between devices with their start and end apart: 12 -> 11, of which waited for: 11 -> 8; matrix products, arithmetic and copies ran while one was open for 2% -> 3% of each run, Pallas kernels for 0% -> 0%
where the time goes in v1:
time: 397 us; the launch traced here: 393 us
  waiting for transfers between devices  293 us (74%)
  blocking collectives  29.2 us (7%)
  starting transfers between devices  22 us (6%)
  Pallas kernels  14.7 us (4%)
  between operations  14.2 us (4%)
  local copies, waits for them, and re-layouts  10.8 us (3%)
  matrix products  8.27 us (2%)
    all_gather x1, waiting for transfers between devices, local(): value_proj = lax.all_gather(value_weight.T, 'seq', axis=0, tiled=True)  75.3 us
    all_gather x1, waiting for transfers between devices, local(): key_proj = lax.all_gather(key_weight.T, 'seq', axis=0, tiled=True)  67.5 us
    all_gather x1, waiting for transfers between devices, local(): lax.all_gather(far_grad, 'seq', axis=0, axis_index_groups=X_GROUPS, tiled...  32.9 us
    all_gather x1, waiting for transfers between devices, local(): lax.all_gather(own_kv, 'seq', axis=0, axis_index_groups=Z_GROUPS, tiled=T...  29.3 us
    all_to_all x1, waiting for transfers between devices, local(): lax.all_to_all(dense, 'seq', 0, 0, axis_index_groups=Z_GROUPS, tiled=True)  27.8 us
    all_gather x1, waiting for transfers between devices, local(): heads = lax.all_gather(kv_grad, 'own', axis=0)  21.8 us
    all_to_all x1, waiting for transfers between devices, local(): lax.all_to_all(chosen, 'seq', 0, 0, axis_index_groups=X_GROUPS, tiled=True)  21.5 us
    all_to_all x1, blocking collectives, local(): lax.all_to_all(heads, 'seq', 0, 0, axis_index_groups=X_GROUPS, tiled=True)  20.4 us
  transfers between devices with their start and end apart: 11, of which 8 were waited for; matrix products, arithmetic and copies ran while one was open for 3% of the time, Pallas kernels for 0%

profile of v1, /device:TPU:1, one launch (start us, length us, event | category | flops | bytes accessed | tf_op | source)
XLA Modules:
  0.0 392.8 jit_solution(7508757840949612299)
XLA Ops:
  9.6 8.8 %all-gather.1 = s32[4,2,4]{2,1,0:T(2,128)S(1)} all-gather(s32[1,2,4]{2,1,0:T(2,128)} %bitcast.42), channel_id=1, replica_groups={{0,64,128,192},{8,72,136,200},{16,80,144,208},{24,88,152,216},{32,96,16..., dimensions={0}, use_global_device_ids=true | all-gather | bytes 160 | tf_op jit(solution)/shard_map/all_gather | solution.py:193
  18.5 29.3 %all-gather.9.cloned.1.call-done.plane_ref = bf16[2048,256]{1,0:T(8,128)(2,1)} async-done(((bf16[256,256]{1,0:T(8,128)(2,1)}), bf16[2048,256]{1,0:T(8,128)(2,1)}) %all-gather.9.cloned.1.call-update) | async-done | bytes 1048592 | tf_op jit(solution)/shard_map/all_gather | solution.py:196
  47.8 1.2 copy-done.1
  49.0 2.3 pick_far.1
  51.3 4.1 %all-to-all-start = ((bf16[32,128,256]{2,1,0:T(8,128)(2,1)}), bf16[32,128,256]{2,1,0:T(8,128)(2,1)S(1)}, u32[]{:S(2)}, u32[]{:S(2)}) async-start(bf16[32,128,256]{2,1,0:T(8,128)(2,1)} %pick_far.1), calls=%async_computation | async-start | bytes 4194304 | tf_op jit(solution)/shard_map/all_to_all | solution.py:198
  55.4 3.0 collective-permute-start
  58.5 21.5 %all-to-all-done.far_kv_ref = bf16[32,128,256]{2,1,0:T(8,128)(2,1)S(1)} async-done(((bf16[32,128,256]{2,1,0:T(8,128)(2,1)}), bf16[32,128,256]{2,1,0:T(8,128)(2,1)S(1)}, u32[]{:S(2)}, u32[]{:S(2)}) %all-to-all-start) | async-done | bytes 2097184 | tf_op jit(solution)/shard_map/all_to_all | solution.py:198
  81.0 9.7 %attend.1 = (bf16[256,1024]{1,0:T(8,128)(2,1)}, f32[512,256]{1,0:T(8,128)S(1)}, bf16[8,128,256]{2,1,0:T(8,128)(2,1)}) custom-call(s32[1]{0:T(128)} %bitcast.at_ref, s32[8]{0:T(128)S(1)} %reshape.42.far_ref, s32[2]{0:T(128)S(1)} %copy-done.6, bf16[256,1024]{1,0:T(8,128)(2,1)S(1)} %copy-done.4, bf16[256,1024]{1,0:T(8,128)(2,1)S(1)} %copy-done.5, ...), custom_call_target="tpu_custom_call" | custom-call | flops 9600000000 | bytes 6291456 | tf_op jit(solution)/shard_map/attend/pallas_call | solution.py:133
  90.8 32.9 %all-gather.11.cloned.1.call-done.far_ref = bf16[32,128,256]{2,1,0:T(8,128)(2,1)} async-done(((bf16[8,128,256]{2,1,0:T(8,128)(2,1)}), bf16[32,128,256]{2,1,0:T(8,128)(2,1)}) %all-gather.11.cloned.1.call-update) | async-done | bytes 2097168 | tf_op jit(solution)/shard_map/all_gather | solution.py:211
  123.7 1.6 copy-done
  125.3 2.7 spread_far.1
  128.0 6.7 %all-to-all-start.1 = ((bf16[8,256,256]{2,1,0:T(8,128)(2,1)}), bf16[8,256,256]{2,1,0:T(8,128)(2,1)S(1)}, u32[]{:S(2)}, u32[]{:S(2)}) async-start(bf16[8,256,256]{2,1,0:T(8,128)(2,1)} %bitcast.3), calls=%async_computation.1 | async-start | bytes 2097152 | tf_op jit(solution)/shard_map/all_to_all | solution.py:214
  134.7 1.3 collective-permute-start.1
  136.0 27.8 %all-to-all-done.1 = bf16[8,256,256]{2,1,0:T(8,128)(2,1)S(1)} async-done(((bf16[8,256,256]{2,1,0:T(8,128)(2,1)}), bf16[8,256,256]{2,1,0:T(8,128)(2,1)S(1)}, u32[]{:S(2)}, u32[]{:S(2)}) %all-to-all-start.1) | async-done | bytes 1048608 | tf_op jit(solution)/shard_map/all_to_all | solution.py:214
  166.5 21.8 %all-gather.19.cloned.1.call-done = bf16[2048,256]{1,0:T(8,128)(2,1)} async-done(((bf16[256,256]{1,0:T(8,128)(2,1)}), bf16[2048,256]{1,0:T(8,128)(2,1)}) %all-gather.19.cloned.1.call-update) | async-done | bytes 1048592 | tf_op jit(solution)/shard_map/all_gather | solution.py:218
  188.3 1.5 copy.21
  189.8 20.4 %all_to_all.20 = bf16[8,256,256]{1,2,0:T(8,128)(2,1)S(1)} all-to-all(bf16[8,256,256]{1,2,0:T(8,128)(2,1)S(1)} %copy.21), channel_id=1, replica_groups={{0,64,128,192},{8,72,136,200},{16,80,144,208},{24,88,152,216},{32,96,16..., dimensions={0} | all-to-all | bytes 2097152 | tf_op jit(solution)/shard_map/all_to_all | solution.py:225
  211.3 14.9 %all-gather.17.cloned.1.call-done = bf16[1024,1024]{1,0:T(8,128)(2,1)} async-done(((bf16[256,1024]{1,0:T(8,128)(2,1)}), bf16[1024,1024]{1,0:T(8,128)(2,1)}) %all-gather.17.cloned.1.call-update) | async-done | bytes 2097168 | tf_op jit(solution)/shard_map/all_gather | solution.py:205
  226.1 2.8 convolution_convert_fusion
  230.1 6.7 %all-to-all-start.3 = ((bf16[8,64,1024]{2,1,0:T(8,128)(2,1)}), bf16[8,64,1024]{2,1,0:T(8,128)(2,1)S(1)}, u32[]{:S(2)}, u32[]{:S(2)}) async-start(bf16[8,64,1024]{2,1,0:T(8,128)(2,1)} %bitcast.15), calls=%async_computation.3 | async-start | bytes 2097152 | tf_op jit(solution)/shard_map/all_to_all | solution.py:231
  236.9 67.5 %all-gather.13.cloned.1.call-done = bf16[1024,1024]{1,0:T(8,128)(2,1)} async-done(((bf16[32,1024]{1,0:T(8,128)(2,1)}), bf16[1024,1024]{1,0:T(8,128)(2,1)}) %all-gather.13.cloned.1.call-update) | async-done | bytes 2097168 | tf_op jit(solution)/shard_map/all_gather | solution.py:203
  304.4 2.3 fusion.2
  306.7 75.3 %all-gather.15.cloned.1.call-done = bf16[1024,1024]{1,0:T(8,128)(2,1)} async-done(((bf16[32,1024]{1,0:T(8,128)(2,1)}), bf16[1024,1024]{1,0:T(8,128)(2,1)}) %all-gather.15.cloned.1.call-update) | async-done | bytes 2097168 | tf_op jit(solution)/shard_map/all_gather | solution.py:204
  382.0 3.1 fusion
  (42 shorter events, 9.4 us)
Async XLA Ops:
  7.2 40.7 %all-gather.9.cloned.1.call-start = ((), (), s32[]{:S(2)}) async-start(), calls=%async_computation.4 | async-start | bytes 1179648 | tf_op jit(solution)/shard_map/all_gather | solution.py:196
  8.9 0.7 copy-start.2
  47.8 1.2 copy-start.1
  51.3 4.1 %copy-start.3 = (bf16[256,256]{1,0:T(8,128)(2,1)S(1)}, bf16[256,256]{1,0:T(8,128)(2,1)}, u32[]{:S(2)}) copy-start(bf16[256,256]{1,0:T(8,128)(2,1)} %copy-done.2) | copy-start | bytes 393220
  51.3 7.1 %copy-start.7 = (s32[2,4]{1,0:T(2,128)S(1)}, s32[2,4]{1,0:T(2,128)}, u32[]{:S(2)}) copy-start(s32[2,4]{1,0:T(2,128)} %param.16) | copy-start | bytes 100
  51.3 28.6 %copy-start.4 = (bf16[256,1024]{1,0:T(8,128)(2,1)S(1)}, bf16[256,1024]{1,0:T(8,128)(2,1)}, u32[]{:S(2)}) copy-start(bf16[256,1024]{1,0:T(8,128)(2,1)} %q_ref.1) | copy-start | bytes 1572868
  51.3 28.6 %copy-start.6 = (s32[2]{0:T(128)S(1)}, s32[2]{0:T(128)}, u32[]{:S(2)}) copy-start(s32[2]{0:T(128)} %count_ref.1) | copy-start | bytes 28
  51.3 28.6 %all-to-all-start = ((bf16[32,128,256]{2,1,0:T(8,128)(2,1)}), bf16[32,128,256]{2,1,0:T(8,128)(2,1)S(1)}, u32[]{:S(2)}, u32[]{:S(2)}) async-start(bf16[32,128,256]{2,1,0:T(8,128)(2,1)} %pick_far.1), calls=%async_computation | async-start | bytes 4194304 | tf_op jit(solution)/shard_map/all_to_all | solution.py:198
  55.4 68.3 %all-gather.11.cloned.1.call-start = ((), (), s32[]{:S(2)}) async-start(), calls=%async_computation.5 | async-start | bytes 2621440 | tf_op jit(solution)/shard_map/all_gather | solution.py:211
  55.4 24.5 %collective-permute-start = (bf16[256,256]{1,0:T(8,128)(2,1)S(1)}, bf16[256,256]{1,0:T(8,128)(2,1)S(1)}, u32[]{:S(2)}, u32[]{:S(2)}) collective-permute-start(bf16[256,256]{1,0:T(8,128)(2,1)S(1)} %copy-done.3), channel_id=1, source_target_pairs={{0,8},{8,16},{16,24},{24,32},{32,40},{40,48},{48,56},{56,64},{64,7... | collective-permute-start | bytes 393224 | tf_op jit(solution)/shard_map/ppermute | solution.py:41
  80.0 1.0 copy-start.5
  123.7 1.6 copy-start
  128.0 35.9 %all-to-all-start.1 = ((bf16[8,256,256]{2,1,0:T(8,128)(2,1)}), bf16[8,256,256]{2,1,0:T(8,128)(2,1)S(1)}, u32[]{:S(2)}, u32[]{:S(2)}) async-start(bf16[8,256,256]{2,1,0:T(8,128)(2,1)} %bitcast.3), calls=%async_computation.1 | async-start | bytes 2097152 | tf_op jit(solution)/shard_map/all_to_all | solution.py:214
  134.7 53.7 %all-gather.19.cloned.1.call-start = ((), (), s32[]{:S(2)}) async-start(), calls=%async_computation.9 | async-start | bytes 1179648 | tf_op jit(solution)/shard_map/all_gather | solution.py:218
  134.7 29.3 %collective-permute-start.1 = (bf16[256,256]{1,0:T(8,128)(2,1)S(1)}, bf16[256,256]{1,0:T(8,128)(2,1)S(1)}, u32[]{:S(2)}, u32[]{:S(2)}) collective-permute-start(bf16[256,256]{1,0:T(8,128)(2,1)S(1)} %slice.34), channel_id=1, source_target_pairs={{8,0},{16,8},{24,16},{32,24},{40,32},{48,40},{56,48},{64,56},{72,6... | collective-permute-start | bytes 393224 | tf_op jit(solution)/shard_map/ppermute | solution.py:41
  164.8 61.4 %all-gather.17.cloned.1.call-start = ((), (), s32[]{:S(2)}) async-start(), calls=%async_computation.8 | async-start | bytes 2621440 | tf_op jit(solution)/shard_map/all_gather | solution.py:205
  165.3 139.1 %all-gather.13.cloned.1.call-start = ((), (), s32[]{:S(2)}) async-start(), calls=%async_computation.6 | async-start | bytes 2162688 | tf_op jit(solution)/shard_map/all_gather | solution.py:203
  165.9 216.1 %all-gather.15.cloned.1.call-start = ((), (), s32[]{:S(2)}) async-start(), calls=%async_computation.7 | async-start | bytes 2162688 | tf_op jit(solution)/shard_map/all_gather | solution.py:204
  230.1 155.0 %all-to-all-start.3 = ((bf16[8,64,1024]{2,1,0:T(8,128)(2,1)}), bf16[8,64,1024]{2,1,0:T(8,128)(2,1)S(1)}, u32[]{:S(2)}, u32[]{:S(2)}) async-start(bf16[8,64,1024]{2,1,0:T(8,128)(2,1)} %bitcast.15), calls=%async_computation.3 | async-start | bytes 2097152 | tf_op jit(solution)/shard_map/all_to_all | solution.py:231
Sparse Core Ops, SparseCore 0:
  10.4 37.4 all-gather.8
  90.9 32.7 all-gather.10
  164.9 23.4 all-gather.18
  190.0 36.0 all-gather.16
  228.6 75.7 all-gather.12
  306.8 75.1 all-gather.14

commit v2 on v1

--- a/solution.py
+++ b/solution.py
@@ -20,6 +20,11 @@
 SLOTS = NB * FARS
 X_GROUPS = [[x * NZ + z for x in range(NX)] for z in range(NZ)]
 Z_GROUPS = [[x * NZ + z for z in range(NZ)] for x in range(NX)]
+Z_UP = [(x * NZ + z, x * NZ + (z + 1) % NZ) for x in range(NX) for z in range(NZ)]
+X_UP = [(x * NZ + z, (x + 1) % NX * NZ + z) for x in range(NX) for z in range(NZ)]
+NY = 4
+Y_UP = [(2 * y + core, 2 * ((y + 1) % NY) + core) for y in range(NY) for core in range(2)]
+CORES = [(own, own ^ 1) for own in range(2 * NY)]
 SCALE = 1.0 / math.sqrt(DH)
 EXP2_SCALE = SCALE * math.log2(math.e)
 NEG = -1e30
@@ -41,24 +46,58 @@
     return lax.ppermute(value, axis, [(source, source + steps) for source in range(leading, last)])
 
 
-def pick_kernel(lists_ref, plane_ref, out_ref):
+def both_ways(upward, downward, axis, pairs):
+    back = [(target, source) for source, target in pairs]
+    return lax.ppermute(upward, axis, pairs), lax.ppermute(downward, axis, back)
+
+
+def ring_gather(value, axis, pairs, count):
+    half = value.shape[0] // 2
+    from_below, from_above = value, value
+    pieces = []
+    for distance in range(1, count // 2 + 1):
+        if distance == count // 2:
+            from_below, from_above = from_below[:half], from_above[half:]
+        from_below, from_above = both_ways(from_below, from_above, axis, pairs)
+        pieces += [from_below, from_above]
+    return pieces
+
+
+def place_pieces(out_ref, at, own_ref, pieces, count, size):
+    half = size // 2
+    out_ref[pl.ds(at * size, size)] = own_ref[...]
+    for distance in range(1, count // 2 + 1):
+        below = lax.rem(at + (count - distance), count) * size
+        above = lax.rem(at + distance, count) * size
+        if distance == count // 2:
+            out_ref[pl.ds(below, half)] = pieces[2 * distance - 2][...]
+            out_ref[pl.ds(below + half, half)] = pieces[2 * distance - 1][...]
+        else:
+            out_ref[pl.ds(below, size)] = pieces[2 * distance - 2][...]
+            out_ref[pl.ds(above, size)] = pieces[2 * distance - 1][...]
+
+
+def pick_kernel(z_ref, lists_ref, own_ref, *refs):
+    *pieces, out_ref, plane_ref = refs
+    place_pieces(plane_ref, z_ref[0], own_ref, pieces, NZ, NB)
+
     def body(i, carry):
-        row = pl.multiple_of(lax.rem(lists_ref[i], PLANE) * BLK, BLK)
-        out_ref[i] = plane_ref[pl.ds(row, BLK), :]
+        out_ref[i] = plane_ref[lax.rem(lists_ref[i], PLANE)]
         return carry
 
     lax.fori_loop(0, NX * SLOTS, body, 0)
 
 
-def pick(lists, plane):
+def pick(z_at, lists, own, pieces):
     return pl.pallas_call(
         pick_kernel,
         out_shape=jax.ShapeDtypeStruct((NX * SLOTS, BLK, 2 * DH), BF16),
-        in_specs=[SMEM, VMEM],
+        in_specs=[SMEM, SMEM] + [VMEM] * (1 + len(pieces)),
         out_specs=VMEM,
+        scratch_shapes=[pltpu.VMEM((PLANE, BLK, 2 * DH), BF16)],
         compiler_params=params(16),
         name="pick_far",
-    )(lists, plane)
+    )(z_at, lists, own, *pieces)
 
 
 def attend_kernel(
@@ -152,7 +191,9 @@
     )(at, far, count, queries, out_grad, prev, own, far_kv)
 
 
-def spread_kernel(x_ref, lists_ref, far_ref, out_ref, acc_ref):
+def spread_kernel(x_ref, lists_ref, own_ref, *refs):
+    *pieces, out_ref, far_ref, acc_ref = refs
+    place_pieces(far_ref, x_ref[0], own_ref, pieces, NX, SLOTS)
     acc_ref[...] = jnp.zeros_like(acc_ref)
 
     def body(i, carry):
@@ -169,16 +210,93 @@
     out_ref[...] = acc_ref[...].astype(BF16)
 
 
-def spread(x_at, lists, far_all):
+def spread(x_at, lists, own, pieces):
     return pl.pallas_call(
         spread_kernel,
         out_shape=jax.ShapeDtypeStruct((PLANE, BLK, 2 * DH), BF16),
-        in_specs=[SMEM, SMEM, VMEM],
+        in_specs=[SMEM, SMEM] + [VMEM] * (1 + len(pieces)),
         out_specs=VMEM,
-        scratch_shapes=[pltpu.VMEM((PLANE, BLK, 2 * DH), F32)],
+        scratch_shapes=[
+            pltpu.VMEM((NX * SLOTS, BLK, 2 * DH), BF16),
+            pltpu.VMEM((PLANE, BLK, 2 * DH), F32),
+        ],
+        compiler_params=params(24),
+        name="spread_far",
+    )(x_at, lists, own, *pieces)
+
+
+def heads_kernel(at_ref, *refs):
+    own_ref, *pieces, other_ref, stack_ref, wide_ref = refs
+    at, core = lax.div(at_ref[0], 2), lax.rem(at_ref[0], 2)
+    half = BLK * NB // 2
+
+    def put(y, which, rows, value):
+        head = 2 * y + which
+        stack_ref[head, rows, :] = value
+        wide_ref[rows, pl.ds(pl.multiple_of(head * 2 * DH, 2 * DH), 2 * DH)] = value
+
+    everything = slice(0, 2 * half)
+    below, above = lax.rem(at + NY - 1, NY), lax.rem(at + 1, NY)
+    across = lax.rem(at + 2, NY)
+    for which, mine in ((core, True), (1 - core, False)):
+        parts = (
+            (own_ref, *pieces)
+            if mine
+            else (
+                other_ref.at[: 2 * half],
+                other_ref.at[2 * half : 4 * half],
+                other_ref.at[4 * half : 6 * half],
+                other_ref.at[6 * half : 7 * half],
+                other_ref.at[7 * half :],
+            )
+        )
+        put(at, which, everything, parts[0][...])
+        put(below, which, everything, parts[1][...])
+        put(above, which, everything, parts[2][...])
+        put(across, which, slice(0, half), parts[3][...])
+        put(across, which, slice(half, 2 * half), parts[4][...])
+
+
+def place_heads(at, own, pieces, other):
+    tokens = own.shape[0]
+    return pl.pallas_call(
+        heads_kernel,
+        out_shape=(
+            jax.ShapeDtypeStruct((2 * NY, tokens, 2 * DH), BF16),
+            jax.ShapeDtypeStruct((tokens, 2 * NY * 2 * DH), BF16),
+        ),
+        in_specs=[SMEM] + [VMEM] * (2 + len(pieces)),
+        out_specs=(VMEM, VMEM),
         compiler_params=params(16),
-        name="spread_far",
-    )(x_at, lists, far_all)
+        name="place_heads",
+    )(at, own, *pieces, other)
+
+
+def weights_kernel(grad_ref, inputs_ref, out_ref):
+    columns = DH // 4
+    for head in range(2):
+        grad = jnp.concatenate([grad_ref[x * 2 + head] for x in range(NX)])
+        term = lax.dot_general(
+            grad, inputs_ref[...], (((0,), (0,)), ((), ())), preferred_element_type=F32
+        ).astype(BF16)
+        for part in range(4):
+            for kind in range(2):
+                lower = kind * DH + part * columns
+                out_ref[head * 4 + part, kind * columns : (kind + 1) * columns, :] = term[
+                    lower : lower + columns
+                ]
+
+
+def weight_terms(grad, inputs_x):
+    return pl.pallas_call(
+        weights_kernel,
+        out_shape=jax.ShapeDtypeStruct((NZ, 2 * DH // 4, inputs_x.shape[1]), BF16),
+        in_specs=[VMEM, VMEM],
+        out_specs=VMEM,
+        compiler_params=params(24),
+        cost_estimate=pl.CostEstimate(flops=1 << 30, bytes_accessed=4 << 20, transcendentals=0),
+        name="weight_terms",
+    )(grad, inputs_x)
 
 
 def local(
@@ -188,53 +306,50 @@
     seq_index = lax.axis_index("seq").astype(jnp.int32)
     x_index = lax.div(seq_index, NZ)
     at = seq_index.reshape(1)
+    own_index = lax.axis_index("own").astype(jnp.int32).reshape(1)
+    z_at = lax.rem(seq_index, NZ).reshape(1)
+    x_at = x_index.reshape(1)
     own_kv = jnp.concatenate([key_rows, value_rows], axis=1)
 
+    inputs_x = lax.all_gather(inputs, "seq", axis=0, axis_index_groups=X_GROUPS, tiled=True)
+    weights = jnp.concatenate([key_weight.T, value_weight.T])
+    weights = lax.all_gather(weights, "seq", axis=0, tiled=True)
+    columns = DH // 4
+    weights = weights.reshape(2 * NY, 4, 2, columns, -1).transpose(0, 2, 1, 3, 4)
+    weights = weights.reshape(2 * NY * 2 * DH, -1)
+
+    own_blocks = own_kv.reshape(NB, BLK, 2 * DH)
+    plane = ring_gather(own_blocks, "seq", Z_UP, NZ)
+    prev_kv = shifted(own_kv, "seq", 1)
     lists = lax.all_gather(far_blocks, "seq", axis=0, axis_index_groups=X_GROUPS, tiled=True)
     lists = lists.reshape(NX * SLOTS)
-    prev_kv = shifted(own_kv, "seq", 1)
-    plane = lax.all_gather(own_kv, "seq", axis=0, axis_index_groups=Z_GROUPS, tiled=True)
-    chosen = pick(lists, plane)
+    chosen = pick(z_at, lists, own_blocks, plane)
     far_kv = lax.all_to_all(chosen, "seq", 0, 0, axis_index_groups=X_GROUPS, tiled=True)
-
-    key_weight, value_weight, inputs, far_kv = lax.optimization_barrier(
-        (key_weight, value_weight, inputs, far_kv)
-    )
-    key_proj = lax.all_gather(key_weight.T, "seq", axis=0, tiled=True)
-    value_proj = lax.all_gather(value_weight.T, "seq", axis=0, tiled=True)
-    inputs_x = lax.all_gather(inputs, "seq", axis=0, axis_index_groups=X_GROUPS, tiled=True)
 
     query_grad, window, far_grad = attend(
         at, far_blocks.reshape(SLOTS), far_count, queries, out_grad, prev_kv, own_kv, far_kv
     )
+    far_all = ring_gather(far_grad, "seq", X_UP, NX)
     back = shifted(window[:tokens].astype(BF16), "seq", -1)
-    far_all = lax.all_gather(far_grad, "seq", axis=0, axis_index_groups=X_GROUPS, tiled=True)
-    dense = spread(x_index.reshape(1), lists, far_all)
+    dense = spread(x_at, lists, far_grad, far_all)
     dense = dense.reshape(NZ, tokens, 2 * DH)
     terms = lax.all_to_all(dense, "seq", 0, 0, axis_index_groups=Z_GROUPS, tiled=True)
     kv_grad = jnp.sum(terms.astype(F32), axis=0) + back.astype(F32) + window[tokens:]
     kv_grad = kv_grad.astype(BF16)
 
-    heads = lax.all_gather(kv_grad, "own", axis=0)
-    key_all = heads[:, :, :DH].transpose(1, 0, 2).reshape(tokens, -1)
-    value_all = heads[:, :, DH:].transpose(1, 0, 2).reshape(tokens, -1)
-    input_grad = jnp.dot(key_all, key_proj, preferred_element_type=F32) + jnp.dot(
-        value_all, value_proj, preferred_element_type=F32
-    )
-
-    quarter = lax.all_to_all(heads, "seq", 0, 0, axis_index_groups=X_GROUPS, tiled=True)
-    quarter = quarter.reshape(NX, 2, tokens, 2, DH).transpose(1, 3, 4, 0, 2)
-    quarter = quarter.reshape(4 * DH, NX * tokens)
-    weight_t = jnp.dot(quarter, inputs_x, preferred_element_type=F32).astype(BF16)
-    width = weight_t.shape[1]
-    weight_t = weight_t.reshape(2, 2, 4, 32, width).transpose(0, 2, 1, 3, 4).reshape(NZ, 64, width)
-    pieces = lax.all_to_all(weight_t, "seq", 0, 0, axis_index_groups=Z_GROUPS, tiled=True)
+    same_core = ring_gather(kv_grad, "own", Y_UP, NY)
+    other_core = lax.ppermute(jnp.concatenate([kv_grad, *same_core]), "own", CORES)
+    stacked, wide = place_heads(own_index, kv_grad, same_core, other_core)
+    quarter = lax.all_to_all(stacked, "seq", 0, 0, axis_index_groups=X_GROUPS, tiled=True)
+    pieces = weight_terms(quarter, inputs_x)
+    pieces = lax.all_to_all(pieces, "seq", 0, 0, axis_index_groups=Z_GROUPS, tiled=True)
+    input_grad = jnp.dot(wide, weights, preferred_element_type=F32)
     weight_grad = jnp.sum(pieces.astype(F32), axis=0)
     return (
         query_grad,
         input_grad.astype(BF16),
-        weight_grad[:32].T,
-        weight_grad[32:].T,
+        weight_grad[:columns].T,
+        weight_grad[columns:].T,
     )
 
 

time: 397 us -> 238 us (0.60)
  waiting for transfers between devices: 293 us -> 101 us
  starting transfers between devices: 22 us -> 52.3 us
  blocking collectives: 29.2 us -> 39.4 us
  matrix products: 8.27 us -> 2.08 us
    all_gather x5 -> x1, waiting for transfers between devices: 227 us -> 0.01 us  [local(): weights = lax.all_gather(weights, 'seq', axis=0, tiled=True)]
    ppermute x0 -> x17, starting transfers between devices: none -> 38.9 us  [the longest x8 23.5 us: both_ways(): lax.ppermute(downward, axis, back)]
    ppermute x0 -> x17, waiting for transfers between devices: none -> 29.9 us  [the longest x8 21.8 us: both_ways(): lax.ppermute(downward, axis, back)]
    all_gather x1, waiting for transfers between devices: 14.9 us -> 0.02 us  [local(): lax.all_gather(inputs, 'seq', axis=0, axis_index_groups=X_GROUPS, tiled=T...]
    all_to_all x1, waiting for transfers between devices: 0.01 us -> 14.8 us  [local(): lax.all_to_all(stacked, 'seq', 0, 0, axis_index_groups=X_GROUPS, tiled=True)]
    all_to_all x1, blocking collectives: 20.4 us -> 30.6 us  [local(): lax.all_to_all(pieces, 'seq', 0, 0, axis_index_groups=Z_GROUPS, tiled=True)]
    dot_general x3 -> x1, matrix products: 8.27 us -> 2.08 us  [local(): input_grad = jnp.dot(wide, weights, preferred_element_type=F32)]
    all_to_all x1, waiting for transfers between devices: 27.8 us -> 33.3 us  [local(): lax.all_to_all(dense, 'seq', 0, 0, axis_index_groups=Z_GROUPS, tiled=True)]
  transfers between devices with their start and end apart: 11 -> 24, of which waited for: 8 -> 14; matrix products, arithmetic and copies ran while one was open for 3% -> 2% of each run, Pallas kernels for 0% -> 7%
where the time goes in v2:
time: 238 us; the launch traced here: 237 us
  waiting for transfers between devices  101 us (42%)
  starting transfers between devices  52.3 us (22%)
  blocking collectives  39.4 us (17%)
  Pallas kernels  17.2 us (7%)
  between operations  14.3 us (6%)
  local copies, waits for them, and re-layouts  9.04 us (4%)
    all_to_all x1, waiting for transfers between devices, local(): lax.all_to_all(dense, 'seq', 0, 0, axis_index_groups=Z_GROUPS, tiled=True)  33.3 us
    all_to_all x1, blocking collectives, local(): lax.all_to_all(pieces, 'seq', 0, 0, axis_index_groups=Z_GROUPS, tiled=True)  30.6 us
    ppermute x8, starting transfers between devices, both_ways(): lax.ppermute(downward, axis, back)  23.5 us
    ppermute x8, waiting for transfers between devices, both_ways(): lax.ppermute(downward, axis, back)  21.8 us
    all_to_all x1, waiting for transfers between devices, local(): lax.all_to_all(chosen, 'seq', 0, 0, axis_index_groups=X_GROUPS, tiled=True)  21.5 us
    all_to_all x1, waiting for transfers between devices, local(): lax.all_to_all(stacked, 'seq', 0, 0, axis_index_groups=X_GROUPS, tiled=True)  14.8 us
    ppermute x1, starting transfers between devices, local(): lax.ppermute(jnp.concatenate([kv_grad, *same_core]), 'own', CORES)  13.5 us
    pallas_call x1, Pallas kernels, attend(): pl.pallas_call(attend_kernel, out_shape=(jax.ShapeDtypeStruct((NB * BLK,...  9.61 us
  transfers between devices with their start and end apart: 24, of which 14 were waited for; matrix products, arithmetic and copies ran while one was open for 2% of the time, Pallas kernels for 7%

profile of v2, /device:TPU:1, one launch (start us, length us, event | category | flops | bytes accessed | tf_op | source)
XLA Modules:
  0.0 236.7 jit_solution(7005778005288647638)
XLA Ops:
  9.7 6.5 %collective-permute-start.2 = (bf16[2,128,256]{2,1,0:T(8,128)(2,1)S(1)}, bf16[2,128,256]{2,1,0:T(8,128)(2,1)S(1)}, u32[]{:S(2)}, u32[]{:S(2)}) collective-permute-start(bf16[2,128,256]{2,1,0:T(8,128)(2,1)S(1)} %bitcast.19), channel_id=1, source_target_pairs={{8,0},{16,8},{24,16},{32,24},{40,32},{48,40},{56,48},{0,56},{72,64... | collective-permute-start | bytes 393224 | tf_op jit(solution)/shard_map/ppermute | solution.py:51
  16.2 2.2 collective-permute-done.2.refs_1_
  18.3 3.4 %collective-permute-start.4 = (bf16[2,128,256]{2,1,0:T(8,128)(2,1)S(1)}, bf16[2,128,256]{2,1,0:T(8,128)(2,1)S(1)}, u32[]{:S(2)}, u32[]{:S(2)}) collective-permute-start(bf16[2,128,256]{2,1,0:T(8,128)(2,1)S(1)} %collective-permute-done.2.refs_1_), channel_id=1, source_target_pairs={{8,0},{16,8},{24,16},{32,24},{40,32},{48,40},{56,48},{0,56},{72,64... | collective-permute-start | bytes 393224 | tf_op jit(solution)/shard_map/ppermute | solution.py:51
  23.7 3.1 %collective-permute-start.6 = (bf16[2,128,256]{2,1,0:T(8,128)(2,1)S(1)}, bf16[2,128,256]{2,1,0:T(8,128)(2,1)S(1)}, u32[]{:S(2)}, u32[]{:S(2)}) collective-permute-start(bf16[2,128,256]{2,1,0:T(8,128)(2,1)S(1)} %collective-permute-done.4.refs_3_), channel_id=1, source_target_pairs={{8,0},{16,8},{24,16},{32,24},{40,32},{48,40},{56,48},{0,56},{72,64... | collective-permute-start | bytes 393224 | tf_op jit(solution)/shard_map/ppermute | solution.py:51
  28.7 3.1 %collective-permute-start.8 = (bf16[1,128,256]{2,1,0:T(8,128)(2,1)S(1)}, bf16[1,128,256]{2,1,0:T(8,128)(2,1)S(1)}, u32[]{:S(2)}, u32[]{:S(2)}) collective-permute-start(bf16[1,128,256]{2,1,0:T(8,128)(2,1)S(1)} %slice.42), channel_id=1, source_target_pairs={{8,0},{16,8},{24,16},{32,24},{40,32},{48,40},{56,48},{0,56},{72,64... | collective-permute-start | bytes 196616 | tf_op jit(solution)/shard_map/ppermute | solution.py:51
  32.2 8.8 %all-gather = s32[4,2,4]{2,1,0:T(2,128)S(1)} all-gather(s32[1,2,4]{2,1,0:T(2,128)} %bitcast.26), channel_id=1, replica_groups={{0,64,128,192},{8,72,136,200},{16,80,144,208},{24,88,152,216},{32,96,16..., dimensions={0}, use_global_device_ids=true | all-gather | bytes 160 | tf_op jit(solution)/shard_map/all_gather | solution.py:324
  41.2 2.4 %pick_far.1 = bf16[32,128,256]{2,1,0:T(8,128)(2,1)} custom-call(s32[1]{0:T(128)} %bitcast.1.z_ref, s32[32]{0:T(128)S(1)} %reshape.41.lists_ref, bf16[2,128,256]{2,1,0:T(8,128)(2,1)S(1)} %bitcast.21, bf16[2,128,256]{2,1,0:T(8,128)(2,1)S(1)} %collective-permute-done.1.refs_0_, bf16[2,128,256]{2,1,0:T(8,128)(2,1)S(1)} %collective-permute-done.2.refs_1_, ...), custom_call_target="tpu_custom_call" | custom-call | tf_op jit(solution)/shard_map/pick_far/pallas_call | solution.py:92
  43.5 3.6 %all-to-all-start = ((bf16[32,128,256]{2,1,0:T(8,128)(2,1)}), bf16[32,128,256]{2,1,0:T(8,128)(2,1)S(1)}, u32[]{:S(2)}, u32[]{:S(2)}) async-start(bf16[32,128,256]{2,1,0:T(8,128)(2,1)} %pick_far.1), calls=%async_computation | async-start | bytes 4194304 | tf_op jit(solution)/shard_map/all_to_all | solution.py:327
  50.4 21.5 %all-to-all-done.far_kv_ref = bf16[32,128,256]{2,1,0:T(8,128)(2,1)S(1)} async-done(((bf16[32,128,256]{2,1,0:T(8,128)(2,1)}), bf16[32,128,256]{2,1,0:T(8,128)(2,1)S(1)}, u32[]{:S(2)}, u32[]{:S(2)}) %all-to-all-start) | async-done | bytes 2097184 | tf_op jit(solution)/shard_map/all_to_all | solution.py:327
  74.1 9.6 %attend.1 = (bf16[256,1024]{1,0:T(8,128)(2,1)}, f32[512,256]{1,0:T(8,128)S(1)}, bf16[8,128,256]{2,1,0:T(8,128)(2,1)S(1)}) custom-call(s32[1]{0:T(128)} %bitcast.at_ref, s32[8]{0:T(128)S(1)} %reshape.39.far_ref, s32[2]{0:T(128)S(1)} %copy-done.3, bf16[256,1024]{1,0:T(8,128)(2,1)S(1)} %copy-done.1, bf16[256,1024]{1,0:T(8,128)(2,1)S(1)} %copy-done.2, ...), custom_call_target="tpu_custom_call" | custom-call | flops 9600000000 | bytes 6291456 | tf_op jit(solution)/shard_map/attend/pallas_call | solution.py:172
  85.2 7.0 %collective-permute-done.10.refs_1_ = bf16[8,128,256]{2,1,0:T(8,128)(2,1)S(1)} collective-permute-done((bf16[8,128,256]{2,1,0:T(8,128)(2,1)S(1)}, bf16[8,128,256]{2,1,0:T(8,128)(2,1)S(1)}, u32[]{:S(2)}, u32[]{:S(2)}) %collective-permute-start.10) | collective-permute-done | bytes 524320 | tf_op jit(solution)/shard_map/ppermute | solution.py:51
  93.8 6.8 %collective-permute-done.12.refs_3_ = bf16[4,128,256]{2,1,0:T(8,128)(2,1)S(1)} collective-permute-done((bf16[4,128,256]{2,1,0:T(8,128)(2,1)S(1)}, bf16[4,128,256]{2,1,0:T(8,128)(2,1)S(1)}, u32[]{:S(2)}, u32[]{:S(2)}) %collective-permute-start.12) | collective-permute-done | bytes 262176 | tf_op jit(solution)/shard_map/ppermute | solution.py:51
  102.5 2.8 %spread_far.1 = bf16[16,128,256]{2,1,0:T(8,128)(2,1)} custom-call(s32[1]{0:T(128)} %bitcast.5.x_ref, s32[32]{0:T(128)S(1)} %reshape.41.lists_ref, bf16[8,128,256]{2,1,0:T(8,128)(2,1)S(1)} %get-tuple-element.10.own_ref, bf16[8,128,256]{2,1,0:T(8,128)(2,1)S(1)} %collective-permute-done.9.refs_0_, bf16[8,128,256]{2,1,0:T(8,128)(2,1)S(1)} %collective-permute-done.10.refs_1_, ...), custom_call_target="tpu_custom_call" | custom-call | tf_op jit(solution)/shard_map/spread_far/pallas_call | solution.py:214
  105.2 3.6 %all-to-all-start.1 = ((bf16[8,256,256]{2,1,0:T(8,128)(2,1)}), bf16[8,256,256]{2,1,0:T(8,128)(2,1)S(1)}, u32[]{:S(2)}, u32[]{:S(2)}) async-start(bf16[8,256,256]{2,1,0:T(8,128)(2,1)} %bitcast.6), calls=%async_computation.1 | async-start | bytes 2097152 | tf_op jit(solution)/shard_map/all_to_all | solution.py:336
  110.1 33.3 %all-to-all-done.1 = bf16[8,256,256]{2,1,0:T(8,128)(2,1)S(1)} async-done(((bf16[8,256,256]{2,1,0:T(8,128)(2,1)}), bf16[8,256,256]{2,1,0:T(8,128)(2,1)S(1)}, u32[]{:S(2)}, u32[]{:S(2)}) %all-to-all-start.1) | async-done | bytes 1048608 | tf_op jit(solution)/shard_map/all_to_all | solution.py:336
  143.6 2.7 %collective-permute-start.15 = (bf16[256,256]{1,0:T(8,128)(2,1)S(1)}, bf16[256,256]{1,0:T(8,128)(2,1)S(1)}, u32[]{:S(2)}, u32[]{:S(2)}) collective-permute-start(bf16[256,256]{1,0:T(8,128)(2,1)S(1)} %get-tuple-element.15.refs_0_), channel_id=1, source_target_pairs={{2,0},{3,1},{4,2},{5,3},{6,4},{7,5},{0,6},{1,7},{10,8},{11,9},{12,... | collective-permute-start | bytes 393224 | tf_op jit(solution)/shard_map/ppermute | solution.py:51
  148.3 3.5 %collective-permute-start.17 = (bf16[128,256]{1,0:T(8,128)(2,1)S(1)}, bf16[128,256]{1,0:T(8,128)(2,1)S(1)}, u32[]{:S(2)}, u32[]{:S(2)}) collective-permute-start(bf16[128,256]{1,0:T(8,128)(2,1)S(1)} %slice.47), channel_id=1, source_target_pairs={{2,0},{3,1},{4,2},{5,3},{6,4},{7,5},{0,6},{1,7},{10,8},{11,9},{12,... | collective-permute-start | bytes 196616 | tf_op jit(solution)/shard_map/ppermute | solution.py:51
  152.0 4.3 %collective-permute-done.16.refs_3_ = bf16[128,256]{1,0:T(8,128)(2,1)S(1)} collective-permute-done((bf16[128,256]{1,0:T(8,128)(2,1)S(1)}, bf16[128,256]{1,0:T(8,128)(2,1)S(1)}, u32[]{:S(2)}, u32[]{:S(2)}) %collective-permute-start.16) | collective-permute-done | bytes 65568 | tf_op jit(solution)/shard_map/ppermute | solution.py:51
  156.3 13.5 %collective-permute-start.18 = (bf16[1024,256]{1,0:T(8,128)(2,1)S(1)}, bf16[1024,256]{1,0:T(8,128)(2,1)S(1)}, u32[]{:S(2)}, u32[]{:S(2)}) collective-permute-start(bf16[1024,256]{1,0:T(8,128)(2,1)S(1)} %constant_dynamic-update-slice_fusion.2), channel_id=1, source_target_pairs={{0,1},{1,0},{2,3},{3,2},{4,5},{5,4},{6,7},{7,6},{8,9},{9,8},{10,11... | collective-permute-start | bytes 1572872 | tf_op jit(solution)/shard_map/ppermute | solution.py:341
  172.5 3.5 %all-to-all-start.2 = ((bf16[8,256,256]{2,1,0:T(8,128)(2,1)}), bf16[8,256,256]{2,1,0:T(8,128)(2,1)S(1)}, u32[]{:S(2)}, u32[]{:S(2)}) async-start(bf16[8,256,256]{2,1,0:T(8,128)(2,1)} %get-tuple-element.13), calls=%async_computation.2 | async-start | bytes 2097152 | tf_op jit(solution)/shard_map/all_to_all | solution.py:343
  176.0 14.8 %all-to-all-done.2.grad_ref = bf16[8,256,256]{2,1,0:T(8,128)(2,1)S(1)} async-done(((bf16[8,256,256]{2,1,0:T(8,128)(2,1)}), bf16[8,256,256]{2,1,0:T(8,128)(2,1)S(1)}, u32[]{:S(2)}, u32[]{:S(2)}) %all-to-all-start.2) | async-done | bytes 1048608 | tf_op jit(solution)/shard_map/all_to_all | solution.py:343
  193.7 30.6 %all_to_all.20 = bf16[8,64,1024]{2,1,0:T(8,128)(2,1)S(1)} all-to-all(bf16[8,64,1024]{2,1,0:T(8,128)(2,1)S(1)} %weight_terms.1), channel_id=1, replica_groups={{0,8,16,24,32,40,48,56},{64,72,80,88,96,104,112,120},{128,136,144,152,1..., dimensions={0} | all-to-all | bytes 2097152 | tf_op jit(solution)/shard_map/all_to_all | solution.py:345
  225.1 2.6 %copy.14 = bf16[8,2,4,32,1024]{4,3,2,1,0:T(8,128)(2,1)S(1)} copy(bf16[8,2,4,32,1024]{4,3,1,2,0:T(8,128)(2,1)} %bitcast.22) | data formatting | bytes 8388608 | tf_op jit(solution)/shard_map/transpose | solution.py:318
  227.8 2.1 convolution_convert_fusion
  (69 shorter events, 27.2 us)
Async XLA Ops:
  7.2 168.8 %all-gather.6.cloned.1.call-start = ((), (), s32[]{:S(2)}) async-start(), calls=%async_computation.5 | async-start | bytes 2621440 | tf_op jit(solution)/shard_map/all_gather | solution.py:314
  9.7 8.6 %collective-permute-start.2 = (bf16[2,128,256]{2,1,0:T(8,128)(2,1)S(1)}, bf16[2,128,256]{2,1,0:T(8,128)(2,1)S(1)}, u32[]{:S(2)}, u32[]{:S(2)}) collective-permute-start(bf16[2,128,256]{2,1,0:T(8,128)(2,1)S(1)} %bitcast.19), channel_id=1, source_target_pairs={{8,0},{16,8},{24,16},{32,24},{40,32},{48,40},{56,48},{0,56},{72,64... | collective-permute-start | bytes 393224 | tf_op jit(solution)/shard_map/ppermute | solution.py:51
  16.2 5.6 %collective-permute-start.1 = (bf16[2,128,256]{2,1,0:T(8,128)(2,1)S(1)}, bf16[2,128,256]{2,1,0:T(8,128)(2,1)S(1)}, u32[]{:S(2)}, u32[]{:S(2)}) collective-permute-start(bf16[2,128,256]{2,1,0:T(8,128)(2,1)S(1)} %bitcast.20), channel_id=1, source_target_pairs={{0,8},{8,16},{16,24},{24,32},{32,40},{40,48},{48,56},{56,0},{64,72... | collective-permute-start | bytes 393224 | tf_op jit(solution)/shard_map/ppermute | solution.py:51
  18.3 5.4 %collective-permute-start.4 = (bf16[2,128,256]{2,1,0:T(8,128)(2,1)S(1)}, bf16[2,128,256]{2,1,0:T(8,128)(2,1)S(1)}, u32[]{:S(2)}, u32[]{:S(2)}) collective-permute-start(bf16[2,128,256]{2,1,0:T(8,128)(2,1)S(1)} %collective-permute-done.2.refs_1_), channel_id=1, source_target_pairs={{8,0},{16,8},{24,16},{32,24},{40,32},{48,40},{56,48},{0,56},{72,64... | collective-permute-start | bytes 393224 | tf_op jit(solution)/shard_map/ppermute | solution.py:51
  21.7 5.0 %collective-permute-start.3 = (bf16[2,128,256]{2,1,0:T(8,128)(2,1)S(1)}, bf16[2,128,256]{2,1,0:T(8,128)(2,1)S(1)}, u32[]{:S(2)}, u32[]{:S(2)}) collective-permute-start(bf16[2,128,256]{2,1,0:T(8,128)(2,1)S(1)} %collective-permute-done.1.refs_0_), channel_id=1, source_target_pairs={{0,8},{8,16},{16,24},{24,32},{32,40},{40,48},{48,56},{56,0},{64,72... | collective-permute-start | bytes 393224 | tf_op jit(solution)/shard_map/ppermute | solution.py:51
  23.7 5.0 %collective-permute-start.6 = (bf16[2,128,256]{2,1,0:T(8,128)(2,1)S(1)}, bf16[2,128,256]{2,1,0:T(8,128)(2,1)S(1)}, u32[]{:S(2)}, u32[]{:S(2)}) collective-permute-start(bf16[2,128,256]{2,1,0:T(8,128)(2,1)S(1)} %collective-permute-done.4.refs_3_), channel_id=1, source_target_pairs={{8,0},{16,8},{24,16},{32,24},{40,32},{48,40},{56,48},{0,56},{72,64... | collective-permute-start | bytes 393224 | tf_op jit(solution)/shard_map/ppermute | solution.py:51
  26.8 5.4 %collective-permute-start.5 = (bf16[2,128,256]{2,1,0:T(8,128)(2,1)S(1)}, bf16[2,128,256]{2,1,0:T(8,128)(2,1)S(1)}, u32[]{:S(2)}, u32[]{:S(2)}) collective-permute-start(bf16[2,128,256]{2,1,0:T(8,128)(2,1)S(1)} %collective-permute-done.3.refs_2_), channel_id=1, source_target_pairs={{0,8},{8,16},{16,24},{24,32},{32,40},{40,48},{48,56},{56,0},{64,72... | collective-permute-start | bytes 393224 | tf_op jit(solution)/shard_map/ppermute | solution.py:51
  28.7 12.4 %collective-permute-start.8 = (bf16[1,128,256]{2,1,0:T(8,128)(2,1)S(1)}, bf16[1,128,256]{2,1,0:T(8,128)(2,1)S(1)}, u32[]{:S(2)}, u32[]{:S(2)}) collective-permute-start(bf16[1,128,256]{2,1,0:T(8,128)(2,1)S(1)} %slice.42), channel_id=1, source_target_pairs={{8,0},{16,8},{24,16},{32,24},{40,32},{48,40},{56,48},{0,56},{72,64... | collective-permute-start | bytes 196616 | tf_op jit(solution)/shard_map/ppermute | solution.py:51
  32.2 8.9 %collective-permute-start.7 = (bf16[1,128,256]{2,1,0:T(8,128)(2,1)S(1)}, bf16[1,128,256]{2,1,0:T(8,128)(2,1)S(1)}, u32[]{:S(2)}, u32[]{:S(2)}) collective-permute-start(bf16[1,128,256]{2,1,0:T(8,128)(2,1)S(1)} %slice.41), channel_id=1, source_target_pairs={{0,8},{8,16},{16,24},{24,32},{32,40},{40,48},{48,56},{56,0},{64,72... | collective-permute-start | bytes 196616 | tf_op jit(solution)/shard_map/ppermute | solution.py:51
  43.5 28.4 %all-to-all-start = ((bf16[32,128,256]{2,1,0:T(8,128)(2,1)}), bf16[32,128,256]{2,1,0:T(8,128)(2,1)S(1)}, u32[]{:S(2)}, u32[]{:S(2)}) async-start(bf16[32,128,256]{2,1,0:T(8,128)(2,1)} %pick_far.1), calls=%async_computation | async-start | bytes 4194304 | tf_op jit(solution)/shard_map/all_to_all | solution.py:327
  47.2 178.0 %all-gather.4.cloned.1.call-start = ((), (), s32[]{:S(2)}) async-start(), calls=%async_computation.4 | async-start | bytes 4325376 | tf_op jit(solution)/shard_map/all_gather | solution.py:316
  47.2 3.2 %collective-permute-start = (bf16[256,256]{1,0:T(8,128)(2,1)S(1)}, bf16[256,256]{1,0:T(8,128)(2,1)S(1)}, u32[]{:S(2)}, u32[]{:S(2)}) collective-permute-start(bf16[256,256]{1,0:T(8,128)(2,1)S(1)} %constant_dynamic-update-slice_fusion.own_ref), channel_id=1, source_target_pairs={{0,8},{8,16},{16,24},{24,32},{32,40},{40,48},{48,56},{56,64},{64,7... | collective-permute-start | bytes 393224 | tf_op jit(solution)/shard_map/ppermute | solution.py:46
  83.7 8.4 %collective-permute-start.10 = (bf16[8,128,256]{2,1,0:T(8,128)(2,1)S(1)}, bf16[8,128,256]{2,1,0:T(8,128)(2,1)S(1)}, u32[]{:S(2)}, u32[]{:S(2)}) collective-permute-start(bf16[8,128,256]{2,1,0:T(8,128)(2,1)S(1)} %get-tuple-element.10.own_ref), channel_id=1, source_target_pairs={{64,0},{72,8},{80,16},{88,24},{96,32},{104,40},{112,48},{120,56},{... | collective-permute-start | bytes 1572872 | tf_op jit(solution)/shard_map/ppermute | solution.py:51
  83.7 9.7 %collective-permute-start.9 = (bf16[8,128,256]{2,1,0:T(8,128)(2,1)S(1)}, bf16[8,128,256]{2,1,0:T(8,128)(2,1)S(1)}, u32[]{:S(2)}, u32[]{:S(2)}) collective-permute-start(bf16[8,128,256]{2,1,0:T(8,128)(2,1)S(1)} %get-tuple-element.10.own_ref), channel_id=1, source_target_pairs={{0,64},{8,72},{16,80},{24,88},{32,96},{40,104},{48,112},{56,120},{... | collective-permute-start | bytes 1572872 | tf_op jit(solution)/shard_map/ppermute | solution.py:51
  92.1 8.5 %collective-permute-start.12 = (bf16[4,128,256]{2,1,0:T(8,128)(2,1)S(1)}, bf16[4,128,256]{2,1,0:T(8,128)(2,1)S(1)}, u32[]{:S(2)}, u32[]{:S(2)}) collective-permute-start(bf16[4,128,256]{2,1,0:T(8,128)(2,1)S(1)} %slice.44), channel_id=1, source_target_pairs={{64,0},{72,8},{80,16},{88,24},{96,32},{104,40},{112,48},{120,56},{... | collective-permute-start | bytes 786440 | tf_op jit(solution)/shard_map/ppermute | solution.py:51
  93.4 9.1 %collective-permute-start.11 = (bf16[4,128,256]{2,1,0:T(8,128)(2,1)S(1)}, bf16[4,128,256]{2,1,0:T(8,128)(2,1)S(1)}, u32[]{:S(2)}, u32[]{:S(2)}) collective-permute-start(bf16[4,128,256]{2,1,0:T(8,128)(2,1)S(1)} %slice.43), channel_id=1, source_target_pairs={{0,64},{8,72},{16,80},{24,88},{32,96},{40,104},{48,112},{56,120},{... | collective-permute-start | bytes 786440 | tf_op jit(solution)/shard_map/ppermute | solution.py:51
  105.2 38.2 %all-to-all-start.1 = ((bf16[8,256,256]{2,1,0:T(8,128)(2,1)}), bf16[8,256,256]{2,1,0:T(8,128)(2,1)S(1)}, u32[]{:S(2)}, u32[]{:S(2)}) async-start(bf16[8,256,256]{2,1,0:T(8,128)(2,1)} %bitcast.6), calls=%async_computation.1 | async-start | bytes 2097152 | tf_op jit(solution)/shard_map/all_to_all | solution.py:336
  108.8 34.8 %collective-permute-start.13 = (bf16[256,256]{1,0:T(8,128)(2,1)S(1)}, bf16[256,256]{1,0:T(8,128)(2,1)S(1)}, u32[]{:S(2)}, u32[]{:S(2)}) collective-permute-start(bf16[256,256]{1,0:T(8,128)(2,1)S(1)} %slice.54), channel_id=1, source_target_pairs={{8,0},{16,8},{24,16},{32,24},{40,32},{48,40},{56,48},{64,56},{72,6... | collective-permute-start | bytes 393224 | tf_op jit(solution)/shard_map/ppermute | solution.py:46
  143.6 4.7 %collective-permute-start.15 = (bf16[256,256]{1,0:T(8,128)(2,1)S(1)}, bf16[256,256]{1,0:T(8,128)(2,1)S(1)}, u32[]{:S(2)}, u32[]{:S(2)}) collective-permute-start(bf16[256,256]{1,0:T(8,128)(2,1)S(1)} %get-tuple-element.15.refs_0_), channel_id=1, source_target_pairs={{2,0},{3,1},{4,2},{5,3},{6,4},{7,5},{0,6},{1,7},{10,8},{11,9},{12,... | collective-permute-start | bytes 393224 | tf_op jit(solution)/shard_map/ppermute | solution.py:51
  146.4 5.4 %collective-permute-start.14 = (bf16[256,256]{1,0:T(8,128)(2,1)S(1)}, bf16[256,256]{1,0:T(8,128)(2,1)S(1)}, u32[]{:S(2)}, u32[]{:S(2)}) collective-permute-start(bf16[256,256]{1,0:T(8,128)(2,1)S(1)} %get-tuple-element.15.refs_0_), channel_id=1, source_target_pairs={{0,2},{1,3},{2,4},{3,5},{4,6},{5,7},{6,0},{7,1},{8,10},{9,11},{10,... | collective-permute-start | bytes 393224 | tf_op jit(solution)/shard_map/ppermute | solution.py:51
  148.3 7.9 %collective-permute-start.17 = (bf16[128,256]{1,0:T(8,128)(2,1)S(1)}, bf16[128,256]{1,0:T(8,128)(2,1)S(1)}, u32[]{:S(2)}, u32[]{:S(2)}) collective-permute-start(bf16[128,256]{1,0:T(8,128)(2,1)S(1)} %slice.47), channel_id=1, source_target_pairs={{2,0},{3,1},{4,2},{5,3},{6,4},{7,5},{0,6},{1,7},{10,8},{11,9},{12,... | collective-permute-start | bytes 196616 | tf_op jit(solution)/shard_map/ppermute | solution.py:51
  151.8 4.4 %collective-permute-start.16 = (bf16[128,256]{1,0:T(8,128)(2,1)S(1)}, bf16[128,256]{1,0:T(8,128)(2,1)S(1)}, u32[]{:S(2)}, u32[]{:S(2)}) collective-permute-start(bf16[128,256]{1,0:T(8,128)(2,1)S(1)} %slice.46), channel_id=1, source_target_pairs={{0,2},{1,3},{2,4},{3,5},{4,6},{5,7},{6,0},{7,1},{8,10},{9,11},{10,... | collective-permute-start | bytes 196616 | tf_op jit(solution)/shard_map/ppermute | solution.py:51
  156.3 15.0 %collective-permute-start.18 = (bf16[1024,256]{1,0:T(8,128)(2,1)S(1)}, bf16[1024,256]{1,0:T(8,128)(2,1)S(1)}, u32[]{:S(2)}, u32[]{:S(2)}) collective-permute-start(bf16[1024,256]{1,0:T(8,128)(2,1)S(1)} %constant_dynamic-update-slice_fusion.2), channel_id=1, source_target_pairs={{0,1},{1,0},{2,3},{3,2},{4,5},{5,4},{6,7},{7,6},{8,9},{9,8},{10,11... | collective-permute-start | bytes 1572872 | tf_op jit(solution)/shard_map/ppermute | solution.py:341
  172.5 18.3 %all-to-all-start.2 = ((bf16[8,256,256]{2,1,0:T(8,128)(2,1)}), bf16[8,256,256]{2,1,0:T(8,128)(2,1)S(1)}, u32[]{:S(2)}, u32[]{:S(2)}) async-start(bf16[8,256,256]{2,1,0:T(8,128)(2,1)} %get-tuple-element.13), calls=%async_computation.2 | async-start | bytes 2097152 | tf_op jit(solution)/shard_map/all_to_all | solution.py:343
  (7 other events, 191.7 us)
Sparse Core Ops, SparseCore 0:
  9.8 37.1 all-gather.5
  51.2 100.3 all-gather.3

commit v3 on v2

--- a/solution.py
+++ b/solution.py
@@ -22,6 +22,7 @@
 Z_GROUPS = [[x * NZ + z for z in range(NZ)] for x in range(NX)]
 Z_UP = [(x * NZ + z, x * NZ + (z + 1) % NZ) for x in range(NX) for z in range(NZ)]
 X_UP = [(x * NZ + z, (x + 1) % NX * NZ + z) for x in range(NX) for z in range(NZ)]
+X_ACROSS = [(x * NZ + z, (x + 2) % NX * NZ + z) for x in range(NX) for z in range(NZ)]
 NY = 4
 Y_UP = [(2 * y + core, 2 * ((y + 1) % NY) + core) for y in range(NY) for core in range(2)]
 CORES = [(own, own ^ 1) for own in range(2 * NY)]
@@ -77,27 +78,27 @@
             out_ref[pl.ds(above, size)] = pieces[2 * distance - 1][...]
 
 
-def pick_kernel(z_ref, lists_ref, own_ref, *refs):
-    *pieces, out_ref, plane_ref = refs
-    place_pieces(plane_ref, z_ref[0], own_ref, pieces, NZ, NB)
-
-    def body(i, carry):
-        out_ref[i] = plane_ref[lax.rem(lists_ref[i], PLANE)]
-        return carry
-
-    lax.fori_loop(0, NX * SLOTS, body, 0)
-
-
-def pick(z_at, lists, own, pieces):
+def pick_kernel(at_ref, *refs):
+    lists, own_ref, pieces = refs[:NX], refs[NX], refs[NX + 1 : -2]
+    out_ref, plane_ref = refs[-2:]
+    x_at, z_at = lax.div(at_ref[0], NZ), lax.rem(at_ref[0], NZ)
+    place_pieces(plane_ref, z_at, own_ref, pieces, NZ, NB)
+    for steps, list_ref in enumerate(lists):
+        first = lax.rem(x_at + steps, NX) * SLOTS
+        for j in range(SLOTS):
+            out_ref[first + j] = plane_ref[lax.rem(list_ref[j], PLANE)]
+
+
+def pick(at, lists, own, pieces):
     return pl.pallas_call(
         pick_kernel,
         out_shape=jax.ShapeDtypeStruct((NX * SLOTS, BLK, 2 * DH), BF16),
-        in_specs=[SMEM, SMEM] + [VMEM] * (1 + len(pieces)),
+        in_specs=[SMEM] * (1 + NX) + [VMEM] * (1 + len(pieces)),
         out_specs=VMEM,
         scratch_shapes=[pltpu.VMEM((PLANE, BLK, 2 * DH), BF16)],
         compiler_params=params(16),
         name="pick_far",
-    )(z_at, lists, own, *pieces)
+    )(at, *lists, own, *pieces)
 
 
 def attend_kernel(
@@ -113,10 +114,7 @@
         index = at_ref[0] * NB + b
         for w in range(WIN):
             local = b + w
-            lower = pl.multiple_of(lax.rem(local, NB) * BLK, BLK)
-            before = prev_ref[pl.ds(lower, BLK), :]
-            mine = own_ref[pl.ds(lower, BLK), :]
-            both = jnp.where(local < NB, before, mine)
+            both = jnp.where(local < NB, prev_ref[lax.rem(local, NB)], own_ref[lax.rem(local, NB)])
             k_ref[w * BLK : (w + 1) * BLK, :] = both[:, :DH]
             v_ref[w * BLK : (w + 1) * BLK, :] = both[:, DH:]
         for j in range(FARS):
@@ -185,44 +183,43 @@
             pltpu.VMEM((keys, 2 * DH), F32),
             pltpu.VMEM((BLK, 2 * BLK), F32),
         ],
-        compiler_params=params(40),
+        compiler_params=params(24),
         cost_estimate=pl.CostEstimate(flops=2_400_000_000 * 4, bytes_accessed=6 << 20, transcendentals=2_000_000),
         name="attend",
     )(at, far, count, queries, out_grad, prev, own, far_kv)
 
 
-def spread_kernel(x_ref, lists_ref, own_ref, *refs):
-    *pieces, out_ref, far_ref, acc_ref = refs
-    place_pieces(far_ref, x_ref[0], own_ref, pieces, NX, SLOTS)
+def spread_kernel(at_ref, *refs):
+    lists, pieces = refs[:NX], refs[NX:-2]
+    out_ref, acc_ref = refs[-2:]
+    mine, below, above, across_low, across_high = pieces
+    x_at = lax.div(at_ref[0], NZ)
     acc_ref[...] = jnp.zeros_like(acc_ref)
 
-    def body(i, carry):
-        listed = lists_ref[i]
-
-        @pl.when(lax.div(listed, PLANE) == x_ref[0])
+    def add(listed, term_ref, j):
+        @pl.when(lax.div(listed, PLANE) == x_at)
         def _():
-            at = lax.rem(listed, PLANE)
-            acc_ref[at] += far_ref[i].astype(F32)
-
-        return carry
-
-    lax.fori_loop(0, NX * SLOTS, body, 0)
+            acc_ref[lax.rem(listed, PLANE)] += term_ref[j].astype(F32)
+
+    half = SLOTS // 2
+    for j in range(SLOTS):
+        add(lists[0][j], mine, j)
+        add(lists[1][j], above, j)
+        add(lists[2][j], across_low if j < half else across_high, j % half)
+        add(lists[3][j], below, j)
     out_ref[...] = acc_ref[...].astype(BF16)
 
 
-def spread(x_at, lists, own, pieces):
+def spread(at, lists, own, pieces):
     return pl.pallas_call(
         spread_kernel,
         out_shape=jax.ShapeDtypeStruct((PLANE, BLK, 2 * DH), BF16),
-        in_specs=[SMEM, SMEM] + [VMEM] * (1 + len(pieces)),
+        in_specs=[SMEM] * (1 + NX) + [VMEM] * (1 + len(pieces)),
         out_specs=VMEM,
-        scratch_shapes=[
-            pltpu.VMEM((NX * SLOTS, BLK, 2 * DH), BF16),
-            pltpu.VMEM((PLANE, BLK, 2 * DH), F32),
-        ],
-        compiler_params=params(24),
+        scratch_shapes=[pltpu.VMEM((PLANE, BLK, 2 * DH), F32)],
+        compiler_params=params(16),
         name="spread_far",
-    )(x_at, lists, own, *pieces)
+    )(at, *lists, own, *pieces)
 
 
 def heads_kernel(at_ref, *refs):
@@ -304,34 +301,32 @@
 ):
     tokens = queries.shape[0]
     seq_index = lax.axis_index("seq").astype(jnp.int32)
-    x_index = lax.div(seq_index, NZ)
     at = seq_index.reshape(1)
     own_index = lax.axis_index("own").astype(jnp.int32).reshape(1)
-    z_at = lax.rem(seq_index, NZ).reshape(1)
-    x_at = x_index.reshape(1)
-    own_kv = jnp.concatenate([key_rows, value_rows], axis=1)
-
-    inputs_x = lax.all_gather(inputs, "seq", axis=0, axis_index_groups=X_GROUPS, tiled=True)
+    own_kv = jnp.concatenate([key_rows, value_rows], axis=1).reshape(NB, BLK, 2 * DH)
+
+    columns = DH // 4
     weights = jnp.concatenate([key_weight.T, value_weight.T])
     weights = lax.all_gather(weights, "seq", axis=0, tiled=True)
-    columns = DH // 4
+    weights, inputs = lax.optimization_barrier((weights, inputs))
+    inputs_x = lax.all_gather(inputs, "seq", axis=0, axis_index_groups=X_GROUPS, tiled=True)
     weights = weights.reshape(2 * NY, 4, 2, columns, -1).transpose(0, 2, 1, 3, 4)
     weights = weights.reshape(2 * NY * 2 * DH, -1)
 
-    own_blocks = own_kv.reshape(NB, BLK, 2 * DH)
-    plane = ring_gather(own_blocks, "seq", Z_UP, NZ)
+    listed = far_blocks.reshape(SLOTS)
+    below, above = both_ways(listed, listed, "seq", X_UP)
+    lists = (listed, above, lax.ppermute(listed, "seq", X_ACROSS), below)
+    plane = ring_gather(own_kv, "seq", Z_UP, NZ)
     prev_kv = shifted(own_kv, "seq", 1)
-    lists = lax.all_gather(far_blocks, "seq", axis=0, axis_index_groups=X_GROUPS, tiled=True)
-    lists = lists.reshape(NX * SLOTS)
-    chosen = pick(z_at, lists, own_blocks, plane)
+    chosen = pick(at, lists, own_kv, plane)
     far_kv = lax.all_to_all(chosen, "seq", 0, 0, axis_index_groups=X_GROUPS, tiled=True)
 
     query_grad, window, far_grad = attend(
-        at, far_blocks.reshape(SLOTS), far_count, queries, out_grad, prev_kv, own_kv, far_kv
+        at, listed, far_count, queries, out_grad, prev_kv, own_kv, far_kv
     )
     far_all = ring_gather(far_grad, "seq", X_UP, NX)
     back = shifted(window[:tokens].astype(BF16), "seq", -1)
-    dense = spread(x_at, lists, far_grad, far_all)
+    dense = spread(at, lists, far_grad, far_all)
     dense = dense.reshape(NZ, tokens, 2 * DH)
     terms = lax.all_to_all(dense, "seq", 0, 0, axis_index_groups=Z_GROUPS, tiled=True)
     kv_grad = jnp.sum(terms.astype(F32), axis=0) + back.astype(F32) + window[tokens:]
@@ -340,6 +335,7 @@
     same_core = ring_gather(kv_grad, "own", Y_UP, NY)
     other_core = lax.ppermute(jnp.concatenate([kv_grad, *same_core]), "own", CORES)
     stacked, wide = place_heads(own_index, kv_grad, same_core, other_core)
+    stacked, weights, inputs_x = lax.optimization_barrier((stacked, weights, inputs_x))
     quarter = lax.all_to_all(stacked, "seq", 0, 0, axis_index_groups=X_GROUPS, tiled=True)
     pieces = weight_terms(quarter, inputs_x)
     pieces = lax.all_to_all(pieces, "seq", 0, 0, axis_index_groups=Z_GROUPS, tiled=True)

time: 238 us -> 227 us (0.954)
  blocking collectives: 39.4 us -> 17.3 us
  starting transfers between devices: 52.3 us -> 60.7 us
    all_to_all x1, waiting for transfers between devices: 33.3 us -> 15.8 us  [local(): lax.all_to_all(dense, 'seq', 0, 0, axis_index_groups=Z_GROUPS, tiled=True)]
    all_to_all x1, blocking collectives: 30.6 us -> 17.3 us  [local(): lax.all_to_all(stacked, 'seq', 0, 0, axis_index_groups=X_GROUPS, tiled=True)]
    all_to_all x1, waiting for transfers between devices: 14.8 us -> 25 us  [local(): lax.all_to_all(pieces, 'seq', 0, 0, axis_index_groups=Z_GROUPS, tiled=True)]
    all_gather x1 -> x0, blocking collectives: 8.85 us -> none  [local(): lax.all_gather(far_blocks, 'seq', axis=0, axis_index_groups=X_GROUPS, til...]
    ppermute x0 -> x1, starting transfers between devices: none -> 3.17 us  [local(): lists = (listed, above, lax.ppermute(listed, 'seq', X_ACROSS), below)]
    ppermute x8 -> x9, waiting for transfers between devices: 21.8 us -> 24.6 us  [both_ways(): lax.ppermute(downward, axis, back)]
    transpose x1, local copies, waits for them, and re-layouts: 2.63 us -> 5.03 us  [local(): weights.reshape(2 * NY, 4, 2, columns, -1).transpose(0, 2, 1, 3, 4)]
    ppermute x8 -> x9, starting transfers between devices: 23.5 us -> 25.8 us  [both_ways(): lax.ppermute(downward, axis, back)]
  transfers between devices with their start and end apart: 24 -> 27, of which waited for: 14 -> 15; matrix products, arithmetic and copies ran while one was open for 2% -> 5% of each run, Pallas kernels for 7% -> 6%
where the time goes in v3:
time: 227 us
  waiting for transfers between devices  101 us (44%)
  starting transfers between devices  60.7 us (27%)
  blocking collectives  17.3 us (8%)
  Pallas kernels  16.7 us (7%)
  between operations  14.2 us (6%)
  local copies, waits for them, and re-layouts  9.26 us (4%)
  matrix products  4.23 us (2%)
  other arithmetic  2.84 us (1%)
    ppermute x9, starting transfers between devices, both_ways(): lax.ppermute(downward, axis, back)  25.8 us
    all_to_all x1, waiting for transfers between devices, local(): lax.all_to_all(pieces, 'seq', 0, 0, axis_index_groups=Z_GROUPS, tiled=True)  25 us
    ppermute x9, waiting for transfers between devices, both_ways(): lax.ppermute(downward, axis, back)  24.6 us
    all_to_all x1, waiting for transfers between devices, local(): lax.all_to_all(chosen, 'seq', 0, 0, axis_index_groups=X_GROUPS, tiled=True)  23.4 us
    all_to_all x1, blocking collectives, local(): lax.all_to_all(stacked, 'seq', 0, 0, axis_index_groups=X_GROUPS, tiled=True)  17.3 us
    all_to_all x1, waiting for transfers between devices, local(): lax.all_to_all(dense, 'seq', 0, 0, axis_index_groups=Z_GROUPS, tiled=True)  15.8 us
    ppermute x1, starting transfers between devices, local(): lax.ppermute(jnp.concatenate([kv_grad, *same_core]), 'own', CORES)  14.4 us
    pallas_call x1, Pallas kernels, attend(): pl.pallas_call(attend_kernel, out_shape=(jax.ShapeDtypeStruct((NB * BLK,...  9.6 us
  transfers between devices with their start and end apart: 27, of which 15 were waited for; matrix products, arithmetic and copies ran while one was open for 5% of the time, Pallas kernels for 6%

profile of v3, /device:TPU:1, one launch (start us, length us, event | category | flops | bytes accessed | tf_op | source)
XLA Modules:
  0.0 226.6 jit_solution(1041554940324947408)
XLA Ops:
  9.7 6.5 %collective-permute-start.5 = (bf16[2,128,256]{2,1,0:T(8,128)(2,1)S(1)}, bf16[2,128,256]{2,1,0:T(8,128)(2,1)S(1)}, u32[]{:S(2)}, u32[]{:S(2)}) collective-permute-start(bf16[2,128,256]{2,1,0:T(8,128)(2,1)S(1)} %bitcast.16), channel_id=1, source_target_pairs={{8,0},{16,8},{24,16},{32,24},{40,32},{48,40},{56,48},{0,56},{72,64... | collective-permute-start | bytes 393224 | tf_op jit(solution)/shard_map/ppermute | solution.py:52
  18.4 3.4 %collective-permute-start.7 = (bf16[2,128,256]{2,1,0:T(8,128)(2,1)S(1)}, bf16[2,128,256]{2,1,0:T(8,128)(2,1)S(1)}, u32[]{:S(2)}, u32[]{:S(2)}) collective-permute-start(bf16[2,128,256]{2,1,0:T(8,128)(2,1)S(1)} %collective-permute-done.5.refs_6_), channel_id=1, source_target_pairs={{8,0},{16,8},{24,16},{32,24},{40,32},{48,40},{56,48},{0,56},{72,64... | collective-permute-start | bytes 393224 | tf_op jit(solution)/shard_map/ppermute | solution.py:52
  23.7 3.1 %collective-permute-start.9 = (bf16[2,128,256]{2,1,0:T(8,128)(2,1)S(1)}, bf16[2,128,256]{2,1,0:T(8,128)(2,1)S(1)}, u32[]{:S(2)}, u32[]{:S(2)}) collective-permute-start(bf16[2,128,256]{2,1,0:T(8,128)(2,1)S(1)} %collective-permute-done.7.refs_8_), channel_id=1, source_target_pairs={{8,0},{16,8},{24,16},{32,24},{40,32},{48,40},{56,48},{0,56},{72,64... | collective-permute-start | bytes 393224 | tf_op jit(solution)/shard_map/ppermute | solution.py:52
  29.1 3.1 %collective-permute-start.11 = (bf16[1,128,256]{2,1,0:T(8,128)(2,1)S(1)}, bf16[1,128,256]{2,1,0:T(8,128)(2,1)S(1)}, u32[]{:S(2)}, u32[]{:S(2)}) collective-permute-start(bf16[1,128,256]{2,1,0:T(8,128)(2,1)S(1)} %slice.42), channel_id=1, source_target_pairs={{8,0},{16,8},{24,16},{32,24},{40,32},{48,40},{56,48},{0,56},{72,64... | collective-permute-start | bytes 196616 | tf_op jit(solution)/shard_map/ppermute | solution.py:52
  34.1 3.2 %collective-permute-start.2 = (s32[8]{0:T(128)S(1)}, s32[8]{0:T(128)S(1)}, u32[]{:S(2)}, u32[]{:S(2)}) collective-permute-start(s32[8]{0:T(128)S(1)} %reshape.30.refs_0_.far_ref), channel_id=1, source_target_pairs={{0,128},{8,136},{16,144},{24,152},{32,160},{40,168},{48,176},{56,1... | collective-permute-start | bytes 104 | tf_op jit(solution)/shard_map/ppermute | solution.py:318
  41.9 3.6 %all-to-all-start = ((bf16[32,128,256]{2,1,0:T(8,128)(2,1)}), bf16[32,128,256]{2,1,0:T(8,128)(2,1)S(1)}, u32[]{:S(2)}, u32[]{:S(2)}) async-start(bf16[32,128,256]{2,1,0:T(8,128)(2,1)} %pick_far.1), calls=%async_computation | async-start | bytes 4194304 | tf_op jit(solution)/shard_map/all_to_all | solution.py:322
  48.8 23.4 %all-to-all-done.far_kv_ref = bf16[32,128,256]{2,1,0:T(8,128)(2,1)S(1)} async-done(((bf16[32,128,256]{2,1,0:T(8,128)(2,1)}), bf16[32,128,256]{2,1,0:T(8,128)(2,1)S(1)}, u32[]{:S(2)}, u32[]{:S(2)}) %all-to-all-start) | async-done | bytes 2097184 | tf_op jit(solution)/shard_map/all_to_all | solution.py:322
  73.3 9.6 %attend.1 = (bf16[256,1024]{1,0:T(8,128)(2,1)}, f32[512,256]{1,0:T(8,128)S(1)}, bf16[8,128,256]{2,1,0:T(8,128)(2,1)S(1)}) custom-call(s32[1]{0:T(128)} %bitcast.at_ref, s32[8]{0:T(128)S(1)} %reshape.30.refs_0_.far_ref, s32[2]{0:T(128)S(1)} %copy-done.3, bf16[256,1024]{1,0:T(8,128)(2,1)S(1)} %copy-done.1, bf16[256,1024]{1,0:T(8,128)(2,1)S(1)} %copy-done.2, ...), custom_call_target="tpu_custom_call" | custom-call | flops 9600000000 | bytes 6291456 | tf_op jit(solution)/shard_map/attend/pallas_call | solution.py:170
  84.3 10.3 %collective-permute-done.13.refs_6_ = bf16[8,128,256]{2,1,0:T(8,128)(2,1)S(1)} collective-permute-done((bf16[8,128,256]{2,1,0:T(8,128)(2,1)S(1)}, bf16[8,128,256]{2,1,0:T(8,128)(2,1)S(1)}, u32[]{:S(2)}, u32[]{:S(2)}) %collective-permute-start.13) | collective-permute-done | bytes 524320 | tf_op jit(solution)/shard_map/ppermute | solution.py:52
  94.7 2.5 %collective-permute-start.15 = (bf16[4,128,256]{2,1,0:T(8,128)(2,1)S(1)}, bf16[4,128,256]{2,1,0:T(8,128)(2,1)S(1)}, u32[]{:S(2)}, u32[]{:S(2)}) collective-permute-start(bf16[4,128,256]{2,1,0:T(8,128)(2,1)S(1)} %slice.44), channel_id=1, source_target_pairs={{64,0},{72,8},{80,16},{88,24},{96,32},{104,40},{112,48},{120,56},{... | collective-permute-start | bytes 786440 | tf_op jit(solution)/shard_map/ppermute | solution.py:52
  97.3 4.4 %collective-permute-done.15.refs_8_ = bf16[4,128,256]{2,1,0:T(8,128)(2,1)S(1)} collective-permute-done((bf16[4,128,256]{2,1,0:T(8,128)(2,1)S(1)}, bf16[4,128,256]{2,1,0:T(8,128)(2,1)S(1)}, u32[]{:S(2)}, u32[]{:S(2)}) %collective-permute-start.15) | collective-permute-done | bytes 262176 | tf_op jit(solution)/shard_map/ppermute | solution.py:52
  101.7 3.3 %collective-permute-done.14.refs_7_ = bf16[4,128,256]{2,1,0:T(8,128)(2,1)S(1)} collective-permute-done((bf16[4,128,256]{2,1,0:T(8,128)(2,1)S(1)}, bf16[4,128,256]{2,1,0:T(8,128)(2,1)S(1)}, u32[]{:S(2)}, u32[]{:S(2)}) %collective-permute-start.14) | collective-permute-done | bytes 262176 | tf_op jit(solution)/shard_map/ppermute | solution.py:52
  105.1 2.4 %spread_far.1 = bf16[16,128,256]{2,1,0:T(8,128)(2,1)} custom-call(s32[1]{0:T(128)} %bitcast.at_ref, s32[8]{0:T(128)S(1)} %reshape.30.refs_0_.far_ref, s32[8]{0:T(128)S(1)} %collective-permute-done.1.refs_1_, s32[8]{0:T(128)S(1)} %collective-permute-done.2.refs_2_, s32[8]{0:T(128)S(1)} %collective-permute-done.3.refs_3_, ...), custom_call_target="tpu_custom_call" | custom-call | tf_op jit(solution)/shard_map/spread_far/pallas_call | solution.py:214
  107.5 4.4 %all-to-all-start.1 = ((bf16[8,256,256]{2,1,0:T(8,128)(2,1)}), bf16[8,256,256]{2,1,0:T(8,128)(2,1)S(1)}, u32[]{:S(2)}, u32[]{:S(2)}) async-start(bf16[8,256,256]{2,1,0:T(8,128)(2,1)} %bitcast.3), calls=%async_computation.1 | async-start | bytes 2097152 | tf_op jit(solution)/shard_map/all_to_all | solution.py:331
  113.9 15.8 %all-to-all-done.1 = bf16[8,256,256]{2,1,0:T(8,128)(2,1)S(1)} async-done(((bf16[8,256,256]{2,1,0:T(8,128)(2,1)}), bf16[8,256,256]{2,1,0:T(8,128)(2,1)S(1)}, u32[]{:S(2)}, u32[]{:S(2)}) %all-to-all-start.1) | async-done | bytes 1048608 | tf_op jit(solution)/shard_map/all_to_all | solution.py:331
  130.0 3.4 %collective-permute-start.18 = (bf16[256,256]{1,0:T(8,128)(2,1)S(1)}, bf16[256,256]{1,0:T(8,128)(2,1)S(1)}, u32[]{:S(2)}, u32[]{:S(2)}) collective-permute-start(bf16[256,256]{1,0:T(8,128)(2,1)S(1)} %get-tuple-element.25.refs_0_), channel_id=1, source_target_pairs={{2,0},{3,1},{4,2},{5,3},{6,4},{7,5},{0,6},{1,7},{10,8},{11,9},{12,... | collective-permute-start | bytes 393224 | tf_op jit(solution)/shard_map/ppermute | solution.py:52
  135.4 3.4 %collective-permute-start.20 = (bf16[128,256]{1,0:T(8,128)(2,1)S(1)}, bf16[128,256]{1,0:T(8,128)(2,1)S(1)}, u32[]{:S(2)}, u32[]{:S(2)}) collective-permute-start(bf16[128,256]{1,0:T(8,128)(2,1)S(1)} %slice.47), channel_id=1, source_target_pairs={{2,0},{3,1},{4,2},{5,3},{6,4},{7,5},{0,6},{1,7},{10,8},{11,9},{12,... | collective-permute-start | bytes 196616 | tf_op jit(solution)/shard_map/ppermute | solution.py:52
  138.9 4.7 %collective-permute-done.19.refs_3_ = bf16[128,256]{1,0:T(8,128)(2,1)S(1)} collective-permute-done((bf16[128,256]{1,0:T(8,128)(2,1)S(1)}, bf16[128,256]{1,0:T(8,128)(2,1)S(1)}, u32[]{:S(2)}, u32[]{:S(2)}) %collective-permute-start.19) | collective-permute-done | bytes 65568 | tf_op jit(solution)/shard_map/ppermute | solution.py:52
  143.6 14.4 %collective-permute-start.21 = (bf16[1024,256]{1,0:T(8,128)(2,1)S(1)}, bf16[1024,256]{1,0:T(8,128)(2,1)S(1)}, u32[]{:S(2)}, u32[]{:S(2)}) collective-permute-start(bf16[1024,256]{1,0:T(8,128)(2,1)S(1)} %constant_dynamic-update-slice_fusion), channel_id=1, source_target_pairs={{0,1},{1,0},{2,3},{3,2},{4,5},{5,4},{6,7},{7,6},{8,9},{9,8},{10,11... | collective-permute-start | bytes 1572872 | tf_op jit(solution)/shard_map/ppermute | solution.py:336
  159.7 5.0 %copy.13 = bf16[8,2,4,32,1024]{4,3,2,1,0:T(8,128)(2,1)} copy(bf16[8,2,4,32,1024]{4,3,1,2,0:T(8,128)(2,1)} %bitcast.21) | data formatting | bytes 8388608 | tf_op jit(solution)/shard_map/transpose | solution.py:313
  164.8 17.3 %all_to_all.20.grad_ref = bf16[8,256,256]{2,1,0:T(8,128)(2,1)S(1)} all-to-all(bf16[8,256,256]{2,1,0:T(8,128)(2,1)S(1)} %get-tuple-element.22), channel_id=1, replica_groups={{0,64,128,192},{8,72,136,200},{16,80,144,208},{24,88,152,216},{32,96,16..., dimensions={0} | all-to-all | bytes 2097152 | tf_op jit(solution)/shard_map/all_to_all | solution.py:339
  185.9 3.9 %all-to-all-start.3 = ((bf16[8,64,1024]{2,1,0:T(8,128)(2,1)}), bf16[8,64,1024]{2,1,0:T(8,128)(2,1)S(1)}, u32[]{:S(2)}, u32[]{:S(2)}) async-start(bf16[8,64,1024]{2,1,0:T(8,128)(2,1)} %weight_terms.1), calls=%async_computation.3 | async-start | bytes 2097152 | tf_op jit(solution)/shard_map/all_to_all | solution.py:341
  189.7 4.2 %convolution_convert_fusion = bf16[256,1024]{1,0:T(8,128)(2,1)} fusion(bf16[256,2048]{1,0:T(8,128)(2,1)S(1)} %get-tuple-element.17, bf16[2048,1024]{1,0:T(8,128)(2,1)} %bitcast.22), kind=kOutput, calls=%fused_computation.2 | convolution fusion | flops 1074003968 | bytes 5767168 | tf_op jit(solution)/shard_map/dot_general | solution.py:342
  193.9 25.0 %all-to-all-done.3 = bf16[8,64,1024]{2,1,0:T(8,128)(2,1)S(1)} async-done(((bf16[8,64,1024]{2,1,0:T(8,128)(2,1)}), bf16[8,64,1024]{2,1,0:T(8,128)(2,1)S(1)}, u32[]{:S(2)}, u32[]{:S(2)}) %all-to-all-start.3) | async-done | bytes 1048608 | tf_op jit(solution)/shard_map/all_to_all | solution.py:341
  (66 shorter events, 32.2 us)
Async XLA Ops:
  7.2 104.7 %all-gather.3.cloned.1.call-start = ((), (), s32[]{:S(2)}) async-start(), calls=%async_computation.4 | async-start | bytes 4325376 | tf_op jit(solution)/shard_map/all_gather | solution.py:310
  9.7 8.6 %collective-permute-start.5 = (bf16[2,128,256]{2,1,0:T(8,128)(2,1)S(1)}, bf16[2,128,256]{2,1,0:T(8,128)(2,1)S(1)}, u32[]{:S(2)}, u32[]{:S(2)}) collective-permute-start(bf16[2,128,256]{2,1,0:T(8,128)(2,1)S(1)} %bitcast.16), channel_id=1, source_target_pairs={{8,0},{16,8},{24,16},{32,24},{40,32},{48,40},{56,48},{0,56},{72,64... | collective-permute-start | bytes 393224 | tf_op jit(solution)/shard_map/ppermute | solution.py:52
  16.2 5.6 %collective-permute-start.4 = (bf16[2,128,256]{2,1,0:T(8,128)(2,1)S(1)}, bf16[2,128,256]{2,1,0:T(8,128)(2,1)S(1)}, u32[]{:S(2)}, u32[]{:S(2)}) collective-permute-start(bf16[2,128,256]{2,1,0:T(8,128)(2,1)S(1)} %bitcast.17), channel_id=1, source_target_pairs={{0,8},{8,16},{16,24},{24,32},{32,40},{40,48},{48,56},{56,0},{64,72... | collective-permute-start | bytes 393224 | tf_op jit(solution)/shard_map/ppermute | solution.py:52
  18.4 5.4 %collective-permute-start.7 = (bf16[2,128,256]{2,1,0:T(8,128)(2,1)S(1)}, bf16[2,128,256]{2,1,0:T(8,128)(2,1)S(1)}, u32[]{:S(2)}, u32[]{:S(2)}) collective-permute-start(bf16[2,128,256]{2,1,0:T(8,128)(2,1)S(1)} %collective-permute-done.5.refs_6_), channel_id=1, source_target_pairs={{8,0},{16,8},{24,16},{32,24},{40,32},{48,40},{56,48},{0,56},{72,64... | collective-permute-start | bytes 393224 | tf_op jit(solution)/shard_map/ppermute | solution.py:52
  21.8 5.0 %collective-permute-start.6 = (bf16[2,128,256]{2,1,0:T(8,128)(2,1)S(1)}, bf16[2,128,256]{2,1,0:T(8,128)(2,1)S(1)}, u32[]{:S(2)}, u32[]{:S(2)}) collective-permute-start(bf16[2,128,256]{2,1,0:T(8,128)(2,1)S(1)} %collective-permute-done.4.refs_5_), channel_id=1, source_target_pairs={{0,8},{8,16},{16,24},{24,32},{32,40},{40,48},{48,56},{56,0},{64,72... | collective-permute-start | bytes 393224 | tf_op jit(solution)/shard_map/ppermute | solution.py:52
  23.7 5.4 %collective-permute-start.9 = (bf16[2,128,256]{2,1,0:T(8,128)(2,1)S(1)}, bf16[2,128,256]{2,1,0:T(8,128)(2,1)S(1)}, u32[]{:S(2)}, u32[]{:S(2)}) collective-permute-start(bf16[2,128,256]{2,1,0:T(8,128)(2,1)S(1)} %collective-permute-done.7.refs_8_), channel_id=1, source_target_pairs={{8,0},{16,8},{24,16},{32,24},{40,32},{48,40},{56,48},{0,56},{72,64... | collective-permute-start | bytes 393224 | tf_op jit(solution)/shard_map/ppermute | solution.py:52
  26.8 5.4 %collective-permute-start.8 = (bf16[2,128,256]{2,1,0:T(8,128)(2,1)S(1)}, bf16[2,128,256]{2,1,0:T(8,128)(2,1)S(1)}, u32[]{:S(2)}, u32[]{:S(2)}) collective-permute-start(bf16[2,128,256]{2,1,0:T(8,128)(2,1)S(1)} %collective-permute-done.6.refs_7_), channel_id=1, source_target_pairs={{0,8},{8,16},{16,24},{24,32},{32,40},{40,48},{48,56},{56,0},{64,72... | collective-permute-start | bytes 393224 | tf_op jit(solution)/shard_map/ppermute | solution.py:52
  29.1 10.6 %collective-permute-start.11 = (bf16[1,128,256]{2,1,0:T(8,128)(2,1)S(1)}, bf16[1,128,256]{2,1,0:T(8,128)(2,1)S(1)}, u32[]{:S(2)}, u32[]{:S(2)}) collective-permute-start(bf16[1,128,256]{2,1,0:T(8,128)(2,1)S(1)} %slice.42), channel_id=1, source_target_pairs={{8,0},{16,8},{24,16},{32,24},{40,32},{48,40},{56,48},{0,56},{72,64... | collective-permute-start | bytes 196616 | tf_op jit(solution)/shard_map/ppermute | solution.py:52
  32.2 7.5 %collective-permute-start.10 = (bf16[1,128,256]{2,1,0:T(8,128)(2,1)S(1)}, bf16[1,128,256]{2,1,0:T(8,128)(2,1)S(1)}, u32[]{:S(2)}, u32[]{:S(2)}) collective-permute-start(bf16[1,128,256]{2,1,0:T(8,128)(2,1)S(1)} %slice.41), channel_id=1, source_target_pairs={{0,8},{8,16},{16,24},{24,32},{32,40},{40,48},{48,56},{56,0},{64,72... | collective-permute-start | bytes 196616 | tf_op jit(solution)/shard_map/ppermute | solution.py:52
  33.1 4.6 %collective-permute-start.3 = (s32[8]{0:T(128)S(1)}, s32[8]{0:T(128)S(1)}, u32[]{:S(2)}, u32[]{:S(2)}) collective-permute-start(s32[8]{0:T(128)S(1)} %reshape.30.refs_0_.far_ref), channel_id=1, source_target_pairs={{0,64},{8,72},{16,80},{24,88},{32,96},{40,104},{48,112},{56,120},{... | collective-permute-start | bytes 104 | tf_op jit(solution)/shard_map/ppermute | solution.py:52
  41.9 30.3 %all-to-all-start = ((bf16[32,128,256]{2,1,0:T(8,128)(2,1)}), bf16[32,128,256]{2,1,0:T(8,128)(2,1)S(1)}, u32[]{:S(2)}, u32[]{:S(2)}) async-start(bf16[32,128,256]{2,1,0:T(8,128)(2,1)} %pick_far.1), calls=%async_computation | async-start | bytes 4194304 | tf_op jit(solution)/shard_map/all_to_all | solution.py:322
  82.9 11.8 %collective-permute-start.13 = (bf16[8,128,256]{2,1,0:T(8,128)(2,1)S(1)}, bf16[8,128,256]{2,1,0:T(8,128)(2,1)S(1)}, u32[]{:S(2)}, u32[]{:S(2)}) collective-permute-start(bf16[8,128,256]{2,1,0:T(8,128)(2,1)S(1)} %get-tuple-element.15.refs_4_), channel_id=1, source_target_pairs={{64,0},{72,8},{80,16},{88,24},{96,32},{104,40},{112,48},{120,56},{... | collective-permute-start | bytes 1572872 | tf_op jit(solution)/shard_map/ppermute | solution.py:52
  82.9 14.3 %collective-permute-start.12 = (bf16[8,128,256]{2,1,0:T(8,128)(2,1)S(1)}, bf16[8,128,256]{2,1,0:T(8,128)(2,1)S(1)}, u32[]{:S(2)}, u32[]{:S(2)}) collective-permute-start(bf16[8,128,256]{2,1,0:T(8,128)(2,1)S(1)} %get-tuple-element.15.refs_4_), channel_id=1, source_target_pairs={{0,64},{8,72},{16,80},{24,88},{32,96},{40,104},{48,112},{56,120},{... | collective-permute-start | bytes 1572872 | tf_op jit(solution)/shard_map/ppermute | solution.py:52
  94.7 7.1 %collective-permute-start.15 = (bf16[4,128,256]{2,1,0:T(8,128)(2,1)S(1)}, bf16[4,128,256]{2,1,0:T(8,128)(2,1)S(1)}, u32[]{:S(2)}, u32[]{:S(2)}) collective-permute-start(bf16[4,128,256]{2,1,0:T(8,128)(2,1)S(1)} %slice.44), channel_id=1, source_target_pairs={{64,0},{72,8},{80,16},{88,24},{96,32},{104,40},{112,48},{120,56},{... | collective-permute-start | bytes 786440 | tf_op jit(solution)/shard_map/ppermute | solution.py:52
  97.2 7.9 %collective-permute-start.14 = (bf16[4,128,256]{2,1,0:T(8,128)(2,1)S(1)}, bf16[4,128,256]{2,1,0:T(8,128)(2,1)S(1)}, u32[]{:S(2)}, u32[]{:S(2)}) collective-permute-start(bf16[4,128,256]{2,1,0:T(8,128)(2,1)S(1)} %slice.43), channel_id=1, source_target_pairs={{0,64},{8,72},{16,80},{24,88},{32,96},{40,104},{48,112},{56,120},{... | collective-permute-start | bytes 786440 | tf_op jit(solution)/shard_map/ppermute | solution.py:52
  107.5 22.3 %all-to-all-start.1 = ((bf16[8,256,256]{2,1,0:T(8,128)(2,1)}), bf16[8,256,256]{2,1,0:T(8,128)(2,1)S(1)}, u32[]{:S(2)}, u32[]{:S(2)}) async-start(bf16[8,256,256]{2,1,0:T(8,128)(2,1)} %bitcast.3), calls=%async_computation.1 | async-start | bytes 2097152 | tf_op jit(solution)/shard_map/all_to_all | solution.py:331
  111.9 52.9 %all-gather.5.cloned.1.call-start = ((), (), s32[]{:S(2)}) async-start(), calls=%async_computation.5 | async-start | bytes 2621440 | tf_op jit(solution)/shard_map/all_gather | solution.py:312
  112.6 17.3 %collective-permute-start.16 = (bf16[256,256]{1,0:T(8,128)(2,1)S(1)}, bf16[256,256]{1,0:T(8,128)(2,1)S(1)}, u32[]{:S(2)}, u32[]{:S(2)}) collective-permute-start(bf16[256,256]{1,0:T(8,128)(2,1)S(1)} %slice.54), channel_id=1, source_target_pairs={{8,0},{16,8},{24,16},{32,24},{40,32},{48,40},{56,48},{64,56},{72,6... | collective-permute-start | bytes 393224 | tf_op jit(solution)/shard_map/ppermute | solution.py:47
  130.0 5.4 %collective-permute-start.18 = (bf16[256,256]{1,0:T(8,128)(2,1)S(1)}, bf16[256,256]{1,0:T(8,128)(2,1)S(1)}, u32[]{:S(2)}, u32[]{:S(2)}) collective-permute-start(bf16[256,256]{1,0:T(8,128)(2,1)S(1)} %get-tuple-element.25.refs_0_), channel_id=1, source_target_pairs={{2,0},{3,1},{4,2},{5,3},{6,4},{7,5},{0,6},{1,7},{10,8},{11,9},{12,... | collective-permute-start | bytes 393224 | tf_op jit(solution)/shard_map/ppermute | solution.py:52
  133.4 5.3 %collective-permute-start.17 = (bf16[256,256]{1,0:T(8,128)(2,1)S(1)}, bf16[256,256]{1,0:T(8,128)(2,1)S(1)}, u32[]{:S(2)}, u32[]{:S(2)}) collective-permute-start(bf16[256,256]{1,0:T(8,128)(2,1)S(1)} %get-tuple-element.25.refs_0_), channel_id=1, source_target_pairs={{0,2},{1,3},{2,4},{3,5},{4,6},{5,7},{6,0},{7,1},{8,10},{9,11},{10,... | collective-permute-start | bytes 393224 | tf_op jit(solution)/shard_map/ppermute | solution.py:52
  135.4 8.2 %collective-permute-start.20 = (bf16[128,256]{1,0:T(8,128)(2,1)S(1)}, bf16[128,256]{1,0:T(8,128)(2,1)S(1)}, u32[]{:S(2)}, u32[]{:S(2)}) collective-permute-start(bf16[128,256]{1,0:T(8,128)(2,1)S(1)} %slice.47), channel_id=1, source_target_pairs={{2,0},{3,1},{4,2},{5,3},{6,4},{7,5},{0,6},{1,7},{10,8},{11,9},{12,... | collective-permute-start | bytes 196616 | tf_op jit(solution)/shard_map/ppermute | solution.py:52
  138.7 4.8 %collective-permute-start.19 = (bf16[128,256]{1,0:T(8,128)(2,1)S(1)}, bf16[128,256]{1,0:T(8,128)(2,1)S(1)}, u32[]{:S(2)}, u32[]{:S(2)}) collective-permute-start(bf16[128,256]{1,0:T(8,128)(2,1)S(1)} %slice.46), channel_id=1, source_target_pairs={{0,2},{1,3},{2,4},{3,5},{4,6},{5,7},{6,0},{7,1},{8,10},{9,11},{10,... | collective-permute-start | bytes 196616 | tf_op jit(solution)/shard_map/ppermute | solution.py:52
  143.6 15.9 %collective-permute-start.21 = (bf16[1024,256]{1,0:T(8,128)(2,1)S(1)}, bf16[1024,256]{1,0:T(8,128)(2,1)S(1)}, u32[]{:S(2)}, u32[]{:S(2)}) collective-permute-start(bf16[1024,256]{1,0:T(8,128)(2,1)S(1)} %constant_dynamic-update-slice_fusion), channel_id=1, source_target_pairs={{0,1},{1,0},{2,3},{3,2},{4,5},{5,4},{6,7},{7,6},{8,9},{9,8},{10,11... | collective-permute-start | bytes 1572872 | tf_op jit(solution)/shard_map/ppermute | solution.py:336
  185.9 33.0 %all-to-all-start.3 = ((bf16[8,64,1024]{2,1,0:T(8,128)(2,1)}), bf16[8,64,1024]{2,1,0:T(8,128)(2,1)S(1)}, u32[]{:S(2)}, u32[]{:S(2)}) async-start(bf16[8,64,1024]{2,1,0:T(8,128)(2,1)} %weight_terms.1), calls=%async_computation.3 | async-start | bytes 2097152 | tf_op jit(solution)/shard_map/all_to_all | solution.py:341
  (7 other events, 142.6 us)
Sparse Core Ops, SparseCore 0:
  11.2 89.5 all-gather.2
  114.5 44.0 all-gather.4

commit v4 on v3

--- a/solution.py
+++ b/solution.py
@@ -26,6 +26,14 @@
 NY = 4
 Y_UP = [(2 * y + core, 2 * ((y + 1) % NY) + core) for y in range(NY) for core in range(2)]
 CORES = [(own, own ^ 1) for own in range(2 * NY)]
+SWAP_XY = [
+    (((x * NZ + z) * NY + y) * 2 + core, ((y * NZ + z) * NY + x) * 2 + core)
+    for x in range(NX)
+    for z in range(NZ)
+    for y in range(NY)
+    for core in range(2)
+]
+PART = DH // 4
 SCALE = 1.0 / math.sqrt(DH)
 EXP2_SCALE = SCALE * math.log2(math.e)
 NEG = -1e30
@@ -222,78 +230,137 @@
     )(at, *lists, own, *pieces)
 
 
-def heads_kernel(at_ref, *refs):
-    own_ref, *pieces, other_ref, stack_ref, wide_ref = refs
+def finish_kernel(terms_ref, back_ref, window_ref, out_ref):
+    total = window_ref[NB * BLK :, :] + back_ref[...].astype(F32)
+    for z in range(NZ):
+        total += terms_ref[z].astype(F32)
+    source = lax.broadcasted_iota(jnp.int32, (2 * DH, 2 * DH), 0)
+    target = lax.broadcasted_iota(jnp.int32, (2 * DH, 2 * DH), 1)
+    part, rest = target // (2 * PART), target % (2 * PART)
+    wanted = (rest // PART) * DH + part * PART + rest % PART
+    order = jnp.where(source == wanted, 1.0, 0.0).astype(BF16)
+    out_ref[...] = jnp.dot(
+        total.astype(BF16), order, preferred_element_type=F32
+    ).astype(BF16)
+
+
+def finish(terms, back, window):
+    return pl.pallas_call(
+        finish_kernel,
+        out_shape=jax.ShapeDtypeStruct((NB * BLK, 2 * DH), BF16),
+        in_specs=[VMEM] * 3,
+        out_specs=VMEM,
+        compiler_params=params(12),
+        name="finish_kv",
+    )(terms, back, window)
+
+
+def heads_kernel(at_ref, own_ref, *refs):
+    *pieces, other_ref, out_ref = refs
     at, core = lax.div(at_ref[0], 2), lax.rem(at_ref[0], 2)
-    half = BLK * NB // 2
-
-    def put(y, which, rows, value):
-        head = 2 * y + which
-        stack_ref[head, rows, :] = value
-        wide_ref[rows, pl.ds(pl.multiple_of(head * 2 * DH, 2 * DH), 2 * DH)] = value
-
-    everything = slice(0, 2 * half)
+    rows = NB * BLK
+    half = rows // 2
     below, above = lax.rem(at + NY - 1, NY), lax.rem(at + 1, NY)
     across = lax.rem(at + 2, NY)
-    for which, mine in ((core, True), (1 - core, False)):
-        parts = (
-            (own_ref, *pieces)
-            if mine
-            else (
-                other_ref.at[: 2 * half],
-                other_ref.at[2 * half : 4 * half],
-                other_ref.at[4 * half : 6 * half],
-                other_ref.at[6 * half : 7 * half],
-                other_ref.at[7 * half :],
-            )
-        )
-        put(at, which, everything, parts[0][...])
-        put(below, which, everything, parts[1][...])
-        put(above, which, everything, parts[2][...])
-        put(across, which, slice(0, half), parts[3][...])
-        put(across, which, slice(half, 2 * half), parts[4][...])
+    starts = (0, rows, 2 * rows, 3 * rows, 3 * rows + half)
+    for k, (y, low, high) in enumerate(
+        ((at, 0, rows), (below, 0, rows), (above, 0, rows), (across, 0, half), (across, half, rows))
+    ):
+        mine = own_ref if k == 0 else pieces[k - 1]
+        out_ref[2 * y + core, low:high, :] = mine[...]
+        out_ref[2 * y + 1 - core, low:high, :] = other_ref[starts[k] : starts[k] + high - low, :]
 
 
 def place_heads(at, own, pieces, other):
-    tokens = own.shape[0]
     return pl.pallas_call(
         heads_kernel,
-        out_shape=(
-            jax.ShapeDtypeStruct((2 * NY, tokens, 2 * DH), BF16),
-            jax.ShapeDtypeStruct((tokens, 2 * NY * 2 * DH), BF16),
-        ),
+        out_shape=jax.ShapeDtypeStruct((2 * NY, *own.shape), BF16),
         in_specs=[SMEM] + [VMEM] * (2 + len(pieces)),
-        out_specs=(VMEM, VMEM),
-        compiler_params=params(16),
+        out_specs=VMEM,
+        compiler_params=params(8),
         name="place_heads",
     )(at, own, *pieces, other)
 
 
 def weights_kernel(grad_ref, inputs_ref, out_ref):
-    columns = DH // 4
+    quarters, wide = 4, inputs_ref.shape[1] // 4
     for head in range(2):
         grad = jnp.concatenate([grad_ref[x * 2 + head] for x in range(NX)])
         term = lax.dot_general(
             grad, inputs_ref[...], (((0,), (0,)), ((), ())), preferred_element_type=F32
         ).astype(BF16)
         for part in range(4):
-            for kind in range(2):
-                lower = kind * DH + part * columns
-                out_ref[head * 4 + part, kind * columns : (kind + 1) * columns, :] = term[
-                    lower : lower + columns
+            for quarter in range(quarters):
+                out_ref[
+                    head * 4 + part, quarter * 2 * PART : (quarter + 1) * 2 * PART, :
+                ] = term[
+                    part * 2 * PART : (part + 1) * 2 * PART, quarter * wide : (quarter + 1) * wide
                 ]
 
 
 def weight_terms(grad, inputs_x):
     return pl.pallas_call(
         weights_kernel,
-        out_shape=jax.ShapeDtypeStruct((NZ, 2 * DH // 4, inputs_x.shape[1]), BF16),
+        out_shape=jax.ShapeDtypeStruct((NZ, 4 * 2 * PART, inputs_x.shape[1] // 4), BF16),
         in_specs=[VMEM, VMEM],
         out_specs=VMEM,
-        compiler_params=params(24),
+        compiler_params=params(16),
         cost_estimate=pl.CostEstimate(flops=1 << 30, bytes_accessed=4 << 20, transcendentals=0),
         name="weight_terms",
     )(grad, inputs_x)
+
+
+def weight_sum_kernel(terms_ref, key_ref, value_ref):
+    total = terms_ref[0].astype(F32)
+    for z in range(1, NZ):
+        total += terms_ref[z].astype(F32)
+    wide = total.shape[1]
+    for quarter in range(4):
+        low = quarter * 2 * PART
+        key_ref[:, quarter * wide : (quarter + 1) * wide] = total[low : low + PART]
+        value_ref[:, quarter * wide : (quarter + 1) * wide] = total[low + PART : low + 2 * PART]
+
+
+def weight_sum(terms):
+    out = jax.ShapeDtypeStruct((PART, 4 * terms.shape[2]), F32)
+    return pl.pallas_call(
+        weight_sum_kernel,
+        out_shape=(out, out),
+        in_specs=[VMEM],
+        out_specs=(VMEM, VMEM),
+        compiler_params=params(8),
+        name="weight_sum",
+    )(terms)
+
+
+def input_kernel(at_ref, grad_ref, weights_ref, mine_ref, above_ref, across_ref, below_ref):
+    x_at = lax.div(at_ref[0], NZ)
+    for steps, out_ref in enumerate((mine_ref, above_ref, across_ref, below_ref)):
+        x = lax.rem(x_at + steps, NX)
+        grad = jnp.concatenate([grad_ref[2 * x], grad_ref[2 * x + 1]], axis=1)
+        out_ref[...] = jnp.dot(grad, weights_ref[...], preferred_element_type=F32).astype(
+            out_ref.dtype
+        )
+
+
+def input_terms(at, grad, weights):
+    shape = (grad.shape[1], weights.shape[1])
+    send = jax.ShapeDtypeStruct(shape, BF16)
+    return pl.pallas_call(
+        input_kernel,
+        out_shape=(jax.ShapeDtypeStruct(shape, F32), send, send, send),
+        in_specs=[SMEM, VMEM, VMEM],
+        out_specs=(VMEM,) * 4,
+        compiler_params=params(16),
+        cost_estimate=pl.CostEstimate(flops=1 << 30, bytes_accessed=4 << 20, transcendentals=0),
+        name="input_terms",
+    )(at, grad, weights)
+
+
+def added(term, arrived, low):
+    high = low + arrived.shape[0]
+    rows = (term[low:high].astype(F32) + arrived.astype(F32)).astype(BF16)
+    return jnp.concatenate([term[:low], rows, term[high:]])
 
 
 def local(
@@ -305,48 +372,57 @@
     own_index = lax.axis_index("own").astype(jnp.int32).reshape(1)
     own_kv = jnp.concatenate([key_rows, value_rows], axis=1).reshape(NB, BLK, 2 * DH)
 
-    columns = DH // 4
+    inputs_x = lax.all_gather(inputs, "seq", axis=0, axis_index_groups=X_GROUPS, tiled=True)
+
+    listed = far_blocks.reshape(SLOTS)
+    list_below, list_above = both_ways(listed, listed, "seq", X_UP)
+    list_across = lax.ppermute(listed, "seq", X_ACROSS)
+    from_below, from_above = both_ways(own_kv, own_kv, "seq", Z_UP)
+    list_below, list_above, list_across, from_below, from_above, key_weight, value_weight = (
+        lax.optimization_barrier(
+            (list_below, list_above, list_across, from_below, from_above, key_weight, value_weight)
+        )
+    )
+    lists = (listed, list_above, list_across, list_below)
     weights = jnp.concatenate([key_weight.T, value_weight.T])
-    weights = lax.all_gather(weights, "seq", axis=0, tiled=True)
-    weights, inputs = lax.optimization_barrier((weights, inputs))
-    inputs_x = lax.all_gather(inputs, "seq", axis=0, axis_index_groups=X_GROUPS, tiled=True)
-    weights = weights.reshape(2 * NY, 4, 2, columns, -1).transpose(0, 2, 1, 3, 4)
-    weights = weights.reshape(2 * NY * 2 * DH, -1)
-
-    listed = far_blocks.reshape(SLOTS)
-    below, above = both_ways(listed, listed, "seq", X_UP)
-    lists = (listed, above, lax.ppermute(listed, "seq", X_ACROSS), below)
-    plane = ring_gather(own_kv, "seq", Z_UP, NZ)
+    weights = lax.all_gather(weights, "seq", axis=0, axis_index_groups=Z_GROUPS, tiled=True)
+    plane = [from_below, from_above]
+    for distance in range(2, NZ // 2 + 1):
+        if distance == NZ // 2:
+            from_below, from_above = from_below[: NB // 2], from_above[NB // 2 :]
+        from_below, from_above = both_ways(from_below, from_above, "seq", Z_UP)
+        plane += [from_below, from_above]
     prev_kv = shifted(own_kv, "seq", 1)
     chosen = pick(at, lists, own_kv, plane)
     far_kv = lax.all_to_all(chosen, "seq", 0, 0, axis_index_groups=X_GROUPS, tiled=True)
 
+    far_kv, inputs_x = lax.optimization_barrier((far_kv, inputs_x))
     query_grad, window, far_grad = attend(
         at, listed, far_count, queries, out_grad, prev_kv, own_kv, far_kv
     )
     far_all = ring_gather(far_grad, "seq", X_UP, NX)
     back = shifted(window[:tokens].astype(BF16), "seq", -1)
     dense = spread(at, lists, far_grad, far_all)
+    dense, weights = lax.optimization_barrier((dense, weights))
     dense = dense.reshape(NZ, tokens, 2 * DH)
     terms = lax.all_to_all(dense, "seq", 0, 0, axis_index_groups=Z_GROUPS, tiled=True)
-    kv_grad = jnp.sum(terms.astype(F32), axis=0) + back.astype(F32) + window[tokens:]
-    kv_grad = kv_grad.astype(BF16)
-
-    same_core = ring_gather(kv_grad, "own", Y_UP, NY)
-    other_core = lax.ppermute(jnp.concatenate([kv_grad, *same_core]), "own", CORES)
-    stacked, wide = place_heads(own_index, kv_grad, same_core, other_core)
-    stacked, weights, inputs_x = lax.optimization_barrier((stacked, weights, inputs_x))
-    quarter = lax.all_to_all(stacked, "seq", 0, 0, axis_index_groups=X_GROUPS, tiled=True)
-    pieces = weight_terms(quarter, inputs_x)
+    kv_grad = finish(terms, back, window)
+
+    moved = lax.ppermute(kv_grad, ("seq", "own"), SWAP_XY)
+    same_core = ring_gather(moved, "own", Y_UP, NY)
+    other_core = lax.ppermute(jnp.concatenate([moved, *same_core]), "own", CORES)
+    heads = place_heads(own_index, moved, same_core, other_core)
+
+    pieces = weight_terms(heads, inputs_x)
     pieces = lax.all_to_all(pieces, "seq", 0, 0, axis_index_groups=Z_GROUPS, tiled=True)
-    input_grad = jnp.dot(wide, weights, preferred_element_type=F32)
-    weight_grad = jnp.sum(pieces.astype(F32), axis=0)
-    return (
-        query_grad,
-        input_grad.astype(BF16),
-        weight_grad[:columns].T,
-        weight_grad[columns:].T,
-    )
+    mine, above, across, below = input_terms(at, heads, weights)
+    half = tokens // 2
+    from_below, from_above = both_ways(across[:half], across[half:], "seq", X_UP)
+    above, below = added(above, from_below, 0), added(below, from_above, half)
+    from_below, from_above = both_ways(above, below, "seq", X_UP)
+    input_grad = mine + from_below.astype(F32) + from_above.astype(F32)
+    key_weight_grad, value_weight_grad = weight_sum(pieces)
+    return (query_grad, input_grad.astype(BF16), key_weight_grad.T, value_weight_grad.T)
 
 
 def solution(mesh):

time: 227 us -> 206 us (0.907)
  blocking collectives: 17.3 us -> 0 us
  starting transfers between devices: 60.7 us -> 71 us
  waiting for transfers between devices: 101 us -> 93.1 us
  matrix products: 4.23 us -> 0 us
  local copies, waits for them, and re-layouts: 9.26 us -> 5.04 us
    all_to_all x1, waiting for transfers between devices: 25 us -> 4.01 us  [local(): lax.all_to_all(pieces, 'seq', 0, 0, axis_index_groups=Z_GROUPS, tiled=True)]
    ppermute x9 -> x11, waiting for transfers between devices: 8.06 us -> 27.4 us  [both_ways(): lax.ppermute(upward, axis, pairs)]
    all_to_all x1 -> x0, blocking collectives: 17.3 us -> none  [local(): lax.all_to_all(stacked, 'seq', 0, 0, axis_index_groups=X_GROUPS, tiled=True)]
    ppermute x2, waiting for transfers between devices: 1.8 us -> 18.2 us  [shifted(): lax.ppermute(value, axis, [(source, source + steps) for source in range(l...]
    all_to_all x1, waiting for transfers between devices: 15.8 us -> 1.97 us  [local(): lax.all_to_all(dense, 'seq', 0, 0, axis_index_groups=Z_GROUPS, tiled=True)]
    ppermute x9 -> x11, waiting for transfers between devices: 24.6 us -> 15.1 us  [both_ways(): lax.ppermute(downward, axis, back)]
    ppermute x9 -> x11, starting transfers between devices: 2.71 us -> 11.6 us  [both_ways(): lax.ppermute(upward, axis, pairs)]
    transpose x2 -> x0, local copies, waits for them, and re-layouts: 5.74 us -> none  [the longest x1 5.03 us: local(): weights.reshape(2 * NY, 4, 2, columns, -1).transpose(0, 2, 1, 3, 4)]
  transfers between devices with their start and end apart: 27 -> 32, of which waited for: 15 -> 16; matrix products, arithmetic and copies ran while one was open for 5% -> 2% of each run, Pallas kernels for 6% -> 7%
where the time goes in v4:
time: 206 us; the launch traced here: 205 us
  waiting for transfers between devices  93.1 us (45%)
  starting transfers between devices  71 us (34%)
  Pallas kernels  18.8 us (9%)
  between operations  14.4 us (7%)
  local copies, waits for them, and re-layouts  5.04 us (2%)
  other arithmetic  2.79 us (1%)
    ppermute x11, starting transfers between devices, both_ways(): lax.ppermute(downward, axis, back)  30.9 us
    ppermute x11, waiting for transfers between devices, both_ways(): lax.ppermute(upward, axis, pairs)  27.4 us
    all_to_all x1, waiting for transfers between devices, local(): lax.all_to_all(chosen, 'seq', 0, 0, axis_index_groups=X_GROUPS, tiled=True)  21.8 us
    ppermute x2, waiting for transfers between devices, shifted(): lax.ppermute(value, axis, [(source, source + steps) for source in range(l...  18.2 us
    ppermute x11, waiting for transfers between devices, both_ways(): lax.ppermute(downward, axis, back)  15.1 us
    ppermute x1, starting transfers between devices, local(): lax.ppermute(jnp.concatenate([moved, *same_core]), 'own', CORES)  11.6 us
    ppermute x11, starting transfers between devices, both_ways(): lax.ppermute(upward, axis, pairs)  11.6 us
    pallas_call x1, Pallas kernels, attend(): pl.pallas_call(attend_kernel, out_shape=(jax.ShapeDtypeStruct((NB * BLK,...  9.56 us
  transfers between devices with their start and end apart: 32, of which 16 were waited for; matrix products, arithmetic and copies ran while one was open for 2% of the time, Pallas kernels for 7%

profile of v4, /device:TPU:1, one launch (start us, length us, event | category | flops | bytes accessed | tf_op | source)
XLA Modules:
  0.0 205.1 jit_solution(14589116497701664370)
XLA Ops:
  11.3 4.0 %collective-permute-start.5 = (bf16[2,128,256]{2,1,0:T(8,128)(2,1)S(1)}, bf16[2,128,256]{2,1,0:T(8,128)(2,1)S(1)}, u32[]{:S(2)}, u32[]{:S(2)}) collective-permute-start(bf16[2,128,256]{2,1,0:T(8,128)(2,1)S(1)} %bitcast.9), channel_id=1, source_target_pairs={{8,0},{16,8},{24,16},{32,24},{40,32},{48,40},{56,48},{0,56},{72,64... | collective-permute-start | bytes 393224 | tf_op jit(solution)/shard_map/ppermute | solution.py:60
  22.7 2.7 %collective-permute-start.7 = (bf16[2,128,256]{2,1,0:T(8,128)(2,1)S(1)}, bf16[2,128,256]{2,1,0:T(8,128)(2,1)S(1)}, u32[]{:S(2)}, u32[]{:S(2)}) collective-permute-start(bf16[2,128,256]{2,1,0:T(8,128)(2,1)S(1)} %collective-permute-done.5.refs_6_), channel_id=1, source_target_pairs={{8,0},{16,8},{24,16},{32,24},{40,32},{48,40},{56,48},{0,56},{72,64... | collective-permute-start | bytes 393224 | tf_op jit(solution)/shard_map/ppermute | solution.py:60
  27.7 2.7 %collective-permute-start.9 = (bf16[2,128,256]{2,1,0:T(8,128)(2,1)S(1)}, bf16[2,128,256]{2,1,0:T(8,128)(2,1)S(1)}, u32[]{:S(2)}, u32[]{:S(2)}) collective-permute-start(bf16[2,128,256]{2,1,0:T(8,128)(2,1)S(1)} %collective-permute-done.7.refs_8_), channel_id=1, source_target_pairs={{8,0},{16,8},{24,16},{32,24},{40,32},{48,40},{56,48},{0,56},{72,64... | collective-permute-start | bytes 393224 | tf_op jit(solution)/shard_map/ppermute | solution.py:60
  30.4 2.7 %collective-permute-done.8.refs_9_ = bf16[2,128,256]{2,1,0:T(8,128)(2,1)S(1)} collective-permute-done((bf16[2,128,256]{2,1,0:T(8,128)(2,1)S(1)}, bf16[2,128,256]{2,1,0:T(8,128)(2,1)S(1)}, u32[]{:S(2)}, u32[]{:S(2)}) %collective-permute-start.8) | collective-permute-done | bytes 131104 | tf_op jit(solution)/shard_map/ppermute | solution.py:60
  33.2 2.7 %collective-permute-start.11 = (bf16[1,128,256]{2,1,0:T(8,128)(2,1)S(1)}, bf16[1,128,256]{2,1,0:T(8,128)(2,1)S(1)}, u32[]{:S(2)}, u32[]{:S(2)}) collective-permute-start(bf16[1,128,256]{2,1,0:T(8,128)(2,1)S(1)} %slice.54), channel_id=1, source_target_pairs={{8,0},{16,8},{24,16},{32,24},{40,32},{48,40},{56,48},{0,56},{72,64... | collective-permute-start | bytes 196616 | tf_op jit(solution)/shard_map/ppermute | solution.py:60
  40.3 3.8 %all-to-all-start = ((bf16[32,128,256]{2,1,0:T(8,128)(2,1)}), bf16[32,128,256]{2,1,0:T(8,128)(2,1)S(1)}, u32[]{:S(2)}, u32[]{:S(2)}) async-start(bf16[32,128,256]{2,1,0:T(8,128)(2,1)} %pick_far.1), calls=%async_computation | async-start | bytes 4194304 | tf_op jit(solution)/shard_map/all_to_all | solution.py:397
  46.3 21.8 %all-to-all-done.far_kv_ref = bf16[32,128,256]{2,1,0:T(8,128)(2,1)S(1)} async-done(((bf16[32,128,256]{2,1,0:T(8,128)(2,1)}), bf16[32,128,256]{2,1,0:T(8,128)(2,1)S(1)}, u32[]{:S(2)}, u32[]{:S(2)}) %all-to-all-start) | async-done | bytes 2097184 | tf_op jit(solution)/shard_map/all_to_all | solution.py:397
  69.2 9.6 %attend.1 = (bf16[256,1024]{1,0:T(8,128)(2,1)}, f32[512,256]{1,0:T(8,128)S(1)}, bf16[8,128,256]{2,1,0:T(8,128)(2,1)S(1)}) custom-call(s32[1]{0:T(128)} %bitcast.at_ref, s32[8]{0:T(128)S(1)} %reshape.24.refs_0_.far_ref, s32[2]{0:T(128)S(1)} %copy-done.5, bf16[256,1024]{1,0:T(8,128)(2,1)S(1)} %copy-done.3, bf16[256,1024]{1,0:T(8,128)(2,1)S(1)} %copy-done.4, ...), custom_call_target="tpu_custom_call" | custom-call | flops 9600000000 | bytes 6291456 | tf_op jit(solution)/shard_map/attend/pallas_call | solution.py:178
  78.7 2.7 %collective-permute-start.13 = (bf16[8,128,256]{2,1,0:T(8,128)(2,1)S(1)}, bf16[8,128,256]{2,1,0:T(8,128)(2,1)S(1)}, u32[]{:S(2)}, u32[]{:S(2)}) collective-permute-start(bf16[8,128,256]{2,1,0:T(8,128)(2,1)S(1)} %get-tuple-element.31.refs_4_), channel_id=1, source_target_pairs={{64,0},{72,8},{80,16},{88,24},{96,32},{104,40},{112,48},{120,56},{... | collective-permute-start | bytes 1572872 | tf_op jit(solution)/shard_map/ppermute | solution.py:60
  81.4 6.9 %collective-permute-done.12.refs_5_ = bf16[8,128,256]{2,1,0:T(8,128)(2,1)S(1)} collective-permute-done((bf16[8,128,256]{2,1,0:T(8,128)(2,1)S(1)}, bf16[8,128,256]{2,1,0:T(8,128)(2,1)S(1)}, u32[]{:S(2)}, u32[]{:S(2)}) %collective-permute-start.12) | collective-permute-done | bytes 524320 | tf_op jit(solution)/shard_map/ppermute | solution.py:60
  88.4 2.7 %collective-permute-start.15 = (bf16[4,128,256]{2,1,0:T(8,128)(2,1)S(1)}, bf16[4,128,256]{2,1,0:T(8,128)(2,1)S(1)}, u32[]{:S(2)}, u32[]{:S(2)}) collective-permute-start(bf16[4,128,256]{2,1,0:T(8,128)(2,1)S(1)} %slice.56), channel_id=1, source_target_pairs={{64,0},{72,8},{80,16},{88,24},{96,32},{104,40},{112,48},{120,56},{... | collective-permute-start | bytes 786440 | tf_op jit(solution)/shard_map/ppermute | solution.py:60
  91.2 6.0 %collective-permute-done.14.refs_7_ = bf16[4,128,256]{2,1,0:T(8,128)(2,1)S(1)} collective-permute-done((bf16[4,128,256]{2,1,0:T(8,128)(2,1)S(1)}, bf16[4,128,256]{2,1,0:T(8,128)(2,1)S(1)}, u32[]{:S(2)}, u32[]{:S(2)}) %collective-permute-start.14) | collective-permute-done | bytes 262176 | tf_op jit(solution)/shard_map/ppermute | solution.py:60
  99.6 3.6 %all-to-all-start.1 = ((bf16[8,256,256]{2,1,0:T(8,128)(2,1)}), bf16[8,256,256]{2,1,0:T(8,128)(2,1)S(1)}, u32[]{:S(2)}, u32[]{:S(2)}) async-start(bf16[8,256,256]{2,1,0:T(8,128)(2,1)} %bitcast.5), calls=%async_computation.1 | async-start | bytes 2097152 | tf_op jit(solution)/shard_map/all_to_all | solution.py:408
  104.5 18.2 %collective-permute-done.16.back_ref = bf16[256,256]{1,0:T(8,128)(2,1)S(1)} collective-permute-done((bf16[256,256]{1,0:T(8,128)(2,1)S(1)}, bf16[256,256]{1,0:T(8,128)(2,1)S(1)}, u32[]{:S(2)}, u32[]{:S(2)}) %collective-permute-start.16) | collective-permute-done | bytes 131104 | tf_op jit(solution)/shard_map/ppermute | solution.py:55
  125.7 7.5 %collective-permute-start.18 = (bf16[256,256]{1,0:T(8,128)(2,1)S(1)}, bf16[256,256]{1,0:T(8,128)(2,1)S(1)}, u32[]{:S(2)}, u32[]{:S(2)}) collective-permute-start(bf16[256,256]{1,0:T(8,128)(2,1)S(1)} %collective-permute-done.17.own_ref), channel_id=1, source_target_pairs={{0,2},{1,3},{2,4},{3,5},{4,6},{5,7},{6,0},{7,1},{8,10},{9,11},{10,... | collective-permute-start | bytes 393224 | tf_op jit(solution)/shard_map/ppermute | solution.py:60
  133.2 5.0 %collective-permute-start.19 = (bf16[256,256]{1,0:T(8,128)(2,1)S(1)}, bf16[256,256]{1,0:T(8,128)(2,1)S(1)}, u32[]{:S(2)}, u32[]{:S(2)}) collective-permute-start(bf16[256,256]{1,0:T(8,128)(2,1)S(1)} %collective-permute-done.17.own_ref), channel_id=1, source_target_pairs={{2,0},{3,1},{4,2},{5,3},{6,4},{7,5},{0,6},{1,7},{10,8},{11,9},{12,... | collective-permute-start | bytes 393224 | tf_op jit(solution)/shard_map/ppermute | solution.py:60
  140.6 2.7 %collective-permute-start.21 = (bf16[128,256]{1,0:T(8,128)(2,1)S(1)}, bf16[128,256]{1,0:T(8,128)(2,1)S(1)}, u32[]{:S(2)}, u32[]{:S(2)}) collective-permute-start(bf16[128,256]{1,0:T(8,128)(2,1)S(1)} %slice.59), channel_id=1, source_target_pairs={{2,0},{3,1},{4,2},{5,3},{6,4},{7,5},{0,6},{1,7},{10,8},{11,9},{12,... | collective-permute-start | bytes 196616 | tf_op jit(solution)/shard_map/ppermute | solution.py:60
  144.9 11.6 %collective-permute-start.22 = (bf16[1024,256]{1,0:T(8,128)(2,1)S(1)}, bf16[1024,256]{1,0:T(8,128)(2,1)S(1)}, u32[]{:S(2)}, u32[]{:S(2)}) collective-permute-start(bf16[1024,256]{1,0:T(8,128)(2,1)S(1)} %constant_dynamic-update-slice_fusion), channel_id=1, source_target_pairs={{0,1},{1,0},{2,3},{3,2},{4,5},{5,4},{6,7},{7,6},{8,9},{9,8},{10,11... | collective-permute-start | bytes 1572872 | tf_op jit(solution)/shard_map/ppermute | solution.py:413
  163.7 4.5 %all-to-all-start.2 = ((bf16[8,256,256]{2,1,0:T(8,128)(2,1)}), bf16[8,256,256]{2,1,0:T(8,128)(2,1)S(1)}, u32[]{:S(2)}, u32[]{:S(2)}) async-start(bf16[8,256,256]{2,1,0:T(8,128)(2,1)} %weight_terms.1), calls=%async_computation.2 | async-start | bytes 2097152 | tf_op jit(solution)/shard_map/all_to_all | solution.py:417
  170.9 5.6 %collective-permute-done.25 = bf16[128,1024]{1,0:T(8,128)(2,1)S(1)} collective-permute-done((bf16[128,1024]{1,0:T(8,128)(2,1)S(1)}, bf16[128,1024]{1,0:T(8,128)(2,1)S(1)}, u32[]{:S(2)}, u32[]{:S(2)}) %collective-permute-start.25) | collective-permute-done | bytes 262176 | tf_op jit(solution)/shard_map/ppermute | solution.py:60
  176.6 2.7 %collective-permute-start.26 = (bf16[256,1024]{1,0:T(8,128)(2,1)S(1)}, bf16[256,1024]{1,0:T(8,128)(2,1)S(1)}, u32[]{:S(2)}, u32[]{:S(2)}) collective-permute-start(bf16[256,1024]{1,0:T(8,128)(2,1)S(1)} %pad_maximum_fusion.1), channel_id=1, source_target_pairs={{64,0},{72,8},{80,16},{88,24},{96,32},{104,40},{112,48},{120,56},{... | collective-permute-start | bytes 1572872 | tf_op jit(solution)/shard_map/ppermute | solution.py:60
  179.6 9.5 %collective-permute-done.26 = bf16[256,1024]{1,0:T(8,128)(2,1)S(1)} collective-permute-done((bf16[256,1024]{1,0:T(8,128)(2,1)S(1)}, bf16[256,1024]{1,0:T(8,128)(2,1)S(1)}, u32[]{:S(2)}, u32[]{:S(2)}) %collective-permute-start.26) | collective-permute-done | bytes 524320 | tf_op jit(solution)/shard_map/ppermute | solution.py:60
  189.1 3.3 %collective-permute-done.24 = bf16[256,1024]{1,0:T(8,128)(2,1)S(1)} collective-permute-done((bf16[256,1024]{1,0:T(8,128)(2,1)S(1)}, bf16[256,1024]{1,0:T(8,128)(2,1)S(1)}, u32[]{:S(2)}, u32[]{:S(2)}) %collective-permute-start.24) | collective-permute-done | bytes 524320 | tf_op jit(solution)/shard_map/ppermute | solution.py:60
  193.4 4.0 %all-to-all-done.2.terms_ref = bf16[8,256,256]{2,1,0:T(8,128)(2,1)S(1)} async-done(((bf16[8,256,256]{2,1,0:T(8,128)(2,1)}), bf16[8,256,256]{2,1,0:T(8,128)(2,1)S(1)}, u32[]{:S(2)}, u32[]{:S(2)}) %all-to-all-start.2) | async-done | bytes 1048608 | tf_op jit(solution)/shard_map/all_to_all | solution.py:417
  (89 shorter events, 44.2 us)
Async XLA Ops:
  7.2 60.9 %all-gather.3.cloned.1.call-start = ((), (), s32[]{:S(2)}) async-start(), calls=%async_computation.3 | async-start | bytes 2621440 | tf_op jit(solution)/shard_map/all_gather | solution.py:375
  8.8 13.9 %collective-permute-start.4 = (bf16[2,128,256]{2,1,0:T(8,128)(2,1)S(1)}, bf16[2,128,256]{2,1,0:T(8,128)(2,1)S(1)}, u32[]{:S(2)}, u32[]{:S(2)}) collective-permute-start(bf16[2,128,256]{2,1,0:T(8,128)(2,1)S(1)} %bitcast.8), channel_id=1, source_target_pairs={{0,8},{8,16},{16,24},{24,32},{32,40},{40,48},{48,56},{56,0},{64,72... | collective-permute-start | bytes 393224 | tf_op jit(solution)/shard_map/ppermute | solution.py:60
  11.3 11.4 %collective-permute-start.5 = (bf16[2,128,256]{2,1,0:T(8,128)(2,1)S(1)}, bf16[2,128,256]{2,1,0:T(8,128)(2,1)S(1)}, u32[]{:S(2)}, u32[]{:S(2)}) collective-permute-start(bf16[2,128,256]{2,1,0:T(8,128)(2,1)S(1)} %bitcast.9), channel_id=1, source_target_pairs={{8,0},{16,8},{24,16},{32,24},{40,32},{48,40},{56,48},{0,56},{72,64... | collective-permute-start | bytes 393224 | tf_op jit(solution)/shard_map/ppermute | solution.py:60
  22.7 5.0 %collective-permute-start.6 = (bf16[2,128,256]{2,1,0:T(8,128)(2,1)S(1)}, bf16[2,128,256]{2,1,0:T(8,128)(2,1)S(1)}, u32[]{:S(2)}, u32[]{:S(2)}) collective-permute-start(bf16[2,128,256]{2,1,0:T(8,128)(2,1)S(1)} %collective-permute-done.4.refs_5_), channel_id=1, source_target_pairs={{0,8},{8,16},{16,24},{24,32},{32,40},{40,48},{48,56},{56,0},{64,72... | collective-permute-start | bytes 393224 | tf_op jit(solution)/shard_map/ppermute | solution.py:60
  22.7 5.0 %collective-permute-start.7 = (bf16[2,128,256]{2,1,0:T(8,128)(2,1)S(1)}, bf16[2,128,256]{2,1,0:T(8,128)(2,1)S(1)}, u32[]{:S(2)}, u32[]{:S(2)}) collective-permute-start(bf16[2,128,256]{2,1,0:T(8,128)(2,1)S(1)} %collective-permute-done.5.refs_6_), channel_id=1, source_target_pairs={{8,0},{16,8},{24,16},{32,24},{40,32},{48,40},{56,48},{0,56},{72,64... | collective-permute-start | bytes 393224 | tf_op jit(solution)/shard_map/ppermute | solution.py:60
  27.7 5.4 %collective-permute-start.8 = (bf16[2,128,256]{2,1,0:T(8,128)(2,1)S(1)}, bf16[2,128,256]{2,1,0:T(8,128)(2,1)S(1)}, u32[]{:S(2)}, u32[]{:S(2)}) collective-permute-start(bf16[2,128,256]{2,1,0:T(8,128)(2,1)S(1)} %collective-permute-done.6.refs_7_), channel_id=1, source_target_pairs={{0,8},{8,16},{16,24},{24,32},{32,40},{40,48},{48,56},{56,0},{64,72... | collective-permute-start | bytes 393224 | tf_op jit(solution)/shard_map/ppermute | solution.py:60
  27.7 5.4 %collective-permute-start.9 = (bf16[2,128,256]{2,1,0:T(8,128)(2,1)S(1)}, bf16[2,128,256]{2,1,0:T(8,128)(2,1)S(1)}, u32[]{:S(2)}, u32[]{:S(2)}) collective-permute-start(bf16[2,128,256]{2,1,0:T(8,128)(2,1)S(1)} %collective-permute-done.7.refs_8_), channel_id=1, source_target_pairs={{8,0},{16,8},{24,16},{32,24},{40,32},{48,40},{56,48},{0,56},{72,64... | collective-permute-start | bytes 393224 | tf_op jit(solution)/shard_map/ppermute | solution.py:60
  40.3 27.8 %all-to-all-start = ((bf16[32,128,256]{2,1,0:T(8,128)(2,1)}), bf16[32,128,256]{2,1,0:T(8,128)(2,1)S(1)}, u32[]{:S(2)}, u32[]{:S(2)}) async-start(bf16[32,128,256]{2,1,0:T(8,128)(2,1)} %pick_far.1), calls=%async_computation | async-start | bytes 4194304 | tf_op jit(solution)/shard_map/all_to_all | solution.py:397
  44.0 55.6 %all-gather.5.cloned.1.call-start = ((), (), s32[]{:S(2)}) async-start(), calls=%async_computation.4 | async-start | bytes 1179648 | tf_op jit(solution)/shard_map/all_gather | solution.py:388
  44.8 23.3 %collective-permute-start = (bf16[2,128,256]{2,1,0:T(8,128)(2,1)S(1)}, bf16[2,128,256]{2,1,0:T(8,128)(2,1)S(1)}, u32[]{:S(2)}, u32[]{:S(2)}) collective-permute-start(bf16[2,128,256]{2,1,0:T(8,128)(2,1)S(1)} %bitcast.11), channel_id=1, source_target_pairs={{0,8},{8,16},{16,24},{24,32},{32,40},{40,48},{48,56},{56,64},{64,7... | collective-permute-start | bytes 393224 | tf_op jit(solution)/shard_map/ppermute | solution.py:55
  78.7 9.6 %collective-permute-start.12 = (bf16[8,128,256]{2,1,0:T(8,128)(2,1)S(1)}, bf16[8,128,256]{2,1,0:T(8,128)(2,1)S(1)}, u32[]{:S(2)}, u32[]{:S(2)}) collective-permute-start(bf16[8,128,256]{2,1,0:T(8,128)(2,1)S(1)} %get-tuple-element.31.refs_4_), channel_id=1, source_target_pairs={{0,64},{8,72},{16,80},{24,88},{32,96},{40,104},{48,112},{56,120},{... | collective-permute-start | bytes 1572872 | tf_op jit(solution)/shard_map/ppermute | solution.py:60
  78.7 9.7 %collective-permute-start.13 = (bf16[8,128,256]{2,1,0:T(8,128)(2,1)S(1)}, bf16[8,128,256]{2,1,0:T(8,128)(2,1)S(1)}, u32[]{:S(2)}, u32[]{:S(2)}) collective-permute-start(bf16[8,128,256]{2,1,0:T(8,128)(2,1)S(1)} %get-tuple-element.31.refs_4_), channel_id=1, source_target_pairs={{64,0},{72,8},{80,16},{88,24},{96,32},{104,40},{112,48},{120,56},{... | collective-permute-start | bytes 1572872 | tf_op jit(solution)/shard_map/ppermute | solution.py:60
  88.3 8.9 %collective-permute-start.14 = (bf16[4,128,256]{2,1,0:T(8,128)(2,1)S(1)}, bf16[4,128,256]{2,1,0:T(8,128)(2,1)S(1)}, u32[]{:S(2)}, u32[]{:S(2)}) collective-permute-start(bf16[4,128,256]{2,1,0:T(8,128)(2,1)S(1)} %slice.55), channel_id=1, source_target_pairs={{0,64},{8,72},{16,80},{24,88},{32,96},{40,104},{48,112},{56,120},{... | collective-permute-start | bytes 786440 | tf_op jit(solution)/shard_map/ppermute | solution.py:60
  88.4 8.8 %collective-permute-start.15 = (bf16[4,128,256]{2,1,0:T(8,128)(2,1)S(1)}, bf16[4,128,256]{2,1,0:T(8,128)(2,1)S(1)}, u32[]{:S(2)}, u32[]{:S(2)}) collective-permute-start(bf16[4,128,256]{2,1,0:T(8,128)(2,1)S(1)} %slice.56), channel_id=1, source_target_pairs={{64,0},{72,8},{80,16},{88,24},{96,32},{104,40},{112,48},{120,56},{... | collective-permute-start | bytes 786440 | tf_op jit(solution)/shard_map/ppermute | solution.py:60
  99.6 25.1 %all-to-all-start.1 = ((bf16[8,256,256]{2,1,0:T(8,128)(2,1)}), bf16[8,256,256]{2,1,0:T(8,128)(2,1)S(1)}, u32[]{:S(2)}, u32[]{:S(2)}) async-start(bf16[8,256,256]{2,1,0:T(8,128)(2,1)} %bitcast.5), calls=%async_computation.1 | async-start | bytes 2097152 | tf_op jit(solution)/shard_map/all_to_all | solution.py:408
  103.2 19.5 %collective-permute-start.16 = (bf16[256,256]{1,0:T(8,128)(2,1)S(1)}, bf16[256,256]{1,0:T(8,128)(2,1)S(1)}, u32[]{:S(2)}, u32[]{:S(2)}) collective-permute-start(bf16[256,256]{1,0:T(8,128)(2,1)S(1)} %slice.63), channel_id=1, source_target_pairs={{8,0},{16,8},{24,16},{32,24},{40,32},{48,40},{56,48},{64,56},{72,6... | collective-permute-start | bytes 393224 | tf_op jit(solution)/shard_map/ppermute | solution.py:55
  125.7 14.9 %collective-permute-start.18 = (bf16[256,256]{1,0:T(8,128)(2,1)S(1)}, bf16[256,256]{1,0:T(8,128)(2,1)S(1)}, u32[]{:S(2)}, u32[]{:S(2)}) collective-permute-start(bf16[256,256]{1,0:T(8,128)(2,1)S(1)} %collective-permute-done.17.own_ref), channel_id=1, source_target_pairs={{0,2},{1,3},{2,4},{3,5},{4,6},{5,7},{6,0},{7,1},{8,10},{9,11},{10,... | collective-permute-start | bytes 393224 | tf_op jit(solution)/shard_map/ppermute | solution.py:60
  133.2 7.4 %collective-permute-start.19 = (bf16[256,256]{1,0:T(8,128)(2,1)S(1)}, bf16[256,256]{1,0:T(8,128)(2,1)S(1)}, u32[]{:S(2)}, u32[]{:S(2)}) collective-permute-start(bf16[256,256]{1,0:T(8,128)(2,1)S(1)} %collective-permute-done.17.own_ref), channel_id=1, source_target_pairs={{2,0},{3,1},{4,2},{5,3},{6,4},{7,5},{0,6},{1,7},{10,8},{11,9},{12,... | collective-permute-start | bytes 393224 | tf_op jit(solution)/shard_map/ppermute | solution.py:60
  144.9 13.1 %collective-permute-start.22 = (bf16[1024,256]{1,0:T(8,128)(2,1)S(1)}, bf16[1024,256]{1,0:T(8,128)(2,1)S(1)}, u32[]{:S(2)}, u32[]{:S(2)}) collective-permute-start(bf16[1024,256]{1,0:T(8,128)(2,1)S(1)} %constant_dynamic-update-slice_fusion), channel_id=1, source_target_pairs={{0,1},{1,0},{2,3},{3,2},{4,5},{5,4},{6,7},{7,6},{8,9},{9,8},{10,11... | collective-permute-start | bytes 1572872 | tf_op jit(solution)/shard_map/ppermute | solution.py:413
  163.7 33.7 %all-to-all-start.2 = ((bf16[8,256,256]{2,1,0:T(8,128)(2,1)}), bf16[8,256,256]{2,1,0:T(8,128)(2,1)S(1)}, u32[]{:S(2)}, u32[]{:S(2)}) async-start(bf16[8,256,256]{2,1,0:T(8,128)(2,1)} %weight_terms.1), calls=%async_computation.2 | async-start | bytes 2097152 | tf_op jit(solution)/shard_map/all_to_all | solution.py:417
  169.3 7.3 %collective-permute-start.25 = (bf16[128,1024]{1,0:T(8,128)(2,1)S(1)}, bf16[128,1024]{1,0:T(8,128)(2,1)S(1)}, u32[]{:S(2)}, u32[]{:S(2)}) collective-permute-start(bf16[128,1024]{1,0:T(8,128)(2,1)S(1)} %get-tuple-element.45), channel_id=1, source_target_pairs={{64,0},{72,8},{80,16},{88,24},{96,32},{104,40},{112,48},{120,56},{... | collective-permute-start | bytes 786440 | tf_op jit(solution)/shard_map/ppermute | solution.py:60
  170.8 8.6 %collective-permute-start.23 = (bf16[128,1024]{1,0:T(8,128)(2,1)S(1)}, bf16[128,1024]{1,0:T(8,128)(2,1)S(1)}, u32[]{:S(2)}, u32[]{:S(2)}) collective-permute-start(bf16[128,1024]{1,0:T(8,128)(2,1)S(1)} %get-tuple-element.44), channel_id=1, source_target_pairs={{0,64},{8,72},{16,80},{24,88},{32,96},{40,104},{48,112},{56,120},{... | collective-permute-start | bytes 786440 | tf_op jit(solution)/shard_map/ppermute | solution.py:60
  176.6 12.4 %collective-permute-start.26 = (bf16[256,1024]{1,0:T(8,128)(2,1)S(1)}, bf16[256,1024]{1,0:T(8,128)(2,1)S(1)}, u32[]{:S(2)}, u32[]{:S(2)}) collective-permute-start(bf16[256,1024]{1,0:T(8,128)(2,1)S(1)} %pad_maximum_fusion.1), channel_id=1, source_target_pairs={{64,0},{72,8},{80,16},{88,24},{96,32},{104,40},{112,48},{120,56},{... | collective-permute-start | bytes 1572872 | tf_op jit(solution)/shard_map/ppermute | solution.py:60
  179.5 12.9 %collective-permute-start.24 = (bf16[256,1024]{1,0:T(8,128)(2,1)S(1)}, bf16[256,1024]{1,0:T(8,128)(2,1)S(1)}, u32[]{:S(2)}, u32[]{:S(2)}) collective-permute-start(bf16[256,1024]{1,0:T(8,128)(2,1)S(1)} %pad_maximum_fusion), channel_id=1, source_target_pairs={{0,64},{8,72},{16,80},{24,88},{32,96},{40,104},{48,112},{56,120},{... | collective-permute-start | bytes 1572872 | tf_op jit(solution)/shard_map/ppermute | solution.py:60
  (16 other events, 98.8 us)
Sparse Core Ops, SparseCore 0:
  9.8 37.1 all-gather.2
  49.4 38.6 all-gather.4

commit v5 on v4

--- a/solution.py
+++ b/solution.py
@@ -24,14 +24,16 @@
 X_UP = [(x * NZ + z, (x + 1) % NX * NZ + z) for x in range(NX) for z in range(NZ)]
 X_ACROSS = [(x * NZ + z, (x + 2) % NX * NZ + z) for x in range(NX) for z in range(NZ)]
 NY = 4
-Y_UP = [(2 * y + core, 2 * ((y + 1) % NY) + core) for y in range(NY) for core in range(2)]
 CORES = [(own, own ^ 1) for own in range(2 * NY)]
 SWAP_XY = [
-    (((x * NZ + z) * NY + y) * 2 + core, ((y * NZ + z) * NY + x) * 2 + core)
-    for x in range(NX)
-    for z in range(NZ)
-    for y in range(NY)
-    for core in range(2)
+    [
+        (((x * NZ + z) * NY + y) * 2 + core, ((y * NZ + z) * NY + (x + step) % NY) * 2 + core)
+        for x in range(NX)
+        for z in range(NZ)
+        for y in range(NY)
+        for core in range(2)
+    ]
+    for step in range(NY)
 ]
 PART = DH // 4
 SCALE = 1.0 / math.sqrt(DH)
@@ -72,41 +74,25 @@
     return pieces
 
 
-def place_pieces(out_ref, at, own_ref, pieces, count, size):
-    half = size // 2
-    out_ref[pl.ds(at * size, size)] = own_ref[...]
-    for distance in range(1, count // 2 + 1):
-        below = lax.rem(at + (count - distance), count) * size
-        above = lax.rem(at + distance, count) * size
-        if distance == count // 2:
-            out_ref[pl.ds(below, half)] = pieces[2 * distance - 2][...]
-            out_ref[pl.ds(below + half, half)] = pieces[2 * distance - 1][...]
-        else:
-            out_ref[pl.ds(below, size)] = pieces[2 * distance - 2][...]
-            out_ref[pl.ds(above, size)] = pieces[2 * distance - 1][...]
-
-
 def pick_kernel(at_ref, *refs):
-    lists, own_ref, pieces = refs[:NX], refs[NX], refs[NX + 1 : -2]
-    out_ref, plane_ref = refs[-2:]
-    x_at, z_at = lax.div(at_ref[0], NZ), lax.rem(at_ref[0], NZ)
-    place_pieces(plane_ref, z_at, own_ref, pieces, NZ, NB)
+    *lists, plane_ref, out_ref = refs
+    x_at = lax.div(at_ref[0], NZ)
     for steps, list_ref in enumerate(lists):
         first = lax.rem(x_at + steps, NX) * SLOTS
         for j in range(SLOTS):
-            out_ref[first + j] = plane_ref[lax.rem(list_ref[j], PLANE)]
-
-
-def pick(at, lists, own, pieces):
+            listed = list_ref[j // FARS, j % FARS]
+            out_ref[first + j] = plane_ref[lax.rem(listed, PLANE)]
+
+
+def pick(at, lists, plane):
     return pl.pallas_call(
         pick_kernel,
         out_shape=jax.ShapeDtypeStruct((NX * SLOTS, BLK, 2 * DH), BF16),
-        in_specs=[SMEM] * (1 + NX) + [VMEM] * (1 + len(pieces)),
+        in_specs=[SMEM] * (1 + NX) + [VMEM],
         out_specs=VMEM,
-        scratch_shapes=[pltpu.VMEM((PLANE, BLK, 2 * DH), BF16)],
-        compiler_params=params(16),
+        compiler_params=params(8),
         name="pick_far",
-    )(at, *lists, own, *pieces)
+    )(at, *lists, plane)
 
 
 def attend_kernel(
@@ -127,7 +113,7 @@
             v_ref[w * BLK : (w + 1) * BLK, :] = both[:, DH:]
         for j in range(FARS):
             slot = b * FARS + j
-            owner = lax.div(far_ref[slot], PLANE)
+            owner = lax.div(far_ref[b, j], PLANE)
             both = far_kv_ref[owner * SLOTS + slot]
             k_ref[(WIN + j) * BLK : (WIN + j + 1) * BLK, :] = both[:, :DH]
             v_ref[(WIN + j) * BLK : (WIN + j + 1) * BLK, :] = both[:, DH:]
@@ -211,10 +197,10 @@
 
     half = SLOTS // 2
     for j in range(SLOTS):
-        add(lists[0][j], mine, j)
-        add(lists[1][j], above, j)
-        add(lists[2][j], across_low if j < half else across_high, j % half)
-        add(lists[3][j], below, j)
+        add(lists[0][j // FARS, j % FARS], mine, j)
+        add(lists[1][j // FARS, j % FARS], above, j)
+        add(lists[2][j // FARS, j % FARS], across_low if j < half else across_high, j % half)
+        add(lists[3][j // FARS, j % FARS], below, j)
     out_ref[...] = acc_ref[...].astype(BF16)
 
 
@@ -255,31 +241,24 @@
     )(terms, back, window)
 
 
-def heads_kernel(at_ref, own_ref, *refs):
-    *pieces, other_ref, out_ref = refs
-    at, core = lax.div(at_ref[0], 2), lax.rem(at_ref[0], 2)
-    rows = NB * BLK
-    half = rows // 2
-    below, above = lax.rem(at + NY - 1, NY), lax.rem(at + 1, NY)
-    across = lax.rem(at + 2, NY)
-    starts = (0, rows, 2 * rows, 3 * rows, 3 * rows + half)
-    for k, (y, low, high) in enumerate(
-        ((at, 0, rows), (below, 0, rows), (above, 0, rows), (across, 0, half), (across, half, rows))
-    ):
-        mine = own_ref if k == 0 else pieces[k - 1]
-        out_ref[2 * y + core, low:high, :] = mine[...]
-        out_ref[2 * y + 1 - core, low:high, :] = other_ref[starts[k] : starts[k] + high - low, :]
-
-
-def place_heads(at, own, pieces, other):
+def heads_kernel(at_ref, *refs):
+    pieces, out_ref = refs[:-1], refs[-1]
+    y_at, core = lax.div(at_ref[0], 2), lax.rem(at_ref[0], 2)
+    for step in range(NY):
+        x = lax.rem(y_at + (NY - step), NY)
+        out_ref[2 * x + core] = pieces[step][...]
+        out_ref[2 * x + 1 - core] = pieces[NY + step][...]
+
+
+def place_heads(at, pieces):
     return pl.pallas_call(
         heads_kernel,
-        out_shape=jax.ShapeDtypeStruct((2 * NY, *own.shape), BF16),
-        in_specs=[SMEM] + [VMEM] * (2 + len(pieces)),
+        out_shape=jax.ShapeDtypeStruct((2 * NY, *pieces[0].shape), BF16),
+        in_specs=[SMEM] + [VMEM] * len(pieces),
         out_specs=VMEM,
         compiler_params=params(8),
         name="place_heads",
-    )(at, own, *pieces, other)
+    )(at, *pieces)
 
 
 def weights_kernel(grad_ref, inputs_ref, out_ref):
@@ -374,31 +353,21 @@
 
     inputs_x = lax.all_gather(inputs, "seq", axis=0, axis_index_groups=X_GROUPS, tiled=True)
 
-    listed = far_blocks.reshape(SLOTS)
-    list_below, list_above = both_ways(listed, listed, "seq", X_UP)
-    list_across = lax.ppermute(listed, "seq", X_ACROSS)
-    from_below, from_above = both_ways(own_kv, own_kv, "seq", Z_UP)
-    list_below, list_above, list_across, from_below, from_above, key_weight, value_weight = (
-        lax.optimization_barrier(
-            (list_below, list_above, list_across, from_below, from_above, key_weight, value_weight)
-        )
-    )
-    lists = (listed, list_above, list_across, list_below)
+    own_copies = jnp.broadcast_to(own_kv[None], (NZ, NB, BLK, 2 * DH)).reshape(-1, BLK, 2 * DH)
+    plane = lax.all_to_all(own_copies, "seq", 0, 0, axis_index_groups=Z_GROUPS, tiled=True)
+    list_below, list_above = both_ways(far_blocks, far_blocks, "seq", X_UP)
+    list_across = lax.ppermute(far_blocks, "seq", X_ACROSS)
+    prev_kv = shifted(own_kv, "seq", 1)
+    lists = (far_blocks, list_above, list_across, list_below)
+    plane, key_weight, value_weight = lax.optimization_barrier((plane, key_weight, value_weight))
     weights = jnp.concatenate([key_weight.T, value_weight.T])
     weights = lax.all_gather(weights, "seq", axis=0, axis_index_groups=Z_GROUPS, tiled=True)
-    plane = [from_below, from_above]
-    for distance in range(2, NZ // 2 + 1):
-        if distance == NZ // 2:
-            from_below, from_above = from_below[: NB // 2], from_above[NB // 2 :]
-        from_below, from_above = both_ways(from_below, from_above, "seq", Z_UP)
-        plane += [from_below, from_above]
-    prev_kv = shifted(own_kv, "seq", 1)
-    chosen = pick(at, lists, own_kv, plane)
+    chosen = pick(at, lists, plane)
     far_kv = lax.all_to_all(chosen, "seq", 0, 0, axis_index_groups=X_GROUPS, tiled=True)
 
     far_kv, inputs_x = lax.optimization_barrier((far_kv, inputs_x))
     query_grad, window, far_grad = attend(
-        at, listed, far_count, queries, out_grad, prev_kv, own_kv, far_kv
+        at, far_blocks, far_count, queries, out_grad, prev_kv, own_kv, far_kv
     )
     far_all = ring_gather(far_grad, "seq", X_UP, NX)
     back = shifted(window[:tokens].astype(BF16), "seq", -1)
@@ -408,12 +377,11 @@
     terms = lax.all_to_all(dense, "seq", 0, 0, axis_index_groups=Z_GROUPS, tiled=True)
     kv_grad = finish(terms, back, window)
 
-    moved = lax.ppermute(kv_grad, ("seq", "own"), SWAP_XY)
-    same_core = ring_gather(moved, "own", Y_UP, NY)
-    other_core = lax.ppermute(jnp.concatenate([moved, *same_core]), "own", CORES)
-    heads = place_heads(own_index, moved, same_core, other_core)
+    moved = [lax.ppermute(kv_grad, ("seq", "own"), pairs) for pairs in SWAP_XY]
+    heads = place_heads(own_index, moved + [lax.ppermute(piece, "own", CORES) for piece in moved])
 
     pieces = weight_terms(heads, inputs_x)
+    heads, pieces = lax.optimization_barrier((heads, pieces))
     pieces = lax.all_to_all(pieces, "seq", 0, 0, axis_index_groups=Z_GROUPS, tiled=True)
     mine, above, across, below = input_terms(at, heads, weights)
     half = tokens // 2

time: 206 us -> 221 us (1.073); the launches traced: 205 us -> 217 us
  waiting for transfers between devices: 93.1 us -> 121 us
  starting transfers between devices: 71 us -> 56.5 us
    all_to_all x0 -> x1, waiting for transfers between devices: none -> 24.8 us  [local(): lax.all_to_all(own_copies, 'seq', 0, 0, axis_index_groups=Z_GROUPS, tiled...]
    ppermute x11 -> x5, starting transfers between devices: 30.9 us -> 9.53 us  [both_ways(): lax.ppermute(downward, axis, back)]
    ppermute x11 -> x5, waiting for transfers between devices: 15.1 us -> 1.22 us  [both_ways(): lax.ppermute(downward, axis, back)]
    all_to_all x0 -> x1, starting transfers between devices: none -> 9.01 us  [local(): lax.all_to_all(own_copies, 'seq', 0, 0, axis_index_groups=Z_GROUPS, tiled...]
    ppermute x11 -> x5, starting transfers between devices: 11.6 us -> 4.66 us  [both_ways(): lax.ppermute(upward, axis, pairs)]
    ppermute x3 -> x9, waiting for transfers between devices: 3.89 us -> 9.39 us  [the longest x4 8.37 us: local(): moved = [lax.ppermute(kv_grad, ('seq', 'own'), pairs) for pairs in SWAP_XY]]
    ppermute x3 -> x9, starting transfers between devices: 13.8 us -> 19.3 us  [the longest x4 10.7 us: local(): moved = [lax.ppermute(kv_grad, ('seq', 'own'), pairs) for pairs in SWAP_XY]]
    all_to_all x1, waiting for transfers between devices: 21.8 us -> 25.9 us  [local(): lax.all_to_all(chosen, 'seq', 0, 0, axis_index_groups=X_GROUPS, tiled=True)]
  transfers between devices with their start and end apart: 32 -> 27, of which waited for: 16 -> 16; matrix products, arithmetic and copies ran while one was open for 2% -> 1% of each run, Pallas kernels for 7% -> 7%
where the time goes in v5:
time: 221 us; the launch traced here: 217 us
  waiting for transfers between devices  121 us (55%)
  starting transfers between devices  56.5 us (26%)
  Pallas kernels  18.8 us (9%)
  between operations  14.2 us (6%)
  local copies, waits for them, and re-layouts  3.84 us (2%)
  other arithmetic  2.8 us (1%)
    ppermute x5, waiting for transfers between devices, both_ways(): lax.ppermute(upward, axis, pairs)  31.1 us
    all_to_all x1, waiting for transfers between devices, local(): lax.all_to_all(chosen, 'seq', 0, 0, axis_index_groups=X_GROUPS, tiled=True)  25.9 us
    all_to_all x1, waiting for transfers between devices, local(): lax.all_to_all(own_copies, 'seq', 0, 0, axis_index_groups=Z_GROUPS, tiled...  24.8 us
    ppermute x2, waiting for transfers between devices, shifted(): lax.ppermute(value, axis, [(source, source + steps) for source in range(l...  22 us
    ppermute x4, starting transfers between devices, local(): moved = [lax.ppermute(kv_grad, ('seq', 'own'), pairs) for pairs in SWAP_XY]  10.7 us
    pallas_call x1, Pallas kernels, attend(): pl.pallas_call(attend_kernel, out_shape=(jax.ShapeDtypeStruct((NB * BLK,...  9.57 us
    ppermute x5, starting transfers between devices, both_ways(): lax.ppermute(downward, axis, back)  9.53 us
    all_to_all x1, starting transfers between devices, local(): lax.all_to_all(own_copies, 'seq', 0, 0, axis_index_groups=Z_GROUPS, tiled...  9.01 us
  transfers between devices with their start and end apart: 27, of which 16 were waited for; matrix products, arithmetic and copies ran while one was open for 1% of the time, Pallas kernels for 7%

profile of v5, /device:TPU:1, one launch (start us, length us, event | category | flops | bytes accessed | tf_op | source)
XLA Modules:
  0.0 217.1 jit_solution(16372470094529204698)
XLA Ops:
  9.1 9.0 %all-to-all-start = ((bf16[16,128,256]{2,1,0:T(8,128)(2,1)}), bf16[16,128,256]{2,1,0:T(8,128)(2,1)S(1)}, u32[]{:S(2)}, u32[]{:S(2)}) async-start(bf16[16,128,256]{2,1,0:T(8,128)(2,1)} %bitcast.2), calls=%async_computation | async-start | bytes 2097152 | tf_op jit(solution)/shard_map/all_to_all | solution.py:357
  18.9 2.6 %collective-permute-start.1 = (s32[2,4]{1,0:T(2,128)S(1)}, s32[2,4]{1,0:T(2,128)S(1)}, u32[]{:S(2)}, u32[]{:S(2)}) collective-permute-start(s32[2,4]{1,0:T(2,128)S(1)} %copy-done.1), channel_id=1, source_target_pairs={{64,0},{72,8},{80,16},{88,24},{96,32},{104,40},{112,48},{120,56},{... | collective-permute-start | bytes 104 | tf_op jit(solution)/shard_map/ppermute | solution.py:62
  22.6 24.8 %all-to-all-done.refs_4_ = bf16[16,128,256]{2,1,0:T(8,128)(2,1)S(1)} async-done(((bf16[16,128,256]{2,1,0:T(8,128)(2,1)}), bf16[16,128,256]{2,1,0:T(8,128)(2,1)S(1)}, u32[]{:S(2)}, u32[]{:S(2)}) %all-to-all-start) | async-done | bytes 1048608 | tf_op jit(solution)/shard_map/all_to_all | solution.py:357
  49.4 4.2 %all-to-all-start.1 = ((bf16[32,128,256]{2,1,0:T(8,128)(2,1)}), bf16[32,128,256]{2,1,0:T(8,128)(2,1)S(1)}, u32[]{:S(2)}, u32[]{:S(2)}) async-start(bf16[32,128,256]{2,1,0:T(8,128)(2,1)} %pick_far.1), calls=%async_computation.1 | async-start | bytes 4194304 | tf_op jit(solution)/shard_map/all_to_all | solution.py:366
  56.2 25.9 %all-to-all-done.1.far_kv_ref = bf16[32,128,256]{2,1,0:T(8,128)(2,1)S(1)} async-done(((bf16[32,128,256]{2,1,0:T(8,128)(2,1)}), bf16[32,128,256]{2,1,0:T(8,128)(2,1)S(1)}, u32[]{:S(2)}, u32[]{:S(2)}) %all-to-all-start.1) | async-done | bytes 2097184 | tf_op jit(solution)/shard_map/all_to_all | solution.py:366
  83.1 9.6 %attend.1 = (bf16[256,1024]{1,0:T(8,128)(2,1)}, f32[512,256]{1,0:T(8,128)S(1)}, bf16[8,128,256]{2,1,0:T(8,128)(2,1)S(1)}) custom-call(s32[1]{0:T(128)} %bitcast.at_ref, s32[2,4]{1,0:T(2,128)S(1)} %copy-done.1, s32[2]{0:T(128)S(1)} %copy-done.5, bf16[256,1024]{1,0:T(8,128)(2,1)S(1)} %copy-done.3, bf16[256,1024]{1,0:T(8,128)(2,1)S(1)} %copy-done.4, ...), custom_call_target="tpu_custom_call" | custom-call | flops 9600000000 | bytes 6291456 | tf_op jit(solution)/shard_map/attend/pallas_call | solution.py:164
  92.7 2.7 %collective-permute-start.5 = (bf16[8,128,256]{2,1,0:T(8,128)(2,1)S(1)}, bf16[8,128,256]{2,1,0:T(8,128)(2,1)S(1)}, u32[]{:S(2)}, u32[]{:S(2)}) collective-permute-start(bf16[8,128,256]{2,1,0:T(8,128)(2,1)S(1)} %get-tuple-element.25.refs_4_), channel_id=1, source_target_pairs={{64,0},{72,8},{80,16},{88,24},{96,32},{104,40},{112,48},{120,56},{... | collective-permute-start | bytes 1572872 | tf_op jit(solution)/shard_map/ppermute | solution.py:62
  95.3 10.3 %collective-permute-done.4.refs_5_ = bf16[8,128,256]{2,1,0:T(8,128)(2,1)S(1)} collective-permute-done((bf16[8,128,256]{2,1,0:T(8,128)(2,1)S(1)}, bf16[8,128,256]{2,1,0:T(8,128)(2,1)S(1)}, u32[]{:S(2)}, u32[]{:S(2)}) %collective-permute-start.4) | collective-permute-done | bytes 524320 | tf_op jit(solution)/shard_map/ppermute | solution.py:62
  105.8 2.7 %collective-permute-start.7 = (bf16[4,128,256]{2,1,0:T(8,128)(2,1)S(1)}, bf16[4,128,256]{2,1,0:T(8,128)(2,1)S(1)}, u32[]{:S(2)}, u32[]{:S(2)}) collective-permute-start(bf16[4,128,256]{2,1,0:T(8,128)(2,1)S(1)} %slice.38), channel_id=1, source_target_pairs={{64,0},{72,8},{80,16},{88,24},{96,32},{104,40},{112,48},{120,56},{... | collective-permute-start | bytes 786440 | tf_op jit(solution)/shard_map/ppermute | solution.py:62
  108.5 3.7 %collective-permute-done.6.refs_7_ = bf16[4,128,256]{2,1,0:T(8,128)(2,1)S(1)} collective-permute-done((bf16[4,128,256]{2,1,0:T(8,128)(2,1)S(1)}, bf16[4,128,256]{2,1,0:T(8,128)(2,1)S(1)}, u32[]{:S(2)}, u32[]{:S(2)}) %collective-permute-start.6) | collective-permute-done | bytes 262176 | tf_op jit(solution)/shard_map/ppermute | solution.py:62
  114.6 3.6 %all-to-all-start.2 = ((bf16[8,256,256]{2,1,0:T(8,128)(2,1)}), bf16[8,256,256]{2,1,0:T(8,128)(2,1)S(1)}, u32[]{:S(2)}, u32[]{:S(2)}) async-start(bf16[8,256,256]{2,1,0:T(8,128)(2,1)} %bitcast.6), calls=%async_computation.2 | async-start | bytes 2097152 | tf_op jit(solution)/shard_map/all_to_all | solution.py:377
  119.5 22.0 %collective-permute-done.8.back_ref = bf16[256,256]{1,0:T(8,128)(2,1)S(1)} collective-permute-done((bf16[256,256]{1,0:T(8,128)(2,1)S(1)}, bf16[256,256]{1,0:T(8,128)(2,1)S(1)}, u32[]{:S(2)}, u32[]{:S(2)}) %collective-permute-start.8) | collective-permute-done | bytes 131104 | tf_op jit(solution)/shard_map/ppermute | solution.py:57
  141.5 2.6 %all-to-all-done.2.terms_ref = bf16[8,256,256]{2,1,0:T(8,128)(2,1)S(1)} async-done(((bf16[8,256,256]{2,1,0:T(8,128)(2,1)}), bf16[8,256,256]{2,1,0:T(8,128)(2,1)S(1)}, u32[]{:S(2)}, u32[]{:S(2)}) %all-to-all-start.2) | async-done | bytes 1048608 | tf_op jit(solution)/shard_map/all_to_all | solution.py:377
  145.0 2.8 %collective-permute-start.10 = (bf16[256,256]{1,0:T(8,128)(2,1)S(1)}, bf16[256,256]{1,0:T(8,128)(2,1)S(1)}, u32[]{:S(2)}, u32[]{:S(2)}) collective-permute-start(bf16[256,256]{1,0:T(8,128)(2,1)S(1)} %finish_kv.1), channel_id=1, source_target_pairs={{0,2},{1,3},{2,66},{3,67},{4,130},{5,131},{6,194},{7,195},{8,10},{... | collective-permute-start | bytes 393224 | tf_op jit(solution)/shard_map/ppermute | solution.py:380
  147.8 4.0 %collective-permute-start.11 = (bf16[256,256]{1,0:T(8,128)(2,1)S(1)}, bf16[256,256]{1,0:T(8,128)(2,1)S(1)}, u32[]{:S(2)}, u32[]{:S(2)}) collective-permute-start(bf16[256,256]{1,0:T(8,128)(2,1)S(1)} %finish_kv.1), channel_id=1, source_target_pairs={{0,4},{1,5},{2,68},{3,69},{4,132},{5,133},{6,196},{7,197},{8,12},{... | collective-permute-start | bytes 393224 | tf_op jit(solution)/shard_map/ppermute | solution.py:380
  151.8 3.3 %collective-permute-start.12 = (bf16[256,256]{1,0:T(8,128)(2,1)S(1)}, bf16[256,256]{1,0:T(8,128)(2,1)S(1)}, u32[]{:S(2)}, u32[]{:S(2)}) collective-permute-start(bf16[256,256]{1,0:T(8,128)(2,1)S(1)} %finish_kv.1), channel_id=1, source_target_pairs={{0,6},{1,7},{2,70},{3,71},{4,134},{5,135},{6,198},{7,199},{8,14},{... | collective-permute-start | bytes 393224 | tf_op jit(solution)/shard_map/ppermute | solution.py:380
  155.1 4.9 %collective-permute-start.13 = (bf16[256,256]{1,0:T(8,128)(2,1)S(1)}, bf16[256,256]{1,0:T(8,128)(2,1)S(1)}, u32[]{:S(2)}, u32[]{:S(2)}) collective-permute-start(bf16[256,256]{1,0:T(8,128)(2,1)S(1)} %collective-permute-done.9.refs_0_), channel_id=1, source_target_pairs={{0,1},{1,0},{2,3},{3,2},{4,5},{5,4},{6,7},{7,6},{8,9},{9,8},{10,11... | collective-permute-start | bytes 393224 | tf_op jit(solution)/shard_map/ppermute | solution.py:381
  160.0 8.4 %collective-permute-done.10.refs_1_ = bf16[256,256]{1,0:T(8,128)(2,1)S(1)} collective-permute-done((bf16[256,256]{1,0:T(8,128)(2,1)S(1)}, bf16[256,256]{1,0:T(8,128)(2,1)S(1)}, u32[]{:S(2)}, u32[]{:S(2)}) %collective-permute-start.10) | collective-permute-done | bytes 131104 | tf_op jit(solution)/shard_map/ppermute | solution.py:380
  168.3 2.7 %collective-permute-start.14 = (bf16[256,256]{1,0:T(8,128)(2,1)S(1)}, bf16[256,256]{1,0:T(8,128)(2,1)S(1)}, u32[]{:S(2)}, u32[]{:S(2)}) collective-permute-start(bf16[256,256]{1,0:T(8,128)(2,1)S(1)} %collective-permute-done.10.refs_1_), channel_id=1, source_target_pairs={{0,1},{1,0},{2,3},{3,2},{4,5},{5,4},{6,7},{7,6},{8,9},{9,8},{10,11... | collective-permute-start | bytes 393224 | tf_op jit(solution)/shard_map/ppermute | solution.py:381
  176.5 3.7 %all-to-all-start.3 = ((bf16[8,256,256]{2,1,0:T(8,128)(2,1)}), bf16[8,256,256]{2,1,0:T(8,128)(2,1)S(1)}, u32[]{:S(2)}, u32[]{:S(2)}) async-start(bf16[8,256,256]{2,1,0:T(8,128)(2,1)} %weight_terms.1), calls=%async_computation.3 | async-start | bytes 2097152 | tf_op jit(solution)/shard_map/all_to_all | solution.py:385
  181.5 2.9 %collective-permute-start.17 = (bf16[128,1024]{1,0:T(8,128)(2,1)S(1)}, bf16[128,1024]{1,0:T(8,128)(2,1)S(1)}, u32[]{:S(2)}, u32[]{:S(2)}) collective-permute-start(bf16[128,1024]{1,0:T(8,128)(2,1)S(1)} %get-tuple-element.40), channel_id=1, source_target_pairs={{0,64},{8,72},{16,80},{24,88},{32,96},{40,104},{48,112},{56,120},{... | collective-permute-start | bytes 786440 | tf_op jit(solution)/shard_map/ppermute | solution.py:62
  184.9 6.2 %collective-permute-done.17 = bf16[128,1024]{1,0:T(8,128)(2,1)S(1)} collective-permute-done((bf16[128,1024]{1,0:T(8,128)(2,1)S(1)}, bf16[128,1024]{1,0:T(8,128)(2,1)S(1)}, u32[]{:S(2)}, u32[]{:S(2)}) %collective-permute-start.17) | collective-permute-done | bytes 262176 | tf_op jit(solution)/shard_map/ppermute | solution.py:62
  194.2 10.9 %collective-permute-done.18 = bf16[256,1024]{1,0:T(8,128)(2,1)S(1)} collective-permute-done((bf16[256,1024]{1,0:T(8,128)(2,1)S(1)}, bf16[256,1024]{1,0:T(8,128)(2,1)S(1)}, u32[]{:S(2)}, u32[]{:S(2)}) %collective-permute-start.18) | collective-permute-done | bytes 524320 | tf_op jit(solution)/shard_map/ppermute | solution.py:62
  206.8 2.7 %all-to-all-done.3.terms_ref = bf16[8,256,256]{2,1,0:T(8,128)(2,1)S(1)} async-done(((bf16[8,256,256]{2,1,0:T(8,128)(2,1)}), bf16[8,256,256]{2,1,0:T(8,128)(2,1)S(1)}, u32[]{:S(2)}, u32[]{:S(2)}) %all-to-all-start.3) | async-done | bytes 1048608 | tf_op jit(solution)/shard_map/all_to_all | solution.py:385
  (70 shorter events, 27.1 us)
Async XLA Ops:
  9.1 38.2 %all-to-all-start = ((bf16[16,128,256]{2,1,0:T(8,128)(2,1)}), bf16[16,128,256]{2,1,0:T(8,128)(2,1)S(1)}, u32[]{:S(2)}, u32[]{:S(2)}) async-start(bf16[16,128,256]{2,1,0:T(8,128)(2,1)} %bitcast.2), calls=%async_computation | async-start | bytes 2097152 | tf_op jit(solution)/shard_map/all_to_all | solution.py:357
  18.2 38.0 %all-gather.3.cloned.1.call-start = ((), (), s32[]{:S(2)}) async-start(), calls=%async_computation.4 | async-start | bytes 2621440 | tf_op jit(solution)/shard_map/all_gather | solution.py:354
  18.9 28.5 %collective-permute-start.1 = (s32[2,4]{1,0:T(2,128)S(1)}, s32[2,4]{1,0:T(2,128)S(1)}, u32[]{:S(2)}, u32[]{:S(2)}) collective-permute-start(s32[2,4]{1,0:T(2,128)S(1)} %copy-done.1), channel_id=1, source_target_pairs={{64,0},{72,8},{80,16},{88,24},{96,32},{104,40},{112,48},{120,56},{... | collective-permute-start | bytes 104 | tf_op jit(solution)/shard_map/ppermute | solution.py:62
  21.5 25.9 %collective-permute-start.2 = (s32[2,4]{1,0:T(2,128)S(1)}, s32[2,4]{1,0:T(2,128)S(1)}, u32[]{:S(2)}, u32[]{:S(2)}) collective-permute-start(s32[2,4]{1,0:T(2,128)S(1)} %copy-done.1), channel_id=1, source_target_pairs={{0,128},{8,136},{16,144},{24,152},{32,160},{40,168},{48,176},{56,1... | collective-permute-start | bytes 104 | tf_op jit(solution)/shard_map/ppermute | solution.py:359
  22.0 25.4 %collective-permute-start.3 = (s32[2,4]{1,0:T(2,128)S(1)}, s32[2,4]{1,0:T(2,128)S(1)}, u32[]{:S(2)}, u32[]{:S(2)}) collective-permute-start(s32[2,4]{1,0:T(2,128)S(1)} %copy-done.1), channel_id=1, source_target_pairs={{0,64},{8,72},{16,80},{24,88},{32,96},{40,104},{48,112},{56,120},{... | collective-permute-start | bytes 104 | tf_op jit(solution)/shard_map/ppermute | solution.py:62
  49.4 32.6 %all-to-all-start.1 = ((bf16[32,128,256]{2,1,0:T(8,128)(2,1)}), bf16[32,128,256]{2,1,0:T(8,128)(2,1)S(1)}, u32[]{:S(2)}, u32[]{:S(2)}) async-start(bf16[32,128,256]{2,1,0:T(8,128)(2,1)} %pick_far.1), calls=%async_computation.1 | async-start | bytes 4194304 | tf_op jit(solution)/shard_map/all_to_all | solution.py:366
  53.6 61.0 %all-gather.5.cloned.1.call-start = ((), (), s32[]{:S(2)}) async-start(), calls=%async_computation.5 | async-start | bytes 1179648 | tf_op jit(solution)/shard_map/all_gather | solution.py:364
  54.3 27.7 %collective-permute-start = (bf16[2,128,256]{2,1,0:T(8,128)(2,1)S(1)}, bf16[2,128,256]{2,1,0:T(8,128)(2,1)S(1)}, u32[]{:S(2)}, u32[]{:S(2)}) collective-permute-start(bf16[2,128,256]{2,1,0:T(8,128)(2,1)S(1)} %bitcast.10), channel_id=1, source_target_pairs={{0,8},{8,16},{16,24},{24,32},{32,40},{40,48},{48,56},{56,64},{64,7... | collective-permute-start | bytes 393224 | tf_op jit(solution)/shard_map/ppermute | solution.py:57
  92.7 13.0 %collective-permute-start.4 = (bf16[8,128,256]{2,1,0:T(8,128)(2,1)S(1)}, bf16[8,128,256]{2,1,0:T(8,128)(2,1)S(1)}, u32[]{:S(2)}, u32[]{:S(2)}) collective-permute-start(bf16[8,128,256]{2,1,0:T(8,128)(2,1)S(1)} %get-tuple-element.25.refs_4_), channel_id=1, source_target_pairs={{0,64},{8,72},{16,80},{24,88},{32,96},{40,104},{48,112},{56,120},{... | collective-permute-start | bytes 1572872 | tf_op jit(solution)/shard_map/ppermute | solution.py:62
  92.7 13.1 %collective-permute-start.5 = (bf16[8,128,256]{2,1,0:T(8,128)(2,1)S(1)}, bf16[8,128,256]{2,1,0:T(8,128)(2,1)S(1)}, u32[]{:S(2)}, u32[]{:S(2)}) collective-permute-start(bf16[8,128,256]{2,1,0:T(8,128)(2,1)S(1)} %get-tuple-element.25.refs_4_), channel_id=1, source_target_pairs={{64,0},{72,8},{80,16},{88,24},{96,32},{104,40},{112,48},{120,56},{... | collective-permute-start | bytes 1572872 | tf_op jit(solution)/shard_map/ppermute | solution.py:62
  105.7 6.5 %collective-permute-start.6 = (bf16[4,128,256]{2,1,0:T(8,128)(2,1)S(1)}, bf16[4,128,256]{2,1,0:T(8,128)(2,1)S(1)}, u32[]{:S(2)}, u32[]{:S(2)}) collective-permute-start(bf16[4,128,256]{2,1,0:T(8,128)(2,1)S(1)} %slice.37), channel_id=1, source_target_pairs={{0,64},{8,72},{16,80},{24,88},{32,96},{40,104},{48,112},{56,120},{... | collective-permute-start | bytes 786440 | tf_op jit(solution)/shard_map/ppermute | solution.py:62
  105.8 6.4 %collective-permute-start.7 = (bf16[4,128,256]{2,1,0:T(8,128)(2,1)S(1)}, bf16[4,128,256]{2,1,0:T(8,128)(2,1)S(1)}, u32[]{:S(2)}, u32[]{:S(2)}) collective-permute-start(bf16[4,128,256]{2,1,0:T(8,128)(2,1)S(1)} %slice.38), channel_id=1, source_target_pairs={{64,0},{72,8},{80,16},{88,24},{96,32},{104,40},{112,48},{120,56},{... | collective-permute-start | bytes 786440 | tf_op jit(solution)/shard_map/ppermute | solution.py:62
  114.6 29.5 %all-to-all-start.2 = ((bf16[8,256,256]{2,1,0:T(8,128)(2,1)}), bf16[8,256,256]{2,1,0:T(8,128)(2,1)S(1)}, u32[]{:S(2)}, u32[]{:S(2)}) async-start(bf16[8,256,256]{2,1,0:T(8,128)(2,1)} %bitcast.6), calls=%async_computation.2 | async-start | bytes 2097152 | tf_op jit(solution)/shard_map/all_to_all | solution.py:377
  118.2 23.3 %collective-permute-start.8 = (bf16[256,256]{1,0:T(8,128)(2,1)S(1)}, bf16[256,256]{1,0:T(8,128)(2,1)S(1)}, u32[]{:S(2)}, u32[]{:S(2)}) collective-permute-start(bf16[256,256]{1,0:T(8,128)(2,1)S(1)} %slice.43), channel_id=1, source_target_pairs={{8,0},{16,8},{24,16},{32,24},{40,32},{48,40},{56,48},{64,56},{72,6... | collective-permute-start | bytes 393224 | tf_op jit(solution)/shard_map/ppermute | solution.py:57
  144.4 10.7 %collective-permute-start.9 = (bf16[256,256]{1,0:T(8,128)(2,1)S(1)}, bf16[256,256]{1,0:T(8,128)(2,1)S(1)}, u32[]{:S(2)}, u32[]{:S(2)}) collective-permute-start(bf16[256,256]{1,0:T(8,128)(2,1)S(1)} %finish_kv.1), channel_id=1, source_target_pairs={{0,0},{1,1},{2,64},{3,65},{4,128},{5,129},{6,192},{7,193},{8,8},{9... | collective-permute-start | bytes 393224 | tf_op jit(solution)/shard_map/ppermute | solution.py:380
  145.0 23.3 %collective-permute-start.10 = (bf16[256,256]{1,0:T(8,128)(2,1)S(1)}, bf16[256,256]{1,0:T(8,128)(2,1)S(1)}, u32[]{:S(2)}, u32[]{:S(2)}) collective-permute-start(bf16[256,256]{1,0:T(8,128)(2,1)S(1)} %finish_kv.1), channel_id=1, source_target_pairs={{0,2},{1,3},{2,66},{3,67},{4,130},{5,131},{6,194},{7,195},{8,10},{... | collective-permute-start | bytes 393224 | tf_op jit(solution)/shard_map/ppermute | solution.py:380
  147.8 23.2 %collective-permute-start.11 = (bf16[256,256]{1,0:T(8,128)(2,1)S(1)}, bf16[256,256]{1,0:T(8,128)(2,1)S(1)}, u32[]{:S(2)}, u32[]{:S(2)}) collective-permute-start(bf16[256,256]{1,0:T(8,128)(2,1)S(1)} %finish_kv.1), channel_id=1, source_target_pairs={{0,4},{1,5},{2,68},{3,69},{4,132},{5,133},{6,196},{7,197},{8,12},{... | collective-permute-start | bytes 393224 | tf_op jit(solution)/shard_map/ppermute | solution.py:380
  151.8 19.2 %collective-permute-start.12 = (bf16[256,256]{1,0:T(8,128)(2,1)S(1)}, bf16[256,256]{1,0:T(8,128)(2,1)S(1)}, u32[]{:S(2)}, u32[]{:S(2)}) collective-permute-start(bf16[256,256]{1,0:T(8,128)(2,1)S(1)} %finish_kv.1), channel_id=1, source_target_pairs={{0,6},{1,7},{2,70},{3,71},{4,134},{5,135},{6,198},{7,199},{8,14},{... | collective-permute-start | bytes 393224 | tf_op jit(solution)/shard_map/ppermute | solution.py:380
  155.1 16.4 %collective-permute-start.13 = (bf16[256,256]{1,0:T(8,128)(2,1)S(1)}, bf16[256,256]{1,0:T(8,128)(2,1)S(1)}, u32[]{:S(2)}, u32[]{:S(2)}) collective-permute-start(bf16[256,256]{1,0:T(8,128)(2,1)S(1)} %collective-permute-done.9.refs_0_), channel_id=1, source_target_pairs={{0,1},{1,0},{2,3},{3,2},{4,5},{5,4},{6,7},{7,6},{8,9},{9,8},{10,11... | collective-permute-start | bytes 393224 | tf_op jit(solution)/shard_map/ppermute | solution.py:381
  176.5 32.9 %all-to-all-start.3 = ((bf16[8,256,256]{2,1,0:T(8,128)(2,1)}), bf16[8,256,256]{2,1,0:T(8,128)(2,1)S(1)}, u32[]{:S(2)}, u32[]{:S(2)}) async-start(bf16[8,256,256]{2,1,0:T(8,128)(2,1)} %weight_terms.1), calls=%async_computation.3 | async-start | bytes 2097152 | tf_op jit(solution)/shard_map/all_to_all | solution.py:385
  181.5 9.7 %collective-permute-start.17 = (bf16[128,1024]{1,0:T(8,128)(2,1)S(1)}, bf16[128,1024]{1,0:T(8,128)(2,1)S(1)}, u32[]{:S(2)}, u32[]{:S(2)}) collective-permute-start(bf16[128,1024]{1,0:T(8,128)(2,1)S(1)} %get-tuple-element.40), channel_id=1, source_target_pairs={{0,64},{8,72},{16,80},{24,88},{32,96},{40,104},{48,112},{56,120},{... | collective-permute-start | bytes 786440 | tf_op jit(solution)/shard_map/ppermute | solution.py:62
  184.5 8.5 %collective-permute-start.19 = (bf16[128,1024]{1,0:T(8,128)(2,1)S(1)}, bf16[128,1024]{1,0:T(8,128)(2,1)S(1)}, u32[]{:S(2)}, u32[]{:S(2)}) collective-permute-start(bf16[128,1024]{1,0:T(8,128)(2,1)S(1)} %get-tuple-element.41), channel_id=1, source_target_pairs={{64,0},{72,8},{80,16},{88,24},{96,32},{104,40},{112,48},{120,56},{... | collective-permute-start | bytes 786440 | tf_op jit(solution)/shard_map/ppermute | solution.py:62
  191.3 13.9 %collective-permute-start.18 = (bf16[256,1024]{1,0:T(8,128)(2,1)S(1)}, bf16[256,1024]{1,0:T(8,128)(2,1)S(1)}, u32[]{:S(2)}, u32[]{:S(2)}) collective-permute-start(bf16[256,1024]{1,0:T(8,128)(2,1)S(1)} %pad_maximum_fusion), channel_id=1, source_target_pairs={{0,64},{8,72},{16,80},{24,88},{32,96},{40,104},{48,112},{56,120},{... | collective-permute-start | bytes 1572872 | tf_op jit(solution)/shard_map/ppermute | solution.py:62
  193.1 12.6 %collective-permute-start.20 = (bf16[256,1024]{1,0:T(8,128)(2,1)S(1)}, bf16[256,1024]{1,0:T(8,128)(2,1)S(1)}, u32[]{:S(2)}, u32[]{:S(2)}) collective-permute-start(bf16[256,1024]{1,0:T(8,128)(2,1)S(1)} %pad_maximum_fusion.1), channel_id=1, source_target_pairs={{64,0},{72,8},{80,16},{88,24},{96,32},{104,40},{112,48},{120,56},{... | collective-permute-start | bytes 1572872 | tf_op jit(solution)/shard_map/ppermute | solution.py:62
  (11 other events, 98.2 us)
Sparse Core Ops, SparseCore 0:
  20.8 35.3 all-gather.2
  58.5 40.0 all-gather.4

commit v6 on v4

--- a/solution.py
+++ b/solution.py
@@ -22,7 +22,6 @@
 Z_GROUPS = [[x * NZ + z for z in range(NZ)] for x in range(NX)]
 Z_UP = [(x * NZ + z, x * NZ + (z + 1) % NZ) for x in range(NX) for z in range(NZ)]
 X_UP = [(x * NZ + z, (x + 1) % NX * NZ + z) for x in range(NX) for z in range(NZ)]
-X_ACROSS = [(x * NZ + z, (x + 2) % NX * NZ + z) for x in range(NX) for z in range(NZ)]
 NY = 4
 Y_UP = [(2 * y + core, 2 * ((y + 1) % NY) + core) for y in range(NY) for core in range(2)]
 CORES = [(own, own ^ 1) for own in range(2 * NY)]
@@ -94,7 +93,7 @@
     for steps, list_ref in enumerate(lists):
         first = lax.rem(x_at + steps, NX) * SLOTS
         for j in range(SLOTS):
-            out_ref[first + j] = plane_ref[lax.rem(list_ref[j], PLANE)]
+            out_ref[first + j] = plane_ref[lax.rem(list_ref[j // FARS, j % FARS], PLANE)]
 
 
 def pick(at, lists, own, pieces):
@@ -127,7 +126,7 @@
             v_ref[w * BLK : (w + 1) * BLK, :] = both[:, DH:]
         for j in range(FARS):
             slot = b * FARS + j
-            owner = lax.div(far_ref[slot], PLANE)
+            owner = lax.div(far_ref[b, j], PLANE)
             both = far_kv_ref[owner * SLOTS + slot]
             k_ref[(WIN + j) * BLK : (WIN + j + 1) * BLK, :] = both[:, :DH]
             v_ref[(WIN + j) * BLK : (WIN + j + 1) * BLK, :] = both[:, DH:]
@@ -211,10 +210,10 @@
 
     half = SLOTS // 2
     for j in range(SLOTS):
-        add(lists[0][j], mine, j)
-        add(lists[1][j], above, j)
-        add(lists[2][j], across_low if j < half else across_high, j % half)
-        add(lists[3][j], below, j)
+        add(lists[0][j // FARS, j % FARS], mine, j)
+        add(lists[1][j // FARS, j % FARS], above, j)
+        add(lists[2][j // FARS, j % FARS], across_low if j < half else across_high, j % half)
+        add(lists[3][j // FARS, j % FARS], below, j)
     out_ref[...] = acc_ref[...].astype(BF16)
 
 
@@ -333,24 +332,29 @@
     )(terms)
 
 
-def input_kernel(at_ref, grad_ref, weights_ref, mine_ref, above_ref, across_ref, below_ref):
+def input_kernel(at_ref, grad_ref, weights_ref, mine_ref, above_ref, low_ref, high_ref, below_ref):
     x_at = lax.div(at_ref[0], NZ)
-    for steps, out_ref in enumerate((mine_ref, above_ref, across_ref, below_ref)):
+    half = low_ref.shape[0]
+    for steps in range(NX):
         x = lax.rem(x_at + steps, NX)
         grad = jnp.concatenate([grad_ref[2 * x], grad_ref[2 * x + 1]], axis=1)
-        out_ref[...] = jnp.dot(grad, weights_ref[...], preferred_element_type=F32).astype(
-            out_ref.dtype
-        )
+        term = jnp.dot(grad, weights_ref[...], preferred_element_type=F32)
+        if steps == 2:
+            low_ref[...] = term[:half].astype(BF16)
+            high_ref[...] = term[half:].astype(BF16)
+        else:
+            out_ref = (mine_ref, above_ref, None, below_ref)[steps]
+            out_ref[...] = term.astype(out_ref.dtype)
 
 
 def input_terms(at, grad, weights):
-    shape = (grad.shape[1], weights.shape[1])
-    send = jax.ShapeDtypeStruct(shape, BF16)
+    rows, wide = grad.shape[1], weights.shape[1]
+    send, half = (jax.ShapeDtypeStruct((size, wide), BF16) for size in (rows, rows // 2))
     return pl.pallas_call(
         input_kernel,
-        out_shape=(jax.ShapeDtypeStruct(shape, F32), send, send, send),
+        out_shape=(jax.ShapeDtypeStruct((rows, wide), F32), send, half, half, send),
         in_specs=[SMEM, VMEM, VMEM],
-        out_specs=(VMEM,) * 4,
+        out_specs=(VMEM,) * 5,
         compiler_params=params(16),
         cost_estimate=pl.CostEstimate(flops=1 << 30, bytes_accessed=4 << 20, transcendentals=0),
         name="input_terms",
@@ -374,31 +378,34 @@
 
     inputs_x = lax.all_gather(inputs, "seq", axis=0, axis_index_groups=X_GROUPS, tiled=True)
 
-    listed = far_blocks.reshape(SLOTS)
-    list_below, list_above = both_ways(listed, listed, "seq", X_UP)
-    list_across = lax.ppermute(listed, "seq", X_ACROSS)
-    from_below, from_above = both_ways(own_kv, own_kv, "seq", Z_UP)
-    list_below, list_above, list_across, from_below, from_above, key_weight, value_weight = (
-        lax.optimization_barrier(
-            (list_below, list_above, list_across, from_below, from_above, key_weight, value_weight)
-        )
-    )
-    lists = (listed, list_above, list_across, list_below)
-    weights = jnp.concatenate([key_weight.T, value_weight.T])
-    weights = lax.all_gather(weights, "seq", axis=0, axis_index_groups=Z_GROUPS, tiled=True)
-    plane = [from_below, from_above]
-    for distance in range(2, NZ // 2 + 1):
+    from_below, from_above, listed = own_kv, own_kv, far_blocks
+    plane, lists = [], []
+    for distance in range(1, NZ // 2 + 1):
         if distance == NZ // 2:
             from_below, from_above = from_below[: NB // 2], from_above[NB // 2 :]
         from_below, from_above = both_ways(from_below, from_above, "seq", Z_UP)
+        if distance < NX:
+            pairs = [(x * NZ + z, (x - distance) % NX * NZ + z) for x in range(NX) for z in range(NZ)]
+            arrived = lax.ppermute(listed, "seq", pairs)
+            arrived, listed, from_below, from_above = lax.optimization_barrier(
+                (arrived, listed, from_below, from_above)
+            )
+            lists.append(arrived)
         plane += [from_below, from_above]
+    lists = [far_blocks, *lists]
+    from_below, key_weight, value_weight = lax.optimization_barrier(
+        (plane[0], key_weight, value_weight)
+    )
+    plane[0] = from_below
+    weights = jnp.concatenate([key_weight.T, value_weight.T])
+    weights = lax.all_gather(weights, "seq", axis=0, axis_index_groups=Z_GROUPS, tiled=True)
     prev_kv = shifted(own_kv, "seq", 1)
     chosen = pick(at, lists, own_kv, plane)
     far_kv = lax.all_to_all(chosen, "seq", 0, 0, axis_index_groups=X_GROUPS, tiled=True)
 
     far_kv, inputs_x = lax.optimization_barrier((far_kv, inputs_x))
     query_grad, window, far_grad = attend(
-        at, listed, far_count, queries, out_grad, prev_kv, own_kv, far_kv
+        at, far_blocks, far_count, queries, out_grad, prev_kv, own_kv, far_kv
     )
     far_all = ring_gather(far_grad, "seq", X_UP, NX)
     back = shifted(window[:tokens].astype(BF16), "seq", -1)
@@ -413,12 +420,12 @@
     other_core = lax.ppermute(jnp.concatenate([moved, *same_core]), "own", CORES)
     heads = place_heads(own_index, moved, same_core, other_core)
 
+    mine, above, low, high, below = input_terms(at, heads, weights)
+    heads, low, high = lax.optimization_barrier((heads, low, high))
+    from_below, from_above = both_ways(low, high, "seq", X_UP)
     pieces = weight_terms(heads, inputs_x)
     pieces = lax.all_to_all(pieces, "seq", 0, 0, axis_index_groups=Z_GROUPS, tiled=True)
-    mine, above, across, below = input_terms(at, heads, weights)
-    half = tokens // 2
-    from_below, from_above = both_ways(across[:half], across[half:], "seq", X_UP)
-    above, below = added(above, from_below, 0), added(below, from_above, half)
+    above, below = added(above, from_below, 0), added(below, from_above, tokens // 2)
     from_below, from_above = both_ways(above, below, "seq", X_UP)
     input_grad = mine + from_below.astype(F32) + from_above.astype(F32)
     key_weight_grad, value_weight_grad = weight_sum(pieces)

time: 206 us -> 206 us (level)
  starting transfers between devices: 71 us -> 74.1 us
    ppermute x11 -> x10, waiting for transfers between devices: 27.4 us -> 22.2 us  [both_ways(): lax.ppermute(upward, axis, pairs)]
    ppermute x1 -> x3, starting transfers between devices: 1.53 us -> 6.16 us  [local(): arrived = lax.ppermute(listed, 'seq', pairs)]
    ppermute x1 -> x3, waiting for transfers between devices: 2.36 us -> 5.99 us  [local(): arrived = lax.ppermute(listed, 'seq', pairs)]
    ppermute x11 -> x10, starting transfers between devices: 30.9 us -> 29.1 us  [both_ways(): lax.ppermute(downward, axis, back)]
    ppermute x11 -> x10, starting transfers between devices: 11.6 us -> 10.4 us  [both_ways(): lax.ppermute(upward, axis, pairs)]
    ppermute x11 -> x10, waiting for transfers between devices: 15.1 us -> 15.3 us  [both_ways(): lax.ppermute(downward, axis, back)]
  transfers between devices with their start and end apart: 32 -> 32, of which waited for: 16 -> 16; matrix products, arithmetic and copies ran while one was open for 2% -> 1% of each run, Pallas kernels for 7% -> 7%
where the time goes in v6:
time: 206 us; the launch traced here: 205 us
  waiting for transfers between devices  91.5 us (44%)
  starting transfers between devices  74.1 us (36%)
  Pallas kernels  18.9 us (9%)
  between operations  14.4 us (7%)
  local copies, waits for them, and re-layouts  3.81 us (2%)
  other arithmetic  2.79 us (1%)
    ppermute x10, starting transfers between devices, both_ways(): lax.ppermute(downward, axis, back)  29.1 us
    ppermute x10, waiting for transfers between devices, both_ways(): lax.ppermute(upward, axis, pairs)  22.2 us
    all_to_all x1, waiting for transfers between devices, local(): lax.all_to_all(chosen, 'seq', 0, 0, axis_index_groups=X_GROUPS, tiled=True)  20.3 us
    ppermute x2, waiting for transfers between devices, shifted(): lax.ppermute(value, axis, [(source, source + steps) for source in range(l...  18.3 us
    ppermute x10, waiting for transfers between devices, both_ways(): lax.ppermute(downward, axis, back)  15.3 us
    ppermute x1, starting transfers between devices, local(): lax.ppermute(jnp.concatenate([moved, *same_core]), 'own', CORES)  11.5 us
    ppermute x10, starting transfers between devices, both_ways(): lax.ppermute(upward, axis, pairs)  10.4 us
    pallas_call x1, Pallas kernels, attend(): pl.pallas_call(attend_kernel, out_shape=(jax.ShapeDtypeStruct((NB * BLK,...  9.59 us
  transfers between devices with their start and end apart: 32, of which 16 were waited for; matrix products, arithmetic and copies ran while one was open for 1% of the time, Pallas kernels for 7%

profile of v6, /device:TPU:1, one launch (start us, length us, event | category | flops | bytes accessed | tf_op | source)
XLA Modules:
  0.0 205.4 jit_solution(16079389306895630268)
XLA Ops:
  11.3 4.0 %collective-permute-start.3 = (bf16[2,128,256]{2,1,0:T(8,128)(2,1)S(1)}, bf16[2,128,256]{2,1,0:T(8,128)(2,1)S(1)}, u32[]{:S(2)}, u32[]{:S(2)}) collective-permute-start(bf16[2,128,256]{2,1,0:T(8,128)(2,1)S(1)} %bitcast.9), channel_id=1, source_target_pairs={{8,0},{16,8},{24,16},{32,24},{40,32},{48,40},{56,48},{0,56},{72,64... | collective-permute-start | bytes 393224 | tf_op jit(solution)/shard_map/ppermute | solution.py:59
  18.8 2.7 %collective-permute-start.6 = (bf16[2,128,256]{2,1,0:T(8,128)(2,1)S(1)}, bf16[2,128,256]{2,1,0:T(8,128)(2,1)S(1)}, u32[]{:S(2)}, u32[]{:S(2)}) collective-permute-start(bf16[2,128,256]{2,1,0:T(8,128)(2,1)S(1)} %collective-permute-done.3.refs_6_), channel_id=1, source_target_pairs={{8,0},{16,8},{24,16},{32,24},{40,32},{48,40},{56,48},{0,56},{72,64... | collective-permute-start | bytes 393224 | tf_op jit(solution)/shard_map/ppermute | solution.py:59
  25.6 2.7 %collective-permute-start.9 = (bf16[2,128,256]{2,1,0:T(8,128)(2,1)S(1)}, bf16[2,128,256]{2,1,0:T(8,128)(2,1)S(1)}, u32[]{:S(2)}, u32[]{:S(2)}) collective-permute-start(bf16[2,128,256]{2,1,0:T(8,128)(2,1)S(1)} %collective-permute-done.6.refs_8_), channel_id=1, source_target_pairs={{8,0},{16,8},{24,16},{32,24},{40,32},{48,40},{56,48},{0,56},{72,64... | collective-permute-start | bytes 393224 | tf_op jit(solution)/shard_map/ppermute | solution.py:59
  29.5 3.4 %collective-permute-done.7.refs_3_ = s32[2,4]{1,0:T(2,128)S(1)} collective-permute-done((s32[2,4]{1,0:T(2,128)}, s32[2,4]{1,0:T(2,128)S(1)}, u32[]{:S(2)}, u32[]{:S(2)}) %collective-permute-start.7) | collective-permute-done | bytes 64 | tf_op jit(solution)/shard_map/ppermute | solution.py:389
  33.0 2.7 %collective-permute-start.11 = (bf16[1,128,256]{2,1,0:T(8,128)(2,1)S(1)}, bf16[1,128,256]{2,1,0:T(8,128)(2,1)S(1)}, u32[]{:S(2)}, u32[]{:S(2)}) collective-permute-start(bf16[1,128,256]{2,1,0:T(8,128)(2,1)S(1)} %slice.35), channel_id=1, source_target_pairs={{8,0},{16,8},{24,16},{32,24},{40,32},{48,40},{56,48},{0,56},{72,64... | collective-permute-start | bytes 196616 | tf_op jit(solution)/shard_map/ppermute | solution.py:59
  40.6 3.8 %all-to-all-start = ((bf16[32,128,256]{2,1,0:T(8,128)(2,1)}), bf16[32,128,256]{2,1,0:T(8,128)(2,1)S(1)}, u32[]{:S(2)}, u32[]{:S(2)}) async-start(bf16[32,128,256]{2,1,0:T(8,128)(2,1)} %pick_far.1), calls=%async_computation | async-start | bytes 4194304 | tf_op jit(solution)/shard_map/all_to_all | solution.py:404
  45.1 3.0 %collective-permute-start = (bf16[2,128,256]{2,1,0:T(8,128)(2,1)S(1)}, bf16[2,128,256]{2,1,0:T(8,128)(2,1)S(1)}, u32[]{:S(2)}, u32[]{:S(2)}) collective-permute-start(bf16[2,128,256]{2,1,0:T(8,128)(2,1)S(1)} %bitcast.11), channel_id=1, source_target_pairs={{0,8},{8,16},{16,24},{24,32},{32,40},{40,48},{48,56},{56,64},{64,7... | collective-permute-start | bytes 393224 | tf_op jit(solution)/shard_map/ppermute | solution.py:54
  48.1 20.3 %all-to-all-done.far_kv_ref = bf16[32,128,256]{2,1,0:T(8,128)(2,1)S(1)} async-done(((bf16[32,128,256]{2,1,0:T(8,128)(2,1)}), bf16[32,128,256]{2,1,0:T(8,128)(2,1)S(1)}, u32[]{:S(2)}, u32[]{:S(2)}) %all-to-all-start) | async-done | bytes 2097184 | tf_op jit(solution)/shard_map/all_to_all | solution.py:404
  69.5 9.6 %attend.1 = (bf16[256,1024]{1,0:T(8,128)(2,1)}, f32[512,256]{1,0:T(8,128)S(1)}, bf16[8,128,256]{2,1,0:T(8,128)(2,1)S(1)}) custom-call(s32[1]{0:T(128)} %bitcast.at_ref, s32[2,4]{1,0:T(2,128)S(1)} %copy-done.2, s32[2]{0:T(128)S(1)} %copy-done.7, bf16[256,1024]{1,0:T(8,128)(2,1)S(1)} %copy-done.4, bf16[256,1024]{1,0:T(8,128)(2,1)S(1)} %copy-done.5, ...), custom_call_target="tpu_custom_call" | custom-call | flops 9600000000 | bytes 6291456 | tf_op jit(solution)/shard_map/attend/pallas_call | solution.py:177
  79.1 2.7 %collective-permute-start.13 = (bf16[8,128,256]{2,1,0:T(8,128)(2,1)S(1)}, bf16[8,128,256]{2,1,0:T(8,128)(2,1)S(1)}, u32[]{:S(2)}, u32[]{:S(2)}) collective-permute-start(bf16[8,128,256]{2,1,0:T(8,128)(2,1)S(1)} %get-tuple-element.49.refs_4_), channel_id=1, source_target_pairs={{64,0},{72,8},{80,16},{88,24},{96,32},{104,40},{112,48},{120,56},{... | collective-permute-start | bytes 1572872 | tf_op jit(solution)/shard_map/ppermute | solution.py:59
  81.7 6.9 %collective-permute-done.12.refs_5_ = bf16[8,128,256]{2,1,0:T(8,128)(2,1)S(1)} collective-permute-done((bf16[8,128,256]{2,1,0:T(8,128)(2,1)S(1)}, bf16[8,128,256]{2,1,0:T(8,128)(2,1)S(1)}, u32[]{:S(2)}, u32[]{:S(2)}) %collective-permute-start.12) | collective-permute-done | bytes 524320 | tf_op jit(solution)/shard_map/ppermute | solution.py:59
  88.8 2.7 %collective-permute-start.15 = (bf16[4,128,256]{2,1,0:T(8,128)(2,1)S(1)}, bf16[4,128,256]{2,1,0:T(8,128)(2,1)S(1)}, u32[]{:S(2)}, u32[]{:S(2)}) collective-permute-start(bf16[4,128,256]{2,1,0:T(8,128)(2,1)S(1)} %slice.46), channel_id=1, source_target_pairs={{64,0},{72,8},{80,16},{88,24},{96,32},{104,40},{112,48},{120,56},{... | collective-permute-start | bytes 786440 | tf_op jit(solution)/shard_map/ppermute | solution.py:59
  91.5 6.1 %collective-permute-done.14.refs_7_ = bf16[4,128,256]{2,1,0:T(8,128)(2,1)S(1)} collective-permute-done((bf16[4,128,256]{2,1,0:T(8,128)(2,1)S(1)}, bf16[4,128,256]{2,1,0:T(8,128)(2,1)S(1)}, u32[]{:S(2)}, u32[]{:S(2)}) %collective-permute-start.14) | collective-permute-done | bytes 262176 | tf_op jit(solution)/shard_map/ppermute | solution.py:59
  100.0 3.6 %all-to-all-start.1 = ((bf16[8,256,256]{2,1,0:T(8,128)(2,1)}), bf16[8,256,256]{2,1,0:T(8,128)(2,1)S(1)}, u32[]{:S(2)}, u32[]{:S(2)}) async-start(bf16[8,256,256]{2,1,0:T(8,128)(2,1)} %bitcast.5), calls=%async_computation.1 | async-start | bytes 2097152 | tf_op jit(solution)/shard_map/all_to_all | solution.py:415
  104.9 18.3 %collective-permute-done.16.back_ref = bf16[256,256]{1,0:T(8,128)(2,1)S(1)} collective-permute-done((bf16[256,256]{1,0:T(8,128)(2,1)S(1)}, bf16[256,256]{1,0:T(8,128)(2,1)S(1)}, u32[]{:S(2)}, u32[]{:S(2)}) %collective-permute-start.16) | collective-permute-done | bytes 131104 | tf_op jit(solution)/shard_map/ppermute | solution.py:54
  126.3 7.4 %collective-permute-start.18 = (bf16[256,256]{1,0:T(8,128)(2,1)S(1)}, bf16[256,256]{1,0:T(8,128)(2,1)S(1)}, u32[]{:S(2)}, u32[]{:S(2)}) collective-permute-start(bf16[256,256]{1,0:T(8,128)(2,1)S(1)} %collective-permute-done.17.own_ref), channel_id=1, source_target_pairs={{0,2},{1,3},{2,4},{3,5},{4,6},{5,7},{6,0},{7,1},{8,10},{9,11},{10,... | collective-permute-start | bytes 393224 | tf_op jit(solution)/shard_map/ppermute | solution.py:59
  133.8 5.0 %collective-permute-start.19 = (bf16[256,256]{1,0:T(8,128)(2,1)S(1)}, bf16[256,256]{1,0:T(8,128)(2,1)S(1)}, u32[]{:S(2)}, u32[]{:S(2)}) collective-permute-start(bf16[256,256]{1,0:T(8,128)(2,1)S(1)} %collective-permute-done.17.own_ref), channel_id=1, source_target_pairs={{2,0},{3,1},{4,2},{5,3},{6,4},{7,5},{0,6},{1,7},{10,8},{11,9},{12,... | collective-permute-start | bytes 393224 | tf_op jit(solution)/shard_map/ppermute | solution.py:59
  141.1 2.7 %collective-permute-start.21 = (bf16[128,256]{1,0:T(8,128)(2,1)S(1)}, bf16[128,256]{1,0:T(8,128)(2,1)S(1)}, u32[]{:S(2)}, u32[]{:S(2)}) collective-permute-start(bf16[128,256]{1,0:T(8,128)(2,1)S(1)} %slice.49), channel_id=1, source_target_pairs={{2,0},{3,1},{4,2},{5,3},{6,4},{7,5},{0,6},{1,7},{10,8},{11,9},{12,... | collective-permute-start | bytes 196616 | tf_op jit(solution)/shard_map/ppermute | solution.py:59
  145.4 11.5 %collective-permute-start.22 = (bf16[1024,256]{1,0:T(8,128)(2,1)S(1)}, bf16[1024,256]{1,0:T(8,128)(2,1)S(1)}, u32[]{:S(2)}, u32[]{:S(2)}) collective-permute-start(bf16[1024,256]{1,0:T(8,128)(2,1)S(1)} %constant_dynamic-update-slice_fusion), channel_id=1, source_target_pairs={{0,1},{1,0},{2,3},{3,2},{4,5},{5,4},{6,7},{7,6},{8,9},{9,8},{10,11... | collective-permute-start | bytes 1572872 | tf_op jit(solution)/shard_map/ppermute | solution.py:420
  164.1 4.5 %all-to-all-start.2 = ((bf16[8,256,256]{2,1,0:T(8,128)(2,1)}), bf16[8,256,256]{2,1,0:T(8,128)(2,1)S(1)}, u32[]{:S(2)}, u32[]{:S(2)}) async-start(bf16[8,256,256]{2,1,0:T(8,128)(2,1)} %weight_terms.1), calls=%async_computation.2 | async-start | bytes 2097152 | tf_op jit(solution)/shard_map/all_to_all | solution.py:427
  170.1 5.8 %collective-permute-done.25 = bf16[128,1024]{1,0:T(8,128)(2,1)S(1)} collective-permute-done((bf16[128,1024]{1,0:T(8,128)(2,1)}, bf16[128,1024]{1,0:T(8,128)(2,1)S(1)}, u32[]{:S(2)}, u32[]{:S(2)}) %collective-permute-start.25) | collective-permute-done | bytes 262176 | tf_op jit(solution)/shard_map/ppermute | solution.py:59
  178.9 9.5 %collective-permute-done.26 = bf16[256,1024]{1,0:T(8,128)(2,1)S(1)} collective-permute-done((bf16[256,1024]{1,0:T(8,128)(2,1)S(1)}, bf16[256,1024]{1,0:T(8,128)(2,1)S(1)}, u32[]{:S(2)}, u32[]{:S(2)}) %collective-permute-start.26) | collective-permute-done | bytes 524320 | tf_op jit(solution)/shard_map/ppermute | solution.py:59
  188.4 3.3 %collective-permute-done.24 = bf16[256,1024]{1,0:T(8,128)(2,1)S(1)} collective-permute-done((bf16[256,1024]{1,0:T(8,128)(2,1)S(1)}, bf16[256,1024]{1,0:T(8,128)(2,1)S(1)}, u32[]{:S(2)}, u32[]{:S(2)}) %collective-permute-start.24) | collective-permute-done | bytes 524320 | tf_op jit(solution)/shard_map/ppermute | solution.py:59
  192.7 5.0 %all-to-all-done.2.terms_ref = bf16[8,256,256]{2,1,0:T(8,128)(2,1)S(1)} async-done(((bf16[8,256,256]{2,1,0:T(8,128)(2,1)}), bf16[8,256,256]{2,1,0:T(8,128)(2,1)S(1)}, u32[]{:S(2)}, u32[]{:S(2)}) %all-to-all-start.2) | async-done | bytes 1048608 | tf_op jit(solution)/shard_map/all_to_all | solution.py:427
  (91 shorter events, 44.0 us)
Async XLA Ops:
  7.2 61.2 %all-gather.3.cloned.1.call-start = ((), (), s32[]{:S(2)}) async-start(), calls=%async_computation.3 | async-start | bytes 2621440 | tf_op jit(solution)/shard_map/all_gather | solution.py:379
  8.8 10.0 %collective-permute-start.2 = (bf16[2,128,256]{2,1,0:T(8,128)(2,1)S(1)}, bf16[2,128,256]{2,1,0:T(8,128)(2,1)S(1)}, u32[]{:S(2)}, u32[]{:S(2)}) collective-permute-start(bf16[2,128,256]{2,1,0:T(8,128)(2,1)S(1)} %bitcast.8), channel_id=1, source_target_pairs={{0,8},{8,16},{16,24},{24,32},{32,40},{40,48},{48,56},{56,0},{64,72... | collective-permute-start | bytes 393224 | tf_op jit(solution)/shard_map/ppermute | solution.py:59
  11.3 7.5 %collective-permute-start.3 = (bf16[2,128,256]{2,1,0:T(8,128)(2,1)S(1)}, bf16[2,128,256]{2,1,0:T(8,128)(2,1)S(1)}, u32[]{:S(2)}, u32[]{:S(2)}) collective-permute-start(bf16[2,128,256]{2,1,0:T(8,128)(2,1)S(1)} %bitcast.9), channel_id=1, source_target_pairs={{8,0},{16,8},{24,16},{32,24},{40,32},{48,40},{56,48},{0,56},{72,64... | collective-permute-start | bytes 393224 | tf_op jit(solution)/shard_map/ppermute | solution.py:59
  18.8 6.8 %collective-permute-start.5 = (bf16[2,128,256]{2,1,0:T(8,128)(2,1)S(1)}, bf16[2,128,256]{2,1,0:T(8,128)(2,1)S(1)}, u32[]{:S(2)}, u32[]{:S(2)}) collective-permute-start(bf16[2,128,256]{2,1,0:T(8,128)(2,1)S(1)} %collective-permute-done.2.refs_5_), channel_id=1, source_target_pairs={{0,8},{8,16},{16,24},{24,32},{32,40},{40,48},{48,56},{56,0},{64,72... | collective-permute-start | bytes 393224 | tf_op jit(solution)/shard_map/ppermute | solution.py:59
  18.8 6.8 %collective-permute-start.6 = (bf16[2,128,256]{2,1,0:T(8,128)(2,1)S(1)}, bf16[2,128,256]{2,1,0:T(8,128)(2,1)S(1)}, u32[]{:S(2)}, u32[]{:S(2)}) collective-permute-start(bf16[2,128,256]{2,1,0:T(8,128)(2,1)S(1)} %collective-permute-done.3.refs_6_), channel_id=1, source_target_pairs={{8,0},{16,8},{24,16},{32,24},{40,32},{48,40},{56,48},{0,56},{72,64... | collective-permute-start | bytes 393224 | tf_op jit(solution)/shard_map/ppermute | solution.py:59
  25.6 7.3 %collective-permute-start.8 = (bf16[2,128,256]{2,1,0:T(8,128)(2,1)S(1)}, bf16[2,128,256]{2,1,0:T(8,128)(2,1)S(1)}, u32[]{:S(2)}, u32[]{:S(2)}) collective-permute-start(bf16[2,128,256]{2,1,0:T(8,128)(2,1)S(1)} %collective-permute-done.5.refs_7_), channel_id=1, source_target_pairs={{0,8},{8,16},{16,24},{24,32},{32,40},{40,48},{48,56},{56,0},{64,72... | collective-permute-start | bytes 393224 | tf_op jit(solution)/shard_map/ppermute | solution.py:59
  25.6 7.3 %collective-permute-start.9 = (bf16[2,128,256]{2,1,0:T(8,128)(2,1)S(1)}, bf16[2,128,256]{2,1,0:T(8,128)(2,1)S(1)}, u32[]{:S(2)}, u32[]{:S(2)}) collective-permute-start(bf16[2,128,256]{2,1,0:T(8,128)(2,1)S(1)} %collective-permute-done.6.refs_8_), channel_id=1, source_target_pairs={{8,0},{16,8},{24,16},{32,24},{40,32},{48,40},{56,48},{0,56},{72,64... | collective-permute-start | bytes 393224 | tf_op jit(solution)/shard_map/ppermute | solution.py:59
  40.6 27.8 %all-to-all-start = ((bf16[32,128,256]{2,1,0:T(8,128)(2,1)}), bf16[32,128,256]{2,1,0:T(8,128)(2,1)S(1)}, u32[]{:S(2)}, u32[]{:S(2)}) async-start(bf16[32,128,256]{2,1,0:T(8,128)(2,1)} %pick_far.1), calls=%async_computation | async-start | bytes 4194304 | tf_op jit(solution)/shard_map/all_to_all | solution.py:404
  44.3 55.7 %all-gather.5.cloned.1.call-start = ((), (), s32[]{:S(2)}) async-start(), calls=%async_computation.4 | async-start | bytes 1179648 | tf_op jit(solution)/shard_map/all_gather | solution.py:401
  45.1 23.3 %collective-permute-start = (bf16[2,128,256]{2,1,0:T(8,128)(2,1)S(1)}, bf16[2,128,256]{2,1,0:T(8,128)(2,1)S(1)}, u32[]{:S(2)}, u32[]{:S(2)}) collective-permute-start(bf16[2,128,256]{2,1,0:T(8,128)(2,1)S(1)} %bitcast.11), channel_id=1, source_target_pairs={{0,8},{8,16},{16,24},{24,32},{32,40},{40,48},{48,56},{56,64},{64,7... | collective-permute-start | bytes 393224 | tf_op jit(solution)/shard_map/ppermute | solution.py:54
  79.1 9.6 %collective-permute-start.12 = (bf16[8,128,256]{2,1,0:T(8,128)(2,1)S(1)}, bf16[8,128,256]{2,1,0:T(8,128)(2,1)S(1)}, u32[]{:S(2)}, u32[]{:S(2)}) collective-permute-start(bf16[8,128,256]{2,1,0:T(8,128)(2,1)S(1)} %get-tuple-element.49.refs_4_), channel_id=1, source_target_pairs={{0,64},{8,72},{16,80},{24,88},{32,96},{40,104},{48,112},{56,120},{... | collective-permute-start | bytes 1572872 | tf_op jit(solution)/shard_map/ppermute | solution.py:59
  79.1 9.7 %collective-permute-start.13 = (bf16[8,128,256]{2,1,0:T(8,128)(2,1)S(1)}, bf16[8,128,256]{2,1,0:T(8,128)(2,1)S(1)}, u32[]{:S(2)}, u32[]{:S(2)}) collective-permute-start(bf16[8,128,256]{2,1,0:T(8,128)(2,1)S(1)} %get-tuple-element.49.refs_4_), channel_id=1, source_target_pairs={{64,0},{72,8},{80,16},{88,24},{96,32},{104,40},{112,48},{120,56},{... | collective-permute-start | bytes 1572872 | tf_op jit(solution)/shard_map/ppermute | solution.py:59
  88.7 8.9 %collective-permute-start.14 = (bf16[4,128,256]{2,1,0:T(8,128)(2,1)S(1)}, bf16[4,128,256]{2,1,0:T(8,128)(2,1)S(1)}, u32[]{:S(2)}, u32[]{:S(2)}) collective-permute-start(bf16[4,128,256]{2,1,0:T(8,128)(2,1)S(1)} %slice.45), channel_id=1, source_target_pairs={{0,64},{8,72},{16,80},{24,88},{32,96},{40,104},{48,112},{56,120},{... | collective-permute-start | bytes 786440 | tf_op jit(solution)/shard_map/ppermute | solution.py:59
  88.8 8.8 %collective-permute-start.15 = (bf16[4,128,256]{2,1,0:T(8,128)(2,1)S(1)}, bf16[4,128,256]{2,1,0:T(8,128)(2,1)S(1)}, u32[]{:S(2)}, u32[]{:S(2)}) collective-permute-start(bf16[4,128,256]{2,1,0:T(8,128)(2,1)S(1)} %slice.46), channel_id=1, source_target_pairs={{64,0},{72,8},{80,16},{88,24},{96,32},{104,40},{112,48},{120,56},{... | collective-permute-start | bytes 786440 | tf_op jit(solution)/shard_map/ppermute | solution.py:59
  100.0 25.3 %all-to-all-start.1 = ((bf16[8,256,256]{2,1,0:T(8,128)(2,1)}), bf16[8,256,256]{2,1,0:T(8,128)(2,1)S(1)}, u32[]{:S(2)}, u32[]{:S(2)}) async-start(bf16[8,256,256]{2,1,0:T(8,128)(2,1)} %bitcast.5), calls=%async_computation.1 | async-start | bytes 2097152 | tf_op jit(solution)/shard_map/all_to_all | solution.py:415
  103.6 19.6 %collective-permute-start.16 = (bf16[256,256]{1,0:T(8,128)(2,1)S(1)}, bf16[256,256]{1,0:T(8,128)(2,1)S(1)}, u32[]{:S(2)}, u32[]{:S(2)}) collective-permute-start(bf16[256,256]{1,0:T(8,128)(2,1)S(1)} %slice.53), channel_id=1, source_target_pairs={{8,0},{16,8},{24,16},{32,24},{40,32},{48,40},{56,48},{64,56},{72,6... | collective-permute-start | bytes 393224 | tf_op jit(solution)/shard_map/ppermute | solution.py:54
  126.3 14.7 %collective-permute-start.18 = (bf16[256,256]{1,0:T(8,128)(2,1)S(1)}, bf16[256,256]{1,0:T(8,128)(2,1)S(1)}, u32[]{:S(2)}, u32[]{:S(2)}) collective-permute-start(bf16[256,256]{1,0:T(8,128)(2,1)S(1)} %collective-permute-done.17.own_ref), channel_id=1, source_target_pairs={{0,2},{1,3},{2,4},{3,5},{4,6},{5,7},{6,0},{7,1},{8,10},{9,11},{10,... | collective-permute-start | bytes 393224 | tf_op jit(solution)/shard_map/ppermute | solution.py:59
  133.8 7.3 %collective-permute-start.19 = (bf16[256,256]{1,0:T(8,128)(2,1)S(1)}, bf16[256,256]{1,0:T(8,128)(2,1)S(1)}, u32[]{:S(2)}, u32[]{:S(2)}) collective-permute-start(bf16[256,256]{1,0:T(8,128)(2,1)S(1)} %collective-permute-done.17.own_ref), channel_id=1, source_target_pairs={{2,0},{3,1},{4,2},{5,3},{6,4},{7,5},{0,6},{1,7},{10,8},{11,9},{12,... | collective-permute-start | bytes 393224 | tf_op jit(solution)/shard_map/ppermute | solution.py:59
  145.4 13.1 %collective-permute-start.22 = (bf16[1024,256]{1,0:T(8,128)(2,1)S(1)}, bf16[1024,256]{1,0:T(8,128)(2,1)S(1)}, u32[]{:S(2)}, u32[]{:S(2)}) collective-permute-start(bf16[1024,256]{1,0:T(8,128)(2,1)S(1)} %constant_dynamic-update-slice_fusion), channel_id=1, source_target_pairs={{0,1},{1,0},{2,3},{3,2},{4,5},{5,4},{6,7},{7,6},{8,9},{9,8},{10,11... | collective-permute-start | bytes 1572872 | tf_op jit(solution)/shard_map/ppermute | solution.py:420
  164.1 33.7 %all-to-all-start.2 = ((bf16[8,256,256]{2,1,0:T(8,128)(2,1)}), bf16[8,256,256]{2,1,0:T(8,128)(2,1)S(1)}, u32[]{:S(2)}, u32[]{:S(2)}) async-start(bf16[8,256,256]{2,1,0:T(8,128)(2,1)} %weight_terms.1), calls=%async_computation.2 | async-start | bytes 2097152 | tf_op jit(solution)/shard_map/all_to_all | solution.py:427
  168.5 7.4 %collective-permute-start.25 = (bf16[128,1024]{1,0:T(8,128)(2,1)}, bf16[128,1024]{1,0:T(8,128)(2,1)S(1)}, u32[]{:S(2)}, u32[]{:S(2)}) collective-permute-start(bf16[128,1024]{1,0:T(8,128)(2,1)} %copy-done.6), channel_id=1, source_target_pairs={{64,0},{72,8},{80,16},{88,24},{96,32},{104,40},{112,48},{120,56},{... | collective-permute-start | bytes 786440 | tf_op jit(solution)/shard_map/ppermute | solution.py:59
  170.0 8.8 %collective-permute-start.23 = (bf16[128,1024]{1,0:T(8,128)(2,1)S(1)}, bf16[128,1024]{1,0:T(8,128)(2,1)S(1)}, u32[]{:S(2)}, u32[]{:S(2)}) collective-permute-start(bf16[128,1024]{1,0:T(8,128)(2,1)S(1)} %get-tuple-element.59), channel_id=1, source_target_pairs={{0,64},{8,72},{16,80},{24,88},{32,96},{40,104},{48,112},{56,120},{... | collective-permute-start | bytes 786440 | tf_op jit(solution)/shard_map/ppermute | solution.py:59
  176.1 12.3 %collective-permute-start.26 = (bf16[256,1024]{1,0:T(8,128)(2,1)S(1)}, bf16[256,1024]{1,0:T(8,128)(2,1)S(1)}, u32[]{:S(2)}, u32[]{:S(2)}) collective-permute-start(bf16[256,1024]{1,0:T(8,128)(2,1)S(1)} %pad_maximum_fusion.1), channel_id=1, source_target_pairs={{64,0},{72,8},{80,16},{88,24},{96,32},{104,40},{112,48},{120,56},{... | collective-permute-start | bytes 1572872 | tf_op jit(solution)/shard_map/ppermute | solution.py:59
  178.8 12.9 %collective-permute-start.24 = (bf16[256,1024]{1,0:T(8,128)(2,1)S(1)}, bf16[256,1024]{1,0:T(8,128)(2,1)S(1)}, u32[]{:S(2)}, u32[]{:S(2)}) collective-permute-start(bf16[256,1024]{1,0:T(8,128)(2,1)S(1)} %pad_maximum_fusion), channel_id=1, source_target_pairs={{0,64},{8,72},{16,80},{24,88},{32,96},{40,104},{48,112},{56,120},{... | collective-permute-start | bytes 1572872 | tf_op jit(solution)/shard_map/ppermute | solution.py:59
  (18 other events, 127.9 us)
Sparse Core Ops, SparseCore 0:
  9.8 37.1 all-gather.2
  49.4 38.6 all-gather.4

commit v7 on v6

--- a/solution.py
+++ b/solution.py
@@ -85,31 +85,64 @@
             out_ref[pl.ds(above, size)] = pieces[2 * distance - 1][...]
 
 
-def pick_kernel(at_ref, *refs):
-    lists, own_ref, pieces = refs[:NX], refs[NX], refs[NX + 1 : -2]
-    out_ref, plane_ref = refs[-2:]
-    x_at, z_at = lax.div(at_ref[0], NZ), lax.rem(at_ref[0], NZ)
-    place_pieces(plane_ref, z_at, own_ref, pieces, NZ, NB)
-    for steps, list_ref in enumerate(lists):
-        first = lax.rem(x_at + steps, NX) * SLOTS
-        for j in range(SLOTS):
-            out_ref[first + j] = plane_ref[lax.rem(list_ref[j // FARS, j % FARS], PLANE)]
-
-
-def pick(at, lists, own, pieces):
+def across_kernel(at_ref, across_ref, own_ref, *refs):
+    *pieces, plane_ref, low_ref, high_ref = refs
+    place_pieces(plane_ref, lax.rem(at_ref[0], NZ), own_ref, pieces, NZ, NB)
+    for b, out_ref in enumerate((low_ref, high_ref)):
+        for j in range(FARS):
+            out_ref[j] = plane_ref[lax.rem(across_ref[b, j], PLANE)]
+
+
+def pick_across(at, across, own, pieces):
+    half = jax.ShapeDtypeStruct((FARS, BLK, 2 * DH), BF16)
+    return pl.pallas_call(
+        across_kernel,
+        out_shape=(jax.ShapeDtypeStruct((PLANE, BLK, 2 * DH), BF16), half, half),
+        in_specs=[SMEM] * 2 + [VMEM] * (1 + len(pieces)),
+        out_specs=(VMEM,) * 3,
+        compiler_params=params(8),
+        name="pick_across",
+    )(at, across, own, *pieces)
+
+
+def pick_kernel(at_ref, above_ref, below_ref, plane_ref, low_ref, high_ref, up_ref, down_ref):
+    x_at = lax.div(at_ref[0], NZ)
+    for list_ref, arrived_ref, behind, passed, out_ref in (
+        (above_ref, low_ref, lax.rem(x_at + NX - 1, NX), 0, up_ref),
+        (below_ref, high_ref, lax.rem(x_at + 1, NX), 1, down_ref),
+    ):
+        for b in range(NB):
+            for j in range(FARS):
+                listed = list_ref[b, j]
+                slot = b * FARS + j
+                if b == passed:
+                    passes = lax.div(listed, PLANE) == behind
+
+                    @pl.when(passes)
+                    def _():
+                        out_ref[slot] = arrived_ref[j]
+
+                    @pl.when(jnp.logical_not(passes))
+                    def _():
+                        out_ref[slot] = plane_ref[lax.rem(listed, PLANE)]
+                else:
+                    out_ref[slot] = plane_ref[lax.rem(listed, PLANE)]
+
+
+def pick(at, above, below, plane, low, high):
+    out = jax.ShapeDtypeStruct((SLOTS, BLK, 2 * DH), BF16)
     return pl.pallas_call(
         pick_kernel,
-        out_shape=jax.ShapeDtypeStruct((NX * SLOTS, BLK, 2 * DH), BF16),
-        in_specs=[SMEM] * (1 + NX) + [VMEM] * (1 + len(pieces)),
-        out_specs=VMEM,
-        scratch_shapes=[pltpu.VMEM((PLANE, BLK, 2 * DH), BF16)],
-        compiler_params=params(16),
+        out_shape=(out, out),
+        in_specs=[SMEM] * 3 + [VMEM] * 3,
+        out_specs=(VMEM, VMEM),
+        compiler_params=params(8),
         name="pick_far",
-    )(at, *lists, own, *pieces)
+    )(at, above, below, plane, low, high)
 
 
 def attend_kernel(
-    at_ref, far_ref, count_ref, q_ref, g_ref, prev_ref, own_ref, far_kv_ref,
+    at_ref, far_ref, count_ref, q_ref, g_ref, prev_ref, own_ref, plane_ref, below_ref, above_ref,
     qg_ref, win_ref, farg_ref, k_ref, v_ref, kt_ref, acc_ref, tri_ref,
 ):
     win_ref[...] = jnp.zeros_like(win_ref)
@@ -126,8 +159,11 @@
             v_ref[w * BLK : (w + 1) * BLK, :] = both[:, DH:]
         for j in range(FARS):
             slot = b * FARS + j
-            owner = lax.div(far_ref[b, j], PLANE)
-            both = far_kv_ref[owner * SLOTS + slot]
+            steps = lax.rem(lax.div(far_ref[b, j], PLANE) + (NX - lax.div(at_ref[0], NZ)), NX)
+            mine = plane_ref[lax.rem(far_ref[b, j], PLANE)]
+            from_below = (steps == NX - 1) | ((steps == 2) & (b == 0))
+            both = jnp.where(from_below, below_ref[slot], above_ref[slot])
+            both = jnp.where(steps == 0, mine, both)
             k_ref[(WIN + j) * BLK : (WIN + j + 1) * BLK, :] = both[:, :DH]
             v_ref[(WIN + j) * BLK : (WIN + j + 1) * BLK, :] = both[:, DH:]
         kt_ref[...] = k_ref[...].astype(F32).T.astype(BF16)
@@ -143,14 +179,19 @@
             q2 = jnp.concatenate([q_ref[rows, lo : lo + DH], q_ref[rows, lo + DH : lo + 2 * DH]])
             g2 = jnp.concatenate([g_ref[rows, lo : lo + DH], g_ref[rows, lo + DH : lo + 2 * DH]])
             scores = lax.dot_general(k_ref[...], q2, NT, preferred_element_type=F32)
-            parts = []
-            for c in range(WIN + FARS):
-                part = scores[c * BLK : (c + 1) * BLK, :]
-                bias = tri_ref[...] if biases[c] is None else biases[c]
-                parts.append(part + bias)
-            scores = jnp.concatenate(parts)
-            top = jnp.max(scores, axis=0, keepdims=True)
-            expo = jnp.exp2((scores - top) * EXP2_SCALE)
+            parts = [scores[c * BLK : (c + 1) * BLK, :] for c in range(WIN + FARS)]
+            parts[WIN - 1] = parts[WIN - 1] + tri_ref[...]
+            tops = [
+                jnp.max(part, axis=0, keepdims=True) + (0.0 if bias is None else bias)
+                for part, bias in zip(parts, biases)
+            ]
+            top = functools.reduce(jnp.maximum, tops)
+            expo = jnp.concatenate(
+                [
+                    jnp.exp2((part - (top if bias is None else top - bias)) * EXP2_SCALE)
+                    for part, bias in zip(parts, biases)
+                ]
+            )
             inv = 1.0 / jnp.sum(expo, axis=0, keepdims=True)
             soft = expo * inv
             grad_p = lax.dot_general(v_ref[...], g2, NT, preferred_element_type=F32)
@@ -169,10 +210,11 @@
             farg_ref[b * FARS + j] = acc_ref[(WIN + j) * BLK : (WIN + j + 1) * BLK, :].astype(BF16)
         return carry
 
-    lax.fori_loop(0, NB, block, 0)
-
-
-def attend(at, far, count, queries, out_grad, prev, own, far_kv):
+    for b in range(NB):
+        block(b, 0)
+
+
+def attend(at, far, count, queries, out_grad, prev, own, plane, below, above):
     keys = (WIN + FARS) * BLK
     return pl.pallas_call(
         attend_kernel,
@@ -181,7 +223,7 @@
             jax.ShapeDtypeStruct((2 * NB * BLK, 2 * DH), F32),
             jax.ShapeDtypeStruct((SLOTS, BLK, 2 * DH), BF16),
         ),
-        in_specs=[SMEM, SMEM, SMEM] + [VMEM] * 5,
+        in_specs=[SMEM, SMEM, SMEM] + [VMEM] * 7,
         out_specs=(VMEM, VMEM, VMEM),
         scratch_shapes=[
             pltpu.VMEM((keys, DH), BF16),
@@ -193,7 +235,7 @@
         compiler_params=params(24),
         cost_estimate=pl.CostEstimate(flops=2_400_000_000 * 4, bytes_accessed=6 << 20, transcendentals=2_000_000),
         name="attend",
-    )(at, far, count, queries, out_grad, prev, own, far_kv)
+    )(at, far, count, queries, out_grad, prev, own, plane, below, above)
 
 
 def spread_kernel(at_ref, *refs):
@@ -400,17 +442,19 @@
     weights = jnp.concatenate([key_weight.T, value_weight.T])
     weights = lax.all_gather(weights, "seq", axis=0, axis_index_groups=Z_GROUPS, tiled=True)
     prev_kv = shifted(own_kv, "seq", 1)
-    chosen = pick(at, lists, own_kv, plane)
-    far_kv = lax.all_to_all(chosen, "seq", 0, 0, axis_index_groups=X_GROUPS, tiled=True)
-
-    far_kv, inputs_x = lax.optimization_barrier((far_kv, inputs_x))
+    plane, low, high = pick_across(at, lists[2], own_kv, plane)
+    low, high = both_ways(low, high, "seq", X_UP)
+    up, down = pick(at, lists[1], lists[3], plane, low, high)
+    from_below, from_above = both_ways(up, down, "seq", X_UP)
+
+    far_count, inputs_x = lax.optimization_barrier((far_count, inputs_x))
     query_grad, window, far_grad = attend(
-        at, far_blocks, far_count, queries, out_grad, prev_kv, own_kv, far_kv
+        at, far_blocks, far_count, queries, out_grad, prev_kv, own_kv, plane, from_below, from_above
     )
     far_all = ring_gather(far_grad, "seq", X_UP, NX)
     back = shifted(window[:tokens].astype(BF16), "seq", -1)
-    dense = spread(at, lists, far_grad, far_all)
-    dense, weights = lax.optimization_barrier((dense, weights))
+    above, weights = lax.optimization_barrier((lists[1], weights))
+    dense = spread(at, [lists[0], above, *lists[2:]], far_grad, far_all)
     dense = dense.reshape(NZ, tokens, 2 * DH)
     terms = lax.all_to_all(dense, "seq", 0, 0, axis_index_groups=Z_GROUPS, tiled=True)
     kv_grad = finish(terms, back, window)
@@ -421,7 +465,6 @@
     heads = place_heads(own_index, moved, same_core, other_core)
 
     mine, above, low, high, below = input_terms(at, heads, weights)
-    heads, low, high = lax.optimization_barrier((heads, low, high))
     from_below, from_above = both_ways(low, high, "seq", X_UP)
     pieces = weight_terms(heads, inputs_x)
     pieces = lax.all_to_all(pieces, "seq", 0, 0, axis_index_groups=Z_GROUPS, tiled=True)

time: 206 us -> 203 us (0.985)
  waiting for transfers between devices: 91.5 us -> 87.3 us
    ppermute x10 -> x12, waiting for transfers between devices: 22.2 us -> 46.7 us  [both_ways(): lax.ppermute(upward, axis, pairs)]
    all_to_all x1 -> x0, waiting for transfers between devices: 20.3 us -> none  [local(): lax.all_to_all(chosen, 'seq', 0, 0, axis_index_groups=X_GROUPS, tiled=True)]
    ppermute x10 -> x12, waiting for transfers between devices: 15.3 us -> 1.45 us  [both_ways(): lax.ppermute(downward, axis, back)]
    ppermute x10 -> x12, starting transfers between devices: 29.1 us -> 36.3 us  [both_ways(): lax.ppermute(downward, axis, back)]
    ppermute x1, starting transfers between devices: 11.5 us -> 7.05 us  [local(): lax.ppermute(jnp.concatenate([moved, *same_core]), 'own', CORES)]
    all_to_all x1 -> x0, starting transfers between devices: 3.75 us -> none  [local(): lax.all_to_all(chosen, 'seq', 0, 0, axis_index_groups=X_GROUPS, tiled=True)]
    all_to_all x1, waiting for transfers between devices: 2.1 us -> 5.31 us  [local(): lax.all_to_all(dense, 'seq', 0, 0, axis_index_groups=Z_GROUPS, tiled=True)]
    ppermute x10 -> x12, starting transfers between devices: 10.4 us -> 10.9 us  [both_ways(): lax.ppermute(upward, axis, pairs)]
  transfers between devices with their start and end apart: 32 -> 35, of which waited for: 16 -> 20; matrix products, arithmetic and copies ran while one was open for 1% -> 1% of each run, Pallas kernels for 7% -> 6%
where the time goes in v7:
time: 203 us
  waiting for transfers between devices  87.3 us (43%)
  starting transfers between devices  75.6 us (37%)
  Pallas kernels  19.1 us (9%)
  between operations  14.4 us (7%)
  local copies, waits for them, and re-layouts  3.59 us (2%)
  other arithmetic  2.8 us (1%)
    ppermute x12, waiting for transfers between devices, both_ways(): lax.ppermute(upward, axis, pairs)  46.7 us
    ppermute x12, starting transfers between devices, both_ways(): lax.ppermute(downward, axis, back)  36.3 us
    ppermute x2, waiting for transfers between devices, shifted(): lax.ppermute(value, axis, [(source, source + steps) for source in range(l...  20.2 us
    ppermute x12, starting transfers between devices, both_ways(): lax.ppermute(upward, axis, pairs)  10.9 us
    pallas_call x1, Pallas kernels, attend(): pl.pallas_call(attend_kernel, out_shape=(jax.ShapeDtypeStruct((NB * BLK,...  9.68 us
    ppermute x1, starting transfers between devices, local(): lax.ppermute(jnp.concatenate([moved, *same_core]), 'own', CORES)  7.05 us
    ppermute x3, starting transfers between devices, local(): arrived = lax.ppermute(listed, 'seq', pairs)  6.16 us
    ppermute x3, waiting for transfers between devices, local(): arrived = lax.ppermute(listed, 'seq', pairs)  5.99 us
  transfers between devices with their start and end apart: 35, of which 20 were waited for; matrix products, arithmetic and copies ran while one was open for 1% of the time, Pallas kernels for 6%

profile of v7, /device:TPU:1, one launch (start us, length us, event | category | flops | bytes accessed | tf_op | source)
XLA Modules:
  0.0 202.7 jit_solution(18337437585160819390)
XLA Ops:
  11.4 4.0 %collective-permute-start.3 = (bf16[2,128,256]{2,1,0:T(8,128)(2,1)S(1)}, bf16[2,128,256]{2,1,0:T(8,128)(2,1)S(1)}, u32[]{:S(2)}, u32[]{:S(2)}) collective-permute-start(bf16[2,128,256]{2,1,0:T(8,128)(2,1)S(1)} %bitcast.9), channel_id=1, source_target_pairs={{8,0},{16,8},{24,16},{32,24},{40,32},{48,40},{56,48},{0,56},{72,64... | collective-permute-start | bytes 393224 | tf_op jit(solution)/shard_map/ppermute | solution.py:59
  18.9 2.7 %collective-permute-start.6 = (bf16[2,128,256]{2,1,0:T(8,128)(2,1)S(1)}, bf16[2,128,256]{2,1,0:T(8,128)(2,1)S(1)}, u32[]{:S(2)}, u32[]{:S(2)}) collective-permute-start(bf16[2,128,256]{2,1,0:T(8,128)(2,1)S(1)} %collective-permute-done.3.refs_1_), channel_id=1, source_target_pairs={{8,0},{16,8},{24,16},{32,24},{40,32},{48,40},{56,48},{0,56},{72,64... | collective-permute-start | bytes 393224 | tf_op jit(solution)/shard_map/ppermute | solution.py:59
  25.7 2.7 %collective-permute-start.9 = (bf16[2,128,256]{2,1,0:T(8,128)(2,1)S(1)}, bf16[2,128,256]{2,1,0:T(8,128)(2,1)S(1)}, u32[]{:S(2)}, u32[]{:S(2)}) collective-permute-start(bf16[2,128,256]{2,1,0:T(8,128)(2,1)S(1)} %collective-permute-done.6.refs_3_), channel_id=1, source_target_pairs={{8,0},{16,8},{24,16},{32,24},{40,32},{48,40},{56,48},{0,56},{72,64... | collective-permute-start | bytes 393224 | tf_op jit(solution)/shard_map/ppermute | solution.py:59
  29.6 3.4 %collective-permute-done.7.below_ref.refs_3_ = s32[2,4]{1,0:T(2,128)S(1)} collective-permute-done((s32[2,4]{1,0:T(2,128)}, s32[2,4]{1,0:T(2,128)S(1)}, u32[]{:S(2)}, u32[]{:S(2)}) %collective-permute-start.7) | collective-permute-done | bytes 64 | tf_op jit(solution)/shard_map/ppermute | solution.py:431
  41.2 9.4 %collective-permute-done.12.low_ref = bf16[4,128,256]{2,1,0:T(8,128)(2,1)S(1)} collective-permute-done((bf16[4,128,256]{2,1,0:T(8,128)(2,1)S(1)}, bf16[4,128,256]{2,1,0:T(8,128)(2,1)S(1)}, u32[]{:S(2)}, u32[]{:S(2)}) %collective-permute-start.12) | collective-permute-done | bytes 262176 | tf_op jit(solution)/shard_map/ppermute | solution.py:59
  55.5 3.3 %collective-permute-start = (bf16[2,128,256]{2,1,0:T(8,128)(2,1)S(1)}, bf16[2,128,256]{2,1,0:T(8,128)(2,1)S(1)}, u32[]{:S(2)}, u32[]{:S(2)}) collective-permute-start(bf16[2,128,256]{2,1,0:T(8,128)(2,1)S(1)} %bitcast.11), channel_id=1, source_target_pairs={{0,8},{8,16},{16,24},{24,32},{32,40},{40,48},{48,56},{56,64},{64,7... | collective-permute-start | bytes 393224 | tf_op jit(solution)/shard_map/ppermute | solution.py:54
  60.6 4.0 %collective-permute-done.14.below_ref = bf16[8,128,256]{2,1,0:T(8,128)(2,1)S(1)} collective-permute-done((bf16[8,128,256]{2,1,0:T(8,128)(2,1)}, bf16[8,128,256]{2,1,0:T(8,128)(2,1)S(1)}, u32[]{:S(2)}, u32[]{:S(2)}) %collective-permute-start.14) | collective-permute-done | bytes 524320 | tf_op jit(solution)/shard_map/ppermute | solution.py:59
  66.5 9.7 %attend.1 = (bf16[256,1024]{1,0:T(8,128)(2,1)}, f32[512,256]{1,0:T(8,128)S(1)}, bf16[8,128,256]{2,1,0:T(8,128)(2,1)S(1)}) custom-call(s32[1]{0:T(128)} %bitcast.at_ref, s32[2,4]{1,0:T(2,128)S(1)} %copy-done.1, s32[2]{0:T(128)S(1)} %copy-done.7, bf16[256,1024]{1,0:T(8,128)(2,1)S(1)} %copy-done.3, bf16[256,1024]{1,0:T(8,128)(2,1)S(1)} %copy-done.4, ...), custom_call_target="tpu_custom_call" | custom-call | flops 9600000000 | bytes 6291456 | tf_op jit(solution)/shard_map/attend/pallas_call | solution.py:219
  78.8 8.6 %collective-permute-done.16.refs_5_ = bf16[8,128,256]{2,1,0:T(8,128)(2,1)S(1)} collective-permute-done((bf16[8,128,256]{2,1,0:T(8,128)(2,1)S(1)}, bf16[8,128,256]{2,1,0:T(8,128)(2,1)S(1)}, u32[]{:S(2)}, u32[]{:S(2)}) %collective-permute-start.16) | collective-permute-done | bytes 524320 | tf_op jit(solution)/shard_map/ppermute | solution.py:59
  87.6 2.7 %collective-permute-start.19 = (bf16[4,128,256]{2,1,0:T(8,128)(2,1)S(1)}, bf16[4,128,256]{2,1,0:T(8,128)(2,1)S(1)}, u32[]{:S(2)}, u32[]{:S(2)}) collective-permute-start(bf16[4,128,256]{2,1,0:T(8,128)(2,1)S(1)} %slice.46), channel_id=1, source_target_pairs={{64,0},{72,8},{80,16},{88,24},{96,32},{104,40},{112,48},{120,56},{... | collective-permute-start | bytes 786440 | tf_op jit(solution)/shard_map/ppermute | solution.py:59
  90.6 3.8 %collective-permute-done.18.refs_7_ = bf16[4,128,256]{2,1,0:T(8,128)(2,1)S(1)} collective-permute-done((bf16[4,128,256]{2,1,0:T(8,128)(2,1)S(1)}, bf16[4,128,256]{2,1,0:T(8,128)(2,1)S(1)}, u32[]{:S(2)}, u32[]{:S(2)}) %collective-permute-start.18) | collective-permute-done | bytes 262176 | tf_op jit(solution)/shard_map/ppermute | solution.py:59
  96.9 5.5 %all-to-all-start = ((bf16[8,256,256]{2,1,0:T(8,128)(2,1)}), bf16[8,256,256]{2,1,0:T(8,128)(2,1)S(1)}, u32[]{:S(2)}, u32[]{:S(2)}) async-start(bf16[8,256,256]{2,1,0:T(8,128)(2,1)} %bitcast.5), calls=%async_computation | async-start | bytes 2097152 | tf_op jit(solution)/shard_map/all_to_all | solution.py:459
  103.7 18.5 %collective-permute-done.20.back_ref = bf16[256,256]{1,0:T(8,128)(2,1)S(1)} collective-permute-done((bf16[256,256]{1,0:T(8,128)(2,1)S(1)}, bf16[256,256]{1,0:T(8,128)(2,1)S(1)}, u32[]{:S(2)}, u32[]{:S(2)}) %collective-permute-start.20) | collective-permute-done | bytes 131104 | tf_op jit(solution)/shard_map/ppermute | solution.py:54
  122.2 5.3 %all-to-all-done.terms_ref = bf16[8,256,256]{2,1,0:T(8,128)(2,1)S(1)} async-done(((bf16[8,256,256]{2,1,0:T(8,128)(2,1)}), bf16[8,256,256]{2,1,0:T(8,128)(2,1)S(1)}, u32[]{:S(2)}, u32[]{:S(2)}) %all-to-all-start) | async-done | bytes 1048608 | tf_op jit(solution)/shard_map/all_to_all | solution.py:459
  128.5 7.3 %collective-permute-start.22 = (bf16[256,256]{1,0:T(8,128)(2,1)S(1)}, bf16[256,256]{1,0:T(8,128)(2,1)S(1)}, u32[]{:S(2)}, u32[]{:S(2)}) collective-permute-start(bf16[256,256]{1,0:T(8,128)(2,1)S(1)} %collective-permute-done.21.own_ref), channel_id=1, source_target_pairs={{0,2},{1,3},{2,4},{3,5},{4,6},{5,7},{6,0},{7,1},{8,10},{9,11},{10,... | collective-permute-start | bytes 393224 | tf_op jit(solution)/shard_map/ppermute | solution.py:59
  135.8 5.5 %collective-permute-start.23 = (bf16[256,256]{1,0:T(8,128)(2,1)S(1)}, bf16[256,256]{1,0:T(8,128)(2,1)S(1)}, u32[]{:S(2)}, u32[]{:S(2)}) collective-permute-start(bf16[256,256]{1,0:T(8,128)(2,1)S(1)} %collective-permute-done.21.own_ref), channel_id=1, source_target_pairs={{2,0},{3,1},{4,2},{5,3},{6,4},{7,5},{0,6},{1,7},{10,8},{11,9},{12,... | collective-permute-start | bytes 393224 | tf_op jit(solution)/shard_map/ppermute | solution.py:59
  144.2 3.1 %collective-permute-start.25 = (bf16[128,256]{1,0:T(8,128)(2,1)S(1)}, bf16[128,256]{1,0:T(8,128)(2,1)S(1)}, u32[]{:S(2)}, u32[]{:S(2)}) collective-permute-start(bf16[128,256]{1,0:T(8,128)(2,1)S(1)} %slice.49), channel_id=1, source_target_pairs={{2,0},{3,1},{4,2},{5,3},{6,4},{7,5},{0,6},{1,7},{10,8},{11,9},{12,... | collective-permute-start | bytes 196616 | tf_op jit(solution)/shard_map/ppermute | solution.py:59
  148.9 7.0 %collective-permute-start.26 = (bf16[1024,256]{1,0:T(8,128)(2,1)S(1)}, bf16[1024,256]{1,0:T(8,128)(2,1)S(1)}, u32[]{:S(2)}, u32[]{:S(2)}) collective-permute-start(bf16[1024,256]{1,0:T(8,128)(2,1)S(1)} %constant_dynamic-update-slice_fusion), channel_id=1, source_target_pairs={{0,1},{1,0},{2,3},{3,2},{4,5},{5,4},{6,7},{7,6},{8,9},{9,8},{10,11... | collective-permute-start | bytes 1572872 | tf_op jit(solution)/shard_map/ppermute | solution.py:464
  161.5 4.3 %all-to-all-start.1 = ((bf16[8,256,256]{2,1,0:T(8,128)(2,1)}), bf16[8,256,256]{2,1,0:T(8,128)(2,1)S(1)}, u32[]{:S(2)}, u32[]{:S(2)}) async-start(bf16[8,256,256]{2,1,0:T(8,128)(2,1)} %weight_terms.1), calls=%async_computation.1 | async-start | bytes 2097152 | tf_op jit(solution)/shard_map/all_to_all | solution.py:470
  167.2 2.7 %collective-permute-start.29 = (bf16[128,1024]{1,0:T(8,128)(2,1)S(1)}, bf16[128,1024]{1,0:T(8,128)(2,1)S(1)}, u32[]{:S(2)}, u32[]{:S(2)}) collective-permute-start(bf16[128,1024]{1,0:T(8,128)(2,1)S(1)} %get-tuple-element.66), channel_id=1, source_target_pairs={{64,0},{72,8},{80,16},{88,24},{96,32},{104,40},{112,48},{120,56},{... | collective-permute-start | bytes 786440 | tf_op jit(solution)/shard_map/ppermute | solution.py:59
  169.9 5.6 %collective-permute-done.27 = bf16[128,1024]{1,0:T(8,128)(2,1)S(1)} collective-permute-done((bf16[128,1024]{1,0:T(8,128)(2,1)S(1)}, bf16[128,1024]{1,0:T(8,128)(2,1)S(1)}, u32[]{:S(2)}, u32[]{:S(2)}) %collective-permute-start.27) | collective-permute-done | bytes 262176 | tf_op jit(solution)/shard_map/ppermute | solution.py:59
  175.9 2.7 %collective-permute-start.30 = (bf16[256,1024]{1,0:T(8,128)(2,1)S(1)}, bf16[256,1024]{1,0:T(8,128)(2,1)S(1)}, u32[]{:S(2)}, u32[]{:S(2)}) collective-permute-start(bf16[256,1024]{1,0:T(8,128)(2,1)S(1)} %pad_maximum_fusion.1), channel_id=1, source_target_pairs={{64,0},{72,8},{80,16},{88,24},{96,32},{104,40},{112,48},{120,56},{... | collective-permute-start | bytes 1572872 | tf_op jit(solution)/shard_map/ppermute | solution.py:59
  178.6 10.2 %collective-permute-done.28 = bf16[256,1024]{1,0:T(8,128)(2,1)S(1)} collective-permute-done((bf16[256,1024]{1,0:T(8,128)(2,1)S(1)}, bf16[256,1024]{1,0:T(8,128)(2,1)S(1)}, u32[]{:S(2)}, u32[]{:S(2)}) %collective-permute-start.28) | collective-permute-done | bytes 524320 | tf_op jit(solution)/shard_map/ppermute | solution.py:59
  189.9 5.2 %all-to-all-done.1.terms_ref = bf16[8,256,256]{2,1,0:T(8,128)(2,1)S(1)} async-done(((bf16[8,256,256]{2,1,0:T(8,128)(2,1)}), bf16[8,256,256]{2,1,0:T(8,128)(2,1)S(1)}, u32[]{:S(2)}, u32[]{:S(2)}) %all-to-all-start.1) | async-done | bytes 1048608 | tf_op jit(solution)/shard_map/all_to_all | solution.py:470
  (98 shorter events, 51.0 us)
Async XLA Ops:
  7.2 51.7 %all-gather.3.cloned.1.call-start = ((), (), s32[]{:S(2)}) async-start(), calls=%async_computation.2 | async-start | bytes 2621440 | tf_op jit(solution)/shard_map/all_gather | solution.py:421
  8.0 82.6 %all-gather.5.cloned.1.call-start = ((), (), s32[]{:S(2)}) async-start(), calls=%async_computation.3 | async-start | bytes 1179648 | tf_op jit(solution)/shard_map/all_gather | solution.py:443
  8.9 10.0 %collective-permute-start.2 = (bf16[2,128,256]{2,1,0:T(8,128)(2,1)S(1)}, bf16[2,128,256]{2,1,0:T(8,128)(2,1)S(1)}, u32[]{:S(2)}, u32[]{:S(2)}) collective-permute-start(bf16[2,128,256]{2,1,0:T(8,128)(2,1)S(1)} %bitcast.8), channel_id=1, source_target_pairs={{0,8},{8,16},{16,24},{24,32},{32,40},{40,48},{48,56},{56,0},{64,72... | collective-permute-start | bytes 393224 | tf_op jit(solution)/shard_map/ppermute | solution.py:59
  11.4 7.5 %collective-permute-start.3 = (bf16[2,128,256]{2,1,0:T(8,128)(2,1)S(1)}, bf16[2,128,256]{2,1,0:T(8,128)(2,1)S(1)}, u32[]{:S(2)}, u32[]{:S(2)}) collective-permute-start(bf16[2,128,256]{2,1,0:T(8,128)(2,1)S(1)} %bitcast.9), channel_id=1, source_target_pairs={{8,0},{16,8},{24,16},{32,24},{40,32},{48,40},{56,48},{0,56},{72,64... | collective-permute-start | bytes 393224 | tf_op jit(solution)/shard_map/ppermute | solution.py:59
  18.9 6.8 %collective-permute-start.5 = (bf16[2,128,256]{2,1,0:T(8,128)(2,1)S(1)}, bf16[2,128,256]{2,1,0:T(8,128)(2,1)S(1)}, u32[]{:S(2)}, u32[]{:S(2)}) collective-permute-start(bf16[2,128,256]{2,1,0:T(8,128)(2,1)S(1)} %collective-permute-done.2.refs_0_), channel_id=1, source_target_pairs={{0,8},{8,16},{16,24},{24,32},{32,40},{40,48},{48,56},{56,0},{64,72... | collective-permute-start | bytes 393224 | tf_op jit(solution)/shard_map/ppermute | solution.py:59
  25.7 7.3 %collective-permute-start.8 = (bf16[2,128,256]{2,1,0:T(8,128)(2,1)S(1)}, bf16[2,128,256]{2,1,0:T(8,128)(2,1)S(1)}, u32[]{:S(2)}, u32[]{:S(2)}) collective-permute-start(bf16[2,128,256]{2,1,0:T(8,128)(2,1)S(1)} %collective-permute-done.5.refs_2_), channel_id=1, source_target_pairs={{0,8},{8,16},{16,24},{24,32},{32,40},{40,48},{48,56},{56,0},{64,72... | collective-permute-start | bytes 393224 | tf_op jit(solution)/shard_map/ppermute | solution.py:59
  25.7 7.3 %collective-permute-start.9 = (bf16[2,128,256]{2,1,0:T(8,128)(2,1)S(1)}, bf16[2,128,256]{2,1,0:T(8,128)(2,1)S(1)}, u32[]{:S(2)}, u32[]{:S(2)}) collective-permute-start(bf16[2,128,256]{2,1,0:T(8,128)(2,1)S(1)} %collective-permute-done.6.refs_3_), channel_id=1, source_target_pairs={{8,0},{16,8},{24,16},{32,24},{40,32},{48,40},{56,48},{0,56},{72,64... | collective-permute-start | bytes 393224 | tf_op jit(solution)/shard_map/ppermute | solution.py:59
  38.5 12.1 %collective-permute-start.12 = (bf16[4,128,256]{2,1,0:T(8,128)(2,1)S(1)}, bf16[4,128,256]{2,1,0:T(8,128)(2,1)S(1)}, u32[]{:S(2)}, u32[]{:S(2)}) collective-permute-start(bf16[4,128,256]{2,1,0:T(8,128)(2,1)S(1)} %get-tuple-element.51), channel_id=1, source_target_pairs={{0,64},{8,72},{16,80},{24,88},{32,96},{40,104},{48,112},{56,120},{... | collective-permute-start | bytes 786440 | tf_op jit(solution)/shard_map/ppermute | solution.py:59
  38.6 12.0 %collective-permute-start.13 = (bf16[4,128,256]{2,1,0:T(8,128)(2,1)S(1)}, bf16[4,128,256]{2,1,0:T(8,128)(2,1)S(1)}, u32[]{:S(2)}, u32[]{:S(2)}) collective-permute-start(bf16[4,128,256]{2,1,0:T(8,128)(2,1)S(1)} %get-tuple-element.52), channel_id=1, source_target_pairs={{64,0},{72,8},{80,16},{88,24},{96,32},{104,40},{112,48},{120,56},{... | collective-permute-start | bytes 786440 | tf_op jit(solution)/shard_map/ppermute | solution.py:59
  52.2 12.5 %collective-permute-start.14 = (bf16[8,128,256]{2,1,0:T(8,128)(2,1)}, bf16[8,128,256]{2,1,0:T(8,128)(2,1)S(1)}, u32[]{:S(2)}, u32[]{:S(2)}) collective-permute-start(bf16[8,128,256]{2,1,0:T(8,128)(2,1)} %get-tuple-element.53), channel_id=1, source_target_pairs={{0,64},{8,72},{16,80},{24,88},{32,96},{40,104},{48,112},{56,120},{... | collective-permute-start | bytes 1572872 | tf_op jit(solution)/shard_map/ppermute | solution.py:59
  52.3 13.1 %collective-permute-start.15 = (bf16[8,128,256]{2,1,0:T(8,128)(2,1)S(1)}, bf16[8,128,256]{2,1,0:T(8,128)(2,1)}, u32[]{:S(2)}, u32[]{:S(2)}) collective-permute-start(bf16[8,128,256]{2,1,0:T(8,128)(2,1)S(1)} %get-tuple-element.54), channel_id=1, source_target_pairs={{64,0},{72,8},{80,16},{88,24},{96,32},{104,40},{112,48},{120,56},{... | collective-permute-start | bytes 1572872 | tf_op jit(solution)/shard_map/ppermute | solution.py:59
  76.2 11.3 %collective-permute-start.16 = (bf16[8,128,256]{2,1,0:T(8,128)(2,1)S(1)}, bf16[8,128,256]{2,1,0:T(8,128)(2,1)S(1)}, u32[]{:S(2)}, u32[]{:S(2)}) collective-permute-start(bf16[8,128,256]{2,1,0:T(8,128)(2,1)S(1)} %get-tuple-element.59.refs_4_), channel_id=1, source_target_pairs={{0,64},{8,72},{16,80},{24,88},{32,96},{40,104},{48,112},{56,120},{... | collective-permute-start | bytes 1572872 | tf_op jit(solution)/shard_map/ppermute | solution.py:59
  76.5 11.1 %collective-permute-start.17 = (bf16[8,128,256]{2,1,0:T(8,128)(2,1)S(1)}, bf16[8,128,256]{2,1,0:T(8,128)(2,1)S(1)}, u32[]{:S(2)}, u32[]{:S(2)}) collective-permute-start(bf16[8,128,256]{2,1,0:T(8,128)(2,1)S(1)} %get-tuple-element.59.refs_4_), channel_id=1, source_target_pairs={{64,0},{72,8},{80,16},{88,24},{96,32},{104,40},{112,48},{120,56},{... | collective-permute-start | bytes 1572872 | tf_op jit(solution)/shard_map/ppermute | solution.py:59
  87.5 6.9 %collective-permute-start.18 = (bf16[4,128,256]{2,1,0:T(8,128)(2,1)S(1)}, bf16[4,128,256]{2,1,0:T(8,128)(2,1)S(1)}, u32[]{:S(2)}, u32[]{:S(2)}) collective-permute-start(bf16[4,128,256]{2,1,0:T(8,128)(2,1)S(1)} %slice.45), channel_id=1, source_target_pairs={{0,64},{8,72},{16,80},{24,88},{32,96},{40,104},{48,112},{56,120},{... | collective-permute-start | bytes 786440 | tf_op jit(solution)/shard_map/ppermute | solution.py:59
  96.9 30.6 %all-to-all-start = ((bf16[8,256,256]{2,1,0:T(8,128)(2,1)}), bf16[8,256,256]{2,1,0:T(8,128)(2,1)S(1)}, u32[]{:S(2)}, u32[]{:S(2)}) async-start(bf16[8,256,256]{2,1,0:T(8,128)(2,1)} %bitcast.5), calls=%async_computation | async-start | bytes 2097152 | tf_op jit(solution)/shard_map/all_to_all | solution.py:459
  102.4 19.8 %collective-permute-start.20 = (bf16[256,256]{1,0:T(8,128)(2,1)S(1)}, bf16[256,256]{1,0:T(8,128)(2,1)S(1)}, u32[]{:S(2)}, u32[]{:S(2)}) collective-permute-start(bf16[256,256]{1,0:T(8,128)(2,1)S(1)} %slice.53), channel_id=1, source_target_pairs={{8,0},{16,8},{24,16},{32,24},{40,32},{48,40},{56,48},{64,56},{72,6... | collective-permute-start | bytes 393224 | tf_op jit(solution)/shard_map/ppermute | solution.py:54
  128.5 15.2 %collective-permute-start.22 = (bf16[256,256]{1,0:T(8,128)(2,1)S(1)}, bf16[256,256]{1,0:T(8,128)(2,1)S(1)}, u32[]{:S(2)}, u32[]{:S(2)}) collective-permute-start(bf16[256,256]{1,0:T(8,128)(2,1)S(1)} %collective-permute-done.21.own_ref), channel_id=1, source_target_pairs={{0,2},{1,3},{2,4},{3,5},{4,6},{5,7},{6,0},{7,1},{8,10},{9,11},{10,... | collective-permute-start | bytes 393224 | tf_op jit(solution)/shard_map/ppermute | solution.py:59
  135.8 8.4 %collective-permute-start.23 = (bf16[256,256]{1,0:T(8,128)(2,1)S(1)}, bf16[256,256]{1,0:T(8,128)(2,1)S(1)}, u32[]{:S(2)}, u32[]{:S(2)}) collective-permute-start(bf16[256,256]{1,0:T(8,128)(2,1)S(1)} %collective-permute-done.21.own_ref), channel_id=1, source_target_pairs={{2,0},{3,1},{4,2},{5,3},{6,4},{7,5},{0,6},{1,7},{10,8},{11,9},{12,... | collective-permute-start | bytes 393224 | tf_op jit(solution)/shard_map/ppermute | solution.py:59
  148.9 8.6 %collective-permute-start.26 = (bf16[1024,256]{1,0:T(8,128)(2,1)S(1)}, bf16[1024,256]{1,0:T(8,128)(2,1)S(1)}, u32[]{:S(2)}, u32[]{:S(2)}) collective-permute-start(bf16[1024,256]{1,0:T(8,128)(2,1)S(1)} %constant_dynamic-update-slice_fusion), channel_id=1, source_target_pairs={{0,1},{1,0},{2,3},{3,2},{4,5},{5,4},{6,7},{7,6},{8,9},{9,8},{10,11... | collective-permute-start | bytes 1572872 | tf_op jit(solution)/shard_map/ppermute | solution.py:464
  161.5 33.6 %all-to-all-start.1 = ((bf16[8,256,256]{2,1,0:T(8,128)(2,1)}), bf16[8,256,256]{2,1,0:T(8,128)(2,1)S(1)}, u32[]{:S(2)}, u32[]{:S(2)}) async-start(bf16[8,256,256]{2,1,0:T(8,128)(2,1)} %weight_terms.1), calls=%async_computation.1 | async-start | bytes 2097152 | tf_op jit(solution)/shard_map/all_to_all | solution.py:470
  167.1 8.5 %collective-permute-start.27 = (bf16[128,1024]{1,0:T(8,128)(2,1)S(1)}, bf16[128,1024]{1,0:T(8,128)(2,1)S(1)}, u32[]{:S(2)}, u32[]{:S(2)}) collective-permute-start(bf16[128,1024]{1,0:T(8,128)(2,1)S(1)} %get-tuple-element.64), channel_id=1, source_target_pairs={{0,64},{8,72},{16,80},{24,88},{32,96},{40,104},{48,112},{56,120},{... | collective-permute-start | bytes 786440 | tf_op jit(solution)/shard_map/ppermute | solution.py:59
  167.2 8.6 %collective-permute-start.29 = (bf16[128,1024]{1,0:T(8,128)(2,1)S(1)}, bf16[128,1024]{1,0:T(8,128)(2,1)S(1)}, u32[]{:S(2)}, u32[]{:S(2)}) collective-permute-start(bf16[128,1024]{1,0:T(8,128)(2,1)S(1)} %get-tuple-element.66), channel_id=1, source_target_pairs={{64,0},{72,8},{80,16},{88,24},{96,32},{104,40},{112,48},{120,56},{... | collective-permute-start | bytes 786440 | tf_op jit(solution)/shard_map/ppermute | solution.py:59
  175.7 13.2 %collective-permute-start.28 = (bf16[256,1024]{1,0:T(8,128)(2,1)S(1)}, bf16[256,1024]{1,0:T(8,128)(2,1)S(1)}, u32[]{:S(2)}, u32[]{:S(2)}) collective-permute-start(bf16[256,1024]{1,0:T(8,128)(2,1)S(1)} %pad_maximum_fusion), channel_id=1, source_target_pairs={{0,64},{8,72},{16,80},{24,88},{32,96},{40,104},{48,112},{56,120},{... | collective-permute-start | bytes 1572872 | tf_op jit(solution)/shard_map/ppermute | solution.py:59
  175.9 13.0 %collective-permute-start.30 = (bf16[256,1024]{1,0:T(8,128)(2,1)S(1)}, bf16[256,1024]{1,0:T(8,128)(2,1)S(1)}, u32[]{:S(2)}, u32[]{:S(2)}) collective-permute-start(bf16[256,1024]{1,0:T(8,128)(2,1)S(1)} %pad_maximum_fusion.1), channel_id=1, source_target_pairs={{64,0},{72,8},{80,16},{88,24},{96,32},{104,40},{112,48},{120,56},{... | collective-permute-start | bytes 1572872 | tf_op jit(solution)/shard_map/ppermute | solution.py:59
  (21 other events, 388.3 us)
Sparse Core Ops, SparseCore 0:
  9.9 39.4 all-gather.2
  55.7 34.9 all-gather.4

commit v8 on v7

--- a/solution.py
+++ b/solution.py
@@ -39,6 +39,7 @@
 
 SMEM = pl.BlockSpec(memory_space=pltpu.SMEM)
 VMEM = pl.BlockSpec(memory_space=pltpu.VMEM)
+HBM = pl.BlockSpec(memory_space=pltpu.HBM)
 NT = (((1,), (1,)), ((), ()))
 F32 = jnp.float32
 BF16 = jnp.bfloat16
@@ -143,8 +144,23 @@
 
 def attend_kernel(
     at_ref, far_ref, count_ref, q_ref, g_ref, prev_ref, own_ref, plane_ref, below_ref, above_ref,
-    qg_ref, win_ref, farg_ref, k_ref, v_ref, kt_ref, acc_ref, tri_ref,
+    qg_ref, win_ref, farg_ref, k_ref, v_ref, kt_ref, acc_ref, tri_ref, got_ref, sems,
 ):
+    places = []
+    for slot in range(SLOTS):
+        listed = far_ref[slot // FARS, slot % FARS]
+        steps = lax.rem(lax.div(listed, PLANE) + (NX - lax.div(at_ref[0], NZ)), NX)
+        upward = (steps == NX - 1) | (steps == 2) if slot < FARS else steps == NX - 1
+        places.append((steps == 0, lax.rem(listed, PLANE)))
+        for here, source in (
+            (upward, below_ref),
+            (jnp.logical_not(upward | (steps == 0)), above_ref),
+        ):
+
+            @pl.when(here)
+            def _():
+                pltpu.make_async_copy(source.at[slot], got_ref.at[slot], sems.at[slot]).start()
+
     win_ref[...] = jnp.zeros_like(win_ref)
     key_at = lax.broadcasted_iota(jnp.int32, (BLK, 2 * BLK), 0)
     query_at = lax.broadcasted_iota(jnp.int32, (BLK, 2 * BLK), 1) % BLK
@@ -159,11 +175,17 @@
             v_ref[w * BLK : (w + 1) * BLK, :] = both[:, DH:]
         for j in range(FARS):
             slot = b * FARS + j
-            steps = lax.rem(lax.div(far_ref[b, j], PLANE) + (NX - lax.div(at_ref[0], NZ)), NX)
-            mine = plane_ref[lax.rem(far_ref[b, j], PLANE)]
-            from_below = (steps == NX - 1) | ((steps == 2) & (b == 0))
-            both = jnp.where(from_below, below_ref[slot], above_ref[slot])
-            both = jnp.where(steps == 0, mine, both)
+            mine, row = places[slot]
+
+            @pl.when(mine)
+            def _():
+                got_ref[slot] = plane_ref[row]
+
+            @pl.when(jnp.logical_not(mine))
+            def _():
+                pltpu.make_async_copy(below_ref.at[slot], got_ref.at[slot], sems.at[slot]).wait()
+
+            both = got_ref[slot]
             k_ref[(WIN + j) * BLK : (WIN + j + 1) * BLK, :] = both[:, :DH]
             v_ref[(WIN + j) * BLK : (WIN + j + 1) * BLK, :] = both[:, DH:]
         kt_ref[...] = k_ref[...].astype(F32).T.astype(BF16)
@@ -223,7 +245,7 @@
             jax.ShapeDtypeStruct((2 * NB * BLK, 2 * DH), F32),
             jax.ShapeDtypeStruct((SLOTS, BLK, 2 * DH), BF16),
         ),
-        in_specs=[SMEM, SMEM, SMEM] + [VMEM] * 7,
+        in_specs=[SMEM, SMEM, SMEM] + [VMEM] * 5 + [HBM] * 2,
         out_specs=(VMEM, VMEM, VMEM),
         scratch_shapes=[
             pltpu.VMEM((keys, DH), BF16),
@@ -231,6 +253,8 @@
             pltpu.VMEM((DH, keys), BF16),
             pltpu.VMEM((keys, 2 * DH), F32),
             pltpu.VMEM((BLK, 2 * BLK), F32),
+            pltpu.VMEM((SLOTS, BLK, 2 * DH), BF16),
+            pltpu.SemaphoreType.DMA((SLOTS,)),
         ],
         compiler_params=params(24),
         cost_estimate=pl.CostEstimate(flops=2_400_000_000 * 4, bytes_accessed=6 << 20, transcendentals=2_000_000),
@@ -323,28 +347,42 @@
     )(at, own, *pieces, other)
 
 
-def weights_kernel(grad_ref, inputs_ref, out_ref):
-    quarters, wide = 4, inputs_ref.shape[1] // 4
-    for head in range(2):
-        grad = jnp.concatenate([grad_ref[x * 2 + head] for x in range(NX)])
-        term = lax.dot_general(
-            grad, inputs_ref[...], (((0,), (0,)), ((), ())), preferred_element_type=F32
-        ).astype(BF16)
-        for part in range(4):
-            for quarter in range(quarters):
-                out_ref[
-                    head * 4 + part, quarter * 2 * PART : (quarter + 1) * 2 * PART, :
-                ] = term[
-                    part * 2 * PART : (part + 1) * 2 * PART, quarter * wide : (quarter + 1) * wide
-                ]
+def weights_kernel(grad_ref, inputs_ref, out_ref, quarters_ref, sems):
+    wide = quarters_ref.shape[2]
+    copies = [
+        pltpu.make_async_copy(
+            inputs_ref.at[:, pl.ds(quarter * wide, wide)], quarters_ref.at[quarter], sems.at[quarter]
+        )
+        for quarter in range(4)
+    ]
+    for copy in copies:
+        copy.start()
+    grads = [jnp.concatenate([grad_ref[x * 2 + head] for x in range(NX)]) for head in range(2)]
+    for quarter in range(4):
+        copies[quarter].wait()
+        rows = slice(quarter * 2 * PART, (quarter + 1) * 2 * PART)
+        for head in range(2):
+            term = lax.dot_general(
+                grads[head],
+                quarters_ref[quarter],
+                (((0,), (0,)), ((), ())),
+                preferred_element_type=F32,
+            ).astype(BF16)
+            for part in range(4):
+                out_ref[head * 4 + part, rows, :] = term[part * 2 * PART : (part + 1) * 2 * PART]
 
 
 def weight_terms(grad, inputs_x):
+    tokens, rows = inputs_x.shape
     return pl.pallas_call(
         weights_kernel,
-        out_shape=jax.ShapeDtypeStruct((NZ, 4 * 2 * PART, inputs_x.shape[1] // 4), BF16),
-        in_specs=[VMEM, VMEM],
+        out_shape=jax.ShapeDtypeStruct((NZ, 4 * 2 * PART, rows // 4), BF16),
+        in_specs=[VMEM, HBM],
         out_specs=VMEM,
+        scratch_shapes=[
+            pltpu.VMEM((4, tokens, rows // 4), BF16),
+            pltpu.SemaphoreType.DMA((4,)),
+        ],
         compiler_params=params(16),
         cost_estimate=pl.CostEstimate(flops=1 << 30, bytes_accessed=4 << 20, transcendentals=0),
         name="weight_terms",
@@ -420,21 +458,18 @@
 
     inputs_x = lax.all_gather(inputs, "seq", axis=0, axis_index_groups=X_GROUPS, tiled=True)
 
-    from_below, from_above, listed = own_kv, own_kv, far_blocks
-    plane, lists = [], []
-    for distance in range(1, NZ // 2 + 1):
+    from_below, from_above = both_ways(own_kv, own_kv, "seq", Z_UP)
+    across = [(x * NZ + z, (x + 2) % NX * NZ + z) for x in range(NX) for z in range(NZ)]
+    list_across = lax.ppermute(far_blocks, "seq", across)
+    from_below, from_above, list_across, listed = lax.optimization_barrier(
+        (from_below, from_above, list_across, far_blocks)
+    )
+    plane = [from_below, from_above]
+    for distance in range(2, NZ // 2 + 1):
         if distance == NZ // 2:
             from_below, from_above = from_below[: NB // 2], from_above[NB // 2 :]
         from_below, from_above = both_ways(from_below, from_above, "seq", Z_UP)
-        if distance < NX:
-            pairs = [(x * NZ + z, (x - distance) % NX * NZ + z) for x in range(NX) for z in range(NZ)]
-            arrived = lax.ppermute(listed, "seq", pairs)
-            arrived, listed, from_below, from_above = lax.optimization_barrier(
-                (arrived, listed, from_below, from_above)
-            )
-            lists.append(arrived)
         plane += [from_below, from_above]
-    lists = [far_blocks, *lists]
     from_below, key_weight, value_weight = lax.optimization_barrier(
         (plane[0], key_weight, value_weight)
     )
@@ -442,9 +477,11 @@
     weights = jnp.concatenate([key_weight.T, value_weight.T])
     weights = lax.all_gather(weights, "seq", axis=0, axis_index_groups=Z_GROUPS, tiled=True)
     prev_kv = shifted(own_kv, "seq", 1)
-    plane, low, high = pick_across(at, lists[2], own_kv, plane)
+    plane, low, high = pick_across(at, list_across, own_kv, plane)
+    low, high, listed = lax.optimization_barrier((low, high, listed))
     low, high = both_ways(low, high, "seq", X_UP)
-    up, down = pick(at, lists[1], lists[3], plane, low, high)
+    list_below, list_above = both_ways(listed, listed, "seq", X_UP)
+    up, down = pick(at, list_above, list_below, plane, low, high)
     from_below, from_above = both_ways(up, down, "seq", X_UP)
 
     far_count, inputs_x = lax.optimization_barrier((far_count, inputs_x))
@@ -453,8 +490,9 @@
     )
     far_all = ring_gather(far_grad, "seq", X_UP, NX)
     back = shifted(window[:tokens].astype(BF16), "seq", -1)
-    above, weights = lax.optimization_barrier((lists[1], weights))
-    dense = spread(at, [lists[0], above, *lists[2:]], far_grad, far_all)
+    list_above, weights = lax.optimization_barrier((list_above, weights))
+    lists = (far_blocks, list_above, list_across, list_below)
+    dense = spread(at, lists, far_grad, far_all)
     dense = dense.reshape(NZ, tokens, 2 * DH)
     terms = lax.all_to_all(dense, "seq", 0, 0, axis_index_groups=Z_GROUPS, tiled=True)
     kv_grad = finish(terms, back, window)

time: 203 us -> 202 us (level)
  waiting for transfers between devices: 87.3 us -> 82.1 us
  starting transfers between devices: 75.6 us -> 78.9 us
    ppermute x12 -> x13, waiting for transfers between devices: 1.45 us -> 9.6 us  [both_ways(): lax.ppermute(downward, axis, back)]
    ppermute x12 -> x13, waiting for transfers between devices: 46.7 us -> 39.2 us  [both_ways(): lax.ppermute(upward, axis, pairs)]
    ppermute x12 -> x13, starting transfers between devices: 10.9 us -> 16.3 us  [both_ways(): lax.ppermute(upward, axis, pairs)]
    ppermute x3 -> x1, waiting for transfers between devices: 5.99 us -> 1.39 us  [local(): list_across = lax.ppermute(far_blocks, 'seq', across)]
    all_to_all x1, waiting for transfers between devices: 5.31 us -> 1.66 us  [local(): lax.all_to_all(dense, 'seq', 0, 0, axis_index_groups=Z_GROUPS, tiled=True)]
    ppermute x3 -> x1, starting transfers between devices: 6.16 us -> 2.74 us  [local(): list_across = lax.ppermute(far_blocks, 'seq', across)]
    all_gather x1, waiting for transfers between devices: 0.23 us -> 3.07 us  [local(): lax.all_gather(weights, 'seq', axis=0, axis_index_groups=Z_GROUPS, tiled=...]
    ppermute x1, starting transfers between devices: 7.05 us -> 9.73 us  [local(): lax.ppermute(jnp.concatenate([moved, *same_core]), 'own', CORES)]
  transfers between devices with their start and end apart: 35 -> 35, of which waited for: 20 -> 21; matrix products, arithmetic and copies ran while one was open for 1% -> 1% of each run, Pallas kernels for 6% -> 7%
where the time goes in v8:
time: 202 us
  waiting for transfers between devices  82.1 us (41%)
  starting transfers between devices  78.9 us (39%)
  Pallas kernels  20.2 us (10%)
  between operations  14.4 us (7%)
  local copies, waits for them, and re-layouts  3.59 us (2%)
  other arithmetic  2.8 us (1%)
    ppermute x13, waiting for transfers between devices, both_ways(): lax.ppermute(upward, axis, pairs)  39.2 us
    ppermute x13, starting transfers between devices, both_ways(): lax.ppermute(downward, axis, back)  37.3 us
    ppermute x2, waiting for transfers between devices, shifted(): lax.ppermute(value, axis, [(source, source + steps) for source in range(l...  19.8 us
    ppermute x13, starting transfers between devices, both_ways(): lax.ppermute(upward, axis, pairs)  16.3 us
    pallas_call x1, Pallas kernels, attend(): pl.pallas_call(attend_kernel, out_shape=(jax.ShapeDtypeStruct((NB * BLK,...  9.89 us
    ppermute x1, starting transfers between devices, local(): lax.ppermute(jnp.concatenate([moved, *same_core]), 'own', CORES)  9.73 us
    ppermute x13, waiting for transfers between devices, both_ways(): lax.ppermute(downward, axis, back)  9.6 us
    all_to_all x1, waiting for transfers between devices, local(): lax.all_to_all(pieces, 'seq', 0, 0, axis_index_groups=Z_GROUPS, tiled=True)  5.12 us
  transfers between devices with their start and end apart: 35, of which 21 were waited for; matrix products, arithmetic and copies ran while one was open for 1% of the time, Pallas kernels for 7%

profile of v8, /device:TPU:1, one launch (start us, length us, event | category | flops | bytes accessed | tf_op | source)
XLA Modules:
  0.0 201.9 jit_solution(12364580289759185583)
XLA Ops:
  11.4 4.0 %collective-permute-start.2 = (bf16[2,128,256]{2,1,0:T(8,128)(2,1)S(1)}, bf16[2,128,256]{2,1,0:T(8,128)(2,1)S(1)}, u32[]{:S(2)}, u32[]{:S(2)}) collective-permute-start(bf16[2,128,256]{2,1,0:T(8,128)(2,1)S(1)} %bitcast.9), channel_id=1, source_target_pairs={{8,0},{16,8},{24,16},{32,24},{40,32},{48,40},{56,48},{0,56},{72,64... | collective-permute-start | bytes 393224 | tf_op jit(solution)/shard_map/ppermute | solution.py:60
  15.5 2.7 %collective-permute-start.3 = (s32[2,4]{1,0:T(2,128)}, s32[2,4]{1,0:T(2,128)S(1)}, u32[]{:S(2)}, u32[]{:S(2)}) collective-permute-start(s32[2,4]{1,0:T(2,128)} %refs_0_.1), channel_id=1, source_target_pairs={{0,128},{8,136},{16,144},{24,152},{32,160},{40,168},{48,176},{56,1... | collective-permute-start | bytes 104 | tf_op jit(solution)/shard_map/ppermute | solution.py:463
  19.6 2.7 %collective-permute-start.5 = (bf16[2,128,256]{2,1,0:T(8,128)(2,1)S(1)}, bf16[2,128,256]{2,1,0:T(8,128)(2,1)S(1)}, u32[]{:S(2)}, u32[]{:S(2)}) collective-permute-start(bf16[2,128,256]{2,1,0:T(8,128)(2,1)S(1)} %collective-permute-done.2.refs_1_), channel_id=1, source_target_pairs={{8,0},{16,8},{24,16},{32,24},{40,32},{48,40},{56,48},{0,56},{72,64... | collective-permute-start | bytes 393224 | tf_op jit(solution)/shard_map/ppermute | solution.py:60
  24.7 2.7 %collective-permute-start.7 = (bf16[2,128,256]{2,1,0:T(8,128)(2,1)S(1)}, bf16[2,128,256]{2,1,0:T(8,128)(2,1)S(1)}, u32[]{:S(2)}, u32[]{:S(2)}) collective-permute-start(bf16[2,128,256]{2,1,0:T(8,128)(2,1)S(1)} %collective-permute-done.5.refs_3_), channel_id=1, source_target_pairs={{8,0},{16,8},{24,16},{32,24},{40,32},{48,40},{56,48},{0,56},{72,64... | collective-permute-start | bytes 393224 | tf_op jit(solution)/shard_map/ppermute | solution.py:60
  29.7 2.7 %collective-permute-start.9 = (bf16[1,128,256]{2,1,0:T(8,128)(2,1)S(1)}, bf16[1,128,256]{2,1,0:T(8,128)(2,1)S(1)}, u32[]{:S(2)}, u32[]{:S(2)}) collective-permute-start(bf16[1,128,256]{2,1,0:T(8,128)(2,1)S(1)} %slice.46), channel_id=1, source_target_pairs={{8,0},{16,8},{24,16},{32,24},{40,32},{48,40},{56,48},{0,56},{72,64... | collective-permute-start | bytes 196616 | tf_op jit(solution)/shard_map/ppermute | solution.py:60
  39.6 8.4 %collective-permute-done.10.above_ref.refs_1_ = s32[2,4]{1,0:T(2,128)S(1)} collective-permute-done((s32[2,4]{1,0:T(2,128)S(1)}, s32[2,4]{1,0:T(2,128)S(1)}, u32[]{:S(2)}, u32[]{:S(2)}) %collective-permute-start.10) | collective-permute-done | bytes 64 | tf_op jit(solution)/shard_map/ppermute | solution.py:60
  57.1 3.9 %collective-permute-done.14.below_ref = bf16[8,128,256]{2,1,0:T(8,128)(2,1)S(1)} collective-permute-done((bf16[8,128,256]{2,1,0:T(8,128)(2,1)}, bf16[8,128,256]{2,1,0:T(8,128)(2,1)S(1)}, u32[]{:S(2)}, u32[]{:S(2)}) %collective-permute-start.14) | collective-permute-done | bytes 524320 | tf_op jit(solution)/shard_map/ppermute | solution.py:60
  62.9 9.9 %attend.1 = (bf16[256,1024]{1,0:T(8,128)(2,1)}, f32[512,256]{1,0:T(8,128)S(1)}, bf16[8,128,256]{2,1,0:T(8,128)(2,1)S(1)}) custom-call(s32[1]{0:T(128)} %bitcast.at_ref, s32[2,4]{1,0:T(2,128)S(1)} %copy-done.1, s32[2]{0:T(128)S(1)} %copy-done.7, bf16[256,1024]{1,0:T(8,128)(2,1)S(1)} %copy-done.3, bf16[256,1024]{1,0:T(8,128)(2,1)S(1)} %copy-done.4, ...), custom_call_target="tpu_custom_call" | custom-call | flops 9600000000 | bytes 6291456 | tf_op jit(solution)/shard_map/attend/pallas_call | solution.py:241
  77.5 7.2 %collective-permute-done.16.refs_5_ = bf16[8,128,256]{2,1,0:T(8,128)(2,1)S(1)} collective-permute-done((bf16[8,128,256]{2,1,0:T(8,128)(2,1)S(1)}, bf16[8,128,256]{2,1,0:T(8,128)(2,1)S(1)}, u32[]{:S(2)}, u32[]{:S(2)}) %collective-permute-start.16) | collective-permute-done | bytes 524320 | tf_op jit(solution)/shard_map/ppermute | solution.py:60
  84.8 2.7 %collective-permute-start.19 = (bf16[4,128,256]{2,1,0:T(8,128)(2,1)S(1)}, bf16[4,128,256]{2,1,0:T(8,128)(2,1)S(1)}, u32[]{:S(2)}, u32[]{:S(2)}) collective-permute-start(bf16[4,128,256]{2,1,0:T(8,128)(2,1)S(1)} %slice.48), channel_id=1, source_target_pairs={{64,0},{72,8},{80,16},{88,24},{96,32},{104,40},{112,48},{120,56},{... | collective-permute-start | bytes 786440 | tf_op jit(solution)/shard_map/ppermute | solution.py:60
  87.6 3.1 %all-gather.5.cloned.1.call-done.weights_ref = bf16[512,1024]{1,0:T(8,128)(2,1)} async-done(((bf16[64,1024]{1,0:T(8,128)(2,1)}), bf16[512,1024]{1,0:T(8,128)(2,1)}) %all-gather.5.cloned.1.call-update) | async-done | bytes 1048592 | tf_op jit(solution)/shard_map/all_gather | solution.py:478
  95.3 4.8 %all-to-all-start = ((bf16[8,256,256]{2,1,0:T(8,128)(2,1)}), bf16[8,256,256]{2,1,0:T(8,128)(2,1)S(1)}, u32[]{:S(2)}, u32[]{:S(2)}) async-start(bf16[8,256,256]{2,1,0:T(8,128)(2,1)} %bitcast.5), calls=%async_computation | async-start | bytes 2097152 | tf_op jit(solution)/shard_map/all_to_all | solution.py:497
  101.6 17.9 %collective-permute-done.20.back_ref = bf16[256,256]{1,0:T(8,128)(2,1)S(1)} collective-permute-done((bf16[256,256]{1,0:T(8,128)(2,1)S(1)}, bf16[256,256]{1,0:T(8,128)(2,1)S(1)}, u32[]{:S(2)}, u32[]{:S(2)}) %collective-permute-start.20) | collective-permute-done | bytes 131104 | tf_op jit(solution)/shard_map/ppermute | solution.py:55
  122.2 9.6 %collective-permute-start.22 = (bf16[256,256]{1,0:T(8,128)(2,1)S(1)}, bf16[256,256]{1,0:T(8,128)(2,1)S(1)}, u32[]{:S(2)}, u32[]{:S(2)}) collective-permute-start(bf16[256,256]{1,0:T(8,128)(2,1)S(1)} %collective-permute-done.21.own_ref), channel_id=1, source_target_pairs={{0,2},{1,3},{2,4},{3,5},{4,6},{5,7},{6,0},{7,1},{8,10},{9,11},{10,... | collective-permute-start | bytes 393224 | tf_op jit(solution)/shard_map/ppermute | solution.py:60
  131.8 5.4 %collective-permute-start.23 = (bf16[256,256]{1,0:T(8,128)(2,1)S(1)}, bf16[256,256]{1,0:T(8,128)(2,1)S(1)}, u32[]{:S(2)}, u32[]{:S(2)}) collective-permute-start(bf16[256,256]{1,0:T(8,128)(2,1)S(1)} %collective-permute-done.21.own_ref), channel_id=1, source_target_pairs={{2,0},{3,1},{4,2},{5,3},{6,4},{7,5},{0,6},{1,7},{10,8},{11,9},{12,... | collective-permute-start | bytes 393224 | tf_op jit(solution)/shard_map/ppermute | solution.py:60
  139.5 3.6 %collective-permute-start.25 = (bf16[128,256]{1,0:T(8,128)(2,1)S(1)}, bf16[128,256]{1,0:T(8,128)(2,1)S(1)}, u32[]{:S(2)}, u32[]{:S(2)}) collective-permute-start(bf16[128,256]{1,0:T(8,128)(2,1)S(1)} %slice.51), channel_id=1, source_target_pairs={{2,0},{3,1},{4,2},{5,3},{6,4},{7,5},{0,6},{1,7},{10,8},{11,9},{12,... | collective-permute-start | bytes 196616 | tf_op jit(solution)/shard_map/ppermute | solution.py:60
  144.5 9.7 %collective-permute-start.26 = (bf16[1024,256]{1,0:T(8,128)(2,1)S(1)}, bf16[1024,256]{1,0:T(8,128)(2,1)S(1)}, u32[]{:S(2)}, u32[]{:S(2)}) collective-permute-start(bf16[1024,256]{1,0:T(8,128)(2,1)S(1)} %constant_dynamic-update-slice_fusion), channel_id=1, source_target_pairs={{0,1},{1,0},{2,3},{3,2},{4,5},{5,4},{6,7},{7,6},{8,9},{9,8},{10,11... | collective-permute-start | bytes 1572872 | tf_op jit(solution)/shard_map/ppermute | solution.py:502
  157.4 3.2 %weight_terms.1 = bf16[8,256,256]{2,1,0:T(8,128)(2,1)} custom-call(bf16[8,256,256]{2,1,0:T(8,128)(2,1)S(1)} %place_heads.1.grad_ref, bf16[1024,1024]{1,0:T(8,128)(2,1)S(1)} %copy-done), custom_call_target="tpu_custom_call" | custom-call | flops 1073741824 | bytes 4194304 | tf_op jit(solution)/shard_map/weight_terms/pallas_call | solution.py:377
  160.6 4.4 %all-to-all-start.1 = ((bf16[8,256,256]{2,1,0:T(8,128)(2,1)}), bf16[8,256,256]{2,1,0:T(8,128)(2,1)S(1)}, u32[]{:S(2)}, u32[]{:S(2)}) async-start(bf16[8,256,256]{2,1,0:T(8,128)(2,1)} %weight_terms.1), calls=%async_computation.1 | async-start | bytes 2097152 | tf_op jit(solution)/shard_map/all_to_all | solution.py:508
  166.4 2.7 %collective-permute-start.29 = (bf16[128,1024]{1,0:T(8,128)(2,1)S(1)}, bf16[128,1024]{1,0:T(8,128)(2,1)S(1)}, u32[]{:S(2)}, u32[]{:S(2)}) collective-permute-start(bf16[128,1024]{1,0:T(8,128)(2,1)S(1)} %get-tuple-element.58), channel_id=1, source_target_pairs={{64,0},{72,8},{80,16},{88,24},{96,32},{104,40},{112,48},{120,56},{... | collective-permute-start | bytes 786440 | tf_op jit(solution)/shard_map/ppermute | solution.py:60
  169.2 5.6 %collective-permute-done.27 = bf16[128,1024]{1,0:T(8,128)(2,1)S(1)} collective-permute-done((bf16[128,1024]{1,0:T(8,128)(2,1)S(1)}, bf16[128,1024]{1,0:T(8,128)(2,1)S(1)}, u32[]{:S(2)}, u32[]{:S(2)}) %collective-permute-start.27) | collective-permute-done | bytes 262176 | tf_op jit(solution)/shard_map/ppermute | solution.py:60
  175.1 2.7 %collective-permute-start.30 = (bf16[256,1024]{1,0:T(8,128)(2,1)S(1)}, bf16[256,1024]{1,0:T(8,128)(2,1)S(1)}, u32[]{:S(2)}, u32[]{:S(2)}) collective-permute-start(bf16[256,1024]{1,0:T(8,128)(2,1)S(1)} %pad_maximum_fusion.1), channel_id=1, source_target_pairs={{64,0},{72,8},{80,16},{88,24},{96,32},{104,40},{112,48},{120,56},{... | collective-permute-start | bytes 1572872 | tf_op jit(solution)/shard_map/ppermute | solution.py:60
  177.9 10.2 %collective-permute-done.28 = bf16[256,1024]{1,0:T(8,128)(2,1)S(1)} collective-permute-done((bf16[256,1024]{1,0:T(8,128)(2,1)S(1)}, bf16[256,1024]{1,0:T(8,128)(2,1)S(1)}, u32[]{:S(2)}, u32[]{:S(2)}) %collective-permute-start.28) | collective-permute-done | bytes 524320 | tf_op jit(solution)/shard_map/ppermute | solution.py:60
  189.2 5.1 %all-to-all-done.1.terms_ref = bf16[8,256,256]{2,1,0:T(8,128)(2,1)S(1)} async-done(((bf16[8,256,256]{2,1,0:T(8,128)(2,1)}), bf16[8,256,256]{2,1,0:T(8,128)(2,1)S(1)}, u32[]{:S(2)}, u32[]{:S(2)}) %all-to-all-start.1) | async-done | bytes 1048608 | tf_op jit(solution)/shard_map/all_to_all | solution.py:508
  (98 shorter events, 52.5 us)
Async XLA Ops:
  7.2 48.0 %all-gather.3.cloned.1.call-start = ((), (), s32[]{:S(2)}) async-start(), calls=%async_computation.2 | async-start | bytes 2621440 | tf_op jit(solution)/shard_map/all_gather | solution.py:459
  8.0 82.7 %all-gather.5.cloned.1.call-start = ((), (), s32[]{:S(2)}) async-start(), calls=%async_computation.3 | async-start | bytes 1179648 | tf_op jit(solution)/shard_map/all_gather | solution.py:478
  8.9 10.7 %collective-permute-start.1 = (bf16[2,128,256]{2,1,0:T(8,128)(2,1)S(1)}, bf16[2,128,256]{2,1,0:T(8,128)(2,1)S(1)}, u32[]{:S(2)}, u32[]{:S(2)}) collective-permute-start(bf16[2,128,256]{2,1,0:T(8,128)(2,1)S(1)} %bitcast.8), channel_id=1, source_target_pairs={{0,8},{8,16},{16,24},{24,32},{32,40},{40,48},{48,56},{56,0},{64,72... | collective-permute-start | bytes 393224 | tf_op jit(solution)/shard_map/ppermute | solution.py:60
  11.4 8.2 %collective-permute-start.2 = (bf16[2,128,256]{2,1,0:T(8,128)(2,1)S(1)}, bf16[2,128,256]{2,1,0:T(8,128)(2,1)S(1)}, u32[]{:S(2)}, u32[]{:S(2)}) collective-permute-start(bf16[2,128,256]{2,1,0:T(8,128)(2,1)S(1)} %bitcast.9), channel_id=1, source_target_pairs={{8,0},{16,8},{24,16},{32,24},{40,32},{48,40},{56,48},{0,56},{72,64... | collective-permute-start | bytes 393224 | tf_op jit(solution)/shard_map/ppermute | solution.py:60
  35.2 13.7 %collective-permute-start.12 = (bf16[4,128,256]{2,1,0:T(8,128)(2,1)S(1)}, bf16[4,128,256]{2,1,0:T(8,128)(2,1)S(1)}, u32[]{:S(2)}, u32[]{:S(2)}) collective-permute-start(bf16[4,128,256]{2,1,0:T(8,128)(2,1)S(1)} %get-tuple-element.43), channel_id=1, source_target_pairs={{0,64},{8,72},{16,80},{24,88},{32,96},{40,104},{48,112},{56,120},{... | collective-permute-start | bytes 786440 | tf_op jit(solution)/shard_map/ppermute | solution.py:60
  36.0 12.8 %collective-permute-start.13 = (bf16[4,128,256]{2,1,0:T(8,128)(2,1)S(1)}, bf16[4,128,256]{2,1,0:T(8,128)(2,1)S(1)}, u32[]{:S(2)}, u32[]{:S(2)}) collective-permute-start(bf16[4,128,256]{2,1,0:T(8,128)(2,1)S(1)} %get-tuple-element.44), channel_id=1, source_target_pairs={{64,0},{72,8},{80,16},{88,24},{96,32},{104,40},{112,48},{120,56},{... | collective-permute-start | bytes 786440 | tf_op jit(solution)/shard_map/ppermute | solution.py:60
  38.1 9.9 %collective-permute-start.10 = (s32[2,4]{1,0:T(2,128)S(1)}, s32[2,4]{1,0:T(2,128)S(1)}, u32[]{:S(2)}, u32[]{:S(2)}) collective-permute-start(s32[2,4]{1,0:T(2,128)S(1)} %copy-done.1), channel_id=1, source_target_pairs={{64,0},{72,8},{80,16},{88,24},{96,32},{104,40},{112,48},{120,56},{... | collective-permute-start | bytes 104 | tf_op jit(solution)/shard_map/ppermute | solution.py:60
  39.5 9.3 %collective-permute-start.11 = (s32[2,4]{1,0:T(2,128)S(1)}, s32[2,4]{1,0:T(2,128)S(1)}, u32[]{:S(2)}, u32[]{:S(2)}) collective-permute-start(s32[2,4]{1,0:T(2,128)S(1)} %copy-done.1), channel_id=1, source_target_pairs={{0,64},{8,72},{16,80},{24,88},{32,96},{40,104},{48,112},{56,120},{... | collective-permute-start | bytes 104 | tf_op jit(solution)/shard_map/ppermute | solution.py:60
  50.4 10.6 %collective-permute-start.14 = (bf16[8,128,256]{2,1,0:T(8,128)(2,1)}, bf16[8,128,256]{2,1,0:T(8,128)(2,1)S(1)}, u32[]{:S(2)}, u32[]{:S(2)}) collective-permute-start(bf16[8,128,256]{2,1,0:T(8,128)(2,1)} %get-tuple-element.45), channel_id=1, source_target_pairs={{0,64},{8,72},{16,80},{24,88},{32,96},{40,104},{48,112},{56,120},{... | collective-permute-start | bytes 1572872 | tf_op jit(solution)/shard_map/ppermute | solution.py:60
  51.0 10.8 %collective-permute-start.15 = (bf16[8,128,256]{2,1,0:T(8,128)(2,1)S(1)}, bf16[8,128,256]{2,1,0:T(8,128)(2,1)}, u32[]{:S(2)}, u32[]{:S(2)}) collective-permute-start(bf16[8,128,256]{2,1,0:T(8,128)(2,1)S(1)} %get-tuple-element.46), channel_id=1, source_target_pairs={{64,0},{72,8},{80,16},{88,24},{96,32},{104,40},{112,48},{120,56},{... | collective-permute-start | bytes 1572872 | tf_op jit(solution)/shard_map/ppermute | solution.py:60
  72.7 11.9 %collective-permute-start.16 = (bf16[8,128,256]{2,1,0:T(8,128)(2,1)S(1)}, bf16[8,128,256]{2,1,0:T(8,128)(2,1)S(1)}, u32[]{:S(2)}, u32[]{:S(2)}) collective-permute-start(bf16[8,128,256]{2,1,0:T(8,128)(2,1)S(1)} %get-tuple-element.51.refs_4_), channel_id=1, source_target_pairs={{0,64},{8,72},{16,80},{24,88},{32,96},{40,104},{48,112},{56,120},{... | collective-permute-start | bytes 1572872 | tf_op jit(solution)/shard_map/ppermute | solution.py:60
  75.0 9.8 %collective-permute-start.17 = (bf16[8,128,256]{2,1,0:T(8,128)(2,1)S(1)}, bf16[8,128,256]{2,1,0:T(8,128)(2,1)S(1)}, u32[]{:S(2)}, u32[]{:S(2)}) collective-permute-start(bf16[8,128,256]{2,1,0:T(8,128)(2,1)S(1)} %get-tuple-element.51.refs_4_), channel_id=1, source_target_pairs={{64,0},{72,8},{80,16},{88,24},{96,32},{104,40},{112,48},{120,56},{... | collective-permute-start | bytes 1572872 | tf_op jit(solution)/shard_map/ppermute | solution.py:60
  84.7 7.7 %collective-permute-start.18 = (bf16[4,128,256]{2,1,0:T(8,128)(2,1)S(1)}, bf16[4,128,256]{2,1,0:T(8,128)(2,1)S(1)}, u32[]{:S(2)}, u32[]{:S(2)}) collective-permute-start(bf16[4,128,256]{2,1,0:T(8,128)(2,1)S(1)} %slice.47), channel_id=1, source_target_pairs={{0,64},{8,72},{16,80},{24,88},{32,96},{40,104},{48,112},{56,120},{... | collective-permute-start | bytes 786440 | tf_op jit(solution)/shard_map/ppermute | solution.py:60
  84.8 8.0 %collective-permute-start.19 = (bf16[4,128,256]{2,1,0:T(8,128)(2,1)S(1)}, bf16[4,128,256]{2,1,0:T(8,128)(2,1)S(1)}, u32[]{:S(2)}, u32[]{:S(2)}) collective-permute-start(bf16[4,128,256]{2,1,0:T(8,128)(2,1)S(1)} %slice.48), channel_id=1, source_target_pairs={{64,0},{72,8},{80,16},{88,24},{96,32},{104,40},{112,48},{120,56},{... | collective-permute-start | bytes 786440 | tf_op jit(solution)/shard_map/ppermute | solution.py:60
  95.3 25.9 %all-to-all-start = ((bf16[8,256,256]{2,1,0:T(8,128)(2,1)}), bf16[8,256,256]{2,1,0:T(8,128)(2,1)S(1)}, u32[]{:S(2)}, u32[]{:S(2)}) async-start(bf16[8,256,256]{2,1,0:T(8,128)(2,1)} %bitcast.5), calls=%async_computation | async-start | bytes 2097152 | tf_op jit(solution)/shard_map/all_to_all | solution.py:497
  100.1 19.4 %collective-permute-start.20 = (bf16[256,256]{1,0:T(8,128)(2,1)S(1)}, bf16[256,256]{1,0:T(8,128)(2,1)S(1)}, u32[]{:S(2)}, u32[]{:S(2)}) collective-permute-start(bf16[256,256]{1,0:T(8,128)(2,1)S(1)} %slice.55), channel_id=1, source_target_pairs={{8,0},{16,8},{24,16},{32,24},{40,32},{48,40},{56,48},{64,56},{72,6... | collective-permute-start | bytes 393224 | tf_op jit(solution)/shard_map/ppermute | solution.py:55
  122.2 17.3 %collective-permute-start.22 = (bf16[256,256]{1,0:T(8,128)(2,1)S(1)}, bf16[256,256]{1,0:T(8,128)(2,1)S(1)}, u32[]{:S(2)}, u32[]{:S(2)}) collective-permute-start(bf16[256,256]{1,0:T(8,128)(2,1)S(1)} %collective-permute-done.21.own_ref), channel_id=1, source_target_pairs={{0,2},{1,3},{2,4},{3,5},{4,6},{5,7},{6,0},{7,1},{8,10},{9,11},{10,... | collective-permute-start | bytes 393224 | tf_op jit(solution)/shard_map/ppermute | solution.py:60
  131.8 7.7 %collective-permute-start.23 = (bf16[256,256]{1,0:T(8,128)(2,1)S(1)}, bf16[256,256]{1,0:T(8,128)(2,1)S(1)}, u32[]{:S(2)}, u32[]{:S(2)}) collective-permute-start(bf16[256,256]{1,0:T(8,128)(2,1)S(1)} %collective-permute-done.21.own_ref), channel_id=1, source_target_pairs={{2,0},{3,1},{4,2},{5,3},{6,4},{7,5},{0,6},{1,7},{10,8},{11,9},{12,... | collective-permute-start | bytes 393224 | tf_op jit(solution)/shard_map/ppermute | solution.py:60
  144.5 11.3 %collective-permute-start.26 = (bf16[1024,256]{1,0:T(8,128)(2,1)S(1)}, bf16[1024,256]{1,0:T(8,128)(2,1)S(1)}, u32[]{:S(2)}, u32[]{:S(2)}) collective-permute-start(bf16[1024,256]{1,0:T(8,128)(2,1)S(1)} %constant_dynamic-update-slice_fusion), channel_id=1, source_target_pairs={{0,1},{1,0},{2,3},{3,2},{4,5},{5,4},{6,7},{7,6},{8,9},{9,8},{10,11... | collective-permute-start | bytes 1572872 | tf_op jit(solution)/shard_map/ppermute | solution.py:502
  160.6 33.6 %all-to-all-start.1 = ((bf16[8,256,256]{2,1,0:T(8,128)(2,1)}), bf16[8,256,256]{2,1,0:T(8,128)(2,1)S(1)}, u32[]{:S(2)}, u32[]{:S(2)}) async-start(bf16[8,256,256]{2,1,0:T(8,128)(2,1)} %weight_terms.1), calls=%async_computation.1 | async-start | bytes 2097152 | tf_op jit(solution)/shard_map/all_to_all | solution.py:508
  166.3 8.5 %collective-permute-start.27 = (bf16[128,1024]{1,0:T(8,128)(2,1)S(1)}, bf16[128,1024]{1,0:T(8,128)(2,1)S(1)}, u32[]{:S(2)}, u32[]{:S(2)}) collective-permute-start(bf16[128,1024]{1,0:T(8,128)(2,1)S(1)} %get-tuple-element.56), channel_id=1, source_target_pairs={{0,64},{8,72},{16,80},{24,88},{32,96},{40,104},{48,112},{56,120},{... | collective-permute-start | bytes 786440 | tf_op jit(solution)/shard_map/ppermute | solution.py:60
  166.4 8.6 %collective-permute-start.29 = (bf16[128,1024]{1,0:T(8,128)(2,1)S(1)}, bf16[128,1024]{1,0:T(8,128)(2,1)S(1)}, u32[]{:S(2)}, u32[]{:S(2)}) collective-permute-start(bf16[128,1024]{1,0:T(8,128)(2,1)S(1)} %get-tuple-element.58), channel_id=1, source_target_pairs={{64,0},{72,8},{80,16},{88,24},{96,32},{104,40},{112,48},{120,56},{... | collective-permute-start | bytes 786440 | tf_op jit(solution)/shard_map/ppermute | solution.py:60
  174.9 13.2 %collective-permute-start.28 = (bf16[256,1024]{1,0:T(8,128)(2,1)S(1)}, bf16[256,1024]{1,0:T(8,128)(2,1)S(1)}, u32[]{:S(2)}, u32[]{:S(2)}) collective-permute-start(bf16[256,1024]{1,0:T(8,128)(2,1)S(1)} %pad_maximum_fusion), channel_id=1, source_target_pairs={{0,64},{8,72},{16,80},{24,88},{32,96},{40,104},{48,112},{56,120},{... | collective-permute-start | bytes 1572872 | tf_op jit(solution)/shard_map/ppermute | solution.py:60
  175.1 13.0 %collective-permute-start.30 = (bf16[256,1024]{1,0:T(8,128)(2,1)S(1)}, bf16[256,1024]{1,0:T(8,128)(2,1)S(1)}, u32[]{:S(2)}, u32[]{:S(2)}) collective-permute-start(bf16[256,1024]{1,0:T(8,128)(2,1)S(1)} %pad_maximum_fusion.1), channel_id=1, source_target_pairs={{64,0},{72,8},{80,16},{88,24},{96,32},{104,40},{112,48},{120,56},{... | collective-permute-start | bytes 1572872 | tf_op jit(solution)/shard_map/ppermute | solution.py:60
  (21 other events, 344.7 us)
Sparse Core Ops, SparseCore 0:
  9.9 41.8 all-gather.2
  54.2 36.4 all-gather.4

commit v9 on v8

--- a/solution.py
+++ b/solution.py
@@ -144,23 +144,8 @@
 
 def attend_kernel(
     at_ref, far_ref, count_ref, q_ref, g_ref, prev_ref, own_ref, plane_ref, below_ref, above_ref,
-    qg_ref, win_ref, farg_ref, k_ref, v_ref, kt_ref, acc_ref, tri_ref, got_ref, sems,
+    qg_ref, win_ref, farg_ref, k_ref, v_ref, kt_ref, acc_ref, tri_ref,
 ):
-    places = []
-    for slot in range(SLOTS):
-        listed = far_ref[slot // FARS, slot % FARS]
-        steps = lax.rem(lax.div(listed, PLANE) + (NX - lax.div(at_ref[0], NZ)), NX)
-        upward = (steps == NX - 1) | (steps == 2) if slot < FARS else steps == NX - 1
-        places.append((steps == 0, lax.rem(listed, PLANE)))
-        for here, source in (
-            (upward, below_ref),
-            (jnp.logical_not(upward | (steps == 0)), above_ref),
-        ):
-
-            @pl.when(here)
-            def _():
-                pltpu.make_async_copy(source.at[slot], got_ref.at[slot], sems.at[slot]).start()
-
     win_ref[...] = jnp.zeros_like(win_ref)
     key_at = lax.broadcasted_iota(jnp.int32, (BLK, 2 * BLK), 0)
     query_at = lax.broadcasted_iota(jnp.int32, (BLK, 2 * BLK), 1) % BLK
@@ -175,17 +160,11 @@
             v_ref[w * BLK : (w + 1) * BLK, :] = both[:, DH:]
         for j in range(FARS):
             slot = b * FARS + j
-            mine, row = places[slot]
-
-            @pl.when(mine)
-            def _():
-                got_ref[slot] = plane_ref[row]
-
-            @pl.when(jnp.logical_not(mine))
-            def _():
-                pltpu.make_async_copy(below_ref.at[slot], got_ref.at[slot], sems.at[slot]).wait()
-
-            both = got_ref[slot]
+            steps = lax.rem(lax.div(far_ref[b, j], PLANE) + (NX - lax.div(at_ref[0], NZ)), NX)
+            mine = plane_ref[lax.rem(far_ref[b, j], PLANE)]
+            from_below = (steps == NX - 1) | ((steps == 2) & (b == 0))
+            both = jnp.where(from_below, below_ref[slot], above_ref[slot])
+            both = jnp.where(steps == 0, mine, both)
             k_ref[(WIN + j) * BLK : (WIN + j + 1) * BLK, :] = both[:, :DH]
             v_ref[(WIN + j) * BLK : (WIN + j + 1) * BLK, :] = both[:, DH:]
         kt_ref[...] = k_ref[...].astype(F32).T.astype(BF16)
@@ -245,7 +224,7 @@
             jax.ShapeDtypeStruct((2 * NB * BLK, 2 * DH), F32),
             jax.ShapeDtypeStruct((SLOTS, BLK, 2 * DH), BF16),
         ),
-        in_specs=[SMEM, SMEM, SMEM] + [VMEM] * 5 + [HBM] * 2,
+        in_specs=[SMEM, SMEM, SMEM] + [VMEM] * 7,
         out_specs=(VMEM, VMEM, VMEM),
         scratch_shapes=[
             pltpu.VMEM((keys, DH), BF16),
@@ -253,8 +232,6 @@
             pltpu.VMEM((DH, keys), BF16),
             pltpu.VMEM((keys, 2 * DH), F32),
             pltpu.VMEM((BLK, 2 * BLK), F32),
-            pltpu.VMEM((SLOTS, BLK, 2 * DH), BF16),
-            pltpu.SemaphoreType.DMA((SLOTS,)),
         ],
         compiler_params=params(24),
         cost_estimate=pl.CostEstimate(flops=2_400_000_000 * 4, bytes_accessed=6 << 20, transcendentals=2_000_000),
@@ -456,8 +433,6 @@
     own_index = lax.axis_index("own").astype(jnp.int32).reshape(1)
     own_kv = jnp.concatenate([key_rows, value_rows], axis=1).reshape(NB, BLK, 2 * DH)
 
-    inputs_x = lax.all_gather(inputs, "seq", axis=0, axis_index_groups=X_GROUPS, tiled=True)
-
     from_below, from_above = both_ways(own_kv, own_kv, "seq", Z_UP)
     across = [(x * NZ + z, (x + 2) % NX * NZ + z) for x in range(NX) for z in range(NZ)]
     list_across = lax.ppermute(far_blocks, "seq", across)
@@ -470,27 +445,25 @@
             from_below, from_above = from_below[: NB // 2], from_above[NB // 2 :]
         from_below, from_above = both_ways(from_below, from_above, "seq", Z_UP)
         plane += [from_below, from_above]
-    from_below, key_weight, value_weight = lax.optimization_barrier(
-        (plane[0], key_weight, value_weight)
+    prev_kv = shifted(own_kv, "seq", 1)
+    plane, low, high = pick_across(at, list_across, own_kv, plane)
+    low, high, listed, key_weight, value_weight = lax.optimization_barrier(
+        (low, high, listed, key_weight, value_weight)
     )
-    plane[0] = from_below
     weights = jnp.concatenate([key_weight.T, value_weight.T])
     weights = lax.all_gather(weights, "seq", axis=0, axis_index_groups=Z_GROUPS, tiled=True)
-    prev_kv = shifted(own_kv, "seq", 1)
-    plane, low, high = pick_across(at, list_across, own_kv, plane)
-    low, high, listed = lax.optimization_barrier((low, high, listed))
     low, high = both_ways(low, high, "seq", X_UP)
     list_below, list_above = both_ways(listed, listed, "seq", X_UP)
     up, down = pick(at, list_above, list_below, plane, low, high)
     from_below, from_above = both_ways(up, down, "seq", X_UP)
 
-    far_count, inputs_x = lax.optimization_barrier((far_count, inputs_x))
     query_grad, window, far_grad = attend(
         at, far_blocks, far_count, queries, out_grad, prev_kv, own_kv, plane, from_below, from_above
     )
     far_all = ring_gather(far_grad, "seq", X_UP, NX)
     back = shifted(window[:tokens].astype(BF16), "seq", -1)
-    list_above, weights = lax.optimization_barrier((list_above, weights))
+    list_above, weights, back, inputs = lax.optimization_barrier((list_above, weights, back, inputs))
+    inputs_x = lax.all_gather(inputs, "seq", axis=0, axis_index_groups=X_GROUPS, tiled=True)
     lists = (far_blocks, list_above, list_across, list_below)
     dense = spread(at, lists, far_grad, far_all)
     dense = dense.reshape(NZ, tokens, 2 * DH)

time: 202 us -> 201 us (level)
  waiting for transfers between devices: 82.1 us -> 59.4 us
  blocking collectives: 0 us -> 22.1 us
    all_to_all x0 -> x1, blocking collectives: none -> 22.1 us  [local(): lax.all_to_all(dense, 'seq', 0, 0, axis_index_groups=Z_GROUPS, tiled=True)]
    ppermute x13, waiting for transfers between devices: 39.2 us -> 24.8 us  [both_ways(): lax.ppermute(upward, axis, pairs)]
    ppermute x2, waiting for transfers between devices: 19.8 us -> 7.72 us  [shifted(): lax.ppermute(value, axis, [(source, source + steps) for source in range(l...]
    ppermute x1, starting transfers between devices: 9.73 us -> 18.6 us  [local(): lax.ppermute(jnp.concatenate([moved, *same_core]), 'own', CORES)]
    ppermute x13, waiting for transfers between devices: 9.6 us -> 17.7 us  [both_ways(): lax.ppermute(downward, axis, back)]
    ppermute x13, starting transfers between devices: 37.3 us -> 31.8 us  [both_ways(): lax.ppermute(downward, axis, back)]
    all_to_all x1 -> x0, starting transfers between devices: 4.76 us -> none  [local(): lax.all_to_all(dense, 'seq', 0, 0, axis_index_groups=Z_GROUPS, tiled=True)]
    all_to_all x1, waiting for transfers between devices: 5.12 us -> 2.75 us  [local(): lax.all_to_all(pieces, 'seq', 0, 0, axis_index_groups=Z_GROUPS, tiled=True)]
  transfers between devices with their start and end apart: 35 -> 34, of which waited for: 21 -> 18; matrix products, arithmetic and copies ran while one was open for 1% -> 1% of each run, Pallas kernels for 7% -> 6%
where the time goes in v9:
time: 201 us; the launch traced here: 200 us
  starting transfers between devices  78.7 us (39%)
  waiting for transfers between devices  59.4 us (30%)
  blocking collectives  22.1 us (11%)
  Pallas kernels  19 us (9%)
  between operations  14.4 us (7%)
  local copies, waits for them, and re-layouts  3.6 us (2%)
  other arithmetic  3 us (1%)
    ppermute x13, starting transfers between devices, both_ways(): lax.ppermute(downward, axis, back)  31.8 us
    ppermute x13, waiting for transfers between devices, both_ways(): lax.ppermute(upward, axis, pairs)  24.8 us
    all_to_all x1, blocking collectives, local(): lax.all_to_all(dense, 'seq', 0, 0, axis_index_groups=Z_GROUPS, tiled=True)  22.1 us
    ppermute x1, starting transfers between devices, local(): lax.ppermute(jnp.concatenate([moved, *same_core]), 'own', CORES)  18.6 us
    ppermute x13, starting transfers between devices, both_ways(): lax.ppermute(upward, axis, pairs)  18 us
    ppermute x13, waiting for transfers between devices, both_ways(): lax.ppermute(downward, axis, back)  17.7 us
    pallas_call x1, Pallas kernels, attend(): pl.pallas_call(attend_kernel, out_shape=(jax.ShapeDtypeStruct((NB * BLK,...  9.69 us
    ppermute x2, waiting for transfers between devices, shifted(): lax.ppermute(value, axis, [(source, source + steps) for source in range(l...  7.72 us
  transfers between devices with their start and end apart: 34, of which 18 were waited for; matrix products, arithmetic and copies ran while one was open for 1% of the time, Pallas kernels for 6%

profile of v9, /device:TPU:1, one launch (start us, length us, event | category | flops | bytes accessed | tf_op | source)
XLA Modules:
  0.0 200.1 jit_solution(16597962055526675904)
XLA Ops:
  10.9 4.0 %collective-permute-start.2 = (bf16[2,128,256]{2,1,0:T(8,128)(2,1)S(1)}, bf16[2,128,256]{2,1,0:T(8,128)(2,1)S(1)}, u32[]{:S(2)}, u32[]{:S(2)}) collective-permute-start(bf16[2,128,256]{2,1,0:T(8,128)(2,1)S(1)} %bitcast.10), channel_id=1, source_target_pairs={{8,0},{16,8},{24,16},{32,24},{40,32},{48,40},{56,48},{0,56},{72,64... | collective-permute-start | bytes 393224 | tf_op jit(solution)/shard_map/ppermute | solution.py:60
  14.9 2.7 %collective-permute-start.3 = (s32[2,4]{1,0:T(2,128)}, s32[2,4]{1,0:T(2,128)S(1)}, u32[]{:S(2)}, u32[]{:S(2)}) collective-permute-start(s32[2,4]{1,0:T(2,128)} %refs_0_.1), channel_id=1, source_target_pairs={{0,128},{8,136},{16,144},{24,152},{32,160},{40,168},{48,176},{56,1... | collective-permute-start | bytes 104 | tf_op jit(solution)/shard_map/ppermute | solution.py:438
  19.1 2.7 %collective-permute-start.5 = (bf16[2,128,256]{2,1,0:T(8,128)(2,1)S(1)}, bf16[2,128,256]{2,1,0:T(8,128)(2,1)S(1)}, u32[]{:S(2)}, u32[]{:S(2)}) collective-permute-start(bf16[2,128,256]{2,1,0:T(8,128)(2,1)S(1)} %collective-permute-done.2.refs_1_), channel_id=1, source_target_pairs={{8,0},{16,8},{24,16},{32,24},{40,32},{48,40},{56,48},{0,56},{72,64... | collective-permute-start | bytes 393224 | tf_op jit(solution)/shard_map/ppermute | solution.py:60
  24.1 2.7 %collective-permute-start.7 = (bf16[2,128,256]{2,1,0:T(8,128)(2,1)S(1)}, bf16[2,128,256]{2,1,0:T(8,128)(2,1)S(1)}, u32[]{:S(2)}, u32[]{:S(2)}) collective-permute-start(bf16[2,128,256]{2,1,0:T(8,128)(2,1)S(1)} %collective-permute-done.5.refs_3_), channel_id=1, source_target_pairs={{8,0},{16,8},{24,16},{32,24},{40,32},{48,40},{56,48},{0,56},{72,64... | collective-permute-start | bytes 393224 | tf_op jit(solution)/shard_map/ppermute | solution.py:60
  29.2 2.7 %collective-permute-start.9 = (bf16[1,128,256]{2,1,0:T(8,128)(2,1)S(1)}, bf16[1,128,256]{2,1,0:T(8,128)(2,1)S(1)}, u32[]{:S(2)}, u32[]{:S(2)}) collective-permute-start(bf16[1,128,256]{2,1,0:T(8,128)(2,1)S(1)} %slice.46), channel_id=1, source_target_pairs={{8,0},{16,8},{24,16},{32,24},{40,32},{48,40},{56,48},{0,56},{72,64... | collective-permute-start | bytes 196616 | tf_op jit(solution)/shard_map/ppermute | solution.py:60
  43.6 2.7 %collective-permute-start.15 = (bf16[8,128,256]{2,1,0:T(8,128)(2,1)S(1)}, bf16[8,128,256]{2,1,0:T(8,128)(2,1)}, u32[]{:S(2)}, u32[]{:S(2)}) collective-permute-start(bf16[8,128,256]{2,1,0:T(8,128)(2,1)S(1)} %get-tuple-element.43), channel_id=1, source_target_pairs={{64,0},{72,8},{80,16},{88,24},{96,32},{104,40},{112,48},{120,56},{... | collective-permute-start | bytes 1572872 | tf_op jit(solution)/shard_map/ppermute | solution.py:60
  50.5 2.6 %collective-permute-done.14.below_ref = bf16[8,128,256]{2,1,0:T(8,128)(2,1)S(1)} collective-permute-done((bf16[8,128,256]{2,1,0:T(8,128)(2,1)}, bf16[8,128,256]{2,1,0:T(8,128)(2,1)S(1)}, u32[]{:S(2)}, u32[]{:S(2)}) %collective-permute-start.14) | collective-permute-done | bytes 524320 | tf_op jit(solution)/shard_map/ppermute | solution.py:60
  55.0 9.7 %attend.1 = (bf16[256,1024]{1,0:T(8,128)(2,1)}, f32[512,256]{1,0:T(8,128)S(1)}, bf16[8,128,256]{2,1,0:T(8,128)(2,1)S(1)}) custom-call(s32[1]{0:T(128)} %bitcast.at_ref, s32[2,4]{1,0:T(2,128)S(1)} %copy-done.1, s32[2]{0:T(128)S(1)} %copy-done.7, bf16[256,1024]{1,0:T(8,128)(2,1)S(1)} %copy-done.3, bf16[256,1024]{1,0:T(8,128)(2,1)S(1)} %copy-done.4, ...), custom_call_target="tpu_custom_call" | custom-call | flops 9600000000 | bytes 6291456 | tf_op jit(solution)/shard_map/attend/pallas_call | solution.py:220
  67.3 6.6 %collective-permute-done.17.refs_5_ = bf16[8,128,256]{2,1,0:T(8,128)(2,1)S(1)} collective-permute-done((bf16[8,128,256]{2,1,0:T(8,128)(2,1)S(1)}, bf16[8,128,256]{2,1,0:T(8,128)(2,1)S(1)}, u32[]{:S(2)}, u32[]{:S(2)}) %collective-permute-start.17) | collective-permute-done | bytes 524320 | tf_op jit(solution)/shard_map/ppermute | solution.py:60
  78.1 6.0 %collective-permute-done.16.back_ref = bf16[256,256]{1,0:T(8,128)(2,1)S(1)} collective-permute-done((bf16[256,256]{1,0:T(8,128)(2,1)S(1)}, bf16[256,256]{1,0:T(8,128)(2,1)S(1)}, u32[]{:S(2)}, u32[]{:S(2)}) %collective-permute-start.16) | collective-permute-done | bytes 131104 | tf_op jit(solution)/shard_map/ppermute | solution.py:55
  84.1 3.4 %all-gather.3.cloned.1.call-done.weights_ref = bf16[512,1024]{1,0:T(8,128)(2,1)} async-done(((bf16[64,1024]{1,0:T(8,128)(2,1)}), bf16[512,1024]{1,0:T(8,128)(2,1)}) %all-gather.3.cloned.1.call-update) | async-done | bytes 1048592 | tf_op jit(solution)/shard_map/all_gather | solution.py:454
  89.0 22.1 %all_to_all.10.terms_ref = bf16[8,256,256]{2,1,0:T(8,128)(2,1)S(1)} all-to-all(bf16[8,256,256]{2,1,0:T(8,128)(2,1)S(1)} %bitcast.8), channel_id=1, replica_groups={{0,8,16,24,32,40,48,56},{64,72,80,88,96,104,112,120},{128,136,144,152,1..., dimensions={0} | all-to-all | bytes 2097152 | tf_op jit(solution)/shard_map/all_to_all | solution.py:470
  112.1 10.1 %collective-permute-start.22 = (bf16[256,256]{1,0:T(8,128)(2,1)S(1)}, bf16[256,256]{1,0:T(8,128)(2,1)S(1)}, u32[]{:S(2)}, u32[]{:S(2)}) collective-permute-start(bf16[256,256]{1,0:T(8,128)(2,1)S(1)} %collective-permute-done.21.own_ref), channel_id=1, source_target_pairs={{0,2},{1,3},{2,4},{3,5},{4,6},{5,7},{6,0},{7,1},{8,10},{9,11},{10,... | collective-permute-start | bytes 393224 | tf_op jit(solution)/shard_map/ppermute | solution.py:60
  122.2 4.8 %collective-permute-start.23 = (bf16[256,256]{1,0:T(8,128)(2,1)S(1)}, bf16[256,256]{1,0:T(8,128)(2,1)S(1)}, u32[]{:S(2)}, u32[]{:S(2)}) collective-permute-start(bf16[256,256]{1,0:T(8,128)(2,1)S(1)} %collective-permute-done.21.own_ref), channel_id=1, source_target_pairs={{2,0},{3,1},{4,2},{5,3},{6,4},{7,5},{0,6},{1,7},{10,8},{11,9},{12,... | collective-permute-start | bytes 393224 | tf_op jit(solution)/shard_map/ppermute | solution.py:60
  127.0 2.7 %collective-permute-done.22.refs_0_ = bf16[256,256]{1,0:T(8,128)(2,1)S(1)} collective-permute-done((bf16[256,256]{1,0:T(8,128)(2,1)S(1)}, bf16[256,256]{1,0:T(8,128)(2,1)S(1)}, u32[]{:S(2)}, u32[]{:S(2)}) %collective-permute-start.22) | collective-permute-done | bytes 131104 | tf_op jit(solution)/shard_map/ppermute | solution.py:60
  129.8 2.7 %collective-permute-start.25 = (bf16[128,256]{1,0:T(8,128)(2,1)S(1)}, bf16[128,256]{1,0:T(8,128)(2,1)S(1)}, u32[]{:S(2)}, u32[]{:S(2)}) collective-permute-start(bf16[128,256]{1,0:T(8,128)(2,1)S(1)} %slice.51), channel_id=1, source_target_pairs={{2,0},{3,1},{4,2},{5,3},{6,4},{7,5},{0,6},{1,7},{10,8},{11,9},{12,... | collective-permute-start | bytes 196616 | tf_op jit(solution)/shard_map/ppermute | solution.py:60
  134.5 18.6 %collective-permute-start.26 = (bf16[1024,256]{1,0:T(8,128)(2,1)S(1)}, bf16[1024,256]{1,0:T(8,128)(2,1)S(1)}, u32[]{:S(2)}, u32[]{:S(2)}) collective-permute-start(bf16[1024,256]{1,0:T(8,128)(2,1)S(1)} %constant_dynamic-update-slice_fusion), channel_id=1, source_target_pairs={{0,1},{1,0},{2,3},{3,2},{4,5},{5,4},{6,7},{7,6},{8,9},{9,8},{10,11... | collective-permute-start | bytes 1572872 | tf_op jit(solution)/shard_map/ppermute | solution.py:475
  156.3 3.2 %weight_terms.1 = bf16[8,256,256]{2,1,0:T(8,128)(2,1)} custom-call(bf16[8,256,256]{2,1,0:T(8,128)(2,1)S(1)} %place_heads.1.grad_ref, bf16[1024,1024]{1,0:T(8,128)(2,1)S(1)} %copy-done), custom_call_target="tpu_custom_call" | custom-call | flops 1073741824 | bytes 4194304 | tf_op jit(solution)/shard_map/weight_terms/pallas_call | solution.py:354
  159.5 3.7 %all-to-all-start.1 = ((bf16[8,256,256]{2,1,0:T(8,128)(2,1)}), bf16[8,256,256]{2,1,0:T(8,128)(2,1)S(1)}, u32[]{:S(2)}, u32[]{:S(2)}) async-start(bf16[8,256,256]{2,1,0:T(8,128)(2,1)} %weight_terms.1), calls=%async_computation.1 | async-start | bytes 2097152 | tf_op jit(solution)/shard_map/all_to_all | solution.py:481
  166.5 5.6 %collective-permute-done.29 = bf16[128,1024]{1,0:T(8,128)(2,1)S(1)} collective-permute-done((bf16[128,1024]{1,0:T(8,128)(2,1)S(1)}, bf16[128,1024]{1,0:T(8,128)(2,1)S(1)}, u32[]{:S(2)}, u32[]{:S(2)}) %collective-permute-start.29) | collective-permute-done | bytes 262176 | tf_op jit(solution)/shard_map/ppermute | solution.py:60
  172.2 3.1 %collective-permute-start.30 = (bf16[256,1024]{1,0:T(8,128)(2,1)S(1)}, bf16[256,1024]{1,0:T(8,128)(2,1)S(1)}, u32[]{:S(2)}, u32[]{:S(2)}) collective-permute-start(bf16[256,1024]{1,0:T(8,128)(2,1)S(1)} %pad_maximum_fusion.1), channel_id=1, source_target_pairs={{64,0},{72,8},{80,16},{88,24},{96,32},{104,40},{112,48},{120,56},{... | collective-permute-start | bytes 1572872 | tf_op jit(solution)/shard_map/ppermute | solution.py:60
  175.5 9.8 %collective-permute-done.30 = bf16[256,1024]{1,0:T(8,128)(2,1)S(1)} collective-permute-done((bf16[256,1024]{1,0:T(8,128)(2,1)S(1)}, bf16[256,1024]{1,0:T(8,128)(2,1)S(1)}, u32[]{:S(2)}, u32[]{:S(2)}) %collective-permute-start.30) | collective-permute-done | bytes 524320 | tf_op jit(solution)/shard_map/ppermute | solution.py:60
  185.3 3.3 %collective-permute-done.28 = bf16[256,1024]{1,0:T(8,128)(2,1)S(1)} collective-permute-done((bf16[256,1024]{1,0:T(8,128)(2,1)S(1)}, bf16[256,1024]{1,0:T(8,128)(2,1)S(1)}, u32[]{:S(2)}, u32[]{:S(2)}) %collective-permute-start.28) | collective-permute-done | bytes 524320 | tf_op jit(solution)/shard_map/ppermute | solution.py:60
  189.7 2.8 %all-to-all-done.1.terms_ref = bf16[8,256,256]{2,1,0:T(8,128)(2,1)S(1)} async-done(((bf16[8,256,256]{2,1,0:T(8,128)(2,1)}), bf16[8,256,256]{2,1,0:T(8,128)(2,1)S(1)}, u32[]{:S(2)}, u32[]{:S(2)}) %all-to-all-start.1) | async-done | bytes 1048608 | tf_op jit(solution)/shard_map/all_to_all | solution.py:481
  (97 shorter events, 47.5 us)
Async XLA Ops:
  7.2 80.3 %all-gather.3.cloned.1.call-start = ((), (), s32[]{:S(2)}) async-start(), calls=%async_computation.2 | async-start | bytes 1179648 | tf_op jit(solution)/shard_map/all_gather | solution.py:454
  8.4 10.7 %collective-permute-start.1 = (bf16[2,128,256]{2,1,0:T(8,128)(2,1)S(1)}, bf16[2,128,256]{2,1,0:T(8,128)(2,1)S(1)}, u32[]{:S(2)}, u32[]{:S(2)}) collective-permute-start(bf16[2,128,256]{2,1,0:T(8,128)(2,1)S(1)} %bitcast.9), channel_id=1, source_target_pairs={{0,8},{8,16},{16,24},{24,32},{32,40},{40,48},{48,56},{56,0},{64,72... | collective-permute-start | bytes 393224 | tf_op jit(solution)/shard_map/ppermute | solution.py:60
  10.9 8.2 %collective-permute-start.2 = (bf16[2,128,256]{2,1,0:T(8,128)(2,1)S(1)}, bf16[2,128,256]{2,1,0:T(8,128)(2,1)S(1)}, u32[]{:S(2)}, u32[]{:S(2)}) collective-permute-start(bf16[2,128,256]{2,1,0:T(8,128)(2,1)S(1)} %bitcast.10), channel_id=1, source_target_pairs={{8,0},{16,8},{24,16},{32,24},{40,32},{48,40},{56,48},{0,56},{72,64... | collective-permute-start | bytes 393224 | tf_op jit(solution)/shard_map/ppermute | solution.py:60
  19.1 5.0 %collective-permute-start.4 = (bf16[2,128,256]{2,1,0:T(8,128)(2,1)S(1)}, bf16[2,128,256]{2,1,0:T(8,128)(2,1)S(1)}, u32[]{:S(2)}, u32[]{:S(2)}) collective-permute-start(bf16[2,128,256]{2,1,0:T(8,128)(2,1)S(1)} %collective-permute-done.1.refs_0_), channel_id=1, source_target_pairs={{0,8},{8,16},{16,24},{24,32},{32,40},{40,48},{48,56},{56,0},{64,72... | collective-permute-start | bytes 393224 | tf_op jit(solution)/shard_map/ppermute | solution.py:60
  24.1 5.0 %collective-permute-start.6 = (bf16[2,128,256]{2,1,0:T(8,128)(2,1)S(1)}, bf16[2,128,256]{2,1,0:T(8,128)(2,1)S(1)}, u32[]{:S(2)}, u32[]{:S(2)}) collective-permute-start(bf16[2,128,256]{2,1,0:T(8,128)(2,1)S(1)} %collective-permute-done.4.refs_2_), channel_id=1, source_target_pairs={{0,8},{8,16},{16,24},{24,32},{32,40},{40,48},{48,56},{56,0},{64,72... | collective-permute-start | bytes 393224 | tf_op jit(solution)/shard_map/ppermute | solution.py:60
  24.1 5.0 %collective-permute-start.7 = (bf16[2,128,256]{2,1,0:T(8,128)(2,1)S(1)}, bf16[2,128,256]{2,1,0:T(8,128)(2,1)S(1)}, u32[]{:S(2)}, u32[]{:S(2)}) collective-permute-start(bf16[2,128,256]{2,1,0:T(8,128)(2,1)S(1)} %collective-permute-done.5.refs_3_), channel_id=1, source_target_pairs={{8,0},{16,8},{24,16},{32,24},{40,32},{48,40},{56,48},{0,56},{72,64... | collective-permute-start | bytes 393224 | tf_op jit(solution)/shard_map/ppermute | solution.py:60
  34.2 7.9 %collective-permute-start.12 = (bf16[4,128,256]{2,1,0:T(8,128)(2,1)S(1)}, bf16[4,128,256]{2,1,0:T(8,128)(2,1)S(1)}, u32[]{:S(2)}, u32[]{:S(2)}) collective-permute-start(bf16[4,128,256]{2,1,0:T(8,128)(2,1)S(1)} %get-tuple-element.40), channel_id=1, source_target_pairs={{0,64},{8,72},{16,80},{24,88},{32,96},{40,104},{48,112},{56,120},{... | collective-permute-start | bytes 786440 | tf_op jit(solution)/shard_map/ppermute | solution.py:60
  35.5 6.6 %collective-permute-start.13 = (bf16[4,128,256]{2,1,0:T(8,128)(2,1)S(1)}, bf16[4,128,256]{2,1,0:T(8,128)(2,1)S(1)}, u32[]{:S(2)}, u32[]{:S(2)}) collective-permute-start(bf16[4,128,256]{2,1,0:T(8,128)(2,1)S(1)} %get-tuple-element.41), channel_id=1, source_target_pairs={{64,0},{72,8},{80,16},{88,24},{96,32},{104,40},{112,48},{120,56},{... | collective-permute-start | bytes 786440 | tf_op jit(solution)/shard_map/ppermute | solution.py:60
  43.6 9.5 %collective-permute-start.14 = (bf16[8,128,256]{2,1,0:T(8,128)(2,1)}, bf16[8,128,256]{2,1,0:T(8,128)(2,1)S(1)}, u32[]{:S(2)}, u32[]{:S(2)}) collective-permute-start(bf16[8,128,256]{2,1,0:T(8,128)(2,1)} %get-tuple-element.42), channel_id=1, source_target_pairs={{0,64},{8,72},{16,80},{24,88},{32,96},{40,104},{48,112},{56,120},{... | collective-permute-start | bytes 1572872 | tf_op jit(solution)/shard_map/ppermute | solution.py:60
  43.6 10.3 %collective-permute-start.15 = (bf16[8,128,256]{2,1,0:T(8,128)(2,1)S(1)}, bf16[8,128,256]{2,1,0:T(8,128)(2,1)}, u32[]{:S(2)}, u32[]{:S(2)}) collective-permute-start(bf16[8,128,256]{2,1,0:T(8,128)(2,1)S(1)} %get-tuple-element.43), channel_id=1, source_target_pairs={{64,0},{72,8},{80,16},{88,24},{96,32},{104,40},{112,48},{120,56},{... | collective-permute-start | bytes 1572872 | tf_op jit(solution)/shard_map/ppermute | solution.py:60
  47.0 107.7 %all-gather.5.cloned.1.call-start = ((), (), s32[]{:S(2)}) async-start(), calls=%async_computation.3 | async-start | bytes 2621440 | tf_op jit(solution)/shard_map/all_gather | solution.py:466
  64.7 9.2 %collective-permute-start.17 = (bf16[8,128,256]{2,1,0:T(8,128)(2,1)S(1)}, bf16[8,128,256]{2,1,0:T(8,128)(2,1)S(1)}, u32[]{:S(2)}, u32[]{:S(2)}) collective-permute-start(bf16[8,128,256]{2,1,0:T(8,128)(2,1)S(1)} %get-tuple-element.49.refs_4_), channel_id=1, source_target_pairs={{0,64},{8,72},{16,80},{24,88},{32,96},{40,104},{48,112},{56,120},{... | collective-permute-start | bytes 1572872 | tf_op jit(solution)/shard_map/ppermute | solution.py:60
  67.1 8.1 %collective-permute-start.18 = (bf16[8,128,256]{2,1,0:T(8,128)(2,1)S(1)}, bf16[8,128,256]{2,1,0:T(8,128)(2,1)S(1)}, u32[]{:S(2)}, u32[]{:S(2)}) collective-permute-start(bf16[8,128,256]{2,1,0:T(8,128)(2,1)S(1)} %get-tuple-element.49.refs_4_), channel_id=1, source_target_pairs={{64,0},{72,8},{80,16},{88,24},{96,32},{104,40},{112,48},{120,56},{... | collective-permute-start | bytes 1572872 | tf_op jit(solution)/shard_map/ppermute | solution.py:60
  73.9 13.6 %collective-permute-start.19 = (bf16[4,128,256]{2,1,0:T(8,128)(2,1)S(1)}, bf16[4,128,256]{2,1,0:T(8,128)(2,1)S(1)}, u32[]{:S(2)}, u32[]{:S(2)}) collective-permute-start(bf16[4,128,256]{2,1,0:T(8,128)(2,1)S(1)} %slice.48), channel_id=1, source_target_pairs={{0,64},{8,72},{16,80},{24,88},{32,96},{40,104},{48,112},{56,120},{... | collective-permute-start | bytes 786440 | tf_op jit(solution)/shard_map/ppermute | solution.py:60
  75.2 12.3 %collective-permute-start.20 = (bf16[4,128,256]{2,1,0:T(8,128)(2,1)S(1)}, bf16[4,128,256]{2,1,0:T(8,128)(2,1)S(1)}, u32[]{:S(2)}, u32[]{:S(2)}) collective-permute-start(bf16[4,128,256]{2,1,0:T(8,128)(2,1)S(1)} %slice.49), channel_id=1, source_target_pairs={{64,0},{72,8},{80,16},{88,24},{96,32},{104,40},{112,48},{120,56},{... | collective-permute-start | bytes 786440 | tf_op jit(solution)/shard_map/ppermute | solution.py:60
  76.8 7.3 %collective-permute-start.16 = (bf16[256,256]{1,0:T(8,128)(2,1)S(1)}, bf16[256,256]{1,0:T(8,128)(2,1)S(1)}, u32[]{:S(2)}, u32[]{:S(2)}) collective-permute-start(bf16[256,256]{1,0:T(8,128)(2,1)S(1)} %slice.55), channel_id=1, source_target_pairs={{8,0},{16,8},{24,16},{32,24},{40,32},{48,40},{56,48},{64,56},{72,6... | collective-permute-start | bytes 393224 | tf_op jit(solution)/shard_map/ppermute | solution.py:55
  112.1 17.7 %collective-permute-start.22 = (bf16[256,256]{1,0:T(8,128)(2,1)S(1)}, bf16[256,256]{1,0:T(8,128)(2,1)S(1)}, u32[]{:S(2)}, u32[]{:S(2)}) collective-permute-start(bf16[256,256]{1,0:T(8,128)(2,1)S(1)} %collective-permute-done.21.own_ref), channel_id=1, source_target_pairs={{0,2},{1,3},{2,4},{3,5},{4,6},{5,7},{6,0},{7,1},{8,10},{9,11},{10,... | collective-permute-start | bytes 393224 | tf_op jit(solution)/shard_map/ppermute | solution.py:60
  122.2 7.6 %collective-permute-start.23 = (bf16[256,256]{1,0:T(8,128)(2,1)S(1)}, bf16[256,256]{1,0:T(8,128)(2,1)S(1)}, u32[]{:S(2)}, u32[]{:S(2)}) collective-permute-start(bf16[256,256]{1,0:T(8,128)(2,1)S(1)} %collective-permute-done.21.own_ref), channel_id=1, source_target_pairs={{2,0},{3,1},{4,2},{5,3},{6,4},{7,5},{0,6},{1,7},{10,8},{11,9},{12,... | collective-permute-start | bytes 393224 | tf_op jit(solution)/shard_map/ppermute | solution.py:60
  134.5 20.1 %collective-permute-start.26 = (bf16[1024,256]{1,0:T(8,128)(2,1)S(1)}, bf16[1024,256]{1,0:T(8,128)(2,1)S(1)}, u32[]{:S(2)}, u32[]{:S(2)}) collective-permute-start(bf16[1024,256]{1,0:T(8,128)(2,1)S(1)} %constant_dynamic-update-slice_fusion), channel_id=1, source_target_pairs={{0,1},{1,0},{2,3},{3,2},{4,5},{5,4},{6,7},{7,6},{8,9},{9,8},{10,11... | collective-permute-start | bytes 1572872 | tf_op jit(solution)/shard_map/ppermute | solution.py:475
  159.5 32.9 %all-to-all-start.1 = ((bf16[8,256,256]{2,1,0:T(8,128)(2,1)}), bf16[8,256,256]{2,1,0:T(8,128)(2,1)S(1)}, u32[]{:S(2)}, u32[]{:S(2)}) async-start(bf16[8,256,256]{2,1,0:T(8,128)(2,1)} %weight_terms.1), calls=%async_computation.1 | async-start | bytes 2097152 | tf_op jit(solution)/shard_map/all_to_all | solution.py:481
  164.5 7.6 %collective-permute-start.29 = (bf16[128,1024]{1,0:T(8,128)(2,1)S(1)}, bf16[128,1024]{1,0:T(8,128)(2,1)S(1)}, u32[]{:S(2)}, u32[]{:S(2)}) collective-permute-start(bf16[128,1024]{1,0:T(8,128)(2,1)S(1)} %get-tuple-element.56), channel_id=1, source_target_pairs={{64,0},{72,8},{80,16},{88,24},{96,32},{104,40},{112,48},{120,56},{... | collective-permute-start | bytes 786440 | tf_op jit(solution)/shard_map/ppermute | solution.py:60
  166.4 8.9 %collective-permute-start.27 = (bf16[128,1024]{1,0:T(8,128)(2,1)S(1)}, bf16[128,1024]{1,0:T(8,128)(2,1)S(1)}, u32[]{:S(2)}, u32[]{:S(2)}) collective-permute-start(bf16[128,1024]{1,0:T(8,128)(2,1)S(1)} %get-tuple-element.54), channel_id=1, source_target_pairs={{0,64},{8,72},{16,80},{24,88},{32,96},{40,104},{48,112},{56,120},{... | collective-permute-start | bytes 786440 | tf_op jit(solution)/shard_map/ppermute | solution.py:60
  172.2 13.1 %collective-permute-start.30 = (bf16[256,1024]{1,0:T(8,128)(2,1)S(1)}, bf16[256,1024]{1,0:T(8,128)(2,1)S(1)}, u32[]{:S(2)}, u32[]{:S(2)}) collective-permute-start(bf16[256,1024]{1,0:T(8,128)(2,1)S(1)} %pad_maximum_fusion.1), channel_id=1, source_target_pairs={{64,0},{72,8},{80,16},{88,24},{96,32},{104,40},{112,48},{120,56},{... | collective-permute-start | bytes 1572872 | tf_op jit(solution)/shard_map/ppermute | solution.py:60
  175.4 13.2 %collective-permute-start.28 = (bf16[256,1024]{1,0:T(8,128)(2,1)S(1)}, bf16[256,1024]{1,0:T(8,128)(2,1)S(1)}, u32[]{:S(2)}, u32[]{:S(2)}) collective-permute-start(bf16[256,1024]{1,0:T(8,128)(2,1)S(1)} %pad_maximum_fusion), channel_id=1, source_target_pairs={{0,64},{8,72},{16,80},{24,88},{32,96},{40,104},{48,112},{56,120},{... | collective-permute-start | bytes 1572872 | tf_op jit(solution)/shard_map/ppermute | solution.py:60
  (20 other events, 311.5 us)
Sparse Core Ops, SparseCore 0:
  47.1 40.3 all-gather.2
  89.3 48.0 all-gather.4

commit v10 on v7

--- a/solution.py
+++ b/solution.py
@@ -418,43 +418,44 @@
     own_index = lax.axis_index("own").astype(jnp.int32).reshape(1)
     own_kv = jnp.concatenate([key_rows, value_rows], axis=1).reshape(NB, BLK, 2 * DH)
 
-    inputs_x = lax.all_gather(inputs, "seq", axis=0, axis_index_groups=X_GROUPS, tiled=True)
-
-    from_below, from_above, listed = own_kv, own_kv, far_blocks
-    plane, lists = [], []
-    for distance in range(1, NZ // 2 + 1):
+    from_below, from_above = both_ways(own_kv, own_kv, "seq", Z_UP)
+    across = [(x * NZ + z, (x + 2) % NX * NZ + z) for x in range(NX) for z in range(NZ)]
+    list_across = lax.ppermute(far_blocks, "seq", across)
+    from_below, from_above, list_across, listed = lax.optimization_barrier(
+        (from_below, from_above, list_across, far_blocks)
+    )
+    plane = [from_below, from_above]
+    for distance in range(2, NZ // 2 + 1):
         if distance == NZ // 2:
             from_below, from_above = from_below[: NB // 2], from_above[NB // 2 :]
         from_below, from_above = both_ways(from_below, from_above, "seq", Z_UP)
-        if distance < NX:
-            pairs = [(x * NZ + z, (x - distance) % NX * NZ + z) for x in range(NX) for z in range(NZ)]
-            arrived = lax.ppermute(listed, "seq", pairs)
-            arrived, listed, from_below, from_above = lax.optimization_barrier(
-                (arrived, listed, from_below, from_above)
-            )
-            lists.append(arrived)
         plane += [from_below, from_above]
-    lists = [far_blocks, *lists]
-    from_below, key_weight, value_weight = lax.optimization_barrier(
-        (plane[0], key_weight, value_weight)
+    prev_kv = shifted(own_kv, "seq", 1)
+    plane, low, high = pick_across(at, list_across, own_kv, plane)
+    low, high, listed, key_weight, value_weight = lax.optimization_barrier(
+        (low, high, listed, key_weight, value_weight)
     )
-    plane[0] = from_below
     weights = jnp.concatenate([key_weight.T, value_weight.T])
     weights = lax.all_gather(weights, "seq", axis=0, axis_index_groups=Z_GROUPS, tiled=True)
-    prev_kv = shifted(own_kv, "seq", 1)
-    plane, low, high = pick_across(at, lists[2], own_kv, plane)
     low, high = both_ways(low, high, "seq", X_UP)
-    up, down = pick(at, lists[1], lists[3], plane, low, high)
+    list_below, list_above = both_ways(listed, listed, "seq", X_UP)
+    up, down = pick(at, list_above, list_below, plane, low, high)
     from_below, from_above = both_ways(up, down, "seq", X_UP)
 
-    far_count, inputs_x = lax.optimization_barrier((far_count, inputs_x))
     query_grad, window, far_grad = attend(
         at, far_blocks, far_count, queries, out_grad, prev_kv, own_kv, plane, from_below, from_above
     )
-    far_all = ring_gather(far_grad, "seq", X_UP, NX)
     back = shifted(window[:tokens].astype(BF16), "seq", -1)
-    above, weights = lax.optimization_barrier((lists[1], weights))
-    dense = spread(at, [lists[0], above, *lists[2:]], far_grad, far_all)
+    far_below, far_above = both_ways(far_grad, far_grad, "seq", X_UP)
+    far_below, far_above, back, inputs = lax.optimization_barrier(
+        (far_below, far_above, back, inputs)
+    )
+    far_across = both_ways(far_below[:FARS], far_above[FARS:], "seq", X_UP)
+    far_all = (far_below, far_above, *far_across)
+    inputs_x = lax.all_gather(inputs, "seq", axis=0, axis_index_groups=X_GROUPS, tiled=True)
+    list_above, weights = lax.optimization_barrier((list_above, weights))
+    lists = (far_blocks, list_above, list_across, list_below)
+    dense = spread(at, lists, far_grad, far_all)
     dense = dense.reshape(NZ, tokens, 2 * DH)
     terms = lax.all_to_all(dense, "seq", 0, 0, axis_index_groups=Z_GROUPS, tiled=True)
     kv_grad = finish(terms, back, window)

time: 203 us -> 193 us (0.951)
  waiting for transfers between devices: 87.3 us -> 57.5 us
  blocking collectives: 0 us -> 22.6 us
  starting transfers between devices: 75.6 us -> 73.5 us
    ppermute x12 -> x13, waiting for transfers between devices: 46.7 us -> 17.5 us  [both_ways(): lax.ppermute(upward, axis, pairs)]
    all_to_all x0 -> x1, blocking collectives: none -> 22.6 us  [local(): lax.all_to_all(dense, 'seq', 0, 0, axis_index_groups=Z_GROUPS, tiled=True)]
    ppermute x12 -> x13, waiting for transfers between devices: 1.45 us -> 18 us  [both_ways(): lax.ppermute(downward, axis, back)]
    ppermute x2, waiting for transfers between devices: 20.2 us -> 6.93 us  [shifted(): lax.ppermute(value, axis, [(source, source + steps) for source in range(l...]
    all_gather x1, waiting for transfers between devices: 0.23 us -> 10.1 us  [local(): lax.all_gather(weights, 'seq', axis=0, axis_index_groups=Z_GROUPS, tiled=...]
    ppermute x12 -> x13, starting transfers between devices: 10.9 us -> 17.5 us  [both_ways(): lax.ppermute(upward, axis, pairs)]
    all_to_all x1 -> x0, starting transfers between devices: 5.45 us -> none  [local(): lax.all_to_all(dense, 'seq', 0, 0, axis_index_groups=Z_GROUPS, tiled=True)]
    all_to_all x1 -> x0, waiting for transfers between devices: 5.31 us -> none  [local(): lax.all_to_all(dense, 'seq', 0, 0, axis_index_groups=Z_GROUPS, tiled=True)]
  transfers between devices with their start and end apart: 35 -> 34, of which waited for: 20 -> 20; matrix products, arithmetic and copies ran while one was open for 1% -> 1% of each run, Pallas kernels for 6% -> 7%
where the time goes in v10:
time: 193 us
  starting transfers between devices  73.5 us (38%)
  waiting for transfers between devices  57.5 us (30%)
  blocking collectives  22.6 us (12%)
  Pallas kernels  18.1 us (9%)
  between operations  14.4 us (7%)
  local copies, waits for them, and re-layouts  3.59 us (2%)
  other arithmetic  3 us (2%)
    ppermute x13, starting transfers between devices, both_ways(): lax.ppermute(downward, axis, back)  33.8 us
    all_to_all x1, blocking collectives, local(): lax.all_to_all(dense, 'seq', 0, 0, axis_index_groups=Z_GROUPS, tiled=True)  22.6 us
    ppermute x13, waiting for transfers between devices, both_ways(): lax.ppermute(downward, axis, back)  18 us
    ppermute x13, starting transfers between devices, both_ways(): lax.ppermute(upward, axis, pairs)  17.5 us
    ppermute x13, waiting for transfers between devices, both_ways(): lax.ppermute(upward, axis, pairs)  17.5 us
    ppermute x1, starting transfers between devices, local(): lax.ppermute(jnp.concatenate([moved, *same_core]), 'own', CORES)  12 us
    all_gather x1, waiting for transfers between devices, local(): lax.all_gather(weights, 'seq', axis=0, axis_index_groups=Z_GROUPS, tiled=...  10.1 us
    pallas_call x1, Pallas kernels, attend(): pl.pallas_call(attend_kernel, out_shape=(jax.ShapeDtypeStruct((NB * BLK,...  9.69 us
  transfers between devices with their start and end apart: 34, of which 20 were waited for; matrix products, arithmetic and copies ran while one was open for 1% of the time, Pallas kernels for 7%

profile of v10, /device:TPU:1, one launch (start us, length us, event | category | flops | bytes accessed | tf_op | source)
XLA Modules:
  0.0 192.6 jit_solution(6242678649711662412)
XLA Ops:
  8.4 2.5 %collective-permute-start.1 = (bf16[2,128,256]{2,1,0:T(8,128)(2,1)S(1)}, bf16[2,128,256]{2,1,0:T(8,128)(2,1)S(1)}, u32[]{:S(2)}, u32[]{:S(2)}) collective-permute-start(bf16[2,128,256]{2,1,0:T(8,128)(2,1)S(1)} %bitcast.9), channel_id=1, source_target_pairs={{0,8},{8,16},{16,24},{24,32},{32,40},{40,48},{48,56},{56,0},{64,72... | collective-permute-start | bytes 393224 | tf_op jit(solution)/shard_map/ppermute | solution.py:59
  10.9 4.0 %collective-permute-start.2 = (bf16[2,128,256]{2,1,0:T(8,128)(2,1)S(1)}, bf16[2,128,256]{2,1,0:T(8,128)(2,1)S(1)}, u32[]{:S(2)}, u32[]{:S(2)}) collective-permute-start(bf16[2,128,256]{2,1,0:T(8,128)(2,1)S(1)} %bitcast.10), channel_id=1, source_target_pairs={{8,0},{16,8},{24,16},{32,24},{40,32},{48,40},{56,48},{0,56},{72,64... | collective-permute-start | bytes 393224 | tf_op jit(solution)/shard_map/ppermute | solution.py:59
  14.9 2.7 %collective-permute-start.3 = (s32[2,4]{1,0:T(2,128)}, s32[2,4]{1,0:T(2,128)S(1)}, u32[]{:S(2)}, u32[]{:S(2)}) collective-permute-start(s32[2,4]{1,0:T(2,128)} %refs_0_.1), channel_id=1, source_target_pairs={{0,128},{8,136},{16,144},{24,152},{32,160},{40,168},{48,176},{56,1... | collective-permute-start | bytes 104 | tf_op jit(solution)/shard_map/ppermute | solution.py:423
  19.1 2.7 %collective-permute-start.5 = (bf16[2,128,256]{2,1,0:T(8,128)(2,1)S(1)}, bf16[2,128,256]{2,1,0:T(8,128)(2,1)S(1)}, u32[]{:S(2)}, u32[]{:S(2)}) collective-permute-start(bf16[2,128,256]{2,1,0:T(8,128)(2,1)S(1)} %collective-permute-done.2.refs_1_), channel_id=1, source_target_pairs={{8,0},{16,8},{24,16},{32,24},{40,32},{48,40},{56,48},{0,56},{72,64... | collective-permute-start | bytes 393224 | tf_op jit(solution)/shard_map/ppermute | solution.py:59
  21.8 2.4 %collective-permute-done.4.refs_2_ = bf16[2,128,256]{2,1,0:T(8,128)(2,1)S(1)} collective-permute-done((bf16[2,128,256]{2,1,0:T(8,128)(2,1)S(1)}, bf16[2,128,256]{2,1,0:T(8,128)(2,1)S(1)}, u32[]{:S(2)}, u32[]{:S(2)}) %collective-permute-start.4) | collective-permute-done | bytes 131104 | tf_op jit(solution)/shard_map/ppermute | solution.py:59
  24.1 2.7 %collective-permute-start.7 = (bf16[2,128,256]{2,1,0:T(8,128)(2,1)S(1)}, bf16[2,128,256]{2,1,0:T(8,128)(2,1)S(1)}, u32[]{:S(2)}, u32[]{:S(2)}) collective-permute-start(bf16[2,128,256]{2,1,0:T(8,128)(2,1)S(1)} %collective-permute-done.5.refs_3_), channel_id=1, source_target_pairs={{8,0},{16,8},{24,16},{32,24},{40,32},{48,40},{56,48},{0,56},{72,64... | collective-permute-start | bytes 393224 | tf_op jit(solution)/shard_map/ppermute | solution.py:59
  29.2 2.7 %collective-permute-start.9 = (bf16[1,128,256]{2,1,0:T(8,128)(2,1)S(1)}, bf16[1,128,256]{2,1,0:T(8,128)(2,1)S(1)}, u32[]{:S(2)}, u32[]{:S(2)}) collective-permute-start(bf16[1,128,256]{2,1,0:T(8,128)(2,1)S(1)} %slice.46), channel_id=1, source_target_pairs={{8,0},{16,8},{24,16},{32,24},{40,32},{48,40},{56,48},{0,56},{72,64... | collective-permute-start | bytes 196616 | tf_op jit(solution)/shard_map/ppermute | solution.py:59
  43.6 2.7 %collective-permute-start.15 = (bf16[8,128,256]{2,1,0:T(8,128)(2,1)S(1)}, bf16[8,128,256]{2,1,0:T(8,128)(2,1)}, u32[]{:S(2)}, u32[]{:S(2)}) collective-permute-start(bf16[8,128,256]{2,1,0:T(8,128)(2,1)S(1)} %get-tuple-element.45), channel_id=1, source_target_pairs={{64,0},{72,8},{80,16},{88,24},{96,32},{104,40},{112,48},{120,56},{... | collective-permute-start | bytes 1572872 | tf_op jit(solution)/shard_map/ppermute | solution.py:59
  50.5 2.6 %collective-permute-done.14.below_ref = bf16[8,128,256]{2,1,0:T(8,128)(2,1)S(1)} collective-permute-done((bf16[8,128,256]{2,1,0:T(8,128)(2,1)}, bf16[8,128,256]{2,1,0:T(8,128)(2,1)S(1)}, u32[]{:S(2)}, u32[]{:S(2)}) %collective-permute-start.14) | collective-permute-done | bytes 524320 | tf_op jit(solution)/shard_map/ppermute | solution.py:59
  55.0 9.7 %attend.1 = (bf16[256,1024]{1,0:T(8,128)(2,1)}, f32[512,256]{1,0:T(8,128)S(1)}, bf16[8,128,256]{2,1,0:T(8,128)(2,1)S(1)}) custom-call(s32[1]{0:T(128)} %bitcast.at_ref, s32[2,4]{1,0:T(2,128)S(1)} %copy-done.1, s32[2]{0:T(128)S(1)} %copy-done.7, bf16[256,1024]{1,0:T(8,128)(2,1)S(1)} %copy-done.3, bf16[256,1024]{1,0:T(8,128)(2,1)S(1)} %copy-done.4, ...), custom_call_target="tpu_custom_call" | custom-call | flops 9600000000 | bytes 6291456 | tf_op jit(solution)/shard_map/attend/pallas_call | solution.py:219
  64.7 2.4 %collective-permute-start.16 = (bf16[8,128,256]{2,1,0:T(8,128)(2,1)S(1)}, bf16[8,128,256]{2,1,0:T(8,128)(2,1)S(1)}, u32[]{:S(2)}, u32[]{:S(2)}) collective-permute-start(bf16[8,128,256]{2,1,0:T(8,128)(2,1)S(1)} %get-tuple-element.50.refs_4_), channel_id=1, source_target_pairs={{0,64},{8,72},{16,80},{24,88},{32,96},{40,104},{48,112},{56,120},{... | collective-permute-start | bytes 1572872 | tf_op jit(solution)/shard_map/ppermute | solution.py:59
  68.7 5.2 %collective-permute-done.18.back_ref = bf16[256,256]{1,0:T(8,128)(2,1)S(1)} collective-permute-done((bf16[256,256]{1,0:T(8,128)(2,1)S(1)}, bf16[256,256]{1,0:T(8,128)(2,1)S(1)}, u32[]{:S(2)}, u32[]{:S(2)}) %collective-permute-start.18) | collective-permute-done | bytes 131104 | tf_op jit(solution)/shard_map/ppermute | solution.py:54
  78.0 10.1 %all-gather.3.cloned.1.call-done.weights_ref = bf16[512,1024]{1,0:T(8,128)(2,1)} async-done(((bf16[64,1024]{1,0:T(8,128)(2,1)}), bf16[512,1024]{1,0:T(8,128)(2,1)}) %all-gather.3.cloned.1.call-update) | async-done | bytes 1048592 | tf_op jit(solution)/shard_map/all_gather | solution.py:439
  89.6 22.6 %all_to_all.10.terms_ref = bf16[8,256,256]{2,1,0:T(8,128)(2,1)S(1)} all-to-all(bf16[8,256,256]{2,1,0:T(8,128)(2,1)S(1)} %bitcast.8), channel_id=1, replica_groups={{0,8,16,24,32,40,48,56},{64,72,80,88,96,104,112,120},{128,136,144,152,1..., dimensions={0} | all-to-all | bytes 2097152 | tf_op jit(solution)/shard_map/all_to_all | solution.py:460
  113.1 10.3 %collective-permute-start.22 = (bf16[256,256]{1,0:T(8,128)(2,1)S(1)}, bf16[256,256]{1,0:T(8,128)(2,1)S(1)}, u32[]{:S(2)}, u32[]{:S(2)}) collective-permute-start(bf16[256,256]{1,0:T(8,128)(2,1)S(1)} %collective-permute-done.21.own_ref), channel_id=1, source_target_pairs={{0,2},{1,3},{2,4},{3,5},{4,6},{5,7},{6,0},{7,1},{8,10},{9,11},{10,... | collective-permute-start | bytes 393224 | tf_op jit(solution)/shard_map/ppermute | solution.py:59
  123.4 4.2 %collective-permute-start.23 = (bf16[256,256]{1,0:T(8,128)(2,1)S(1)}, bf16[256,256]{1,0:T(8,128)(2,1)S(1)}, u32[]{:S(2)}, u32[]{:S(2)}) collective-permute-start(bf16[256,256]{1,0:T(8,128)(2,1)S(1)} %collective-permute-done.21.own_ref), channel_id=1, source_target_pairs={{2,0},{3,1},{4,2},{5,3},{6,4},{7,5},{0,6},{1,7},{10,8},{11,9},{12,... | collective-permute-start | bytes 393224 | tf_op jit(solution)/shard_map/ppermute | solution.py:59
  130.0 2.7 %collective-permute-start.25 = (bf16[128,256]{1,0:T(8,128)(2,1)S(1)}, bf16[128,256]{1,0:T(8,128)(2,1)S(1)}, u32[]{:S(2)}, u32[]{:S(2)}) collective-permute-start(bf16[128,256]{1,0:T(8,128)(2,1)S(1)} %slice.49), channel_id=1, source_target_pairs={{2,0},{3,1},{4,2},{5,3},{6,4},{7,5},{0,6},{1,7},{10,8},{11,9},{12,... | collective-permute-start | bytes 196616 | tf_op jit(solution)/shard_map/ppermute | solution.py:59
  134.4 12.0 %collective-permute-start.26 = (bf16[1024,256]{1,0:T(8,128)(2,1)S(1)}, bf16[1024,256]{1,0:T(8,128)(2,1)S(1)}, u32[]{:S(2)}, u32[]{:S(2)}) collective-permute-start(bf16[1024,256]{1,0:T(8,128)(2,1)S(1)} %constant_dynamic-update-slice_fusion), channel_id=1, source_target_pairs={{0,1},{1,0},{2,3},{3,2},{4,5},{5,4},{6,7},{7,6},{8,9},{9,8},{10,11... | collective-permute-start | bytes 1572872 | tf_op jit(solution)/shard_map/ppermute | solution.py:465
  151.9 3.7 %all-to-all-start.1 = ((bf16[8,256,256]{2,1,0:T(8,128)(2,1)}), bf16[8,256,256]{2,1,0:T(8,128)(2,1)S(1)}, u32[]{:S(2)}, u32[]{:S(2)}) async-start(bf16[8,256,256]{2,1,0:T(8,128)(2,1)} %weight_terms.1), calls=%async_computation.1 | async-start | bytes 2097152 | tf_op jit(solution)/shard_map/all_to_all | solution.py:471
  156.9 3.4 %collective-permute-start.29 = (bf16[128,1024]{1,0:T(8,128)(2,1)S(1)}, bf16[128,1024]{1,0:T(8,128)(2,1)S(1)}, u32[]{:S(2)}, u32[]{:S(2)}) collective-permute-start(bf16[128,1024]{1,0:T(8,128)(2,1)S(1)} %get-tuple-element.60), channel_id=1, source_target_pairs={{64,0},{72,8},{80,16},{88,24},{96,32},{104,40},{112,48},{120,56},{... | collective-permute-start | bytes 786440 | tf_op jit(solution)/shard_map/ppermute | solution.py:59
  160.4 4.8 %collective-permute-done.29 = bf16[128,1024]{1,0:T(8,128)(2,1)S(1)} collective-permute-done((bf16[128,1024]{1,0:T(8,128)(2,1)S(1)}, bf16[128,1024]{1,0:T(8,128)(2,1)S(1)}, u32[]{:S(2)}, u32[]{:S(2)}) %collective-permute-start.29) | collective-permute-done | bytes 262176 | tf_op jit(solution)/shard_map/ppermute | solution.py:59
  165.4 3.5 %collective-permute-start.30 = (bf16[256,1024]{1,0:T(8,128)(2,1)S(1)}, bf16[256,1024]{1,0:T(8,128)(2,1)S(1)}, u32[]{:S(2)}, u32[]{:S(2)}) collective-permute-start(bf16[256,1024]{1,0:T(8,128)(2,1)S(1)} %pad_maximum_fusion.1), channel_id=1, source_target_pairs={{64,0},{72,8},{80,16},{88,24},{96,32},{104,40},{112,48},{120,56},{... | collective-permute-start | bytes 1572872 | tf_op jit(solution)/shard_map/ppermute | solution.py:59
  169.1 9.5 %collective-permute-done.30 = bf16[256,1024]{1,0:T(8,128)(2,1)S(1)} collective-permute-done((bf16[256,1024]{1,0:T(8,128)(2,1)S(1)}, bf16[256,1024]{1,0:T(8,128)(2,1)S(1)}, u32[]{:S(2)}, u32[]{:S(2)}) %collective-permute-start.30) | collective-permute-done | bytes 524320 | tf_op jit(solution)/shard_map/ppermute | solution.py:59
  178.6 3.3 %collective-permute-done.28 = bf16[256,1024]{1,0:T(8,128)(2,1)S(1)} collective-permute-done((bf16[256,1024]{1,0:T(8,128)(2,1)S(1)}, bf16[256,1024]{1,0:T(8,128)(2,1)S(1)}, u32[]{:S(2)}, u32[]{:S(2)}) %collective-permute-start.28) | collective-permute-done | bytes 524320 | tf_op jit(solution)/shard_map/ppermute | solution.py:59
  (97 shorter events, 45.8 us)
Async XLA Ops:
  7.2 80.9 %all-gather.3.cloned.1.call-start = ((), (), s32[]{:S(2)}) async-start(), calls=%async_computation.2 | async-start | bytes 1179648 | tf_op jit(solution)/shard_map/all_gather | solution.py:439
  8.4 10.7 %collective-permute-start.1 = (bf16[2,128,256]{2,1,0:T(8,128)(2,1)S(1)}, bf16[2,128,256]{2,1,0:T(8,128)(2,1)S(1)}, u32[]{:S(2)}, u32[]{:S(2)}) collective-permute-start(bf16[2,128,256]{2,1,0:T(8,128)(2,1)S(1)} %bitcast.9), channel_id=1, source_target_pairs={{0,8},{8,16},{16,24},{24,32},{32,40},{40,48},{48,56},{56,0},{64,72... | collective-permute-start | bytes 393224 | tf_op jit(solution)/shard_map/ppermute | solution.py:59
  10.9 8.2 %collective-permute-start.2 = (bf16[2,128,256]{2,1,0:T(8,128)(2,1)S(1)}, bf16[2,128,256]{2,1,0:T(8,128)(2,1)S(1)}, u32[]{:S(2)}, u32[]{:S(2)}) collective-permute-start(bf16[2,128,256]{2,1,0:T(8,128)(2,1)S(1)} %bitcast.10), channel_id=1, source_target_pairs={{8,0},{16,8},{24,16},{32,24},{40,32},{48,40},{56,48},{0,56},{72,64... | collective-permute-start | bytes 393224 | tf_op jit(solution)/shard_map/ppermute | solution.py:59
  19.1 5.0 %collective-permute-start.4 = (bf16[2,128,256]{2,1,0:T(8,128)(2,1)S(1)}, bf16[2,128,256]{2,1,0:T(8,128)(2,1)S(1)}, u32[]{:S(2)}, u32[]{:S(2)}) collective-permute-start(bf16[2,128,256]{2,1,0:T(8,128)(2,1)S(1)} %collective-permute-done.1.refs_0_), channel_id=1, source_target_pairs={{0,8},{8,16},{16,24},{24,32},{32,40},{40,48},{48,56},{56,0},{64,72... | collective-permute-start | bytes 393224 | tf_op jit(solution)/shard_map/ppermute | solution.py:59
  24.1 5.0 %collective-permute-start.6 = (bf16[2,128,256]{2,1,0:T(8,128)(2,1)S(1)}, bf16[2,128,256]{2,1,0:T(8,128)(2,1)S(1)}, u32[]{:S(2)}, u32[]{:S(2)}) collective-permute-start(bf16[2,128,256]{2,1,0:T(8,128)(2,1)S(1)} %collective-permute-done.4.refs_2_), channel_id=1, source_target_pairs={{0,8},{8,16},{16,24},{24,32},{32,40},{40,48},{48,56},{56,0},{64,72... | collective-permute-start | bytes 393224 | tf_op jit(solution)/shard_map/ppermute | solution.py:59
  24.1 5.0 %collective-permute-start.7 = (bf16[2,128,256]{2,1,0:T(8,128)(2,1)S(1)}, bf16[2,128,256]{2,1,0:T(8,128)(2,1)S(1)}, u32[]{:S(2)}, u32[]{:S(2)}) collective-permute-start(bf16[2,128,256]{2,1,0:T(8,128)(2,1)S(1)} %collective-permute-done.5.refs_3_), channel_id=1, source_target_pairs={{8,0},{16,8},{24,16},{32,24},{40,32},{48,40},{56,48},{0,56},{72,64... | collective-permute-start | bytes 393224 | tf_op jit(solution)/shard_map/ppermute | solution.py:59
  34.2 7.9 %collective-permute-start.12 = (bf16[4,128,256]{2,1,0:T(8,128)(2,1)S(1)}, bf16[4,128,256]{2,1,0:T(8,128)(2,1)S(1)}, u32[]{:S(2)}, u32[]{:S(2)}) collective-permute-start(bf16[4,128,256]{2,1,0:T(8,128)(2,1)S(1)} %get-tuple-element.42), channel_id=1, source_target_pairs={{0,64},{8,72},{16,80},{24,88},{32,96},{40,104},{48,112},{56,120},{... | collective-permute-start | bytes 786440 | tf_op jit(solution)/shard_map/ppermute | solution.py:59
  35.5 6.6 %collective-permute-start.13 = (bf16[4,128,256]{2,1,0:T(8,128)(2,1)S(1)}, bf16[4,128,256]{2,1,0:T(8,128)(2,1)S(1)}, u32[]{:S(2)}, u32[]{:S(2)}) collective-permute-start(bf16[4,128,256]{2,1,0:T(8,128)(2,1)S(1)} %get-tuple-element.43), channel_id=1, source_target_pairs={{64,0},{72,8},{80,16},{88,24},{96,32},{104,40},{112,48},{120,56},{... | collective-permute-start | bytes 786440 | tf_op jit(solution)/shard_map/ppermute | solution.py:59
  43.6 9.5 %collective-permute-start.14 = (bf16[8,128,256]{2,1,0:T(8,128)(2,1)}, bf16[8,128,256]{2,1,0:T(8,128)(2,1)S(1)}, u32[]{:S(2)}, u32[]{:S(2)}) collective-permute-start(bf16[8,128,256]{2,1,0:T(8,128)(2,1)} %get-tuple-element.44), channel_id=1, source_target_pairs={{0,64},{8,72},{16,80},{24,88},{32,96},{40,104},{48,112},{56,120},{... | collective-permute-start | bytes 1572872 | tf_op jit(solution)/shard_map/ppermute | solution.py:59
  43.6 10.3 %collective-permute-start.15 = (bf16[8,128,256]{2,1,0:T(8,128)(2,1)S(1)}, bf16[8,128,256]{2,1,0:T(8,128)(2,1)}, u32[]{:S(2)}, u32[]{:S(2)}) collective-permute-start(bf16[8,128,256]{2,1,0:T(8,128)(2,1)S(1)} %get-tuple-element.45), channel_id=1, source_target_pairs={{64,0},{72,8},{80,16},{88,24},{96,32},{104,40},{112,48},{120,56},{... | collective-permute-start | bytes 1572872 | tf_op jit(solution)/shard_map/ppermute | solution.py:59
  47.0 101.0 %all-gather.5.cloned.1.call-start = ((), (), s32[]{:S(2)}) async-start(), calls=%async_computation.3 | async-start | bytes 2621440 | tf_op jit(solution)/shard_map/all_gather | solution.py:455
  64.7 9.2 %collective-permute-start.16 = (bf16[8,128,256]{2,1,0:T(8,128)(2,1)S(1)}, bf16[8,128,256]{2,1,0:T(8,128)(2,1)S(1)}, u32[]{:S(2)}, u32[]{:S(2)}) collective-permute-start(bf16[8,128,256]{2,1,0:T(8,128)(2,1)S(1)} %get-tuple-element.50.refs_4_), channel_id=1, source_target_pairs={{0,64},{8,72},{16,80},{24,88},{32,96},{40,104},{48,112},{56,120},{... | collective-permute-start | bytes 1572872 | tf_op jit(solution)/shard_map/ppermute | solution.py:59
  67.1 8.0 %collective-permute-start.17 = (bf16[8,128,256]{2,1,0:T(8,128)(2,1)S(1)}, bf16[8,128,256]{2,1,0:T(8,128)(2,1)S(1)}, u32[]{:S(2)}, u32[]{:S(2)}) collective-permute-start(bf16[8,128,256]{2,1,0:T(8,128)(2,1)S(1)} %get-tuple-element.50.refs_4_), channel_id=1, source_target_pairs={{64,0},{72,8},{80,16},{88,24},{96,32},{104,40},{112,48},{120,56},{... | collective-permute-start | bytes 1572872 | tf_op jit(solution)/shard_map/ppermute | solution.py:59
  67.4 6.5 %collective-permute-start.18 = (bf16[256,256]{1,0:T(8,128)(2,1)S(1)}, bf16[256,256]{1,0:T(8,128)(2,1)S(1)}, u32[]{:S(2)}, u32[]{:S(2)}) collective-permute-start(bf16[256,256]{1,0:T(8,128)(2,1)S(1)} %slice.53), channel_id=1, source_target_pairs={{8,0},{16,8},{24,16},{32,24},{40,32},{48,40},{56,48},{64,56},{72,6... | collective-permute-start | bytes 393224 | tf_op jit(solution)/shard_map/ppermute | solution.py:54
  75.1 13.0 %collective-permute-start.19 = (bf16[4,128,256]{2,1,0:T(8,128)(2,1)S(1)}, bf16[4,128,256]{2,1,0:T(8,128)(2,1)S(1)}, u32[]{:S(2)}, u32[]{:S(2)}) collective-permute-start(bf16[4,128,256]{2,1,0:T(8,128)(2,1)S(1)} %slice.37), channel_id=1, source_target_pairs={{0,64},{8,72},{16,80},{24,88},{32,96},{40,104},{48,112},{56,120},{... | collective-permute-start | bytes 786440 | tf_op jit(solution)/shard_map/ppermute | solution.py:59
  75.8 12.3 %collective-permute-start.20 = (bf16[4,128,256]{2,1,0:T(8,128)(2,1)S(1)}, bf16[4,128,256]{2,1,0:T(8,128)(2,1)S(1)}, u32[]{:S(2)}, u32[]{:S(2)}) collective-permute-start(bf16[4,128,256]{2,1,0:T(8,128)(2,1)S(1)} %slice.38), channel_id=1, source_target_pairs={{64,0},{72,8},{80,16},{88,24},{96,32},{104,40},{112,48},{120,56},{... | collective-permute-start | bytes 786440 | tf_op jit(solution)/shard_map/ppermute | solution.py:59
  113.1 16.8 %collective-permute-start.22 = (bf16[256,256]{1,0:T(8,128)(2,1)S(1)}, bf16[256,256]{1,0:T(8,128)(2,1)S(1)}, u32[]{:S(2)}, u32[]{:S(2)}) collective-permute-start(bf16[256,256]{1,0:T(8,128)(2,1)S(1)} %collective-permute-done.21.own_ref), channel_id=1, source_target_pairs={{0,2},{1,3},{2,4},{3,5},{4,6},{5,7},{6,0},{7,1},{8,10},{9,11},{10,... | collective-permute-start | bytes 393224 | tf_op jit(solution)/shard_map/ppermute | solution.py:59
  123.4 6.6 %collective-permute-start.23 = (bf16[256,256]{1,0:T(8,128)(2,1)S(1)}, bf16[256,256]{1,0:T(8,128)(2,1)S(1)}, u32[]{:S(2)}, u32[]{:S(2)}) collective-permute-start(bf16[256,256]{1,0:T(8,128)(2,1)S(1)} %collective-permute-done.21.own_ref), channel_id=1, source_target_pairs={{2,0},{3,1},{4,2},{5,3},{6,4},{7,5},{0,6},{1,7},{10,8},{11,9},{12,... | collective-permute-start | bytes 393224 | tf_op jit(solution)/shard_map/ppermute | solution.py:59
  134.4 13.5 %collective-permute-start.26 = (bf16[1024,256]{1,0:T(8,128)(2,1)S(1)}, bf16[1024,256]{1,0:T(8,128)(2,1)S(1)}, u32[]{:S(2)}, u32[]{:S(2)}) collective-permute-start(bf16[1024,256]{1,0:T(8,128)(2,1)S(1)} %constant_dynamic-update-slice_fusion), channel_id=1, source_target_pairs={{0,1},{1,0},{2,3},{3,2},{4,5},{5,4},{6,7},{7,6},{8,9},{9,8},{10,11... | collective-permute-start | bytes 1572872 | tf_op jit(solution)/shard_map/ppermute | solution.py:465
  151.9 33.0 %all-to-all-start.1 = ((bf16[8,256,256]{2,1,0:T(8,128)(2,1)}), bf16[8,256,256]{2,1,0:T(8,128)(2,1)S(1)}, u32[]{:S(2)}, u32[]{:S(2)}) async-start(bf16[8,256,256]{2,1,0:T(8,128)(2,1)} %weight_terms.1), calls=%async_computation.1 | async-start | bytes 2097152 | tf_op jit(solution)/shard_map/all_to_all | solution.py:471
  156.9 8.3 %collective-permute-start.29 = (bf16[128,1024]{1,0:T(8,128)(2,1)S(1)}, bf16[128,1024]{1,0:T(8,128)(2,1)S(1)}, u32[]{:S(2)}, u32[]{:S(2)}) collective-permute-start(bf16[128,1024]{1,0:T(8,128)(2,1)S(1)} %get-tuple-element.60), channel_id=1, source_target_pairs={{64,0},{72,8},{80,16},{88,24},{96,32},{104,40},{112,48},{120,56},{... | collective-permute-start | bytes 786440 | tf_op jit(solution)/shard_map/ppermute | solution.py:59
  160.3 8.5 %collective-permute-start.27 = (bf16[128,1024]{1,0:T(8,128)(2,1)S(1)}, bf16[128,1024]{1,0:T(8,128)(2,1)S(1)}, u32[]{:S(2)}, u32[]{:S(2)}) collective-permute-start(bf16[128,1024]{1,0:T(8,128)(2,1)S(1)} %get-tuple-element.58), channel_id=1, source_target_pairs={{0,64},{8,72},{16,80},{24,88},{32,96},{40,104},{48,112},{56,120},{... | collective-permute-start | bytes 786440 | tf_op jit(solution)/shard_map/ppermute | solution.py:59
  165.4 13.2 %collective-permute-start.30 = (bf16[256,1024]{1,0:T(8,128)(2,1)S(1)}, bf16[256,1024]{1,0:T(8,128)(2,1)S(1)}, u32[]{:S(2)}, u32[]{:S(2)}) collective-permute-start(bf16[256,1024]{1,0:T(8,128)(2,1)S(1)} %pad_maximum_fusion.1), channel_id=1, source_target_pairs={{64,0},{72,8},{80,16},{88,24},{96,32},{104,40},{112,48},{120,56},{... | collective-permute-start | bytes 1572872 | tf_op jit(solution)/shard_map/ppermute | solution.py:59
  169.0 12.9 %collective-permute-start.28 = (bf16[256,1024]{1,0:T(8,128)(2,1)S(1)}, bf16[256,1024]{1,0:T(8,128)(2,1)S(1)}, u32[]{:S(2)}, u32[]{:S(2)}) collective-permute-start(bf16[256,1024]{1,0:T(8,128)(2,1)S(1)} %pad_maximum_fusion), channel_id=1, source_target_pairs={{0,64},{8,72},{16,80},{24,88},{32,96},{40,104},{48,112},{56,120},{... | collective-permute-start | bytes 1572872 | tf_op jit(solution)/shard_map/ppermute | solution.py:59
  (20 other events, 310.8 us)
Sparse Core Ops, SparseCore 0:
  47.1 40.9 all-gather.2
  89.9 39.0 all-gather.4

commit v11 on v10

--- a/solution.py
+++ b/solution.py
@@ -461,6 +461,7 @@
     kv_grad = finish(terms, back, window)
 
     moved = lax.ppermute(kv_grad, ("seq", "own"), SWAP_XY)
+    moved, inputs_x = lax.optimization_barrier((moved, inputs_x))
     same_core = ring_gather(moved, "own", Y_UP, NY)
     other_core = lax.ppermute(jnp.concatenate([moved, *same_core]), "own", CORES)
     heads = place_heads(own_index, moved, same_core, other_core)

time: 193 us -> 192 us (level)
  waiting for transfers between devices: 57.5 us -> 74.6 us
  starting transfers between devices: 73.5 us -> 57.1 us
    all_gather x1, waiting for transfers between devices: 0.02 us -> 15.9 us  [local(): lax.all_gather(inputs, 'seq', axis=0, axis_index_groups=X_GROUPS, tiled=T...]
    ppermute x13, waiting for transfers between devices: 18 us -> 4.26 us  [both_ways(): lax.ppermute(downward, axis, back)]
    ppermute x13, waiting for transfers between devices: 17.5 us -> 29.4 us  [both_ways(): lax.ppermute(upward, axis, pairs)]
    ppermute x13, starting transfers between devices: 17.5 us -> 7.26 us  [both_ways(): lax.ppermute(upward, axis, pairs)]
    ppermute x1, starting transfers between devices: 12 us -> 7.8 us  [local(): lax.ppermute(jnp.concatenate([moved, *same_core]), 'own', CORES)]
    all_to_all x1, waiting for transfers between devices: 1.97 us -> 5.13 us  [local(): lax.all_to_all(pieces, 'seq', 0, 0, axis_index_groups=Z_GROUPS, tiled=True)]
    ppermute x13, starting transfers between devices: 33.8 us -> 31.2 us  [both_ways(): lax.ppermute(downward, axis, back)]
  transfers between devices with their start and end apart: 34 -> 34, of which waited for: 20 -> 21; matrix products, arithmetic and copies ran while one was open for 1% -> 1% of each run, Pallas kernels for 7% -> 7%
where the time goes in v11:
time: 192 us
  waiting for transfers between devices  74.6 us (39%)
  starting transfers between devices  57.1 us (30%)
  blocking collectives  22.5 us (12%)
  Pallas kernels  18.1 us (9%)
  between operations  14.4 us (8%)
  other arithmetic  2.88 us (2%)
  local copies, waits for them, and re-layouts  2.01 us (1%)
    ppermute x13, starting transfers between devices, both_ways(): lax.ppermute(downward, axis, back)  31.2 us
    ppermute x13, waiting for transfers between devices, both_ways(): lax.ppermute(upward, axis, pairs)  29.4 us
    all_to_all x1, blocking collectives, local(): lax.all_to_all(dense, 'seq', 0, 0, axis_index_groups=Z_GROUPS, tiled=True)  22.5 us
    all_gather x1, waiting for transfers between devices, local(): lax.all_gather(inputs, 'seq', axis=0, axis_index_groups=X_GROUPS, tiled=T...  15.9 us
    all_gather x1, waiting for transfers between devices, local(): lax.all_gather(weights, 'seq', axis=0, axis_index_groups=Z_GROUPS, tiled=...  10.1 us
    pallas_call x1, Pallas kernels, attend(): pl.pallas_call(attend_kernel, out_shape=(jax.ShapeDtypeStruct((NB * BLK,...  9.68 us
    ppermute x1, starting transfers between devices, local(): lax.ppermute(jnp.concatenate([moved, *same_core]), 'own', CORES)  7.8 us
    ppermute x13, starting transfers between devices, both_ways(): lax.ppermute(upward, axis, pairs)  7.26 us
  transfers between devices with their start and end apart: 34, of which 21 were waited for; matrix products, arithmetic and copies ran while one was open for 1% of the time, Pallas kernels for 7%

profile of v11, /device:TPU:1, one launch (start us, length us, event | category | flops | bytes accessed | tf_op | source)
XLA Modules:
  0.0 191.6 jit_solution(17998693443120909029)
XLA Ops:
  8.2 2.5 %collective-permute-start.1 = (bf16[2,128,256]{2,1,0:T(8,128)(2,1)S(1)}, bf16[2,128,256]{2,1,0:T(8,128)(2,1)S(1)}, u32[]{:S(2)}, u32[]{:S(2)}) collective-permute-start(bf16[2,128,256]{2,1,0:T(8,128)(2,1)S(1)} %bitcast.9), channel_id=1, source_target_pairs={{0,8},{8,16},{16,24},{24,32},{32,40},{40,48},{48,56},{56,0},{64,72... | collective-permute-start | bytes 393224 | tf_op jit(solution)/shard_map/ppermute | solution.py:59
  10.8 4.0 %collective-permute-start.2 = (bf16[2,128,256]{2,1,0:T(8,128)(2,1)S(1)}, bf16[2,128,256]{2,1,0:T(8,128)(2,1)S(1)}, u32[]{:S(2)}, u32[]{:S(2)}) collective-permute-start(bf16[2,128,256]{2,1,0:T(8,128)(2,1)S(1)} %bitcast.10), channel_id=1, source_target_pairs={{8,0},{16,8},{24,16},{32,24},{40,32},{48,40},{56,48},{0,56},{72,64... | collective-permute-start | bytes 393224 | tf_op jit(solution)/shard_map/ppermute | solution.py:59
  14.8 2.7 %collective-permute-start.3 = (s32[2,4]{1,0:T(2,128)}, s32[2,4]{1,0:T(2,128)S(1)}, u32[]{:S(2)}, u32[]{:S(2)}) collective-permute-start(s32[2,4]{1,0:T(2,128)} %refs_0_.1), channel_id=1, source_target_pairs={{0,128},{8,136},{16,144},{24,152},{32,160},{40,168},{48,176},{56,1... | collective-permute-start | bytes 104 | tf_op jit(solution)/shard_map/ppermute | solution.py:423
  19.0 2.7 %collective-permute-start.5 = (bf16[2,128,256]{2,1,0:T(8,128)(2,1)S(1)}, bf16[2,128,256]{2,1,0:T(8,128)(2,1)S(1)}, u32[]{:S(2)}, u32[]{:S(2)}) collective-permute-start(bf16[2,128,256]{2,1,0:T(8,128)(2,1)S(1)} %collective-permute-done.2.refs_1_), channel_id=1, source_target_pairs={{8,0},{16,8},{24,16},{32,24},{40,32},{48,40},{56,48},{0,56},{72,64... | collective-permute-start | bytes 393224 | tf_op jit(solution)/shard_map/ppermute | solution.py:59
  21.6 2.4 %collective-permute-done.4.refs_2_ = bf16[2,128,256]{2,1,0:T(8,128)(2,1)S(1)} collective-permute-done((bf16[2,128,256]{2,1,0:T(8,128)(2,1)S(1)}, bf16[2,128,256]{2,1,0:T(8,128)(2,1)S(1)}, u32[]{:S(2)}, u32[]{:S(2)}) %collective-permute-start.4) | collective-permute-done | bytes 131104 | tf_op jit(solution)/shard_map/ppermute | solution.py:59
  24.0 2.7 %collective-permute-start.7 = (bf16[2,128,256]{2,1,0:T(8,128)(2,1)S(1)}, bf16[2,128,256]{2,1,0:T(8,128)(2,1)S(1)}, u32[]{:S(2)}, u32[]{:S(2)}) collective-permute-start(bf16[2,128,256]{2,1,0:T(8,128)(2,1)S(1)} %collective-permute-done.5.refs_3_), channel_id=1, source_target_pairs={{8,0},{16,8},{24,16},{32,24},{40,32},{48,40},{56,48},{0,56},{72,64... | collective-permute-start | bytes 393224 | tf_op jit(solution)/shard_map/ppermute | solution.py:59
  29.1 2.7 %collective-permute-start.9 = (bf16[1,128,256]{2,1,0:T(8,128)(2,1)S(1)}, bf16[1,128,256]{2,1,0:T(8,128)(2,1)S(1)}, u32[]{:S(2)}, u32[]{:S(2)}) collective-permute-start(bf16[1,128,256]{2,1,0:T(8,128)(2,1)S(1)} %slice.46), channel_id=1, source_target_pairs={{8,0},{16,8},{24,16},{32,24},{40,32},{48,40},{56,48},{0,56},{72,64... | collective-permute-start | bytes 196616 | tf_op jit(solution)/shard_map/ppermute | solution.py:59
  43.5 2.7 %collective-permute-start.15 = (bf16[8,128,256]{2,1,0:T(8,128)(2,1)S(1)}, bf16[8,128,256]{2,1,0:T(8,128)(2,1)}, u32[]{:S(2)}, u32[]{:S(2)}) collective-permute-start(bf16[8,128,256]{2,1,0:T(8,128)(2,1)S(1)} %get-tuple-element.47), channel_id=1, source_target_pairs={{64,0},{72,8},{80,16},{88,24},{96,32},{104,40},{112,48},{120,56},{... | collective-permute-start | bytes 1572872 | tf_op jit(solution)/shard_map/ppermute | solution.py:59
  50.4 2.6 %collective-permute-done.14.below_ref = bf16[8,128,256]{2,1,0:T(8,128)(2,1)S(1)} collective-permute-done((bf16[8,128,256]{2,1,0:T(8,128)(2,1)}, bf16[8,128,256]{2,1,0:T(8,128)(2,1)S(1)}, u32[]{:S(2)}, u32[]{:S(2)}) %collective-permute-start.14) | collective-permute-done | bytes 524320 | tf_op jit(solution)/shard_map/ppermute | solution.py:59
  54.9 9.7 %attend.1 = (bf16[256,1024]{1,0:T(8,128)(2,1)}, f32[512,256]{1,0:T(8,128)S(1)}, bf16[8,128,256]{2,1,0:T(8,128)(2,1)S(1)}) custom-call(s32[1]{0:T(128)} %bitcast.at_ref, s32[2,4]{1,0:T(2,128)S(1)} %copy-done.1, s32[2]{0:T(128)S(1)} %copy-done.7, bf16[256,1024]{1,0:T(8,128)(2,1)S(1)} %copy-done.3, bf16[256,1024]{1,0:T(8,128)(2,1)S(1)} %copy-done.4, ...), custom_call_target="tpu_custom_call" | custom-call | flops 9600000000 | bytes 6291456 | tf_op jit(solution)/shard_map/attend/pallas_call | solution.py:219
  64.5 2.4 %collective-permute-start.16 = (bf16[8,128,256]{2,1,0:T(8,128)(2,1)S(1)}, bf16[8,128,256]{2,1,0:T(8,128)(2,1)S(1)}, u32[]{:S(2)}, u32[]{:S(2)}) collective-permute-start(bf16[8,128,256]{2,1,0:T(8,128)(2,1)S(1)} %get-tuple-element.52.refs_4_), channel_id=1, source_target_pairs={{0,64},{8,72},{16,80},{24,88},{32,96},{40,104},{48,112},{56,120},{... | collective-permute-start | bytes 1572872 | tf_op jit(solution)/shard_map/ppermute | solution.py:59
  68.5 5.2 %collective-permute-done.18.back_ref = bf16[256,256]{1,0:T(8,128)(2,1)S(1)} collective-permute-done((bf16[256,256]{1,0:T(8,128)(2,1)S(1)}, bf16[256,256]{1,0:T(8,128)(2,1)S(1)}, u32[]{:S(2)}, u32[]{:S(2)}) %collective-permute-start.18) | collective-permute-done | bytes 131104 | tf_op jit(solution)/shard_map/ppermute | solution.py:54
  77.9 10.1 %all-gather.3.cloned.1.call-done.weights_ref = bf16[512,1024]{1,0:T(8,128)(2,1)} async-done(((bf16[64,1024]{1,0:T(8,128)(2,1)}), bf16[512,1024]{1,0:T(8,128)(2,1)}) %all-gather.3.cloned.1.call-update) | async-done | bytes 1048592 | tf_op jit(solution)/shard_map/all_gather | solution.py:439
  89.5 22.5 %all_to_all.10.terms_ref = bf16[8,256,256]{2,1,0:T(8,128)(2,1)S(1)} all-to-all(bf16[8,256,256]{2,1,0:T(8,128)(2,1)S(1)} %bitcast.8), channel_id=1, replica_groups={{0,8,16,24,32,40,48,56},{64,72,80,88,96,104,112,120},{128,136,144,152,1..., dimensions={0} | all-to-all | bytes 2097152 | tf_op jit(solution)/shard_map/all_to_all | solution.py:460
  113.0 15.9 %all-gather.5.cloned.1.call-done.inputs_ref = bf16[1024,1024]{1,0:T(8,128)(2,1)} async-done(((bf16[256,1024]{1,0:T(8,128)(2,1)}), bf16[1024,1024]{1,0:T(8,128)(2,1)}) %all-gather.5.cloned.1.call-update) | async-done | bytes 2097168 | tf_op jit(solution)/shard_map/all_gather | solution.py:455
  128.9 2.7 %collective-permute-start.23 = (bf16[256,256]{1,0:T(8,128)(2,1)S(1)}, bf16[256,256]{1,0:T(8,128)(2,1)S(1)}, u32[]{:S(2)}, u32[]{:S(2)}) collective-permute-start(bf16[256,256]{1,0:T(8,128)(2,1)S(1)} %collective-permute-done.21.own_ref), channel_id=1, source_target_pairs={{2,0},{3,1},{4,2},{5,3},{6,4},{7,5},{0,6},{1,7},{10,8},{11,9},{12,... | collective-permute-start | bytes 393224 | tf_op jit(solution)/shard_map/ppermute | solution.py:59
  134.2 3.1 %collective-permute-start.25 = (bf16[128,256]{1,0:T(8,128)(2,1)S(1)}, bf16[128,256]{1,0:T(8,128)(2,1)S(1)}, u32[]{:S(2)}, u32[]{:S(2)}) collective-permute-start(bf16[128,256]{1,0:T(8,128)(2,1)S(1)} %slice.49), channel_id=1, source_target_pairs={{2,0},{3,1},{4,2},{5,3},{6,4},{7,5},{0,6},{1,7},{10,8},{11,9},{12,... | collective-permute-start | bytes 196616 | tf_op jit(solution)/shard_map/ppermute | solution.py:59
  138.6 7.8 %collective-permute-start.26 = (bf16[1024,256]{1,0:T(8,128)(2,1)S(1)}, bf16[1024,256]{1,0:T(8,128)(2,1)S(1)}, u32[]{:S(2)}, u32[]{:S(2)}) collective-permute-start(bf16[1024,256]{1,0:T(8,128)(2,1)S(1)} %constant_dynamic-update-slice_fusion), channel_id=1, source_target_pairs={{0,1},{1,0},{2,3},{3,2},{4,5},{5,4},{6,7},{7,6},{8,9},{9,8},{10,11... | collective-permute-start | bytes 1572872 | tf_op jit(solution)/shard_map/ppermute | solution.py:466
  150.3 4.3 %all-to-all-start.1 = ((bf16[8,256,256]{2,1,0:T(8,128)(2,1)}), bf16[8,256,256]{2,1,0:T(8,128)(2,1)S(1)}, u32[]{:S(2)}, u32[]{:S(2)}) async-start(bf16[8,256,256]{2,1,0:T(8,128)(2,1)} %weight_terms.1), calls=%async_computation.1 | async-start | bytes 2097152 | tf_op jit(solution)/shard_map/all_to_all | solution.py:472
  156.1 2.7 %collective-permute-start.29 = (bf16[128,1024]{1,0:T(8,128)(2,1)S(1)}, bf16[128,1024]{1,0:T(8,128)(2,1)S(1)}, u32[]{:S(2)}, u32[]{:S(2)}) collective-permute-start(bf16[128,1024]{1,0:T(8,128)(2,1)S(1)} %get-tuple-element.64), channel_id=1, source_target_pairs={{64,0},{72,8},{80,16},{88,24},{96,32},{104,40},{112,48},{120,56},{... | collective-permute-start | bytes 786440 | tf_op jit(solution)/shard_map/ppermute | solution.py:59
  158.8 5.6 %collective-permute-done.27 = bf16[128,1024]{1,0:T(8,128)(2,1)S(1)} collective-permute-done((bf16[128,1024]{1,0:T(8,128)(2,1)S(1)}, bf16[128,1024]{1,0:T(8,128)(2,1)S(1)}, u32[]{:S(2)}, u32[]{:S(2)}) %collective-permute-start.27) | collective-permute-done | bytes 262176 | tf_op jit(solution)/shard_map/ppermute | solution.py:59
  164.8 2.7 %collective-permute-start.30 = (bf16[256,1024]{1,0:T(8,128)(2,1)S(1)}, bf16[256,1024]{1,0:T(8,128)(2,1)S(1)}, u32[]{:S(2)}, u32[]{:S(2)}) collective-permute-start(bf16[256,1024]{1,0:T(8,128)(2,1)S(1)} %pad_maximum_fusion.1), channel_id=1, source_target_pairs={{64,0},{72,8},{80,16},{88,24},{96,32},{104,40},{112,48},{120,56},{... | collective-permute-start | bytes 1572872 | tf_op jit(solution)/shard_map/ppermute | solution.py:59
  167.5 10.2 %collective-permute-done.28 = bf16[256,1024]{1,0:T(8,128)(2,1)S(1)} collective-permute-done((bf16[256,1024]{1,0:T(8,128)(2,1)S(1)}, bf16[256,1024]{1,0:T(8,128)(2,1)S(1)}, u32[]{:S(2)}, u32[]{:S(2)}) %collective-permute-start.28) | collective-permute-done | bytes 524320 | tf_op jit(solution)/shard_map/ppermute | solution.py:59
  178.8 5.1 %all-to-all-done.1.terms_ref = bf16[8,256,256]{2,1,0:T(8,128)(2,1)S(1)} async-done(((bf16[8,256,256]{2,1,0:T(8,128)(2,1)}), bf16[8,256,256]{2,1,0:T(8,128)(2,1)S(1)}, u32[]{:S(2)}, u32[]{:S(2)}) %all-to-all-start.1) | async-done | bytes 1048608 | tf_op jit(solution)/shard_map/all_to_all | solution.py:472
  (97 shorter events, 42.1 us)
Async XLA Ops:
  7.2 80.8 %all-gather.3.cloned.1.call-start = ((), (), s32[]{:S(2)}) async-start(), calls=%async_computation.2 | async-start | bytes 1179648 | tf_op jit(solution)/shard_map/all_gather | solution.py:439
  8.2 10.7 %collective-permute-start.1 = (bf16[2,128,256]{2,1,0:T(8,128)(2,1)S(1)}, bf16[2,128,256]{2,1,0:T(8,128)(2,1)S(1)}, u32[]{:S(2)}, u32[]{:S(2)}) collective-permute-start(bf16[2,128,256]{2,1,0:T(8,128)(2,1)S(1)} %bitcast.9), channel_id=1, source_target_pairs={{0,8},{8,16},{16,24},{24,32},{32,40},{40,48},{48,56},{56,0},{64,72... | collective-permute-start | bytes 393224 | tf_op jit(solution)/shard_map/ppermute | solution.py:59
  10.8 8.2 %collective-permute-start.2 = (bf16[2,128,256]{2,1,0:T(8,128)(2,1)S(1)}, bf16[2,128,256]{2,1,0:T(8,128)(2,1)S(1)}, u32[]{:S(2)}, u32[]{:S(2)}) collective-permute-start(bf16[2,128,256]{2,1,0:T(8,128)(2,1)S(1)} %bitcast.10), channel_id=1, source_target_pairs={{8,0},{16,8},{24,16},{32,24},{40,32},{48,40},{56,48},{0,56},{72,64... | collective-permute-start | bytes 393224 | tf_op jit(solution)/shard_map/ppermute | solution.py:59
  19.0 5.0 %collective-permute-start.4 = (bf16[2,128,256]{2,1,0:T(8,128)(2,1)S(1)}, bf16[2,128,256]{2,1,0:T(8,128)(2,1)S(1)}, u32[]{:S(2)}, u32[]{:S(2)}) collective-permute-start(bf16[2,128,256]{2,1,0:T(8,128)(2,1)S(1)} %collective-permute-done.1.refs_0_), channel_id=1, source_target_pairs={{0,8},{8,16},{16,24},{24,32},{32,40},{40,48},{48,56},{56,0},{64,72... | collective-permute-start | bytes 393224 | tf_op jit(solution)/shard_map/ppermute | solution.py:59
  24.0 5.0 %collective-permute-start.6 = (bf16[2,128,256]{2,1,0:T(8,128)(2,1)S(1)}, bf16[2,128,256]{2,1,0:T(8,128)(2,1)S(1)}, u32[]{:S(2)}, u32[]{:S(2)}) collective-permute-start(bf16[2,128,256]{2,1,0:T(8,128)(2,1)S(1)} %collective-permute-done.4.refs_2_), channel_id=1, source_target_pairs={{0,8},{8,16},{16,24},{24,32},{32,40},{40,48},{48,56},{56,0},{64,72... | collective-permute-start | bytes 393224 | tf_op jit(solution)/shard_map/ppermute | solution.py:59
  24.0 5.0 %collective-permute-start.7 = (bf16[2,128,256]{2,1,0:T(8,128)(2,1)S(1)}, bf16[2,128,256]{2,1,0:T(8,128)(2,1)S(1)}, u32[]{:S(2)}, u32[]{:S(2)}) collective-permute-start(bf16[2,128,256]{2,1,0:T(8,128)(2,1)S(1)} %collective-permute-done.5.refs_3_), channel_id=1, source_target_pairs={{8,0},{16,8},{24,16},{32,24},{40,32},{48,40},{56,48},{0,56},{72,64... | collective-permute-start | bytes 393224 | tf_op jit(solution)/shard_map/ppermute | solution.py:59
  34.1 7.9 %collective-permute-start.12 = (bf16[4,128,256]{2,1,0:T(8,128)(2,1)S(1)}, bf16[4,128,256]{2,1,0:T(8,128)(2,1)S(1)}, u32[]{:S(2)}, u32[]{:S(2)}) collective-permute-start(bf16[4,128,256]{2,1,0:T(8,128)(2,1)S(1)} %get-tuple-element.44), channel_id=1, source_target_pairs={{0,64},{8,72},{16,80},{24,88},{32,96},{40,104},{48,112},{56,120},{... | collective-permute-start | bytes 786440 | tf_op jit(solution)/shard_map/ppermute | solution.py:59
  35.4 6.6 %collective-permute-start.13 = (bf16[4,128,256]{2,1,0:T(8,128)(2,1)S(1)}, bf16[4,128,256]{2,1,0:T(8,128)(2,1)S(1)}, u32[]{:S(2)}, u32[]{:S(2)}) collective-permute-start(bf16[4,128,256]{2,1,0:T(8,128)(2,1)S(1)} %get-tuple-element.45), channel_id=1, source_target_pairs={{64,0},{72,8},{80,16},{88,24},{96,32},{104,40},{112,48},{120,56},{... | collective-permute-start | bytes 786440 | tf_op jit(solution)/shard_map/ppermute | solution.py:59
  43.5 9.5 %collective-permute-start.14 = (bf16[8,128,256]{2,1,0:T(8,128)(2,1)}, bf16[8,128,256]{2,1,0:T(8,128)(2,1)S(1)}, u32[]{:S(2)}, u32[]{:S(2)}) collective-permute-start(bf16[8,128,256]{2,1,0:T(8,128)(2,1)} %get-tuple-element.46), channel_id=1, source_target_pairs={{0,64},{8,72},{16,80},{24,88},{32,96},{40,104},{48,112},{56,120},{... | collective-permute-start | bytes 1572872 | tf_op jit(solution)/shard_map/ppermute | solution.py:59
  43.5 10.3 %collective-permute-start.15 = (bf16[8,128,256]{2,1,0:T(8,128)(2,1)S(1)}, bf16[8,128,256]{2,1,0:T(8,128)(2,1)}, u32[]{:S(2)}, u32[]{:S(2)}) collective-permute-start(bf16[8,128,256]{2,1,0:T(8,128)(2,1)S(1)} %get-tuple-element.47), channel_id=1, source_target_pairs={{64,0},{72,8},{80,16},{88,24},{96,32},{104,40},{112,48},{120,56},{... | collective-permute-start | bytes 1572872 | tf_op jit(solution)/shard_map/ppermute | solution.py:59
  46.9 82.0 %all-gather.5.cloned.1.call-start = ((), (), s32[]{:S(2)}) async-start(), calls=%async_computation.3 | async-start | bytes 2621440 | tf_op jit(solution)/shard_map/all_gather | solution.py:455
  64.5 9.2 %collective-permute-start.16 = (bf16[8,128,256]{2,1,0:T(8,128)(2,1)S(1)}, bf16[8,128,256]{2,1,0:T(8,128)(2,1)S(1)}, u32[]{:S(2)}, u32[]{:S(2)}) collective-permute-start(bf16[8,128,256]{2,1,0:T(8,128)(2,1)S(1)} %get-tuple-element.52.refs_4_), channel_id=1, source_target_pairs={{0,64},{8,72},{16,80},{24,88},{32,96},{40,104},{48,112},{56,120},{... | collective-permute-start | bytes 1572872 | tf_op jit(solution)/shard_map/ppermute | solution.py:59
  67.0 8.0 %collective-permute-start.17 = (bf16[8,128,256]{2,1,0:T(8,128)(2,1)S(1)}, bf16[8,128,256]{2,1,0:T(8,128)(2,1)S(1)}, u32[]{:S(2)}, u32[]{:S(2)}) collective-permute-start(bf16[8,128,256]{2,1,0:T(8,128)(2,1)S(1)} %get-tuple-element.52.refs_4_), channel_id=1, source_target_pairs={{64,0},{72,8},{80,16},{88,24},{96,32},{104,40},{112,48},{120,56},{... | collective-permute-start | bytes 1572872 | tf_op jit(solution)/shard_map/ppermute | solution.py:59
  67.2 6.5 %collective-permute-start.18 = (bf16[256,256]{1,0:T(8,128)(2,1)S(1)}, bf16[256,256]{1,0:T(8,128)(2,1)S(1)}, u32[]{:S(2)}, u32[]{:S(2)}) collective-permute-start(bf16[256,256]{1,0:T(8,128)(2,1)S(1)} %slice.53), channel_id=1, source_target_pairs={{8,0},{16,8},{24,16},{32,24},{40,32},{48,40},{56,48},{64,56},{72,6... | collective-permute-start | bytes 393224 | tf_op jit(solution)/shard_map/ppermute | solution.py:54
  75.1 12.9 %collective-permute-start.19 = (bf16[4,128,256]{2,1,0:T(8,128)(2,1)S(1)}, bf16[4,128,256]{2,1,0:T(8,128)(2,1)S(1)}, u32[]{:S(2)}, u32[]{:S(2)}) collective-permute-start(bf16[4,128,256]{2,1,0:T(8,128)(2,1)S(1)} %slice.37), channel_id=1, source_target_pairs={{0,64},{8,72},{16,80},{24,88},{32,96},{40,104},{48,112},{56,120},{... | collective-permute-start | bytes 786440 | tf_op jit(solution)/shard_map/ppermute | solution.py:59
  75.7 12.3 %collective-permute-start.20 = (bf16[4,128,256]{2,1,0:T(8,128)(2,1)S(1)}, bf16[4,128,256]{2,1,0:T(8,128)(2,1)S(1)}, u32[]{:S(2)}, u32[]{:S(2)}) collective-permute-start(bf16[4,128,256]{2,1,0:T(8,128)(2,1)S(1)} %slice.38), channel_id=1, source_target_pairs={{64,0},{72,8},{80,16},{88,24},{96,32},{104,40},{112,48},{120,56},{... | collective-permute-start | bytes 786440 | tf_op jit(solution)/shard_map/ppermute | solution.py:59
  128.9 5.0 %collective-permute-start.22 = (bf16[256,256]{1,0:T(8,128)(2,1)S(1)}, bf16[256,256]{1,0:T(8,128)(2,1)S(1)}, u32[]{:S(2)}, u32[]{:S(2)}) collective-permute-start(bf16[256,256]{1,0:T(8,128)(2,1)S(1)} %collective-permute-done.21.own_ref), channel_id=1, source_target_pairs={{0,2},{1,3},{2,4},{3,5},{4,6},{5,7},{6,0},{7,1},{8,10},{9,11},{10,... | collective-permute-start | bytes 393224 | tf_op jit(solution)/shard_map/ppermute | solution.py:59
  128.9 5.3 %collective-permute-start.23 = (bf16[256,256]{1,0:T(8,128)(2,1)S(1)}, bf16[256,256]{1,0:T(8,128)(2,1)S(1)}, u32[]{:S(2)}, u32[]{:S(2)}) collective-permute-start(bf16[256,256]{1,0:T(8,128)(2,1)S(1)} %collective-permute-done.21.own_ref), channel_id=1, source_target_pairs={{2,0},{3,1},{4,2},{5,3},{6,4},{7,5},{0,6},{1,7},{10,8},{11,9},{12,... | collective-permute-start | bytes 393224 | tf_op jit(solution)/shard_map/ppermute | solution.py:59
  138.6 9.3 %collective-permute-start.26 = (bf16[1024,256]{1,0:T(8,128)(2,1)S(1)}, bf16[1024,256]{1,0:T(8,128)(2,1)S(1)}, u32[]{:S(2)}, u32[]{:S(2)}) collective-permute-start(bf16[1024,256]{1,0:T(8,128)(2,1)S(1)} %constant_dynamic-update-slice_fusion), channel_id=1, source_target_pairs={{0,1},{1,0},{2,3},{3,2},{4,5},{5,4},{6,7},{7,6},{8,9},{9,8},{10,11... | collective-permute-start | bytes 1572872 | tf_op jit(solution)/shard_map/ppermute | solution.py:466
  150.3 33.6 %all-to-all-start.1 = ((bf16[8,256,256]{2,1,0:T(8,128)(2,1)}), bf16[8,256,256]{2,1,0:T(8,128)(2,1)S(1)}, u32[]{:S(2)}, u32[]{:S(2)}) async-start(bf16[8,256,256]{2,1,0:T(8,128)(2,1)} %weight_terms.1), calls=%async_computation.1 | async-start | bytes 2097152 | tf_op jit(solution)/shard_map/all_to_all | solution.py:472
  155.9 8.5 %collective-permute-start.27 = (bf16[128,1024]{1,0:T(8,128)(2,1)S(1)}, bf16[128,1024]{1,0:T(8,128)(2,1)S(1)}, u32[]{:S(2)}, u32[]{:S(2)}) collective-permute-start(bf16[128,1024]{1,0:T(8,128)(2,1)S(1)} %get-tuple-element.62), channel_id=1, source_target_pairs={{0,64},{8,72},{16,80},{24,88},{32,96},{40,104},{48,112},{56,120},{... | collective-permute-start | bytes 786440 | tf_op jit(solution)/shard_map/ppermute | solution.py:59
  156.1 8.6 %collective-permute-start.29 = (bf16[128,1024]{1,0:T(8,128)(2,1)S(1)}, bf16[128,1024]{1,0:T(8,128)(2,1)S(1)}, u32[]{:S(2)}, u32[]{:S(2)}) collective-permute-start(bf16[128,1024]{1,0:T(8,128)(2,1)S(1)} %get-tuple-element.64), channel_id=1, source_target_pairs={{64,0},{72,8},{80,16},{88,24},{96,32},{104,40},{112,48},{120,56},{... | collective-permute-start | bytes 786440 | tf_op jit(solution)/shard_map/ppermute | solution.py:59
  164.5 13.2 %collective-permute-start.28 = (bf16[256,1024]{1,0:T(8,128)(2,1)S(1)}, bf16[256,1024]{1,0:T(8,128)(2,1)S(1)}, u32[]{:S(2)}, u32[]{:S(2)}) collective-permute-start(bf16[256,1024]{1,0:T(8,128)(2,1)S(1)} %pad_maximum_fusion), channel_id=1, source_target_pairs={{0,64},{8,72},{16,80},{24,88},{32,96},{40,104},{48,112},{56,120},{... | collective-permute-start | bytes 1572872 | tf_op jit(solution)/shard_map/ppermute | solution.py:59
  164.8 13.0 %collective-permute-start.30 = (bf16[256,1024]{1,0:T(8,128)(2,1)S(1)}, bf16[256,1024]{1,0:T(8,128)(2,1)S(1)}, u32[]{:S(2)}, u32[]{:S(2)}) collective-permute-start(bf16[256,1024]{1,0:T(8,128)(2,1)S(1)} %pad_maximum_fusion.1), channel_id=1, source_target_pairs={{64,0},{72,8},{80,16},{88,24},{96,32},{104,40},{112,48},{120,56},{... | collective-permute-start | bytes 1572872 | tf_op jit(solution)/shard_map/ppermute | solution.py:59
  (20 other events, 310.7 us)
Sparse Core Ops, SparseCore 0:
  47.0 40.9 all-gather.2
  89.8 39.0 all-gather.4

commit v12 on v10

--- a/solution.py
+++ b/solution.py
@@ -453,7 +453,6 @@
     far_across = both_ways(far_below[:FARS], far_above[FARS:], "seq", X_UP)
     far_all = (far_below, far_above, *far_across)
     inputs_x = lax.all_gather(inputs, "seq", axis=0, axis_index_groups=X_GROUPS, tiled=True)
-    list_above, weights = lax.optimization_barrier((list_above, weights))
     lists = (far_blocks, list_above, list_across, list_below)
     dense = spread(at, lists, far_grad, far_all)
     dense = dense.reshape(NZ, tokens, 2 * DH)
@@ -461,6 +460,7 @@
     kv_grad = finish(terms, back, window)
 
     moved = lax.ppermute(kv_grad, ("seq", "own"), SWAP_XY)
+    moved, inputs_x, weights = lax.optimization_barrier((moved, inputs_x, weights))
     same_core = ring_gather(moved, "own", Y_UP, NY)
     other_core = lax.ppermute(jnp.concatenate([moved, *same_core]), "own", CORES)
     heads = place_heads(own_index, moved, same_core, other_core)

time: 193 us -> 192 us (level)
  starting transfers between devices: 73.5 us -> 57.1 us
  waiting for transfers between devices: 57.5 us -> 71.9 us
  blocking collectives: 22.6 us -> 25.2 us
    ppermute x13, waiting for transfers between devices: 17.5 us -> 36.3 us  [both_ways(): lax.ppermute(upward, axis, pairs)]
    all_gather x1, waiting for transfers between devices: 0.02 us -> 16.3 us  [local(): lax.all_gather(inputs, 'seq', axis=0, axis_index_groups=X_GROUPS, tiled=T...]
    ppermute x13, waiting for transfers between devices: 18 us -> 4.27 us  [both_ways(): lax.ppermute(downward, axis, back)]
    ppermute x13, starting transfers between devices: 17.5 us -> 7.26 us  [both_ways(): lax.ppermute(upward, axis, pairs)]
    all_gather x1, waiting for transfers between devices: 10.1 us -> 0.02 us  [local(): lax.all_gather(weights, 'seq', axis=0, axis_index_groups=Z_GROUPS, tiled=...]
    ppermute x1, starting transfers between devices: 12 us -> 7.76 us  [local(): lax.ppermute(jnp.concatenate([moved, *same_core]), 'own', CORES)]
    all_to_all x1, waiting for transfers between devices: 1.97 us -> 5.13 us  [local(): lax.all_to_all(pieces, 'seq', 0, 0, axis_index_groups=Z_GROUPS, tiled=True)]
    all_to_all x1, blocking collectives: 22.6 us -> 25.2 us  [local(): lax.all_to_all(dense, 'seq', 0, 0, axis_index_groups=Z_GROUPS, tiled=True)]
  transfers between devices with their start and end apart: 34 -> 34, of which waited for: 20 -> 21; matrix products, arithmetic and copies ran while one was open for 1% -> 1% of each run, Pallas kernels for 7% -> 7%
where the time goes in v12:
time: 192 us
  waiting for transfers between devices  71.9 us (37%)
  starting transfers between devices  57.1 us (30%)
  blocking collectives  25.2 us (13%)
  Pallas kernels  18.1 us (9%)
  between operations  14.4 us (8%)
  other arithmetic  2.88 us (2%)
  local copies, waits for them, and re-layouts  2.01 us (1%)
    ppermute x13, waiting for transfers between devices, both_ways(): lax.ppermute(upward, axis, pairs)  36.3 us
    ppermute x13, starting transfers between devices, both_ways(): lax.ppermute(downward, axis, back)  31.2 us
    all_to_all x1, blocking collectives, local(): lax.all_to_all(dense, 'seq', 0, 0, axis_index_groups=Z_GROUPS, tiled=True)  25.2 us
    all_gather x1, waiting for transfers between devices, local(): lax.all_gather(inputs, 'seq', axis=0, axis_index_groups=X_GROUPS, tiled=T...  16.3 us
    pallas_call x1, Pallas kernels, attend(): pl.pallas_call(attend_kernel, out_shape=(jax.ShapeDtypeStruct((NB * BLK,...  9.69 us
    ppermute x1, starting transfers between devices, local(): lax.ppermute(jnp.concatenate([moved, *same_core]), 'own', CORES)  7.76 us
    ppermute x13, starting transfers between devices, both_ways(): lax.ppermute(upward, axis, pairs)  7.26 us
    ppermute x2, waiting for transfers between devices, shifted(): lax.ppermute(value, axis, [(source, source + steps) for source in range(l...  6.88 us
  transfers between devices with their start and end apart: 34, of which 21 were waited for; matrix products, arithmetic and copies ran while one was open for 1% of the time, Pallas kernels for 7%

profile of v12, /device:TPU:1, one launch (start us, length us, event | category | flops | bytes accessed | tf_op | source)
XLA Modules:
  0.0 191.6 jit_solution(1793519155068815402)
XLA Ops:
  8.2 2.5 %collective-permute-start.1 = (bf16[2,128,256]{2,1,0:T(8,128)(2,1)S(1)}, bf16[2,128,256]{2,1,0:T(8,128)(2,1)S(1)}, u32[]{:S(2)}, u32[]{:S(2)}) collective-permute-start(bf16[2,128,256]{2,1,0:T(8,128)(2,1)S(1)} %bitcast.9), channel_id=1, source_target_pairs={{0,8},{8,16},{16,24},{24,32},{32,40},{40,48},{48,56},{56,0},{64,72... | collective-permute-start | bytes 393224 | tf_op jit(solution)/shard_map/ppermute | solution.py:59
  10.8 4.0 %collective-permute-start.2 = (bf16[2,128,256]{2,1,0:T(8,128)(2,1)S(1)}, bf16[2,128,256]{2,1,0:T(8,128)(2,1)S(1)}, u32[]{:S(2)}, u32[]{:S(2)}) collective-permute-start(bf16[2,128,256]{2,1,0:T(8,128)(2,1)S(1)} %bitcast.10), channel_id=1, source_target_pairs={{8,0},{16,8},{24,16},{32,24},{40,32},{48,40},{56,48},{0,56},{72,64... | collective-permute-start | bytes 393224 | tf_op jit(solution)/shard_map/ppermute | solution.py:59
  14.8 2.7 %collective-permute-start.3 = (s32[2,4]{1,0:T(2,128)}, s32[2,4]{1,0:T(2,128)S(1)}, u32[]{:S(2)}, u32[]{:S(2)}) collective-permute-start(s32[2,4]{1,0:T(2,128)} %refs_0_.1), channel_id=1, source_target_pairs={{0,128},{8,136},{16,144},{24,152},{32,160},{40,168},{48,176},{56,1... | collective-permute-start | bytes 104 | tf_op jit(solution)/shard_map/ppermute | solution.py:423
  19.0 2.7 %collective-permute-start.5 = (bf16[2,128,256]{2,1,0:T(8,128)(2,1)S(1)}, bf16[2,128,256]{2,1,0:T(8,128)(2,1)S(1)}, u32[]{:S(2)}, u32[]{:S(2)}) collective-permute-start(bf16[2,128,256]{2,1,0:T(8,128)(2,1)S(1)} %collective-permute-done.2.refs_1_), channel_id=1, source_target_pairs={{8,0},{16,8},{24,16},{32,24},{40,32},{48,40},{56,48},{0,56},{72,64... | collective-permute-start | bytes 393224 | tf_op jit(solution)/shard_map/ppermute | solution.py:59
  21.6 2.4 %collective-permute-done.4.refs_2_ = bf16[2,128,256]{2,1,0:T(8,128)(2,1)S(1)} collective-permute-done((bf16[2,128,256]{2,1,0:T(8,128)(2,1)S(1)}, bf16[2,128,256]{2,1,0:T(8,128)(2,1)S(1)}, u32[]{:S(2)}, u32[]{:S(2)}) %collective-permute-start.4) | collective-permute-done | bytes 131104 | tf_op jit(solution)/shard_map/ppermute | solution.py:59
  24.0 2.7 %collective-permute-start.7 = (bf16[2,128,256]{2,1,0:T(8,128)(2,1)S(1)}, bf16[2,128,256]{2,1,0:T(8,128)(2,1)S(1)}, u32[]{:S(2)}, u32[]{:S(2)}) collective-permute-start(bf16[2,128,256]{2,1,0:T(8,128)(2,1)S(1)} %collective-permute-done.5.refs_3_), channel_id=1, source_target_pairs={{8,0},{16,8},{24,16},{32,24},{40,32},{48,40},{56,48},{0,56},{72,64... | collective-permute-start | bytes 393224 | tf_op jit(solution)/shard_map/ppermute | solution.py:59
  29.1 2.7 %collective-permute-start.9 = (bf16[1,128,256]{2,1,0:T(8,128)(2,1)S(1)}, bf16[1,128,256]{2,1,0:T(8,128)(2,1)S(1)}, u32[]{:S(2)}, u32[]{:S(2)}) collective-permute-start(bf16[1,128,256]{2,1,0:T(8,128)(2,1)S(1)} %slice.46), channel_id=1, source_target_pairs={{8,0},{16,8},{24,16},{32,24},{40,32},{48,40},{56,48},{0,56},{72,64... | collective-permute-start | bytes 196616 | tf_op jit(solution)/shard_map/ppermute | solution.py:59
  43.5 2.7 %collective-permute-start.15 = (bf16[8,128,256]{2,1,0:T(8,128)(2,1)S(1)}, bf16[8,128,256]{2,1,0:T(8,128)(2,1)}, u32[]{:S(2)}, u32[]{:S(2)}) collective-permute-start(bf16[8,128,256]{2,1,0:T(8,128)(2,1)S(1)} %get-tuple-element.46), channel_id=1, source_target_pairs={{64,0},{72,8},{80,16},{88,24},{96,32},{104,40},{112,48},{120,56},{... | collective-permute-start | bytes 1572872 | tf_op jit(solution)/shard_map/ppermute | solution.py:59
  50.4 2.6 %collective-permute-done.14.below_ref = bf16[8,128,256]{2,1,0:T(8,128)(2,1)S(1)} collective-permute-done((bf16[8,128,256]{2,1,0:T(8,128)(2,1)}, bf16[8,128,256]{2,1,0:T(8,128)(2,1)S(1)}, u32[]{:S(2)}, u32[]{:S(2)}) %collective-permute-start.14) | collective-permute-done | bytes 524320 | tf_op jit(solution)/shard_map/ppermute | solution.py:59
  54.9 9.7 %attend.1 = (bf16[256,1024]{1,0:T(8,128)(2,1)}, f32[512,256]{1,0:T(8,128)S(1)}, bf16[8,128,256]{2,1,0:T(8,128)(2,1)S(1)}) custom-call(s32[1]{0:T(128)} %bitcast.at_ref, s32[2,4]{1,0:T(2,128)S(1)} %copy-done.1, s32[2]{0:T(128)S(1)} %copy-done.7, bf16[256,1024]{1,0:T(8,128)(2,1)S(1)} %copy-done.3, bf16[256,1024]{1,0:T(8,128)(2,1)S(1)} %copy-done.4, ...), custom_call_target="tpu_custom_call" | custom-call | flops 9600000000 | bytes 6291456 | tf_op jit(solution)/shard_map/attend/pallas_call | solution.py:219
  64.5 2.4 %collective-permute-start.16 = (bf16[8,128,256]{2,1,0:T(8,128)(2,1)S(1)}, bf16[8,128,256]{2,1,0:T(8,128)(2,1)S(1)}, u32[]{:S(2)}, u32[]{:S(2)}) collective-permute-start(bf16[8,128,256]{2,1,0:T(8,128)(2,1)S(1)} %get-tuple-element.48.refs_4_), channel_id=1, source_target_pairs={{0,64},{8,72},{16,80},{24,88},{32,96},{40,104},{48,112},{56,120},{... | collective-permute-start | bytes 1572872 | tf_op jit(solution)/shard_map/ppermute | solution.py:59
  68.5 5.1 %collective-permute-done.18.back_ref = bf16[256,256]{1,0:T(8,128)(2,1)S(1)} collective-permute-done((bf16[256,256]{1,0:T(8,128)(2,1)S(1)}, bf16[256,256]{1,0:T(8,128)(2,1)S(1)}, u32[]{:S(2)}, u32[]{:S(2)}) %collective-permute-start.18) | collective-permute-done | bytes 131104 | tf_op jit(solution)/shard_map/ppermute | solution.py:54
  77.9 6.9 %collective-permute-done.19.refs_7_ = bf16[4,128,256]{2,1,0:T(8,128)(2,1)S(1)} collective-permute-done((bf16[4,128,256]{2,1,0:T(8,128)(2,1)S(1)}, bf16[4,128,256]{2,1,0:T(8,128)(2,1)S(1)}, u32[]{:S(2)}, u32[]{:S(2)}) %collective-permute-start.19) | collective-permute-done | bytes 262176 | tf_op jit(solution)/shard_map/ppermute | solution.py:59
  86.3 25.2 %all_to_all.10.terms_ref = bf16[8,256,256]{2,1,0:T(8,128)(2,1)S(1)} all-to-all(bf16[8,256,256]{2,1,0:T(8,128)(2,1)S(1)} %bitcast.8), channel_id=1, replica_groups={{0,8,16,24,32,40,48,56},{64,72,80,88,96,104,112,120},{128,136,144,152,1..., dimensions={0} | all-to-all | bytes 2097152 | tf_op jit(solution)/shard_map/all_to_all | solution.py:459
  112.5 16.3 %all-gather.3.cloned.1.call-done.inputs_ref = bf16[1024,1024]{1,0:T(8,128)(2,1)} async-done(((bf16[256,1024]{1,0:T(8,128)(2,1)}), bf16[1024,1024]{1,0:T(8,128)(2,1)}) %all-gather.3.cloned.1.call-update) | async-done | bytes 2097168 | tf_op jit(solution)/shard_map/all_gather | solution.py:455
  128.9 2.7 %collective-permute-start.23 = (bf16[256,256]{1,0:T(8,128)(2,1)S(1)}, bf16[256,256]{1,0:T(8,128)(2,1)S(1)}, u32[]{:S(2)}, u32[]{:S(2)}) collective-permute-start(bf16[256,256]{1,0:T(8,128)(2,1)S(1)} %collective-permute-done.21.own_ref), channel_id=1, source_target_pairs={{2,0},{3,1},{4,2},{5,3},{6,4},{7,5},{0,6},{1,7},{10,8},{11,9},{12,... | collective-permute-start | bytes 393224 | tf_op jit(solution)/shard_map/ppermute | solution.py:59
  134.2 3.1 %collective-permute-start.25 = (bf16[128,256]{1,0:T(8,128)(2,1)S(1)}, bf16[128,256]{1,0:T(8,128)(2,1)S(1)}, u32[]{:S(2)}, u32[]{:S(2)}) collective-permute-start(bf16[128,256]{1,0:T(8,128)(2,1)S(1)} %slice.49), channel_id=1, source_target_pairs={{2,0},{3,1},{4,2},{5,3},{6,4},{7,5},{0,6},{1,7},{10,8},{11,9},{12,... | collective-permute-start | bytes 196616 | tf_op jit(solution)/shard_map/ppermute | solution.py:59
  138.6 7.8 %collective-permute-start.26 = (bf16[1024,256]{1,0:T(8,128)(2,1)S(1)}, bf16[1024,256]{1,0:T(8,128)(2,1)S(1)}, u32[]{:S(2)}, u32[]{:S(2)}) collective-permute-start(bf16[1024,256]{1,0:T(8,128)(2,1)S(1)} %constant_dynamic-update-slice_fusion), channel_id=1, source_target_pairs={{0,1},{1,0},{2,3},{3,2},{4,5},{5,4},{6,7},{7,6},{8,9},{9,8},{10,11... | collective-permute-start | bytes 1572872 | tf_op jit(solution)/shard_map/ppermute | solution.py:465
  150.3 4.4 %all-to-all-start.1 = ((bf16[8,256,256]{2,1,0:T(8,128)(2,1)}), bf16[8,256,256]{2,1,0:T(8,128)(2,1)S(1)}, u32[]{:S(2)}, u32[]{:S(2)}) async-start(bf16[8,256,256]{2,1,0:T(8,128)(2,1)} %weight_terms.1), calls=%async_computation.1 | async-start | bytes 2097152 | tf_op jit(solution)/shard_map/all_to_all | solution.py:471
  156.1 2.7 %collective-permute-start.29 = (bf16[128,1024]{1,0:T(8,128)(2,1)S(1)}, bf16[128,1024]{1,0:T(8,128)(2,1)S(1)}, u32[]{:S(2)}, u32[]{:S(2)}) collective-permute-start(bf16[128,1024]{1,0:T(8,128)(2,1)S(1)} %get-tuple-element.62), channel_id=1, source_target_pairs={{64,0},{72,8},{80,16},{88,24},{96,32},{104,40},{112,48},{120,56},{... | collective-permute-start | bytes 786440 | tf_op jit(solution)/shard_map/ppermute | solution.py:59
  158.8 5.6 %collective-permute-done.27 = bf16[128,1024]{1,0:T(8,128)(2,1)S(1)} collective-permute-done((bf16[128,1024]{1,0:T(8,128)(2,1)S(1)}, bf16[128,1024]{1,0:T(8,128)(2,1)S(1)}, u32[]{:S(2)}, u32[]{:S(2)}) %collective-permute-start.27) | collective-permute-done | bytes 262176 | tf_op jit(solution)/shard_map/ppermute | solution.py:59
  164.8 2.7 %collective-permute-start.30 = (bf16[256,1024]{1,0:T(8,128)(2,1)S(1)}, bf16[256,1024]{1,0:T(8,128)(2,1)S(1)}, u32[]{:S(2)}, u32[]{:S(2)}) collective-permute-start(bf16[256,1024]{1,0:T(8,128)(2,1)S(1)} %pad_maximum_fusion.1), channel_id=1, source_target_pairs={{64,0},{72,8},{80,16},{88,24},{96,32},{104,40},{112,48},{120,56},{... | collective-permute-start | bytes 1572872 | tf_op jit(solution)/shard_map/ppermute | solution.py:59
  167.5 10.2 %collective-permute-done.28 = bf16[256,1024]{1,0:T(8,128)(2,1)S(1)} collective-permute-done((bf16[256,1024]{1,0:T(8,128)(2,1)S(1)}, bf16[256,1024]{1,0:T(8,128)(2,1)S(1)}, u32[]{:S(2)}, u32[]{:S(2)}) %collective-permute-start.28) | collective-permute-done | bytes 524320 | tf_op jit(solution)/shard_map/ppermute | solution.py:59
  178.8 5.1 %all-to-all-done.1.terms_ref = bf16[8,256,256]{2,1,0:T(8,128)(2,1)S(1)} async-done(((bf16[8,256,256]{2,1,0:T(8,128)(2,1)}), bf16[8,256,256]{2,1,0:T(8,128)(2,1)S(1)}, u32[]{:S(2)}, u32[]{:S(2)}) %all-to-all-start.1) | async-done | bytes 1048608 | tf_op jit(solution)/shard_map/all_to_all | solution.py:471
  (97 shorter events, 42.2 us)
Async XLA Ops:
  7.2 105.3 %all-gather.5.cloned.1.call-start = ((), (), s32[]{:S(2)}) async-start(), calls=%async_computation.3 | async-start | bytes 1179648 | tf_op jit(solution)/shard_map/all_gather | solution.py:439
  8.2 10.7 %collective-permute-start.1 = (bf16[2,128,256]{2,1,0:T(8,128)(2,1)S(1)}, bf16[2,128,256]{2,1,0:T(8,128)(2,1)S(1)}, u32[]{:S(2)}, u32[]{:S(2)}) collective-permute-start(bf16[2,128,256]{2,1,0:T(8,128)(2,1)S(1)} %bitcast.9), channel_id=1, source_target_pairs={{0,8},{8,16},{16,24},{24,32},{32,40},{40,48},{48,56},{56,0},{64,72... | collective-permute-start | bytes 393224 | tf_op jit(solution)/shard_map/ppermute | solution.py:59
  10.8 8.2 %collective-permute-start.2 = (bf16[2,128,256]{2,1,0:T(8,128)(2,1)S(1)}, bf16[2,128,256]{2,1,0:T(8,128)(2,1)S(1)}, u32[]{:S(2)}, u32[]{:S(2)}) collective-permute-start(bf16[2,128,256]{2,1,0:T(8,128)(2,1)S(1)} %bitcast.10), channel_id=1, source_target_pairs={{8,0},{16,8},{24,16},{32,24},{40,32},{48,40},{56,48},{0,56},{72,64... | collective-permute-start | bytes 393224 | tf_op jit(solution)/shard_map/ppermute | solution.py:59
  19.0 5.0 %collective-permute-start.4 = (bf16[2,128,256]{2,1,0:T(8,128)(2,1)S(1)}, bf16[2,128,256]{2,1,0:T(8,128)(2,1)S(1)}, u32[]{:S(2)}, u32[]{:S(2)}) collective-permute-start(bf16[2,128,256]{2,1,0:T(8,128)(2,1)S(1)} %collective-permute-done.1.refs_0_), channel_id=1, source_target_pairs={{0,8},{8,16},{16,24},{24,32},{32,40},{40,48},{48,56},{56,0},{64,72... | collective-permute-start | bytes 393224 | tf_op jit(solution)/shard_map/ppermute | solution.py:59
  24.0 5.0 %collective-permute-start.6 = (bf16[2,128,256]{2,1,0:T(8,128)(2,1)S(1)}, bf16[2,128,256]{2,1,0:T(8,128)(2,1)S(1)}, u32[]{:S(2)}, u32[]{:S(2)}) collective-permute-start(bf16[2,128,256]{2,1,0:T(8,128)(2,1)S(1)} %collective-permute-done.4.refs_2_), channel_id=1, source_target_pairs={{0,8},{8,16},{16,24},{24,32},{32,40},{40,48},{48,56},{56,0},{64,72... | collective-permute-start | bytes 393224 | tf_op jit(solution)/shard_map/ppermute | solution.py:59
  24.0 5.0 %collective-permute-start.7 = (bf16[2,128,256]{2,1,0:T(8,128)(2,1)S(1)}, bf16[2,128,256]{2,1,0:T(8,128)(2,1)S(1)}, u32[]{:S(2)}, u32[]{:S(2)}) collective-permute-start(bf16[2,128,256]{2,1,0:T(8,128)(2,1)S(1)} %collective-permute-done.5.refs_3_), channel_id=1, source_target_pairs={{8,0},{16,8},{24,16},{32,24},{40,32},{48,40},{56,48},{0,56},{72,64... | collective-permute-start | bytes 393224 | tf_op jit(solution)/shard_map/ppermute | solution.py:59
  34.1 7.9 %collective-permute-start.12 = (bf16[4,128,256]{2,1,0:T(8,128)(2,1)S(1)}, bf16[4,128,256]{2,1,0:T(8,128)(2,1)S(1)}, u32[]{:S(2)}, u32[]{:S(2)}) collective-permute-start(bf16[4,128,256]{2,1,0:T(8,128)(2,1)S(1)} %get-tuple-element.43), channel_id=1, source_target_pairs={{0,64},{8,72},{16,80},{24,88},{32,96},{40,104},{48,112},{56,120},{... | collective-permute-start | bytes 786440 | tf_op jit(solution)/shard_map/ppermute | solution.py:59
  35.4 6.6 %collective-permute-start.13 = (bf16[4,128,256]{2,1,0:T(8,128)(2,1)S(1)}, bf16[4,128,256]{2,1,0:T(8,128)(2,1)S(1)}, u32[]{:S(2)}, u32[]{:S(2)}) collective-permute-start(bf16[4,128,256]{2,1,0:T(8,128)(2,1)S(1)} %get-tuple-element.44), channel_id=1, source_target_pairs={{64,0},{72,8},{80,16},{88,24},{96,32},{104,40},{112,48},{120,56},{... | collective-permute-start | bytes 786440 | tf_op jit(solution)/shard_map/ppermute | solution.py:59
  43.5 9.5 %collective-permute-start.14 = (bf16[8,128,256]{2,1,0:T(8,128)(2,1)}, bf16[8,128,256]{2,1,0:T(8,128)(2,1)S(1)}, u32[]{:S(2)}, u32[]{:S(2)}) collective-permute-start(bf16[8,128,256]{2,1,0:T(8,128)(2,1)} %get-tuple-element.45), channel_id=1, source_target_pairs={{0,64},{8,72},{16,80},{24,88},{32,96},{40,104},{48,112},{56,120},{... | collective-permute-start | bytes 1572872 | tf_op jit(solution)/shard_map/ppermute | solution.py:59
  43.5 10.3 %collective-permute-start.15 = (bf16[8,128,256]{2,1,0:T(8,128)(2,1)S(1)}, bf16[8,128,256]{2,1,0:T(8,128)(2,1)}, u32[]{:S(2)}, u32[]{:S(2)}) collective-permute-start(bf16[8,128,256]{2,1,0:T(8,128)(2,1)S(1)} %get-tuple-element.46), channel_id=1, source_target_pairs={{64,0},{72,8},{80,16},{88,24},{96,32},{104,40},{112,48},{120,56},{... | collective-permute-start | bytes 1572872 | tf_op jit(solution)/shard_map/ppermute | solution.py:59
  46.9 82.0 %all-gather.3.cloned.1.call-start = ((), (), s32[]{:S(2)}) async-start(), calls=%async_computation.2 | async-start | bytes 2621440 | tf_op jit(solution)/shard_map/all_gather | solution.py:455
  64.5 9.2 %collective-permute-start.16 = (bf16[8,128,256]{2,1,0:T(8,128)(2,1)S(1)}, bf16[8,128,256]{2,1,0:T(8,128)(2,1)S(1)}, u32[]{:S(2)}, u32[]{:S(2)}) collective-permute-start(bf16[8,128,256]{2,1,0:T(8,128)(2,1)S(1)} %get-tuple-element.48.refs_4_), channel_id=1, source_target_pairs={{0,64},{8,72},{16,80},{24,88},{32,96},{40,104},{48,112},{56,120},{... | collective-permute-start | bytes 1572872 | tf_op jit(solution)/shard_map/ppermute | solution.py:59
  67.0 8.0 %collective-permute-start.17 = (bf16[8,128,256]{2,1,0:T(8,128)(2,1)S(1)}, bf16[8,128,256]{2,1,0:T(8,128)(2,1)S(1)}, u32[]{:S(2)}, u32[]{:S(2)}) collective-permute-start(bf16[8,128,256]{2,1,0:T(8,128)(2,1)S(1)} %get-tuple-element.48.refs_4_), channel_id=1, source_target_pairs={{64,0},{72,8},{80,16},{88,24},{96,32},{104,40},{112,48},{120,56},{... | collective-permute-start | bytes 1572872 | tf_op jit(solution)/shard_map/ppermute | solution.py:59
  67.2 6.4 %collective-permute-start.18 = (bf16[256,256]{1,0:T(8,128)(2,1)S(1)}, bf16[256,256]{1,0:T(8,128)(2,1)S(1)}, u32[]{:S(2)}, u32[]{:S(2)}) collective-permute-start(bf16[256,256]{1,0:T(8,128)(2,1)S(1)} %slice.53), channel_id=1, source_target_pairs={{8,0},{16,8},{24,16},{32,24},{40,32},{48,40},{56,48},{64,56},{72,6... | collective-permute-start | bytes 393224 | tf_op jit(solution)/shard_map/ppermute | solution.py:54
  75.1 9.8 %collective-permute-start.19 = (bf16[4,128,256]{2,1,0:T(8,128)(2,1)S(1)}, bf16[4,128,256]{2,1,0:T(8,128)(2,1)S(1)}, u32[]{:S(2)}, u32[]{:S(2)}) collective-permute-start(bf16[4,128,256]{2,1,0:T(8,128)(2,1)S(1)} %slice.37), channel_id=1, source_target_pairs={{0,64},{8,72},{16,80},{24,88},{32,96},{40,104},{48,112},{56,120},{... | collective-permute-start | bytes 786440 | tf_op jit(solution)/shard_map/ppermute | solution.py:59
  75.7 9.1 %collective-permute-start.20 = (bf16[4,128,256]{2,1,0:T(8,128)(2,1)S(1)}, bf16[4,128,256]{2,1,0:T(8,128)(2,1)S(1)}, u32[]{:S(2)}, u32[]{:S(2)}) collective-permute-start(bf16[4,128,256]{2,1,0:T(8,128)(2,1)S(1)} %slice.38), channel_id=1, source_target_pairs={{64,0},{72,8},{80,16},{88,24},{96,32},{104,40},{112,48},{120,56},{... | collective-permute-start | bytes 786440 | tf_op jit(solution)/shard_map/ppermute | solution.py:59
  128.9 5.0 %collective-permute-start.22 = (bf16[256,256]{1,0:T(8,128)(2,1)S(1)}, bf16[256,256]{1,0:T(8,128)(2,1)S(1)}, u32[]{:S(2)}, u32[]{:S(2)}) collective-permute-start(bf16[256,256]{1,0:T(8,128)(2,1)S(1)} %collective-permute-done.21.own_ref), channel_id=1, source_target_pairs={{0,2},{1,3},{2,4},{3,5},{4,6},{5,7},{6,0},{7,1},{8,10},{9,11},{10,... | collective-permute-start | bytes 393224 | tf_op jit(solution)/shard_map/ppermute | solution.py:59
  128.9 5.3 %collective-permute-start.23 = (bf16[256,256]{1,0:T(8,128)(2,1)S(1)}, bf16[256,256]{1,0:T(8,128)(2,1)S(1)}, u32[]{:S(2)}, u32[]{:S(2)}) collective-permute-start(bf16[256,256]{1,0:T(8,128)(2,1)S(1)} %collective-permute-done.21.own_ref), channel_id=1, source_target_pairs={{2,0},{3,1},{4,2},{5,3},{6,4},{7,5},{0,6},{1,7},{10,8},{11,9},{12,... | collective-permute-start | bytes 393224 | tf_op jit(solution)/shard_map/ppermute | solution.py:59
  138.6 9.3 %collective-permute-start.26 = (bf16[1024,256]{1,0:T(8,128)(2,1)S(1)}, bf16[1024,256]{1,0:T(8,128)(2,1)S(1)}, u32[]{:S(2)}, u32[]{:S(2)}) collective-permute-start(bf16[1024,256]{1,0:T(8,128)(2,1)S(1)} %constant_dynamic-update-slice_fusion), channel_id=1, source_target_pairs={{0,1},{1,0},{2,3},{3,2},{4,5},{5,4},{6,7},{7,6},{8,9},{9,8},{10,11... | collective-permute-start | bytes 1572872 | tf_op jit(solution)/shard_map/ppermute | solution.py:465
  150.3 33.6 %all-to-all-start.1 = ((bf16[8,256,256]{2,1,0:T(8,128)(2,1)}), bf16[8,256,256]{2,1,0:T(8,128)(2,1)S(1)}, u32[]{:S(2)}, u32[]{:S(2)}) async-start(bf16[8,256,256]{2,1,0:T(8,128)(2,1)} %weight_terms.1), calls=%async_computation.1 | async-start | bytes 2097152 | tf_op jit(solution)/shard_map/all_to_all | solution.py:471
  155.9 8.5 %collective-permute-start.27 = (bf16[128,1024]{1,0:T(8,128)(2,1)S(1)}, bf16[128,1024]{1,0:T(8,128)(2,1)S(1)}, u32[]{:S(2)}, u32[]{:S(2)}) collective-permute-start(bf16[128,1024]{1,0:T(8,128)(2,1)S(1)} %get-tuple-element.60), channel_id=1, source_target_pairs={{0,64},{8,72},{16,80},{24,88},{32,96},{40,104},{48,112},{56,120},{... | collective-permute-start | bytes 786440 | tf_op jit(solution)/shard_map/ppermute | solution.py:59
  156.1 8.6 %collective-permute-start.29 = (bf16[128,1024]{1,0:T(8,128)(2,1)S(1)}, bf16[128,1024]{1,0:T(8,128)(2,1)S(1)}, u32[]{:S(2)}, u32[]{:S(2)}) collective-permute-start(bf16[128,1024]{1,0:T(8,128)(2,1)S(1)} %get-tuple-element.62), channel_id=1, source_target_pairs={{64,0},{72,8},{80,16},{88,24},{96,32},{104,40},{112,48},{120,56},{... | collective-permute-start | bytes 786440 | tf_op jit(solution)/shard_map/ppermute | solution.py:59
  164.5 13.2 %collective-permute-start.28 = (bf16[256,1024]{1,0:T(8,128)(2,1)S(1)}, bf16[256,1024]{1,0:T(8,128)(2,1)S(1)}, u32[]{:S(2)}, u32[]{:S(2)}) collective-permute-start(bf16[256,1024]{1,0:T(8,128)(2,1)S(1)} %pad_maximum_fusion), channel_id=1, source_target_pairs={{0,64},{8,72},{16,80},{24,88},{32,96},{40,104},{48,112},{56,120},{... | collective-permute-start | bytes 1572872 | tf_op jit(solution)/shard_map/ppermute | solution.py:59
  164.8 13.0 %collective-permute-start.30 = (bf16[256,1024]{1,0:T(8,128)(2,1)S(1)}, bf16[256,1024]{1,0:T(8,128)(2,1)S(1)}, u32[]{:S(2)}, u32[]{:S(2)}) collective-permute-start(bf16[256,1024]{1,0:T(8,128)(2,1)S(1)} %pad_maximum_fusion.1), channel_id=1, source_target_pairs={{64,0},{72,8},{80,16},{88,24},{96,32},{104,40},{112,48},{120,56},{... | collective-permute-start | bytes 1572872 | tf_op jit(solution)/shard_map/ppermute | solution.py:59
  (20 other events, 310.8 us)
Sparse Core Ops, SparseCore 0:
  47.0 40.9 all-gather.4
  89.8 39.0 all-gather.2
